TPU v7x, 32 devices: a whole 2x2x4 slice. The times are simulated.
32 devices in a mesh: seq: 2 (over x), fsdp: 16 (over z, y, core).
Axes of the slice: x: 2, y: 2, z: 4, core: 2. Of those that a mesh axis runs over, the one named last changes fastest.
Arguments:
- hidden_in: bfloat16 [16, 2, 192, 2560], P('fsdp', 'seq'), may hold values from -6 to 6
- cotangent: bfloat16 [16, 2, 192, 2560], P('fsdp', 'seq'), may hold values from -6 to 6
- lengths: int32 [2, 3], replicated, may hold values from 1 to 2560, 3072 in all within a row
- weight_qkv: float32 [2560, 3072], P('fsdp'), may hold values from -0.125 to 0.125
- first_qkv: float32 [2560, 3072], P('fsdp'), may hold values from -160 to 160
- second_qkv: float32 [2560, 3072], P('fsdp'), may hold values from 2764.8 to 11059.2
- weight_out: float32 [2560, 2560], P('fsdp'), may hold values from -2 to 2
- first_out: float32 [2560, 2560], P('fsdp'), may hold values from -6 to 6
- second_out: float32 [2560, 2560], P('fsdp'), may hold values from 1.50528 to 6.02112
- weight_mlp: float32 [2560, 3, 7680], P('fsdp'), may hold values from -0.125 to 0.125
- first_mlp: float32 [2560, 3, 7680], P('fsdp'), may hold values from -32 to 32
- second_mlp: float32 [2560, 3, 7680], P('fsdp'), may hold values from 110.592 to 442.368
- norm_gains: float32 [2560, 2], P('fsdp'), may hold values from 0.5 to 1.5
- first_gains: float32 [2560, 2], P('fsdp'), may hold values from -128 to 128
- second_gains: float32 [2560, 2], P('fsdp'), may hold values from 1904.64 to 7680
Outputs:
- hidden_out: bfloat16 [16, 2, 192, 2560], P('fsdp', 'seq')
- hidden_grad: float32 [16, 2, 192, 2560], P('fsdp', 'seq')
- grad_qkv: float32 [2560, 3072], P('fsdp')
- new_second_qkv: float32 [2560, 3072], P('fsdp')
- new_qkv: float32 [2560, 3072], P('fsdp')
- grad_out: float32 [2560, 2560], P('fsdp')
- new_second_out: float32 [2560, 2560], P('fsdp')
- new_out: float32 [2560, 2560], P('fsdp')
- grad_mlp: float32 [2560, 3, 7680], P('fsdp')
- new_second_mlp: float32 [2560, 3, 7680], P('fsdp')
- new_mlp: float32 [2560, 3, 7680], P('fsdp')
- grad_gains: float32 [2560, 2], P('fsdp')
- new_second_gains: float32 [2560, 2], P('fsdp')
- new_gains: float32 [2560, 2], P('fsdp')
Inputs may be any that keep to these rules, and one draw needn't show every extreme that they name: Each row holds the lengths of 3 documents packed in order into one sequence of 3072 tokens; a row sums to 3072 and its longest document has exactly 2560 tokens.
All inputs are finite; a program needn't handle non-finite values.
Results may differ from a plain program's by a relative error of at most 0.02.
Values may be sent and summed in bfloat16 or wider, within the bound.
No kernel may reach another device: no remote copies, remote signals or barrier semaphores. Data moves between devices by JAX's collectives and lax.ppermute only.
A program may use at most 648 MiB of HBM per device.

v0:
```python
import math

import jax
import jax.numpy as jnp
from jax import lax
from jax.sharding import PartitionSpec as P

D = 2560
HEAD_DIM = 256
WINDOW = 2048
STEP = 10
SEQ_LEN = 3072
BACK = 6


NORM_EPS = 1e-06
BETA_ONE = 0.9
BETA_TWO = 0.95
ADAM_EPS = 1e-08
DECAY_RATE = 0.1
MASKED_SCORE = -1e30


def passed_along(value, axis, steps):
    count = lax.axis_size(axis)
    initial, last = (max(0, -steps), min(count, count - steps))
    return lax.ppermute(value, axis, [(source, source + steps) for source in range(initial, last)])


def rms_norm(values, gain):
    factor = lax.rsqrt(jnp.mean(values * values, axis=-1, keepdims=True) + NORM_EPS)
    return values * factor * gain


def rotate(values, cosine, sine):
    half_dim = values.shape[-1] // 2
    first_half = values[..., :half_dim]
    second_half = values[..., half_dim:]
    return jnp.concatenate(
        [first_half * cosine - second_half * sine, second_half * cosine + first_half * sine],
        axis=-1,
    )


def doc_places(lengths_row, offsets):
    doc_ends = jnp.cumsum(lengths_row)
    passed = (doc_ends[None, :] <= offsets[:, None]).astype(jnp.int32)
    document = jnp.sum(passed, axis=1)
    starts = jnp.sum(passed * lengths_row[None, :], axis=1)
    return (document, offsets - starts)


def rope_angles(places, head_dim):
    freq_index = jnp.arange(head_dim // 2, dtype=jnp.float32)
    inverse = jnp.exp(freq_index * (-2.0 * math.log(10000.0) / head_dim))
    angles = places.astype(jnp.float32)[:, None] * inverse[None, :]
    return (jnp.cos(angles), jnp.sin(angles))


def adam_step(weight, first, second, grad, rate):
    first_new = BETA_ONE * first + (1.0 - BETA_ONE) * grad
    second_new = BETA_TWO * second + (1.0 - BETA_TWO) * grad * grad
    first_hat = first_new / (1.0 - BETA_ONE**STEP)
    second_hat = second_new / (1.0 - BETA_TWO**STEP)
    update = first_hat / (jnp.sqrt(second_hat) + ADAM_EPS)
    return (second_new, weight - rate * (update + DECAY_RATE * weight))


def glu_values(gate_in, up_in):
    return jax.nn.gelu(gate_in, approximate=True) * up_in


def split_halves(term, owners, halves):
    rows = term.shape[0]
    cols = term.shape[1]
    halved = term.reshape(rows, halves, cols // halves).transpose(1, 0, 2)
    return halved.reshape(halves * owners, rows // owners, cols // halves)


def join_halves(pieces):
    halves = pieces.shape[0]
    return pieces.transpose(1, 0, 2).reshape(pieces.shape[1], halves * pieces.shape[2])


def on_device(
    hidden_in,
    cotangent,
    lengths,
    weight_qkv,
    first_qkv,
    second_qkv,
    weight_out,
    first_out,
    second_out,
    weight_mlp,
    first_mlp,
    second_mlp,
    norm_gains,
    first_gains,
    second_gains,
):
    tok_rows = hidden_in.shape[2]
    width = hidden_in.shape[3]
    head_count = width // HEAD_DIM
    pair_rows = lax.axis_size("seq") * tok_rows
    tokens = hidden_in.reshape(tok_rows, width).astype(jnp.float32)
    incoming = cotangent.reshape(tok_rows, width)
    pair_index = lax.axis_index("fsdp")
    first_row = (pair_index * lax.axis_size("seq") + lax.axis_index("seq")) * tok_rows
    packed_index = pair_index * pair_rows // SEQ_LEN
    seq_start = packed_index * SEQ_LEN
    lengths_row = lax.dynamic_index_in_dim(lengths, packed_index, 0, keepdims=False)
    query_docs, query_places = doc_places(
        lengths_row, first_row - seq_start + jnp.arange(tok_rows, dtype=jnp.int32)
    )
    key_offsets = (
        (pair_index - BACK) * pair_rows
        - seq_start
        + jnp.arange((BACK + 1) * pair_rows, dtype=jnp.int32)
    )
    key_docs, key_places = doc_places(lengths_row, key_offsets)
    key_docs = jnp.where(key_offsets >= 0, key_docs, -1)
    distance = query_places[:, None] - key_places[None, :]
    allowed = (query_docs[:, None] == key_docs[None, :]) & (distance >= 0) & (distance < WINDOW)
    cosine, sine = rope_angles(query_places, HEAD_DIM)
    query_scale = HEAD_DIM ** (-0.5)
    qkv_full, out_full, gains_full = (
        lax.all_gather(weight_qkv.astype(jnp.bfloat16), "fsdp", axis=0, tiled=True),
        lax.all_gather(weight_out.astype(jnp.bfloat16), "fsdp", axis=0, tiled=True),
        lax.all_gather(norm_gains.astype(jnp.bfloat16), "fsdp", axis=0, tiled=True),
    )
    gain_one = gains_full[:, 0].astype(jnp.float32)
    gain_two = gains_full[:, 1].astype(jnp.float32)
    normed, norm_back_one = jax.vjp(rms_norm, tokens, gain_one)
    normed_low = normed.astype(jnp.bfloat16)
    projected = jnp.dot(normed_low, qkv_full, preferred_element_type=jnp.float32)
    query_pre = projected[:, :width].reshape(tok_rows, head_count, HEAD_DIM)
    key_pre = projected[:, width : width + HEAD_DIM]
    value_low = projected[:, width + HEAD_DIM :].astype(jnp.bfloat16)
    queries = (rotate(query_pre, cosine[:, None, :], sine[:, None, :]) * query_scale).astype(
        jnp.bfloat16
    )
    key_low = rotate(key_pre, cosine, sine).astype(jnp.bfloat16)
    local_kv = jnp.concatenate([key_low, value_low], axis=1)
    pair_kv = lax.all_gather(local_kv, "seq", axis=0, tiled=True)
    earlier = [passed_along(pair_kv, "fsdp", BACK - position) for position in range(BACK)]
    window_kv = jnp.concatenate(earlier + [pair_kv], axis=0)
    keys_win = window_kv[:, :HEAD_DIM]
    values_win = window_kv[:, HEAD_DIM:]
    scores = jnp.einsum("thd,kd->thk", queries, keys_win, preferred_element_type=jnp.float32)
    scores = jnp.where(allowed[:, None, :], scores, MASKED_SCORE)
    row_top = jnp.max(scores, axis=-1, keepdims=True)
    exps = jnp.exp(scores - row_top)
    totals = jnp.sum(exps, axis=-1, keepdims=True)
    probs = exps / totals
    log_total = row_top + jnp.log(totals)
    mixed = jnp.einsum(
        "thk,kd->thd", probs.astype(jnp.bfloat16), values_win, preferred_element_type=jnp.float32
    )
    attn_low = mixed.astype(jnp.bfloat16).reshape(tok_rows, width)
    middle = tokens + jnp.dot(attn_low, out_full, preferred_element_type=jnp.float32)
    mlp_full = lax.all_gather(weight_mlp.astype(jnp.bfloat16), "fsdp", axis=0, tiled=True)
    normed_two, norm_back_two = jax.vjp(rms_norm, middle, gain_two)
    normed_two_low = normed_two.astype(jnp.bfloat16)
    gate_up = jnp.einsum(
        "td,dcf->tcf", normed_two_low, mlp_full[:, :2, :], preferred_element_type=jnp.float32
    )
    activated, glu_back = jax.vjp(glu_values, gate_up[:, 0, :], gate_up[:, 1, :])
    activated_low = activated.astype(jnp.bfloat16)
    result = middle + jnp.einsum(
        "tf,df->td", activated_low, mlp_full[:, 2, :], preferred_element_type=jnp.float32
    )
    hidden_out = result.astype(jnp.bfloat16).reshape(1, 1, tok_rows, width)
    mlp_back = lax.all_gather(weight_mlp.astype(jnp.bfloat16), "fsdp", axis=0, tiled=True)
    grad_act = jnp.einsum(
        "td,df->tf", incoming, mlp_back[:, 2, :], preferred_element_type=jnp.float32
    ).astype(jnp.bfloat16)
    grad_gate, grad_up = glu_back(grad_act.astype(jnp.float32))
    grad_gate_up = jnp.stack([grad_gate, grad_up], axis=1).astype(jnp.bfloat16)
    grad_normed_two = jnp.einsum(
        "tcf,dcf->td", grad_gate_up, mlp_back[:, :2, :], preferred_element_type=jnp.float32
    )
    grad_middle_norm, grad_gain_two = norm_back_two(grad_normed_two)
    grad_middle = incoming.astype(jnp.float32) + grad_middle_norm
    own_rows = weight_mlp.shape[0]
    ff_width = weight_mlp.shape[2]
    seq_count = lax.axis_size("seq")
    fsdp_count = lax.axis_size("fsdp")
    half_ff = ff_width // seq_count

    def one_piece(index):
        owner = index % fsdp_count
        column_half = index // fsdp_count
        rows_two = lax.dynamic_slice_in_dim(normed_two_low, owner * own_rows, own_rows, 1)
        rows_back = lax.dynamic_slice_in_dim(incoming, owner * own_rows, own_rows, 1)
        grads_half = lax.dynamic_slice_in_dim(grad_gate_up, column_half * half_ff, half_ff, 2)
        act_half = lax.dynamic_slice_in_dim(activated_low, column_half * half_ff, half_ff, 1)
        upper = jnp.einsum("td,tcf->dcf", rows_two, grads_half, preferred_element_type=jnp.float32)
        lower = jnp.einsum("td,tf->df", rows_back, act_half, preferred_element_type=jnp.float32)
        return jnp.concatenate([upper, lower[:, None, :]], axis=1)

    mlp_piece = lax.psum_scatter(
        lax.map(one_piece, jnp.arange(1 * lax.axis_size(("seq", "fsdp")), dtype=jnp.int32)),
        ("seq", "fsdp"),
        scatter_dimension=0,
        tiled=True,
    )
    qkv_back, out_back = (
        lax.all_gather(weight_qkv.astype(jnp.bfloat16), "fsdp", axis=0, tiled=True),
        lax.all_gather(weight_out.astype(jnp.bfloat16), "fsdp", axis=0, tiled=True),
    )
    grad_branch_low = grad_middle.astype(jnp.bfloat16)
    grad_mixed = jnp.einsum(
        "te,de->td", grad_branch_low, out_back, preferred_element_type=jnp.float32
    )
    grad_mixed_low = grad_mixed.astype(jnp.bfloat16).reshape(tok_rows, head_count, HEAD_DIM)
    out_term = jnp.einsum(
        "td,te->de", attn_low, grad_branch_low, preferred_element_type=jnp.float32
    )
    scores_again = jnp.einsum("thd,kd->thk", queries, keys_win, preferred_element_type=jnp.float32)
    scores_again = jnp.where(allowed[:, None, :], scores_again, MASKED_SCORE)
    probs_again = jnp.exp(scores_again - log_total)
    grad_probs = jnp.einsum(
        "thd,kd->thk", grad_mixed_low, values_win, preferred_element_type=jnp.float32
    )
    row_delta = jnp.sum(probs_again * grad_probs, axis=-1, keepdims=True)
    grad_scores = (probs_again * (grad_probs - row_delta)).astype(jnp.bfloat16)
    grad_query = jnp.einsum(
        "thk,kd->thd", grad_scores, keys_win, preferred_element_type=jnp.float32
    )
    grad_keys = jnp.einsum("thk,thd->kd", grad_scores, queries, preferred_element_type=jnp.float32)
    grad_values = jnp.einsum(
        "thk,thd->kd",
        probs_again.astype(jnp.bfloat16),
        grad_mixed_low,
        preferred_element_type=jnp.float32,
    )
    grad_window = jnp.concatenate([grad_keys, grad_values], axis=1)
    grad_pair = grad_window[BACK * pair_rows :]
    for position in range(BACK):
        grad_pair = grad_pair + passed_along(
            grad_window[position * pair_rows : (position + 1) * pair_rows].astype(jnp.bfloat16),
            "fsdp",
            position - BACK,
        ).astype(jnp.float32)
    grad_local = lax.psum_scatter(
        grad_pair.astype(jnp.bfloat16), "seq", scatter_dimension=0, tiled=True
    ).astype(jnp.float32)
    grad_query_pre = rotate(
        grad_query * query_scale, cosine[:, None, :], -sine[:, None, :]
    ).reshape(tok_rows, width)
    grad_key_pre = rotate(grad_local[:, :HEAD_DIM], cosine, -sine)
    grad_proj = jnp.concatenate(
        [grad_query_pre, grad_key_pre, grad_local[:, HEAD_DIM:]], axis=1
    ).astype(jnp.bfloat16)
    grad_normed = jnp.einsum("tc,dc->td", grad_proj, qkv_back, preferred_element_type=jnp.float32)
    qkv_term = jnp.einsum("td,tc->dc", normed_low, grad_proj, preferred_element_type=jnp.float32)
    grad_tokens_norm, grad_gain_one = norm_back_one(grad_normed)
    hidden_grad = (grad_middle + grad_tokens_norm).reshape(1, 1, tok_rows, width)
    gains_term = jnp.stack([grad_gain_one, grad_gain_two], axis=1)
    qkv_piece, out_piece, gains_piece = (
        lax.psum_scatter(
            split_halves(qkv_term, fsdp_count, seq_count),
            ("seq", "fsdp"),
            scatter_dimension=0,
            tiled=True,
        ),
        lax.psum_scatter(
            split_halves(out_term, fsdp_count, seq_count),
            ("seq", "fsdp"),
            scatter_dimension=0,
            tiled=True,
        ),
        lax.psum_scatter(
            split_halves(gains_term, fsdp_count, seq_count),
            ("seq", "fsdp"),
            scatter_dimension=0,
            tiled=True,
        ),
    )
    mlp_flat = mlp_piece.reshape(1, own_rows, 3 * (ff_width // seq_count))
    qkv_all, out_all, mlp_all, gains_all = (
        lax.all_gather(qkv_piece.astype(jnp.bfloat16), "seq", axis=0, tiled=True).astype(
            qkv_piece.dtype
        ),
        lax.all_gather(out_piece.astype(jnp.bfloat16), "seq", axis=0, tiled=True).astype(
            out_piece.dtype
        ),
        lax.all_gather(mlp_flat.astype(jnp.bfloat16), "seq", axis=0, tiled=True).astype(
            mlp_flat.dtype
        ),
        lax.all_gather(gains_piece.astype(jnp.bfloat16), "seq", axis=0, tiled=True).astype(
            gains_piece.dtype
        ),
    )
    grad_qkv = join_halves(qkv_all)
    grad_out = join_halves(out_all)
    grad_gains = join_halves(gains_all)
    grad_mlp = (
        mlp_all.reshape(seq_count, own_rows, 3, ff_width // seq_count)
        .transpose(1, 2, 0, 3)
        .reshape(own_rows, 3, ff_width)
    )
    rate_main = 2.0 * D ** (-0.5)
    rate_out = 2.0 * max(1, 6 * D // WINDOW) ** (-0.5)
    rate_gains = 0.4
    second_new_qkv, new_qkv = adam_step(weight_qkv, first_qkv, second_qkv, grad_qkv, rate_main)
    second_new_out, new_out = adam_step(weight_out, first_out, second_out, grad_out, rate_out)
    second_new_mlp, new_mlp = adam_step(weight_mlp, first_mlp, second_mlp, grad_mlp, rate_main)
    second_new_gains, new_gains = adam_step(
        norm_gains, first_gains, second_gains, grad_gains, rate_gains
    )
    return (
        hidden_out,
        hidden_grad,
        grad_qkv,
        second_new_qkv,
        new_qkv,
        grad_out,
        second_new_out,
        new_out,
        grad_mlp,
        second_new_mlp,
        new_mlp,
        grad_gains,
        second_new_gains,
        new_gains,
    )


def solution(mesh):
    return jax.shard_map(
        on_device,
        mesh=mesh,
        in_specs=(
            P("fsdp", "seq", None, None),
            P("fsdp", "seq", None, None),
            P(),
            P("fsdp", None),
            P("fsdp", None),
            P("fsdp", None),
            P("fsdp", None),
            P("fsdp", None),
            P("fsdp", None),
            P("fsdp", None, None),
            P("fsdp", None, None),
            P("fsdp", None, None),
            P("fsdp", None),
            P("fsdp", None),
            P("fsdp", None),
        ),
        out_specs=(
            P("fsdp", "seq", None, None),
            P("fsdp", "seq", None, None),
            P("fsdp", None),
            P("fsdp", None),
            P("fsdp", None),
            P("fsdp", None),
            P("fsdp", None),
            P("fsdp", None),
            P("fsdp", None, None),
            P("fsdp", None, None),
            P("fsdp", None, None),
            P("fsdp", None),
            P("fsdp", None),
            P("fsdp", None),
        ),
        check_vma=False,
    )
```

profile of v0, /device:TPU:13, one launch (start us, length us, event | category | flops | bytes accessed | tf_op | source)
XLA Modules:
  0.0 3999.9 jit_solution(6499694492075315947)
XLA Ops:
  11.1 9.0 convert_element_type.187
  21.0 15.6 all-gather
  38.7 91.4 %all-gather.6.cloned.1.call-done = bf16[2560,3072]{1,0:T(8,128)(2,1)} async-done(((bf16[160,3072]{1,0:T(8,128)(2,1)}), bf16[2560,3072]{1,0:T(8,128)(2,1)}) %all-gather.6.cloned.1.call-update) | async-done | bytes 15728656 | tf_op jit(solution)/shard_map/all_gather | solution.py:128
  130.1 7.2 fusion.88
  138.7 7.0 all_gather.32
  145.8 5.9 collective-permute-start.5
  170.4 96.6 %collective-permute-done = bf16[384,512]{1,0:T(8,128)(2,1)} collective-permute-done((bf16[384,512]{1,0:T(8,128)(2,1)}, bf16[384,512]{1,0:T(8,128)(2,1)}, u32[]{:S(2)}, u32[]{:S(2)}) %collective-permute-start) | collective-permute-done | bytes 393248 | tf_op jit(solution)/shard_map/ppermute | solution.py:27
  273.1 8.2 collective-permute-done.4
  284.9 4.7 select_reduce_fusion
  289.6 5.9 fusion.15
  295.5 4.5 copy-done
  300.0 7.2 fusion.82
  308.6 6.7 multiply_reduce_fusion.3
  316.8 534.7 %all-gather.10.cloned.1.call-done = bf16[2560,3,7680]{2,0,1:T(8,128)(2,1)} async-done(((bf16[160,3,7680]{2,0,1:T(8,128)(2,1)}), bf16[2560,3,7680]{2,0,1:T(8,128)(2,1)}) %all-gather.10.cloned.1.call-update) | async-done | bytes 117964816 | tf_op jit(solution)/shard_map/all_gather | solution.py:162
  851.5 32.0 fusion.11
  883.4 23.4 fusion.61
  906.8 35.6 multiply_reduce_fusion.1
  945.7 9.1 convolution_convert_fusion
  955.4 10.2 fusion.46
  965.6 16.5 multiply_reduce_fusion
  982.1 15.1 multiply_convert_fusion
  1018.3 12.2 collective-permute-start.7
  1030.6 5.8 pad_maximum_fusion.1
  1036.4 20.3 collective-permute-done.7
  1057.9 347.4 %while.12 = (s32[]{:T(128)}, f32[32,160,3,3840]{3,1,2,0:T(8,128)}, s32[32]{0:T(128)S(1)}, bf16[192,2560]{0,1:T(8,128)(2,1)}, bf16[192,2,7680]{2,0,1:T(8,128)(2,1...) while((s32[]{:T(128)}, f32[32,160,3,3840]{3,1,2,0:T(8,128)}, ...), condition=%wide.region_16.17_spmd, body=%wide.region_15.16_spmd.sunk | while | flops 709632000 | bytes 26722780 | solution.py:203
  1076.4 3.5 fusion.183
  1087.3 3.4 fusion.183
  1098.1 3.5 fusion.183
  1109.0 3.5 fusion.183
  1130.7 3.5 fusion.183
  1174.0 3.6 fusion.183
  1185.0 3.5 fusion.183
  1217.5 3.5 fusion.183
  1228.4 3.5 fusion.183
  1239.2 3.5 fusion.183
  1250.1 3.4 fusion.183
  1260.9 3.4 fusion.183
  1271.8 3.5 fusion.183
  1293.5 3.5 fusion.183
  1304.3 3.4 fusion.183
  1315.2 3.5 fusion.183
  1347.6 3.5 fusion.183
  1358.5 3.5 fusion.183
  1369.4 3.5 fusion.183
  1401.8 3.5 fusion.183
  1407.1 5.6 convolution_multiply_fusion
  1417.2 19.3 fusion.86
  1438.2 18.0 fusion.90
  1456.3 1779.0 %reduce-scatter.14.cloned.1.call-done = f32[1,160,3,3840]{3,1,2,0:T(8,128)} async-done(((f32[32,160,3,3840]{3,1,2,0:T(8,128)}), f32[1,160,3,3840]{3,1,2,0:T(8,128)}) %reduce-scatter.14.cloned.1.call-update) | async-done | bytes 7372816
  3235.3 3.5 convert_bitcast_fusion
  3242.4 24.7 fusion.54
  3267.2 14.8 fusion.71
  3282.1 42.4 %all-reduce.1 = bf16[32,160,1]{1,0,2:T(8,128)(2,1)S(1)} all-reduce(f32[32,160,1]{1,0,2:T(8,128)S(1)} %reshape.391), channel_id=6, replica_groups=mesh['seq'=2,'fsdp'=16] {'seq','fsdp'}, use_global_device_ids=true, to_apply=%region_20.21.clone | all-reduce | flops 5120 | bytes 30720
  3324.5 3.6 all_gather.38
  3328.8 5.0 fusion.78
  3333.8 191.2 %reduce-scatter.10.cloned.1.call-done = f32[1,160,1536]{2,1,0:T(8,128)} async-done(((f32[32,160,1536]{2,1,0:T(8,128)}), f32[1,160,1536]{2,1,0:T(8,128)}) %reduce-scatter.10.cloned.1.call-update) | async-done | bytes 983056 | tf_op jit(solution)/shard_map/reduce_scatter | solution.py:262
  3526.3 12.7 all_gather.35
  3545.9 259.6 %reduce-scatter.12.cloned.1.call-done = f32[1,160,1280]{2,1,0:T(8,128)} async-done(((f32[32,160,1280]{2,1,0:T(8,128)}), f32[1,160,1280]{2,1,0:T(8,128)}) %reduce-scatter.12.cloned.1.call-update) | async-done | bytes 819216 | tf_op jit(solution)/shard_map/reduce_scatter | solution.py:268
  3806.7 8.6 all_gather.36
  3821.8 81.6 %all-gather.12.cloned.1.call-done = bf16[2,160,11520]{2,1,0:T(8,128)(2,1)} async-done(((bf16[1,160,11520]{2,1,0:T(8,128)(2,1)}), bf16[2,160,11520]{2,1,0:T(8,128)(2,1)}) %all-gather.12.cloned.1.call-update) | async-done | bytes 7372816 | tf_op jit(solution)/shard_map/all_gather | solution.py:289
  3903.4 18.7 reshape.410
  3922.1 22.0 copy.152
  3944.2 18.4 reshape.402
  3962.5 30.1 multiply_subtract_fusion
  (333 shorter events, 286.5 us)
Async XLA Ops:
  7.2 2.9 copy-start.14
  7.2 122.9 %all-gather.6.cloned.1.call-start = ((), (), s32[]{:S(2)}) async-start(), calls=%async_computation.4 | async-start | bytes 16711680 | tf_op jit(solution)/shard_map/all_gather | solution.py:128
  10.0 298.6 %all-gather.8.cloned.1.call-start = ((), (), s32[]{:S(2)}) async-start(), calls=%async_computation.5 | async-start | bytes 13926400 | tf_op jit(solution)/shard_map/all_gather | solution.py:129
  11.0 840.4 %all-gather.10.cloned.1.call-start = ((), (), s32[]{:S(2)}) async-start(), calls=%async_computation.6 | async-start | bytes 125337600 | tf_op jit(solution)/shard_map/all_gather | solution.py:162
  20.1 17.0 copy-start.3
  20.2 1393.7 %reduce-scatter.8.cloned.1.call-start = ((), (), s32[]{:S(2)}) async-start(), calls=%async_computation.7 | async-start | bytes 589824 | tf_op jit(solution)/shard_map/reduce_scatter | solution.py:246
  36.8 100.8 %copy-start.54 = (f32[128]{0:T(128)}, f32[128]{0:T(128)S(1)}, u32[]{:S(2)}) copy-start(f32[128]{0:T(128)S(1)} %multiply_exponential_fusion) | copy-start | bytes 1540
  37.0 100.4 %copy-start.35 = (f32[2560]{0:T(1024)}, f32[2560]{0:T(1024)S(1)}, u32[]{:S(2)}) copy-start(f32[2560]{0:T(1024)S(1)} %get-tuple-element.156) | copy-start | bytes 30724
  37.0 905.5 %copy-start.37 = (f32[2560]{0:T(1024)}, f32[2560]{0:T(1024)S(1)}, u32[]{:S(2)}) copy-start(f32[2560]{0:T(1024)S(1)} %get-tuple-element.155) | copy-start | bytes 30724
  37.4 99.9 %copy-start.39 = (f32[192]{0:T(256)}, f32[192]{0:T(256)S(1)}, u32[]{:S(2)}) copy-start(f32[192]{0:T(256)S(1)} %fusion.132) | copy-start | bytes 2308
  37.4 100.1 %copy-start.44 = (f32[192]{0:T(256)}, f32[192]{0:T(256)S(1)}, u32[]{:S(2)}) copy-start(f32[192]{0:T(256)S(1)} %get-tuple-element.182) | copy-start | bytes 2308
  145.8 135.5 %collective-permute-start.5 = (bf16[384,512]{1,0:T(8,128)(2,1)}, bf16[384,512]{1,0:T(8,128)(2,1)}, u32[]{:S(2)}, u32[]{:S(2)}) collective-permute-start(bf16[384,512]{1,0:T(8,128)(2,1)} %all_gather.32), channel_id=1, source_target_pairs={{0,1},{1,2},{2,3},{3,4},{4,5},{5,6},{6,7},{7,8},{8,9},{9,10},{10,1... | collective-permute-start | bytes 1179656 | tf_op jit(solution)/shard_map/ppermute | solution.py:27
  151.7 120.4 %collective-permute-start.3 = (bf16[384,512]{1,0:T(8,128)(2,1)}, bf16[384,512]{1,0:T(8,128)(2,1)}, u32[]{:S(2)}, u32[]{:S(2)}) collective-permute-start(bf16[384,512]{1,0:T(8,128)(2,1)} %all_gather.32), channel_id=1, source_target_pairs={{0,3},{1,4},{2,5},{3,6},{4,7},{5,8},{6,9},{7,10},{8,11},{9,12},{10... | collective-permute-start | bytes 1179656 | tf_op jit(solution)/shard_map/ppermute | solution.py:27
  153.6 117.4 %collective-permute-start.2 = (bf16[384,512]{1,0:T(8,128)(2,1)}, bf16[384,512]{1,0:T(8,128)(2,1)}, u32[]{:S(2)}, u32[]{:S(2)}) collective-permute-start(bf16[384,512]{1,0:T(8,128)(2,1)} %all_gather.32), channel_id=1, source_target_pairs={{0,4},{1,5},{2,6},{3,7},{4,8},{5,9},{6,10},{7,11},{8,12},{9,13},{1... | collective-permute-start | bytes 1179656 | tf_op jit(solution)/shard_map/ppermute | solution.py:27
  155.7 114.3 %collective-permute-start.1 = (bf16[384,512]{1,0:T(8,128)(2,1)}, bf16[384,512]{1,0:T(8,128)(2,1)}, u32[]{:S(2)}, u32[]{:S(2)}) collective-permute-start(bf16[384,512]{1,0:T(8,128)(2,1)} %all_gather.32), channel_id=1, source_target_pairs={{0,5},{1,6},{2,7},{3,8},{4,9},{5,10},{6,11},{7,12},{8,13},{9,14},{... | collective-permute-start | bytes 1179656 | tf_op jit(solution)/shard_map/ppermute | solution.py:27
  157.6 109.4 %collective-permute-start = (bf16[384,512]{1,0:T(8,128)(2,1)}, bf16[384,512]{1,0:T(8,128)(2,1)}, u32[]{:S(2)}, u32[]{:S(2)}) collective-permute-start(bf16[384,512]{1,0:T(8,128)(2,1)} %all_gather.32), channel_id=1, source_target_pairs={{0,6},{1,7},{2,8},{3,9},{4,10},{5,11},{6,12},{7,13},{8,14},{9,15},... | collective-permute-start | bytes 1179656 | tf_op jit(solution)/shard_map/ppermute | solution.py:27
  164.6 4.1 copy-start.31
  164.6 4.1 copy-start.34
  170.4 114.5 %copy-start.27 = (f32[192,10,128]{2,0,1:T(8,128)}, f32[192,10,128]{2,0,1:T(8,128)S(1)}, u32[]{:S(2)}) copy-start(f32[192,10,128]{2,0,1:T(8,128)S(1)} %get-tuple-element.199) | copy-start | bytes 2949124
  170.4 114.5 %copy-start.29 = (f32[192,10,128]{2,0,1:T(8,128)}, f32[192,10,128]{2,0,1:T(8,128)S(1)}, u32[]{:S(2)}) copy-start(f32[192,10,128]{2,0,1:T(8,128)S(1)} %get-tuple-element.200) | copy-start | bytes 2949124
  267.0 14.2 collective-permute-start.4
  289.5 10.5 copy-start
  315.3 627.2 %copy-start.1 = (f32[192,2560]{1,0:T(8,128)}, f32[192,2560]{1,0:T(8,128)S(1)}, u32[]{:S(2)}) copy-start(f32[192,2560]{1,0:T(8,128)S(1)} %get-tuple-element.213) | copy-start | bytes 5898244
  315.3 627.1 %copy-start.41 = (f32[192]{0:T(256)}, f32[192]{0:T(256)S(1)}, u32[]{:S(2)}) copy-start(f32[192]{0:T(256)S(1)} %fusion.133) | copy-start | bytes 2308
  316.8 566.7 %copy-start.17 = (bf16[1,1,192,2560]{3,2,1,0:T(8,128)(2,1)S(1)}, bf16[1,1,192,2560]{3,2,1,0:T(8,128)(2,1)}, u32[]{:S(2)}) copy-start(bf16[1,1,192,2560]{3,2,1,0:T(8,128)(2,1)} %param.18) | copy-start | bytes 2949124
  965.6 34.9 copy-start.7
  982.1 15.1 copy-start.28
  982.1 15.1 copy-start.30
  997.2 4.0 copy-start.11
  1002.8 4.4 copy-start.20
  1004.1 14.2 collective-permute-start.6
  1008.7 27.7 collective-permute-start.11
  1011.1 25.3 collective-permute-start.10
  1013.0 23.4 collective-permute-start.9
  1015.8 20.6 collective-permute-start.8
  1018.3 38.4 copy-start.8
  1018.3 38.4 copy-start.10
  1018.3 38.4 collective-permute-start.7
  1036.4 21.5 copy-start.6
  1057.8 2177.5 %reduce-scatter.14.cloned.1.call-start = ((), (), s32[]{:S(2)}) async-start(), calls=%async_computation.11 | async-start | bytes 243302400
  1405.4 7.4 copy-start.32
  1405.4 7.4 copy-start.33
  1405.4 2119.6 %reduce-scatter.10.cloned.1.call-start = ((), (), s32[]{:S(2)}) async-start(), calls=%async_computation.8 | async-start | bytes 32440320 | tf_op jit(solution)/shard_map/reduce_scatter | solution.py:262
  1413.0 3.2 copy-start.45
  1413.1 3.2 copy-start.55
  1413.8 22.7 copy-start.18
  1413.8 3.4 copy-start.4
  1413.8 3.4 copy-start.36
  1413.8 3.4 copy-start.40
  1436.5 2369.0 %reduce-scatter.12.cloned.1.call-start = ((), (), s32[]{:S(2)}) async-start(), calls=%async_computation.9 | async-start | bytes 27033600 | tf_op jit(solution)/shard_map/reduce_scatter | solution.py:268
  1456.2 2447.2 %all-gather.12.cloned.1.call-start = ((), (), s32[]{:S(2)}) async-start(), calls=%async_computation.10 | async-start | bytes 11059200 | tf_op jit(solution)/shard_map/all_gather | solution.py:289
  3242.4 24.7 copy-start.43
  3267.1 61.0 %copy-start.47 = (f32[192]{0:T(256)S(1)}, f32[192]{0:T(256)}, u32[]{:S(2)}) copy-start(f32[192]{0:T(256)} %copy-done.46) | copy-start | bytes 2308
  3267.1 61.1 %copy-start.51 = (f32[160,2]{0,1:T(2,128)S(1)}, f32[160,2]{0,1:T(2,128)}, u32[]{:S(2)}) copy-start(f32[160,2]{0,1:T(2,128)} %param.29) | copy-start | bytes 3844
  3267.1 61.1 %copy-start.52 = (f32[160,2]{0,1:T(2,128)S(1)}, f32[160,2]{0,1:T(2,128)}, u32[]{:S(2)}) copy-start(f32[160,2]{0,1:T(2,128)} %param.30) | copy-start | bytes 3844
  3267.1 61.1 %copy-start.53 = (f32[160,2]{0,1:T(2,128)S(1)}, f32[160,2]{0,1:T(2,128)}, u32[]{:S(2)}) copy-start(f32[160,2]{0,1:T(2,128)} %param.31) | copy-start | bytes 3844
  3267.1 61.7 %copy-start.38 = (f32[2560]{0:T(1024)S(1)}, f32[2560]{0:T(1024)}, u32[]{:S(2)}) copy-start(f32[2560]{0:T(1024)} %copy-done.37) | copy-start | bytes 30724
  3267.1 61.7 %copy-start.42 = (f32[192]{0:T(256)S(1)}, f32[192]{0:T(256)}, u32[]{:S(2)}) copy-start(f32[192]{0:T(256)} %copy-done.41) | copy-start | bytes 2308
  3267.1 61.6 %copy-start.49 = (f32[192]{0:T(256)S(1)}, f32[192]{0:T(256)}, u32[]{:S(2)}) copy-start(f32[192]{0:T(256)} %copy-done.48) | copy-start | bytes 2308
  3538.9 2.9 copy-start.21
  3538.9 3.6 copy-start.22
  3539.3 6.5 copy-start.13
  3815.3 3.5 copy-start.24
  3815.5 6.2 copy-start.16
  (13 other events, 20.2 us)
Sparse Core Ops, SparseCore 0:
  10.9 119.1 all-gather.5
  133.0 147.4 all-gather.7
  282.6 568.8 all-gather.9
  1057.9 23.2 reduce-scatter.7
  1405.5 1829.7 reduce-scatter.13
  3242.7 282.2 reduce-scatter.9
  3527.4 278.0 reduce-scatter.11
  3807.7 95.6 all-gather.11
where the time goes:
time: 4010 us; the launch traced here: 4000 us
  waiting for transfers between devices  3060 us (76%)
  matrix products  372 us (9%)
  other arithmetic  210 us (5%)
  local copies, waits for them, and re-layouts  124 us (3%)
  blocking collectives  90 us (2%)
  loops' own time  84.4 us (2%)
  starting transfers between devices  40.3 us (1%)
    unnamed x9, waiting for transfers between devices  1780 us
    all_gather x1, waiting for transfers between devices, on_device(): lax.all_gather(weight_mlp.astype(jnp.bfloat16), 'fsdp', axis=0, tiled=True)  535 us
    reduce_scatter x1, waiting for transfers between devices, on_device(): lax.psum_scatter(split_halves(out_term, fsdp_count, seq_count), ('seq', '...  260 us
    reduce_scatter x1, waiting for transfers between devices, on_device(): lax.psum_scatter(split_halves(qkv_term, fsdp_count, seq_count), ('seq', '...  191 us
    ppermute x12, waiting for transfers between devices, passed_along(): lax.ppermute(value, axis, [(source, source + steps) for source in range(i...  126 us
    dynamic_update_slice x32, other arithmetic, on_device(): lax.map(one_piece, jnp.arange(1 * lax.axis_size(('seq', 'fsdp')), dtype=j...  111 us
    all_gather x1, waiting for transfers between devices, on_device(): lax.all_gather(weight_qkv.astype(jnp.bfloat16), 'fsdp', axis=0, tiled=True)  91.4 us
    dot_general x32, matrix products, one_piece(): jnp.einsum('td,tcf->dcf', rows_two, grads_half, preferred_element_type=jn...  86 us
  transfers between devices with their start and end apart: 20, of which 10 were waited for; matrix products, arithmetic and copies ran while one was open for 11% of the time, Pallas kernels for 0%

commit v1 on v0

v1 whole, which is shorter than its diff:
```python
import math

import jax
import jax.numpy as jnp
from jax import lax
from jax.experimental import pallas as pl
from jax.experimental.pallas import tpu as pltpu
from jax.sharding import Mesh, PartitionSpec as P

D = 2560
HEAD_DIM = 256
WINDOW = 2048
STEP = 10
SEQ_LEN = 3072

NORM_EPS = 1e-06
BETA_ONE = 0.9
BETA_TWO = 0.95
ADAM_EPS = 1e-08
DECAY_RATE = 0.1
MASKED_SCORE = -1e30

LANES = 512
KEY_BLOCK = 768
PLANES = ("g", "h")
OWNERS = ("g", "h", "k", "c")
CHIPS = ("seq", "k")
GROUP = ("seq", "k", "c")
RING = ("seq", "h", "k")
EVERY = ("seq", "g", "h", "k", "c")


def rotate(values, cosine, sine):
    half_dim = values.shape[-1] // 2
    first_half = values[..., :half_dim]
    second_half = values[..., half_dim:]
    return jnp.concatenate(
        [first_half * cosine - second_half * sine, second_half * cosine + first_half * sine],
        axis=-1,
    )


def doc_places(lengths_row, offsets):
    doc_ends = jnp.cumsum(lengths_row)
    passed = (doc_ends[None, :] <= offsets[:, None]).astype(jnp.int32)
    document = jnp.sum(passed, axis=1)
    starts = jnp.sum(passed * lengths_row[None, :], axis=1)
    return (document, offsets - starts)


def rope_angles(places, head_dim):
    freq_index = jnp.arange(head_dim // 2, dtype=jnp.float32)
    inverse = jnp.exp(freq_index * (-2.0 * math.log(10000.0) / head_dim))
    angles = places.astype(jnp.float32)[:, None] * inverse[None, :]
    return (jnp.cos(angles), jnp.sin(angles))


def adam_step(weight, first, second, grad, rate):
    first_new = BETA_ONE * first + (1.0 - BETA_ONE) * grad
    second_new = BETA_TWO * second + (1.0 - BETA_TWO) * grad * grad
    first_hat = first_new / (1.0 - BETA_ONE**STEP)
    second_hat = second_new / (1.0 - BETA_TWO**STEP)
    update = first_hat / (jnp.sqrt(second_hat) + ADAM_EPS)
    return (second_new, weight - rate * (update + DECAY_RATE * weight))


def glu_values(gate_in, up_in):
    return jax.nn.gelu(gate_in, approximate=True) * up_in


def low(value):
    return value.astype(jnp.bfloat16)


def wide(value):
    return value.astype(jnp.float32)


def dot(left, right, contract):
    return lax.dot_general(
        left, right, ((contract[:1], contract[1:]), ((), ())), preferred_element_type=jnp.float32
    )


def traded(axes, step):
    count = math.prod(lax.axis_size(axis) for axis in axes)
    return [(source, source ^ step) for source in range(count)]


def swapped(value, axis):
    return lax.ppermute(value, axis, [(0, 1), (1, 0)])


def after(value, *others):
    return lax.optimization_barrier((value,) + others)[0]


def doubled(value, axis, step, place):
    other = lax.ppermute(value, axis, traded((axis,), step))
    first = (lax.axis_index(axis) & step) == 0
    return jnp.stack([jnp.where(first, value, other), jnp.where(first, other, value)], axis=place)


def next_plane(block):
    count = math.prod(lax.axis_size(axis) for axis in PLANES)
    return lax.ppermute(block, PLANES, [(one, (one + 1) % count) for one in range(count)])


def joined_planes(blocks):
    count, rows = len(blocks), blocks[0].shape[0]
    whole = jnp.zeros((count * rows, blocks[0].shape[1]), blocks[0].dtype)
    for step, block in enumerate(blocks):
        start = lax.rem(lax.axis_index(PLANES) + (count - step), count) * rows
        whole = lax.dynamic_update_slice_in_dim(whole, block, start, 0)
    return whole


def spread_ring(value):
    chips = math.prod(lax.axis_size(axis) for axis in RING)
    place = lax.axis_index(RING)
    whole = jnp.zeros((chips,) + value.shape, value.dtype)
    for step in range(chips):
        arrived = lax.ppermute(value, RING, traded(RING, step)) if step else value
        whole = lax.dynamic_update_index_in_dim(whole, arrived, place ^ step, 0)
    return whole


def ring_sum(terms):
    chips = terms.shape[0]
    place = lax.axis_index(CHIPS)
    total = 0.0
    for step in range(chips):
        term = lax.dynamic_index_in_dim(terms, place ^ step, 0, keepdims=False)
        if step:
            term = lax.ppermute(term, CHIPS, traded(CHIPS, step))
        total = total + wide(term)
    return total


def exchanged(value, axes):
    return lax.all_to_all(value, axes, split_axis=0, concat_axis=0, tiled=True)


def half_sum(terms, axis, place):
    here = lax.axis_index(axis)
    kept = lax.dynamic_index_in_dim(terms, here, place, keepdims=False)
    given = lax.dynamic_index_in_dim(terms, 1 - here, place, keepdims=False)
    return low(wide(kept) + wide(swapped(given, axis)))


def mlp_chunks_kernel(slices, side_ref, weight_ref, gain_ref, gate_up_ref, down_ref):
    per_piece = pl.num_programs(1)
    index = side_ref[0] * pl.num_programs(0) + pl.program_id(0)
    index = index * per_piece + pl.program_id(1)
    width = weight_ref.shape[2]
    lane = pl.program_id(1) * width
    gain = gain_ref[...]
    for part in range(3):
        weight = wide(low(weight_ref[part]))
        if part < 2:
            weight = weight * gain
        weight = low(jnp.where(index < slices, weight, 0.0))
        if part < 2:
            place = pl.multiple_of(part * per_piece * width + lane, width)
            gate_up_ref[0, :, pl.ds(place, width)] = weight
        else:
            down_ref[0, :, pl.ds(pl.multiple_of(lane, width), width)] = weight


def mlp_chunks(weight, gain, side, members, piece):
    parts, rows, ff_width = weight.shape
    slices = ff_width // LANES
    per_piece = piece // LANES

    def weight_block(m, b, side_ref):
        return (0, 0, jnp.minimum((side_ref[0] * members + m) * per_piece + b, slices - 1))

    def out_block(m, b, side_ref):
        return (m, 0, 0)

    return pl.pallas_call(
        lambda *refs: mlp_chunks_kernel(slices, *refs),
        grid_spec=pltpu.PrefetchScalarGridSpec(
            num_scalar_prefetch=1,
            grid=(members, per_piece),
            in_specs=[
                pl.BlockSpec((parts, rows, LANES), weight_block),
                pl.BlockSpec((rows, 1), lambda m, b, side_ref: (0, 0)),
            ],
            out_specs=[
                pl.BlockSpec((1, rows, 2 * piece), out_block),
                pl.BlockSpec((1, rows, piece), out_block),
            ],
        ),
        out_shape=[
            jax.ShapeDtypeStruct((members, rows, 2 * piece), jnp.bfloat16),
            jax.ShapeDtypeStruct((members, rows, piece), jnp.bfloat16),
        ],
        compiler_params=pltpu.CompilerParams(vmem_limit_bytes=48 * 1024 * 1024),
        cost_estimate=pl.CostEstimate(
            flops=weight.size, bytes_accessed=3 * weight.size, transcendentals=0
        ),
        name="mlp_chunks",
    )(jnp.full((1,), side, jnp.int32), weight, gain)


def mlp_adam_kernel(rate, per_side, scaled, side_ref, ours_ref, theirs_ref, weight_ref, first_ref,
                    second_ref, gain_ref, *refs):
    grad_out, second_out, weight_out, dot_out = refs[-4:]
    block = pl.program_id(0)
    ours = block // per_side == side_ref[0]
    grad = wide(jnp.where(ours, ours_ref[0], theirs_ref[0]))
    weight = weight_ref[0]
    dot_part = jnp.sum(wide(low(weight)) * grad, axis=1, keepdims=True)
    dot_out[...] = jnp.where(block == 0, dot_part, dot_out[...] + dot_part)
    if scaled:
        grad = grad * gain_ref[...]
    grad_out[0] = grad
    second_out[0], weight_out[0] = adam_step(weight, first_ref[0], second_ref[0], grad, rate)


def mlp_adam(part, side, pieces, states, gain, rate, outs):
    _, rows, ff_width = states[0].shape
    members, _, piece = pieces[0].shape
    per_piece = piece // LANES
    per_side = members * per_piece

    def grad_block(own):
        def place(b, side_ref):
            used = (b // per_side == side_ref[0]) == own
            inner = jnp.where(used, b % per_side, 0)
            return (inner // per_piece, 0, inner % per_piece)

        return pl.BlockSpec((1, rows, LANES), place)

    state = pl.BlockSpec((1, rows, LANES), lambda b, side_ref: (part, 0, b))
    gains = pl.BlockSpec((rows, 1), lambda b, side_ref: (0, 0))
    size = rows * ff_width
    return pl.pallas_call(
        lambda *refs: mlp_adam_kernel(rate, per_side, part < 2, *refs),
        grid_spec=pltpu.PrefetchScalarGridSpec(
            num_scalar_prefetch=1,
            grid=(ff_width // LANES,),
            in_specs=[grad_block(True), grad_block(False), state, state, state, gains]
            + [pl.BlockSpec(memory_space=pl.ANY)] * len(outs),
            out_specs=[state, state, state, gains],
        ),
        out_shape=[jax.ShapeDtypeStruct(states[0].shape, jnp.float32)] * 3
        + [jax.ShapeDtypeStruct((rows, 1), jnp.float32)],
        input_output_aliases={7 + index: index for index in range(len(outs))},
        compiler_params=pltpu.CompilerParams(vmem_limit_bytes=48 * 1024 * 1024),
        cost_estimate=pl.CostEstimate(
            flops=20 * size, bytes_accessed=26 * size, transcendentals=size
        ),
        name="mlp_adam",
    )(jnp.full((1,), side, jnp.int32), *pieces, *states, gain, *outs)


def stacked_heads(ref):
    return jnp.concatenate([ref[:, :HEAD_DIM], ref[:, HEAD_DIM:]], axis=0)


def attend_kernel(query_ref, key_ref, value_t_ref, bias_ref, out_ref, lse_ref, score_ref):
    rows = query_ref.shape[0]
    queries = stacked_heads(query_ref)
    blocks = key_ref.shape[0] // KEY_BLOCK

    def first(block, top):
        part = pl.ds(pl.multiple_of(block * KEY_BLOCK, KEY_BLOCK), KEY_BLOCK)
        scores = dot(key_ref[part, :], queries, (1, 1)) + bias_ref[part, :]
        score_ref[part, :] = scores
        return jnp.maximum(top, jnp.max(scores, axis=0, keepdims=True))

    top = jnp.full((1, 2 * rows), -jnp.inf, jnp.float32)
    top = lax.fori_loop(0, blocks, first, top, unroll=2)

    def second(block, carry):
        total, mixed = carry
        part = pl.ds(pl.multiple_of(block * KEY_BLOCK, KEY_BLOCK), KEY_BLOCK)
        exps = jnp.exp(score_ref[part, :] - top)
        total = total + jnp.sum(exps, axis=0, keepdims=True)
        return total, mixed + dot(value_t_ref[:, part], low(exps), (1, 0))

    total, mixed = lax.fori_loop(
        0,
        blocks,
        second,
        (jnp.zeros((1, 2 * rows), jnp.float32), jnp.zeros((HEAD_DIM, 2 * rows), jnp.float32)),
        unroll=2,
    )
    mixed = low((mixed / total).T)
    out_ref[:, :HEAD_DIM] = mixed[:rows]
    out_ref[:, HEAD_DIM:] = mixed[rows:]
    lse_ref[0] = top + jnp.log(total)


def attend(queries, keys, values, bias):
    rows, width = queries.shape
    pairs = width // (2 * HEAD_DIM)
    count = keys.shape[0]

    def whole(shape):
        return pl.BlockSpec(shape, lambda p: (0,) * len(shape))

    pair = pl.BlockSpec((rows, 2 * HEAD_DIM), lambda p: (0, p))
    return pl.pallas_call(
        attend_kernel,
        grid=(pairs,),
        in_specs=[pair, whole(keys.shape), whole((HEAD_DIM, count)), whole(bias.shape)],
        out_specs=[pair, pl.BlockSpec((1, 1, 2 * rows), lambda p: (p, 0, 0))],
        out_shape=[
            jax.ShapeDtypeStruct((rows, width), jnp.bfloat16),
            jax.ShapeDtypeStruct((pairs, 1, 2 * rows), jnp.float32),
        ],
        scratch_shapes=[pltpu.VMEM((count, 2 * rows), jnp.float32)],
        compiler_params=pltpu.CompilerParams(vmem_limit_bytes=48 * 1024 * 1024),
        cost_estimate=pl.CostEstimate(
            flops=4 * rows * width * count,
            bytes_accessed=8 * rows * width + 12 * bias.size,
            transcendentals=pairs * bias.size,
        ),
        name="attend",
    )(queries, keys, values.T, bias)


def attend_back_kernel(query_ref, grad_ref, key_ref, key_t_ref, value_ref, bias_ref, lse_ref,
                       delta_ref, grad_query_ref, grad_window_ref):
    rows = query_ref.shape[0]
    queries = stacked_heads(query_ref)
    grads = stacked_heads(grad_ref)
    blocks = key_ref.shape[0] // KEY_BLOCK

    @pl.when(pl.program_id(0) == 0)
    def _():
        grad_window_ref[...] = jnp.zeros_like(grad_window_ref)

    lse = lse_ref[0]
    delta = delta_ref[0]

    def body(block, grad_query):
        part = pl.ds(pl.multiple_of(block * KEY_BLOCK, KEY_BLOCK), KEY_BLOCK)
        probs = jnp.exp(dot(key_ref[part, :], queries, (1, 1)) + bias_ref[part, :] - lse)
        grad_probs = dot(value_ref[part, :], grads, (1, 1))
        grad_scores = low(probs * (grad_probs - delta))
        grad_window_ref[part, :HEAD_DIM] += dot(grad_scores, queries, (1, 0))
        grad_window_ref[part, HEAD_DIM:] += dot(low(probs), grads, (1, 0))
        return grad_query + dot(key_t_ref[:, part], grad_scores, (1, 0))

    grad_query = jnp.zeros((HEAD_DIM, 2 * rows), jnp.float32)
    grad_query = lax.fori_loop(0, blocks, body, grad_query, unroll=2).T
    grad_query_ref[:, :HEAD_DIM] = grad_query[:rows]
    grad_query_ref[:, HEAD_DIM:] = grad_query[rows:]


def attend_back(queries, grads, keys, values, bias, lse, delta):
    rows, width = queries.shape
    pairs = width // (2 * HEAD_DIM)
    count = keys.shape[0]

    def whole(shape):
        return pl.BlockSpec(shape, lambda p: (0,) * len(shape))

    pair = pl.BlockSpec((rows, 2 * HEAD_DIM), lambda p: (0, p))
    line = pl.BlockSpec((1, 1, 2 * rows), lambda p: (p, 0, 0))
    return pl.pallas_call(
        attend_back_kernel,
        grid=(pairs,),
        in_specs=[
            pair,
            pair,
            whole(keys.shape),
            whole((HEAD_DIM, count)),
            whole(values.shape),
            whole(bias.shape),
            line,
            line,
        ],
        out_specs=[pair, whole((count, 2 * HEAD_DIM))],
        out_shape=[
            jax.ShapeDtypeStruct((rows, width), jnp.float32),
            jax.ShapeDtypeStruct((count, 2 * HEAD_DIM), jnp.float32),
        ],
        compiler_params=pltpu.CompilerParams(vmem_limit_bytes=48 * 1024 * 1024),
        cost_estimate=pl.CostEstimate(
            flops=10 * rows * width * count,
            bytes_accessed=8 * rows * width + 16 * bias.size,
            transcendentals=pairs * bias.size,
        ),
        name="attend_back",
    )(queries, grads, keys, keys.T, values, bias, lse, delta)


def on_device(
    hidden_in,
    cotangent,
    lengths,
    weight_qkv,
    first_qkv,
    second_qkv,
    weight_out,
    first_out,
    second_out,
    weight_mlp,
    first_mlp,
    second_mlp,
    norm_gains,
    first_gains,
    second_gains,
):
    tok_rows = hidden_in.shape[2]
    width = hidden_in.shape[3]
    head_count = width // HEAD_DIM
    sides = lax.axis_size("seq")
    columns = lax.axis_size("k")
    members = columns * lax.axis_size("c")
    planes = lax.axis_size("g") * lax.axis_size("h")
    owner_count = planes * members
    blocks_in_side = lax.axis_size("h") * members
    side = lax.axis_index("seq")
    core = lax.axis_index("c")
    packed_index = lax.axis_index("g")
    place = lax.axis_index(("h", "k", "c"))
    own_rows = weight_mlp.shape[0]
    ff_width = weight_mlp.shape[2]
    piece = -(-ff_width // (sides * members * LANES)) * LANES

    gains_low = wide(low(norm_gains))
    gain_one = gains_low[:, :1]
    gain_two = gains_low[:, 1:]
    qkv_low = wide(low(weight_qkv))
    def gathered(weight):
        half = weight.shape[1] // sides
        weight = lax.dynamic_slice_in_dim(weight, side * half, half, 1)
        whole = lax.all_gather(weight, EVERY, axis=0, tiled=True)
        return whole.reshape(sides, owner_count * own_rows, half)

    qkv_halves = gathered(low(qkv_low * gain_one))
    out_halves = gathered(low(weight_out))
    mlp_planes = weight_mlp.transpose(1, 0, 2)
    gate_up_chunks, down_chunks = mlp_chunks(mlp_planes, gain_two, side, members, piece)

    def to_members(chunks):
        return exchanged(chunks, ("k", "c")).reshape(members * own_rows, chunks.shape[2])

    incoming = cotangent.reshape(tok_rows, width)
    gate_up_blocks = [to_members(gate_up_chunks)]
    gate_up_blocks.append(next_plane(gate_up_blocks[0]))
    down_blocks = [to_members(down_chunks)]
    incoming_columns = doubled(incoming, "k", 1, 0)

    tokens = wide(hidden_in.reshape(tok_rows, width))
    lengths_row = lax.dynamic_index_in_dim(lengths, packed_index, 0, keepdims=False)
    row_numbers = jnp.arange(tok_rows, dtype=jnp.int32)
    query_docs, query_places = doc_places(
        lengths_row, (place * sides + side) * tok_rows + row_numbers
    )
    blocks = jnp.arange(blocks_in_side, dtype=jnp.int32)[None, :] * sides
    blocks = blocks + jnp.arange(sides, dtype=jnp.int32)[:, None]
    key_offsets = (blocks[:, :, None] * tok_rows + row_numbers).reshape(-1)
    key_docs, key_places = doc_places(lengths_row, key_offsets)
    distance = query_places[:, None] - key_places[None, :]
    allowed = (query_docs[:, None] == key_docs[None, :]) & (distance >= 0) & (distance < WINDOW)
    cosine, sine = rope_angles(query_places, HEAD_DIM)
    query_scale = HEAD_DIM ** (-0.5)

    factor_one = lax.rsqrt(jnp.mean(tokens * tokens, axis=-1, keepdims=True) + NORM_EPS)
    normed_one = low(tokens * factor_one)
    normed_one = after(normed_one, incoming_columns, gate_up_blocks[1], down_blocks[0])
    projected = jnp.concatenate([dot(normed_one, half, (1, 0)) for half in qkv_halves], axis=1)
    key_pre = projected[:, width : width + HEAD_DIM]
    value_low = low(projected[:, width + HEAD_DIM :])
    key_low = low(rotate(key_pre, cosine, sine))
    window_kv = spread_ring(jnp.concatenate([key_low, value_low], axis=1))
    window_kv = doubled(window_kv, "c", 1, 1)
    window_kv = window_kv.reshape(SEQ_LEN, 2 * HEAD_DIM)
    gate_up_blocks.append(next_plane(after(gate_up_blocks[1], window_kv)))
    for _ in range(planes - 3):
        gate_up_blocks.append(next_plane(gate_up_blocks[-1]))
    down_blocks.append(next_plane(after(down_blocks[0], window_kv)))
    for _ in range(planes - 2):
        down_blocks.append(next_plane(down_blocks[-1]))
    gate_up_own = joined_planes(gate_up_blocks)
    down_own = joined_planes(down_blocks)
    incoming_sides = doubled(after(incoming_columns, window_kv), "seq", 1, 0)
    query_pre = projected[:, :width].reshape(tok_rows, head_count, HEAD_DIM)
    queries = low(rotate(query_pre, cosine[:, None, :], sine[:, None, :]) * query_scale)
    queries = queries.reshape(tok_rows, width)
    incoming_all = doubled(incoming_sides, "c", 1, incoming_sides.ndim - 2)
    incoming_all = incoming_all.reshape(sides * members * tok_rows, width)
    keys_win = window_kv[:, :HEAD_DIM]
    values_win = window_kv[:, HEAD_DIM:]
    bias = jnp.where(allowed.T, 0.0, MASKED_SCORE)
    bias = jnp.concatenate([bias, bias], axis=1)
    attn_low, log_total = attend(queries, keys_win, values_win, bias)
    attn_low = after(attn_low, gate_up_blocks[2], down_blocks[1], incoming_sides)
    branch = [dot(attn_low, half, (1, 0)) for half in out_halves]
    middle = tokens + jnp.concatenate(branch, axis=1)

    factor_two = lax.rsqrt(jnp.mean(middle * middle, axis=-1, keepdims=True) + NORM_EPS)
    normed_two = low(middle * factor_two)
    normed_two_all = lax.all_gather(normed_two, GROUP, axis=0, tiled=True)
    grad_act = low(dot(incoming_all, down_own, (1, 0)))
    gate_up = dot(normed_two_all, gate_up_own, (1, 0))
    activated, glu_back = jax.vjp(glu_values, gate_up[:, :piece], gate_up[:, piece:])
    activated_low = low(activated)
    attn_all = lax.all_gather(after(attn_low, normed_two_all), GROUP, axis=0, tiled=True)
    normed_one_all = lax.all_gather(after(normed_one, normed_two_all), GROUP, axis=0, tiled=True)
    grad_gate, grad_up = glu_back(wide(grad_act))
    grad_gate_up = low(jnp.concatenate([grad_gate, grad_up], axis=1))
    def to_owners(term):
        return lax.psum_scatter(term, PLANES, scatter_dimension=0, tiled=True)

    def in_plane(term, *others):
        term = term.reshape(members, own_rows, term.shape[1])
        ours = exchanged(after(term, *others), ("k", "c"))
        return (ours, swapped(ours, "seq"))

    by_core = grad_gate_up.reshape(sides * columns, 2, tok_rows, 2 * piece)

    def core_term(which):
        rows = lax.dynamic_index_in_dim(by_core, which, 1, keepdims=False)
        return dot(rows.reshape(-1, 2 * piece), gate_up_own, (1, 1))

    given = swapped(low(core_term(1 - core)), "c")
    terms = low(core_term(core) + wide(given)).reshape(sides * columns, tok_rows, width)
    half = width // sides
    first, second = terms[:, :, :half], terms[:, :, half:]
    down_term = low(dot(incoming_all, after(activated_low, terms), (0, 0)))
    down_term = after(down_term, attn_all, normed_one_all)
    first = exchanged(first, CHIPS)
    late = after(grad_gate_up, first)
    gate_term = low(dot(normed_two_all, late[:, :piece], (0, 0)))
    second = exchanged(after(second, first), CHIPS)
    up_term = low(dot(normed_two_all, late[:, piece:], (0, 0)))
    branch = low(dot(after(activated_low, first), down_own, (1, 1)))
    grad_normed_two = jnp.sum(wide(jnp.concatenate([first, second], axis=2)), axis=0)
    grad_normed_two = after(grad_normed_two, gate_term, up_term, branch)

    down_rows = to_owners(down_term)
    gate_rows = to_owners(gate_term)
    up_rows = to_owners(up_term)
    down_pieces = in_plane(down_rows)
    grad_middle = (
        wide(incoming)
        + factor_two * grad_normed_two
        - middle * factor_two**3 * jnp.mean(grad_normed_two * middle, axis=-1, keepdims=True)
    )

    grad_branch_low = low(grad_middle)
    half = width // sides
    grad_mixed = sum(
        dot(grad_branch_low[:, index * half : (index + 1) * half], out_halves[index], (1, 1))
        for index in range(sides)
    )
    grad_mixed_low = low(grad_mixed)
    delta = (wide(grad_mixed_low) * wide(attn_low)).reshape(tok_rows, head_count, HEAD_DIM)
    delta = jnp.sum(delta, axis=-1).T.reshape(log_total.shape)
    grad_query, grad_window = attend_back(
        queries, grad_mixed_low, keys_win, values_win, bias, log_total, delta
    )
    grad_window = after(low(grad_window), down_pieces[0])
    branch = lax.psum_scatter(
        after(branch, grad_window), GROUP, scatter_dimension=0, tiled=True
    )
    grad_window = half_sum(grad_window.reshape(-1, 2, tok_rows, 2 * HEAD_DIM), "c", 1)
    grad_window = grad_window.reshape(sides, -1, columns, tok_rows, 2 * HEAD_DIM)
    grad_window = half_sum(grad_window, "h", 1).reshape(-1, tok_rows, 2 * HEAD_DIM)
    grad_local = ring_sum(grad_window)
    grad_query = grad_query.reshape(tok_rows, head_count, HEAD_DIM)
    grad_query_pre = rotate(
        grad_query * query_scale, cosine[:, None, :], -sine[:, None, :]
    ).reshape(tok_rows, width)
    grad_key_pre = rotate(grad_local[:, :HEAD_DIM], cosine, -sine)
    grad_proj = low(
        jnp.concatenate([grad_query_pre, grad_key_pre, grad_local[:, HEAD_DIM:]], axis=1)
    )

    grad_proj = after(grad_proj, down_pieces[1])

    shares = sides * members

    def by_column(terms):
        terms = terms.reshape(tok_rows, shares, terms.shape[1] // shares).transpose(1, 0, 2)
        return exchanged(terms, GROUP).reshape(shares * tok_rows, -1)

    def to_rows(total):
        total = exchanged(total.reshape(owner_count, own_rows, -1), OWNERS)
        return low(jnp.sum(wide(total.reshape(planes, members, own_rows, -1)), axis=0))

    def joined(total):
        total = doubled(total, "seq", 1, 0).reshape(shares, own_rows, -1)
        return wide(total.transpose(1, 0, 2).reshape(own_rows, -1))

    out_columns = by_column(grad_branch_low)
    qkv_columns = by_column(grad_proj)
    out_total = after(low(dot(attn_all, out_columns, (0, 0))), qkv_columns)
    qkv_total = low(dot(normed_one_all, qkv_columns, (0, 0)))
    out_total = to_rows(out_total)
    gate_pieces = in_plane(gate_rows, qkv_columns)
    up_pieces = in_plane(up_rows, gate_pieces[0])
    grad_out = joined(out_total)
    qkv_total = to_rows(after(qkv_total, out_total, up_pieces[0]))

    mlp_states = (mlp_planes, first_mlp.transpose(1, 0, 2), second_mlp.transpose(1, 0, 2))
    mlp_outs = ()
    gain_dots = {}
    rate_main = 2.0 * D ** (-0.5)
    for part, pieces in ((2, down_pieces), (0, gate_pieces), (1, up_pieces)):
        if part == 1:
            qkv_total = after(qkv_total, *mlp_outs)
        *mlp_outs, gain_dots[part] = mlp_adam(
            part, side, pieces, mlp_states, gain_two, rate_main, mlp_outs
        )
    grad_mlp, second_new_mlp, new_mlp = mlp_outs
    grad_gain_two = gain_dots[0] + gain_dots[1]
    grad_qkv = joined(qkv_total)
    hidden_out = low(middle + wide(after(branch, grad_qkv))).reshape(1, 1, tok_rows, width)

    half = grad_proj.shape[1] // sides
    grad_normed = sum(
        dot(grad_proj[:, index * half : (index + 1) * half], qkv_halves[index], (1, 1))
        for index in range(sides)
    )
    hidden_grad = (
        grad_middle
        + factor_one * grad_normed
        - tokens * factor_one**3 * jnp.mean(grad_normed * tokens, axis=-1, keepdims=True)
    ).reshape(1, 1, tok_rows, width)

    rate_out = 2.0 * max(1, 6 * D // WINDOW) ** (-0.5)
    rate_gains = 0.4
    grad_gain_one = jnp.sum(qkv_low * grad_qkv, axis=1, keepdims=True)
    grad_qkv = grad_qkv * gain_one
    second_new_qkv, new_qkv = adam_step(weight_qkv, first_qkv, second_qkv, grad_qkv, rate_main)
    second_new_out, new_out = adam_step(weight_out, first_out, second_out, grad_out, rate_out)
    grad_gains = jnp.concatenate([grad_gain_one, grad_gain_two], axis=1)
    second_new_gains, new_gains = adam_step(
        norm_gains, first_gains, second_gains, grad_gains, rate_gains
    )
    return (
        hidden_out,
        hidden_grad,
        grad_qkv,
        second_new_qkv,
        new_qkv,
        grad_out,
        second_new_out,
        new_out,
        grad_mlp.transpose(1, 0, 2),
        second_new_mlp.transpose(1, 0, 2),
        new_mlp.transpose(1, 0, 2),
        grad_gains,
        second_new_gains,
        new_gains,
    )


def solution(mesh):
    seq_count, owner_count = mesh.devices.shape

    def whole(*arguments):
        members = SEQ_LEN // (seq_count * arguments[0].shape[2])
        shape = (seq_count, owner_count // members, members // 4, 2, 2)
        split = Mesh(mesh.devices.reshape(shape), ("seq", "g", "h", "k", "c"))
        acts = P(OWNERS, "seq", None, None)
        flat = P(OWNERS, None)
        planes = P(OWNERS, None, None)
        return jax.shard_map(
            on_device,
            mesh=split,
            in_specs=(acts, acts, P()) + (flat,) * 6 + (planes,) * 3 + (flat,) * 3,
            out_specs=(acts, acts) + (flat,) * 6 + (planes,) * 3 + (flat,) * 3,
            check_vma=False,
        )(*arguments)

    return whole
```

time: 4010 us -> 1160 us (0.29)
  waiting for transfers between devices: 3060 us -> 588 us
  matrix products: 372 us -> 175 us
  other arithmetic: 210 us -> 82.8 us
  Pallas kernels: 0 us -> 109 us
  blocking collectives: 90 us -> 0 us
  loops' own time: 84.4 us -> 0 us
  starting transfers between devices: 40.3 us -> 93 us
    unnamed x9, waiting for transfers between devices: 1780 us -> 0.84 us
    all_gather x4 -> x5, waiting for transfers between devices: 708 us -> 52.9 us  [the longest x1 52.8 us: on_device(): normed_two_all = lax.all_gather(normed_two, GROUP, axis=0, tiled=True)]
    reduce_scatter x3 -> x4, waiting for transfers between devices: 451 us -> 21.5 us  [the longest x3 21.5 us: to_owners(): return lax.psum_scatter(term, PLANES, scatter_dimension=0, tiled=True)]
    ppermute x12 -> x28, waiting for transfers between devices: 126 us -> 356 us  [the longest x6 202 us: next_plane(): lax.ppermute(block, PLANES, [(one, (one + 1) % count) for one in range(co...]
    dot_general x80 -> x18, matrix products: 372 us -> 175 us  [dot(): lax.dot_general(left, right, ((contract[:1], contract[1:]), ((), ())), pr...]
    all_to_all x0 -> x11, waiting for transfers between devices: none -> 157 us  [exchanged(): return lax.all_to_all(value, axes, split_axis=0, concat_axis=0, tiled=True)]
    dynamic_update_slice x32 -> x1, other arithmetic: 111 us -> 0.03 us  [spread_ring(): whole = lax.dynamic_update_index_in_dim(whole, arrived, place ^ step, 0)]
    pallas_call x0 -> x6, Pallas kernels: none -> 109 us  [the longest x3 54.4 us: mlp_adam(): pl.pallas_call(lambda *refs: mlp_adam_kernel(rate, per_side, part < 2, *r...]
  transfers between devices with their start and end apart: 20 -> 48, of which waited for: 10 -> 29; matrix products, arithmetic and copies ran while one was open for 11% -> 27% of each run, Pallas kernels for 0% -> 9%
where the time goes in v1:
time: 1160 us; the launch traced here: 1150 us
  waiting for transfers between devices  588 us (51%)
  matrix products  175 us (15%)
  Pallas kernels  109 us (9%)
  starting transfers between devices  93 us (8%)
  local copies, waits for them, and re-layouts  84.4 us (7%)
  other arithmetic  82.8 us (7%)
  between operations  15.2 us (1%)
    ppermute x6, waiting for transfers between devices, next_plane(): lax.ppermute(block, PLANES, [(one, (one + 1) % count) for one in range(co...  202 us
    dot_general x18, matrix products, dot(): lax.dot_general(left, right, ((contract[:1], contract[1:]), ((), ())), pr...  175 us
    all_to_all x11, waiting for transfers between devices, exchanged(): return lax.all_to_all(value, axes, split_axis=0, concat_axis=0, tiled=True)  157 us
    ppermute x6, waiting for transfers between devices, swapped(): return lax.ppermute(value, axis, [(0, 1), (1, 0)])  70.5 us
    all_to_all x11, starting transfers between devices, exchanged(): return lax.all_to_all(value, axes, split_axis=0, concat_axis=0, tiled=True)  58.7 us
    ppermute x6, waiting for transfers between devices, doubled(): other = lax.ppermute(value, axis, traded((axis,), step))  55.2 us
    pallas_call x3, Pallas kernels, mlp_adam(): pl.pallas_call(lambda *refs: mlp_adam_kernel(rate, per_side, part < 2, *r...  54.4 us
    all_gather x1, waiting for transfers between devices, on_device(): normed_two_all = lax.all_gather(normed_two, GROUP, axis=0, tiled=True)  52.8 us
  transfers between devices with their start and end apart: 48, of which 29 were waited for; matrix products, arithmetic and copies ran while one was open for 27% of the time, Pallas kernels for 9%

profile of v1, /device:TPU:13, one launch (start us, length us, event | category | flops | bytes accessed | tf_op | source)
XLA Modules:
  0.0 1147.4 jit_solution(1311343064282472814)
XLA Ops:
  12.9 8.1 mlp_chunks.1
  21.0 5.5 all-to-all-start
  27.5 35.6 %all-to-all-done = bf16[4,160,2048]{2,1,0:T(8,128)(2,1)} async-done(((bf16[4,160,2048]{2,1,0:T(8,128)(2,1)}), bf16[4,160,2048]{2,1,0:T(8,128)(2,1)}, u32[]{:S(2)}, u32[]{:S(2)}) %all-to-all-start) | async-done | bytes 2621472 | tf_op jit(solution)/shard_map/all_to_all | solution.py:141
  63.0 5.9 all-to-all-start.1
  71.0 21.2 %collective-permute-done = bf16[192,2560]{1,0:T(8,128)(2,1)} collective-permute-done((bf16[192,2560]{1,0:T(8,128)(2,1)}, bf16[192,2560]{1,0:T(8,128)(2,1)}, u32[]{:S(2)}, u32[]{:S(2)}) %collective-permute-start) | collective-permute-done | bytes 983072 | tf_op jit(solution)/shard_map/ppermute | solution.py:99
  95.2 25.0 %all-to-all-done.1 = bf16[4,160,1024]{2,1,0:T(8,128)(2,1)S(1)} async-done(((bf16[4,160,1024]{2,1,0:T(8,128)(2,1)}), bf16[4,160,1024]{2,1,0:T(8,128)(2,1)S(1)}, u32[]{:S(2)}, u32[]{:S(2)}) %all-to-all-start.1) | async-done | bytes 1310752 | tf_op jit(solution)/shard_map/all_to_all | solution.py:141
  120.2 49.2 %collective-permute-done.1 = bf16[640,2048]{1,0:T(8,128)(2,1)} collective-permute-done((bf16[640,2048]{1,0:T(8,128)(2,1)}, bf16[640,2048]{1,0:T(8,128)(2,1)}, u32[]{:S(2)}, u32[]{:S(2)}) %collective-permute-start.1) | collective-permute-done | bytes 2621472 | tf_op jit(solution)/shard_map/ppermute | solution.py:106
  169.5 4.9 fusion.2
  188.1 7.1 collective-permute-done.4
  195.3 4.5 collective-permute-done.7
  203.6 4.9 collective-permute-start.9
  222.5 4.3 fusion.89
  234.3 16.2 %attend.1 = (bf16[192,2560]{1,0:T(8,128)(2,1)}, f32[5,1,384]{2,1,0:T(1,128)S(1)}) custom-call(bf16[192,2560]{1,0:T(8,128)(2,1)S(1)} %copy-done.9, bf16[3072,256]{1,0:T(8,128)(2,1)S(1)} %get-tuple-element.151.key_ref, bf16[256,3072]{1,0:T(8,128)(2,1)S(1)} %copy.120.value_t_ref, f32[3072,384]{1,0:T(8,128)} %pad_maximum_fusion.2.bias_ref), custom_call_target="tpu_custom_call" | custom-call | flops 6039797760 | bytes 18087936 | tf_op jit(solution)/shard_map/attend/pallas_call | solution.py:306
  250.5 34.0 %collective-permute-done.12 = bf16[2,192,2560]{2,1,0:T(8,128)(2,1)} collective-permute-done((bf16[2,192,2560]{2,1,0:T(8,128)(2,1)}, bf16[2,192,2560]{2,1,0:T(8,128)(2,1)}, u32[]{:S(2)}, u32[]{:S(2)}) %collective-permute-start.12) | collective-permute-done | bytes 1966112 | tf_op jit(solution)/shard_map/ppermute | solution.py:99
  289.5 57.6 %collective-permute-done.11 = bf16[640,1024]{1,0:T(8,128)(2,1)S(1)} collective-permute-done((bf16[640,1024]{1,0:T(8,128)(2,1)}, bf16[640,1024]{1,0:T(8,128)(2,1)S(1)}, u32[]{:S(2)}, u32[]{:S(2)}) %collective-permute-start.11) | collective-permute-done | bytes 1310752 | tf_op jit(solution)/shard_map/ppermute | solution.py:106
  348.2 4.6 fusion.18
  352.8 5.0 fusion.22
  360.0 52.8 %all-gather.10.cloned.1.call-done = bf16[1536,2560]{1,0:T(8,128)(2,1)} async-done(((bf16[192,2560]{1,0:T(8,128)(2,1)}), bf16[1536,2560]{1,0:T(8,128)(2,1)}) %all-gather.10.cloned.1.call-update) | async-done | bytes 7864336 | tf_op jit(solution)/shard_map/all_gather | solution.py:501
  415.7 28.0 %collective-permute-done.15 = bf16[640,1024]{1,0:T(8,128)(2,1)} collective-permute-done((bf16[640,1024]{1,0:T(8,128)(2,1)}, bf16[640,1024]{1,0:T(8,128)(2,1)}, u32[]{:S(2)}, u32[]{:S(2)}) %collective-permute-start.15) | collective-permute-done | bytes 1310752 | tf_op jit(solution)/shard_map/ppermute | solution.py:106
  460.7 67.3 %collective-permute-done.16 = bf16[640,1024]{1,0:T(8,128)(2,1)} collective-permute-done((bf16[640,1024]{1,0:T(8,128)(2,1)}, bf16[640,1024]{1,0:T(8,128)(2,1)}, u32[]{:S(2)}, u32[]{:S(2)}) %collective-permute-start.16) | collective-permute-done | bytes 1310752 | tf_op jit(solution)/shard_map/ppermute | solution.py:106
  532.8 7.3 select_bitcast_fusion.1
  540.1 4.0 pad_maximum_fusion
  548.2 22.9 %fusion.90 = f32[1536,2048]{1,0:T(8,128)} fusion(bf16[1536,2560]{1,0:T(8,128)(2,1)} %all-gather.10.cloned.1.call-done, bf16[2560,2048]{1,0:T(8,128)(2,1)} %copy-done.27), kind=kOutput, calls=%fused_computation.205 | convolution fusion | flops 16106127360 | bytes 30932992 | tf_op jit(solution)/shard_map/dot_general | solution.py:80
  571.1 17.9 %fusion.8 = (bf16[1536,1024]{1,0:T(8,128)(2,1)S(1)}, bf16[1536,1024]{1,0:T(8,128)(2,1)S(1)}, bf16[1536,1024]{1,0:T(8,128)(2,1)}) fusion(f32[1536,2048]{1,0:T(8,128)} %fusion.90, bf16[1536,2560]{1,0:T(8,128)(2,1)S(1)} %bitcast.198, bf16[2560,1024]{1,0:T(8,128)(2,1)} %constant_dynamic-update-slice_fusion), kind=kOutput, calls=%fused_computation.20 | convolution fusion | flops 8097103872 | bytes 35127296 | tf_op jit(solution)/shard_map/dot_general | solution.py:80
  590.7 12.4 %convolution_convert_fusion.4 = bf16[768,2560]{1,0:T(8,128)(2,1)} fusion(bf16[768,2048]{1,0:T(8,128)(2,1)S(1)} %bitcast.214, bf16[2560,2048]{1,0:T(8,128)(2,1)} %copy-done.27), kind=kOutput, calls=%fused_computation.42 | convolution fusion | flops 8055029760 | bytes 17563648 | tf_op jit(solution)/shard_map/dot_general | solution.py:80
  604.2 6.8 collective-permute-done.17
  610.9 11.7 %add_convert_fusion = bf16[768,2560]{1,0:T(8,128)(2,1)} fusion(bf16[768,2560]{1,0:T(8,128)(2,1)} %collective-permute-done.17, bf16[768,2048]{1,0:T(8,128)(2,1)S(1)} %bitcast.213, bf16[2560,2048]{1,0:T(8,128)(2,1)S(1)} %bitcast.195), kind=kOutput, calls=%fused_computation.5 | convolution fusion | flops 8058961920 | bytes 21495808 | tf_op jit(solution)/shard_map/dot_general | solution.py:80
  622.6 13.2 %convolution_convert_fusion.1 = bf16[2560,1024]{1,0:T(8,128)(2,1)} fusion(bf16[1536,2560]{1,0:T(8,128)(2,1)} %bitcast.197, bf16[1536,1024]{1,0:T(8,128)(2,1)} %get-tuple-element.67), kind=kOutput, calls=%fused_computation.39 | convolution fusion | flops 8055685120 | bytes 16252928 | tf_op jit(solution)/shard_map/dot_general | solution.py:80
  635.8 4.3 fusion.88
  640.1 5.2 all-to-all-start.2
  645.3 5.4 pad_maximum_fusion.1
  650.7 17.6 %all-to-all-done.2 = bf16[4,192,1280]{2,1,0:T(8,128)(2,1)} async-done(((bf16[4,192,1280]{2,1,0:T(8,128)(2,1)}), bf16[4,192,1280]{2,1,0:T(8,128)(2,1)}, u32[]{:S(2)}, u32[]{:S(2)}) %all-to-all-start.2) | async-done | bytes 1966112 | tf_op jit(solution)/shard_map/all_to_all | solution.py:141
  668.3 13.8 %convolution_convert_fusion.3 = bf16[2560,1024]{1,0:T(8,128)(2,1)} fusion(bf16[1536,2560]{1,0:T(8,128)(2,1)} %all-gather.10.cloned.1.call-done, bf16[1536,2048]{1,0:T(8,128)(2,1)} %pad_maximum_fusion.1), kind=kOutput, calls=%fused_computation.41 | convolution fusion | flops 8055685120 | bytes 16252928 | tf_op jit(solution)/shard_map/dot_general | solution.py:80
  685.3 4.6 all-to-all-start.3
  690.0 14.1 %convolution_convert_fusion.2 = bf16[2560,1024]{1,0:T(8,128)(2,1)} fusion(bf16[1536,2560]{1,0:T(8,128)(2,1)} %all-gather.10.cloned.1.call-done, bf16[1536,2048]{1,0:T(8,128)(2,1)} %pad_maximum_fusion.1), kind=kOutput, calls=%fused_computation.40 | convolution fusion | flops 8055685120 | bytes 16252928 | tf_op jit(solution)/shard_map/dot_general | solution.py:80
  705.9 12.8 %convolution_convert_fusion = bf16[1536,2560]{1,0:T(8,128)(2,1)} fusion(bf16[1536,1024]{1,0:T(8,128)(2,1)S(1)} %copy-done.65, bf16[2560,1024]{1,0:T(8,128)(2,1)} %constant_dynamic-update-slice_fusion), kind=kOutput, calls=%fused_computation | convolution fusion | flops 8056995840 | bytes 16252928 | tf_op jit(solution)/shard_map/dot_general | solution.py:80
  725.9 5.5 fusion.16
  731.5 5.1 convert_multiply_fusion.6
  738.9 5.4 all-to-all-start.4
  748.2 30.0 %attend_back.1 = (f32[192,2560]{1,0:T(8,128)}, f32[3072,512]{1,0:T(8,128)}) custom-call(bf16[192,2560]{1,0:T(8,128)(2,1)S(1)} %copy-done.10, bf16[192,2560]{1,0:T(8,128)(2,1)S(1)} %copy-done.11, bf16[3072,256]{1,0:T(8,128)(2,1)S(1)} %copy-done.5, bf16[256,3072]{1,0:T(8,128)(2,1)S(1)} %copy-done.6, bf16[3072,256]{1,0:T(8,128)(2,1)} %get-tuple-element.148.value_ref, ...), custom_call_target="tpu_custom_call" | custom-call | flops 15099494400 | bytes 22806528 | tf_op jit(solution)/shard_map/attend_back/pallas_call | solution.py:365
  778.2 4.8 convert_element_type.215
  799.6 41.0 %collective-permute-done.19 = bf16[2,2,192,512]{3,2,1,0:T(8,128)(2,1)} collective-permute-done((bf16[2,2,192,512]{3,2,1,0:T(8,128)(2,1)}, bf16[2,2,192,512]{3,2,1,0:T(8,128)(2,1)}, u32[]{:S(2)}, u32[]{:S(2)}) %collective-permute-start.19) | collective-permute-done | bytes 786464 | tf_op jit(solution)/shard_map/ppermute | solution.py:91
  860.9 4.9 all-to-all-start.5
  868.9 11.8 %all-to-all-done.5 = bf16[8,192,384]{2,1,0:T(8,128)(2,1)} async-done(((bf16[8,192,384]{2,1,0:T(8,128)(2,1)}), bf16[8,192,384]{2,1,0:T(8,128)(2,1)}, u32[]{:S(2)}, u32[]{:S(2)}) %all-to-all-start.5) | async-done | bytes 1179680 | tf_op jit(solution)/shard_map/all_to_all | solution.py:141
  880.7 4.5 all-to-all-start.6
  886.0 14.2 %all-to-all-done.6 = bf16[8,192,320]{2,1,0:T(8,128)(2,1)S(1)} async-done(((bf16[8,192,320]{2,1,0:T(8,128)(2,1)}), bf16[8,192,320]{2,1,0:T(8,128)(2,1)S(1)}, u32[]{:S(2)}, u32[]{:S(2)}) %all-to-all-start.6) | async-done | bytes 983072 | tf_op jit(solution)/shard_map/all_to_all | solution.py:141
  901.2 4.5 all-to-all-start.8
  905.7 7.4 convolution_convert_fusion.6
  916.9 4.2 all-to-all-done.8.refs_1_
  922.2 7.9 all-to-all-start.7
  930.1 21.5 %reduce-scatter.9.cloned.1.call-done = bf16[640,1024]{1,0:T(8,128)(2,1)} async-done(((bf16[2560,1024]{1,0:T(8,128)(2,1)}), bf16[640,1024]{1,0:T(8,128)(2,1)}) %reduce-scatter.9.cloned.1.call-update) | async-done | bytes 1310736 | tf_op jit(solution)/shard_map/reduce_scatter | solution.py:511
  951.6 30.2 %all-to-all-done.7 = bf16[16,160,320]{2,1,0:T(8,128)(2,1)} async-done(((bf16[16,160,320]{2,1,0:T(8,128)(2,1)}), bf16[16,160,320]{2,1,0:T(8,128)(2,1)}, u32[]{:S(2)}, u32[]{:S(2)}) %all-to-all-start.7) | async-done | bytes 1638432 | tf_op jit(solution)/shard_map/all_to_all | solution.py:141
  985.6 9.1 convolution_convert_fusion.5
  996.6 18.4 %all-to-all-done.9.refs_1_ = bf16[4,160,1024]{2,1,0:T(8,128)(2,1)S(1)} async-done(((bf16[4,160,1024]{2,1,0:T(8,128)(2,1)}), bf16[4,160,1024]{2,1,0:T(8,128)(2,1)S(1)}, u32[]{:S(2)}, u32[]{:S(2)}) %all-to-all-start.9) | async-done | bytes 1310752 | tf_op jit(solution)/shard_map/all_to_all | solution.py:141
  1015.0 6.6 all-to-all-start.10
  1022.9 17.5 %mlp_adam.3 = (f32[3,160,7680]{2,1,0:T(8,128)}, f32[3,160,7680]{2,1,0:T(8,128)}, f32[3,160,7680]{2,1,0:T(8,128)}, f32[160,1]{1,0:T(8,128)}) custom-call(s32[1]{0:T(128)} %bitcast.5.refs_0_, bf16[4,160,1024]{2,1,0:T(8,128)(2,1)S(1)} %all-to-all-done.4.refs_1_, bf16[4,160,1024]{2,1,0:T(8,128)(2,1)S(1)} %copy-done.8, f32[3,160,7680]{2,1,0:T(8,128)} %bitcast.174, ...), custom_call_target="tpu_custom_call" | custom-call | flops 24576000 | bytes 31948800 | tf_op jit(solution)/shard_map/mlp_adam/pallas_call | solution.py:239
  1041.7 6.1 fusion
  1048.1 7.3 fusion.48
  1056.6 13.9 %collective-permute-done.24.refs_2_ = bf16[4,160,1024]{2,1,0:T(8,128)(2,1)S(1)} collective-permute-done((bf16[4,160,1024]{2,1,0:T(8,128)(2,1)S(1)}, bf16[4,160,1024]{2,1,0:T(8,128)(2,1)S(1)}, u32[]{:S(2)}, u32[]{:S(2)}) %collective-permute-start.24) | collective-permute-done | bytes 1310752 | tf_op jit(solution)/shard_map/ppermute | solution.py:91
  1070.5 18.3 %mlp_adam.4 = (f32[3,160,7680]{2,1,0:T(8,128)}, f32[3,160,7680]{2,1,0:T(8,128)}, f32[3,160,7680]{2,1,0:T(8,128)}, f32[160,1]{1,0:T(8,128)S(1)}) custom-call(s32[1]{0:T(128)} %bitcast.5.refs_0_, bf16[4,160,1024]{2,1,0:T(8,128)(2,1)S(1)} %copy-done.1, ...), custom_call_target="tpu_custom_call", output_to_operand_aliasing={{0}: (7, {}), {1}: (8, {}), {2}: (9, {})} | custom-call | flops 24576000 | bytes 31948800 | tf_op jit(solution)/shard_map/mlp_adam/pallas_call | solution.py:239
  1097.6 5.8 multiply_subtract_fusion.2
  1103.4 5.7 collective-permute-done.27.refs_2_
  1109.1 18.5 %mlp_adam.5 = (f32[3,160,7680]{2,1,0:T(8,128)}, f32[3,160,7680]{2,1,0:T(8,128)}, f32[3,160,7680]{2,1,0:T(8,128)}, f32[160,1]{1,0:T(8,128)S(1)}) custom-call(s32[1]{0:T(128)} %bitcast.5.refs_0_, bf16[4,160,1024]{2,1,0:T(8,128)(2,1)S(1)} %all-to-all-done.9.refs_1_, ...), custom_call_target="tpu_custom_call", output_to_operand_aliasing={{0}: (7, {}), {1}: (8, {}), {2}: (9, {})} | custom-call | flops 24576000 | bytes 31948800 | tf_op jit(solution)/shard_map/mlp_adam/pallas_call | solution.py:239
  1135.9 4.7 fusion.47
  (332 shorter events, 181.7 us)
Async XLA Ops:
  7.2 162.3 %all-gather.6.cloned.1.call-start = ((), (), s32[]{:S(2)}) async-start(), calls=%async_computation.15 | async-start | bytes 16220160 | tf_op jit(solution)/shard_map/all_gather | solution.py:434
  10.8 337.3 %all-gather.8.cloned.1.call-start = ((), (), s32[]{:S(2)}) async-start(), calls=%async_computation.16 | async-start | bytes 13516800 | tf_op jit(solution)/shard_map/all_gather | solution.py:434
  21.0 42.0 %all-to-all-start = ((bf16[4,160,2048]{2,1,0:T(8,128)(2,1)}), bf16[4,160,2048]{2,1,0:T(8,128)(2,1)}, u32[]{:S(2)}, u32[]{:S(2)}) async-start(bf16[4,160,2048]{2,1,0:T(8,128)(2,1)} %get-tuple-element.53), calls=%async_computation | async-start | bytes 5242880 | tf_op jit(solution)/shard_map/all_to_all | solution.py:141
  26.5 43.7 %copy-start.63 = (s32[2,3]{1,0:T(2,128)S(1)}, s32[2,3]{1,0:T(2,128)}, u32[]{:S(2)}) copy-start(s32[2,3]{1,0:T(2,128)} %param.17) | copy-start | bytes 76
  26.5 65.7 %collective-permute-start = (bf16[192,2560]{1,0:T(8,128)(2,1)}, bf16[192,2560]{1,0:T(8,128)(2,1)}, u32[]{:S(2)}, u32[]{:S(2)}) collective-permute-start(bf16[192,2560]{1,0:T(8,128)(2,1)} %bitcast.2), channel_id=1, source_target_pairs={{0,2},{2,0},{1,3},{3,1},{4,6},{6,4},{5,7},{7,5},{8,10},{10,8},{9,1... | collective-permute-start | bytes 2949128 | tf_op jit(solution)/shard_map/ppermute | solution.py:99
  27.5 43.5 %copy-start.48 = (f32[192]{0:T(256)}, f32[192]{0:T(256)S(1)}, u32[]{:S(2)}) copy-start(f32[192]{0:T(256)S(1)} %get-tuple-element.179) | copy-start | bytes 2308
  63.0 57.2 %all-to-all-start.1 = ((bf16[4,160,1024]{2,1,0:T(8,128)(2,1)}), bf16[4,160,1024]{2,1,0:T(8,128)(2,1)S(1)}, u32[]{:S(2)}, u32[]{:S(2)}) async-start(bf16[4,160,1024]{2,1,0:T(8,128)(2,1)} %get-tuple-element.54), calls=%async_computation.1 | async-start | bytes 2621440 | tf_op jit(solution)/shard_map/all_to_all | solution.py:141
  68.9 344.0 %all-gather.10.cloned.1.call-start = ((), (), s32[]{:S(2)}) async-start(), calls=%async_computation.17 | async-start | bytes 8847360 | tf_op jit(solution)/shard_map/all_gather | solution.py:501
  68.9 100.5 %collective-permute-start.1 = (bf16[640,2048]{1,0:T(8,128)(2,1)}, bf16[640,2048]{1,0:T(8,128)(2,1)}, u32[]{:S(2)}, u32[]{:S(2)}) collective-permute-start(bf16[640,2048]{1,0:T(8,128)(2,1)} %bitcast.7), channel_id=1, source_target_pairs={{0,4},{4,8},{8,12},{12,0},{1,5},{5,9},{9,13},{13,1},{2,6},{6,10},{... | collective-permute-start | bytes 7864328 | tf_op jit(solution)/shard_map/ppermute | solution.py:106
  70.6 103.9 %copy-start.61 = (f32[128]{0:T(128)}, f32[128]{0:T(128)S(1)}, u32[]{:S(2)}) copy-start(f32[128]{0:T(128)S(1)} %multiply_exponential_fusion) | copy-start | bytes 1540
  70.7 103.7 %copy-start.50 = (f32[192]{0:T(256)}, f32[192]{0:T(256)S(1)}, u32[]{:S(2)}) copy-start(f32[192]{0:T(256)S(1)} %get-tuple-element.134) | copy-start | bytes 2308
  71.0 141.5 %copy-start.36 = (bf16[192,2560]{1,0:T(8,128)(2,1)}, bf16[192,2560]{1,0:T(8,128)(2,1)S(1)}, u32[]{:S(2)}) copy-start(bf16[192,2560]{1,0:T(8,128)(2,1)S(1)} %fusion.44) | copy-start | bytes 2949124
  120.2 54.1 %copy-start.34 = (bf16[4,160,1024]{2,1,0:T(8,128)(2,1)}, bf16[4,160,1024]{2,1,0:T(8,128)(2,1)S(1)}, u32[]{:S(2)}) copy-start(bf16[4,160,1024]{2,1,0:T(8,128)(2,1)S(1)} %all-to-all-done.1) | copy-start | bytes 3932164
  176.5 7.7 collective-permute-start.2
  177.1 10.2 collective-permute-start.3
  179.5 15.7 %collective-permute-start.4 = (bf16[192,512]{1,0:T(8,128)(2,1)S(1)}, bf16[192,512]{1,0:T(8,128)(2,1)S(1)}, u32[]{:S(2)}, u32[]{:S(2)}) collective-permute-start(bf16[192,512]{1,0:T(8,128)(2,1)S(1)} %pad_maximum_fusion.11), channel_id=1, source_target_pairs={{0,6},{2,4},{4,2},{6,0},{16,22},{18,20},{20,18},{22,16},{1,7},{3,5... | collective-permute-start | bytes 589832 | tf_op jit(solution)/shard_map/ppermute | solution.py:123
  180.6 14.7 %collective-permute-start.5 = (bf16[192,512]{1,0:T(8,128)(2,1)S(1)}, bf16[192,512]{1,0:T(8,128)(2,1)S(1)}, u32[]{:S(2)}, u32[]{:S(2)}) collective-permute-start(bf16[192,512]{1,0:T(8,128)(2,1)S(1)} %pad_maximum_fusion.11), channel_id=1, source_target_pairs={{0,16},{2,18},{4,20},{6,22},{16,0},{18,2},{20,4},{22,6},{1,17},{3,... | collective-permute-start | bytes 589832 | tf_op jit(solution)/shard_map/ppermute | solution.py:123
  180.8 14.5 %collective-permute-start.6 = (bf16[192,512]{1,0:T(8,128)(2,1)S(1)}, bf16[192,512]{1,0:T(8,128)(2,1)S(1)}, u32[]{:S(2)}, u32[]{:S(2)}) collective-permute-start(bf16[192,512]{1,0:T(8,128)(2,1)S(1)} %pad_maximum_fusion.11), channel_id=1, source_target_pairs={{0,18},{2,16},{4,22},{6,20},{16,2},{18,0},{20,6},{22,4},{1,19},{3,... | collective-permute-start | bytes 589832 | tf_op jit(solution)/shard_map/ppermute | solution.py:123
  182.0 30.5 %copy-start.64 = (bf16[5120,1536]{1,0:T(8,128)(2,1)S(1)}, bf16[5120,1536]{1,0:T(8,128)(2,1)}, u32[]{:S(2)}) copy-start(bf16[5120,1536]{1,0:T(8,128)(2,1)} %all-gather.6.cloned.1.call-done) | copy-start | bytes 47185924
  184.2 15.6 %collective-permute-start.7 = (bf16[192,512]{1,0:T(8,128)(2,1)S(1)}, bf16[192,512]{1,0:T(8,128)(2,1)S(1)}, u32[]{:S(2)}, u32[]{:S(2)}) collective-permute-start(bf16[192,512]{1,0:T(8,128)(2,1)S(1)} %pad_maximum_fusion.11), channel_id=1, source_target_pairs={{0,20},{2,22},{4,16},{6,18},{16,4},{18,6},{20,0},{22,2},{1,21},{3,... | collective-permute-start | bytes 589832 | tf_op jit(solution)/shard_map/ppermute | solution.py:123
  187.3 16.3 %collective-permute-start.8 = (bf16[192,512]{1,0:T(8,128)(2,1)S(1)}, bf16[192,512]{1,0:T(8,128)(2,1)S(1)}, u32[]{:S(2)}, u32[]{:S(2)}) collective-permute-start(bf16[192,512]{1,0:T(8,128)(2,1)S(1)} %pad_maximum_fusion.11), channel_id=1, source_target_pairs={{0,22},{2,20},{4,18},{6,16},{16,6},{18,4},{20,2},{22,0},{1,23},{3,... | collective-permute-start | bytes 589832 | tf_op jit(solution)/shard_map/ppermute | solution.py:123
  203.6 10.6 collective-permute-start.9
  216.4 68.1 %collective-permute-start.12 = (bf16[2,192,2560]{2,1,0:T(8,128)(2,1)}, bf16[2,192,2560]{2,1,0:T(8,128)(2,1)}, u32[]{:S(2)}, u32[]{:S(2)}) collective-permute-start(bf16[2,192,2560]{2,1,0:T(8,128)(2,1)} %pad_maximum_fusion.6), channel_id=1, source_target_pairs={{0,16},{16,0},{1,17},{17,1},{2,18},{18,2},{3,19},{19,3},{4,20},{20... | collective-permute-start | bytes 5898248 | tf_op jit(solution)/shard_map/ppermute | solution.py:99
  222.4 125.8 %collective-permute-start.10 = (bf16[640,2048]{1,0:T(8,128)(2,1)}, bf16[640,2048]{1,0:T(8,128)(2,1)}, u32[]{:S(2)}, u32[]{:S(2)}) collective-permute-start(bf16[640,2048]{1,0:T(8,128)(2,1)} %collective-permute-done.1), channel_id=1, source_target_pairs={{0,4},{4,8},{8,12},{12,0},{1,5},{5,9},{9,13},{13,1},{2,6},{6,10},{... | collective-permute-start | bytes 7864328 | tf_op jit(solution)/shard_map/ppermute | solution.py:106
  226.8 23.7 %copy-start.4 = (bf16[3072,256]{1,0:T(8,128)(2,1)}, bf16[3072,256]{1,0:T(8,128)(2,1)S(1)}, u32[]{:S(2)}) copy-start(bf16[3072,256]{1,0:T(8,128)(2,1)S(1)} %get-tuple-element.151.key_ref) | copy-start | bytes 4718596
  229.1 118.0 %collective-permute-start.11 = (bf16[640,1024]{1,0:T(8,128)(2,1)}, bf16[640,1024]{1,0:T(8,128)(2,1)S(1)}, u32[]{:S(2)}, u32[]{:S(2)}) collective-permute-start(bf16[640,1024]{1,0:T(8,128)(2,1)} %bitcast.203), channel_id=1, source_target_pairs={{0,4},{4,8},{8,12},{12,0},{1,5},{5,9},{9,13},{13,1},{2,6},{6,10},{... | collective-permute-start | bytes 3932168 | tf_op jit(solution)/shard_map/ppermute | solution.py:106
  360.0 275.8 %all-gather.12.cloned.1.call-start = ((), (), s32[]{:S(2)}) async-start(), calls=%async_computation.18 | async-start | bytes 8847360 | tf_op jit(solution)/shard_map/all_gather | solution.py:506
  412.9 222.9 %all-gather.14.cloned.1.call-start = ((), (), s32[]{:S(2)}) async-start(), calls=%async_computation.19 | async-start | bytes 8847360 | tf_op jit(solution)/shard_map/all_gather | solution.py:507
  412.9 119.8 %collective-permute-start.14 = (bf16[2,2,192,2560]{3,2,1,0:T(8,128)(2,1)}, bf16[2,2,192,2560]{3,2,1,0:T(8,128)(2,1)}, u32[]{:S(2)}, u32[]{:S(2)}) collective-permute-start(bf16[2,2,192,2560]{3,2,1,0:T(8,128)(2,1)} %pad_maximum_fusion.3), channel_id=1, source_target_pairs={{0,1},{1,0},{2,3},{3,2},{4,5},{5,4},{6,7},{7,6},{8,9},{9,8},{10,11... | collective-permute-start | bytes 11796488 | tf_op jit(solution)/shard_map/ppermute | solution.py:99
  413.3 30.4 %collective-permute-start.15 = (bf16[640,1024]{1,0:T(8,128)(2,1)}, bf16[640,1024]{1,0:T(8,128)(2,1)}, u32[]{:S(2)}, u32[]{:S(2)}) collective-permute-start(bf16[640,1024]{1,0:T(8,128)(2,1)} %copy-done.42), channel_id=1, source_target_pairs={{0,4},{4,8},{8,12},{12,0},{1,5},{5,9},{9,13},{13,1},{2,6},{6,10},{... | collective-permute-start | bytes 3932168 | tf_op jit(solution)/shard_map/ppermute | solution.py:106
  414.5 116.0 %collective-permute-start.13 = (bf16[640,2048]{1,0:T(8,128)(2,1)}, bf16[640,2048]{1,0:T(8,128)(2,1)}, u32[]{:S(2)}, u32[]{:S(2)}) collective-permute-start(bf16[640,2048]{1,0:T(8,128)(2,1)} %collective-permute-done.10), channel_id=1, source_target_pairs={{0,4},{4,8},{8,12},{12,0},{1,5},{5,9},{9,13},{13,1},{2,6},{6,10},{... | collective-permute-start | bytes 7864328 | tf_op jit(solution)/shard_map/ppermute | solution.py:106
  443.7 84.3 %collective-permute-start.16 = (bf16[640,1024]{1,0:T(8,128)(2,1)}, bf16[640,1024]{1,0:T(8,128)(2,1)}, u32[]{:S(2)}, u32[]{:S(2)}) collective-permute-start(bf16[640,1024]{1,0:T(8,128)(2,1)} %collective-permute-done.15), channel_id=1, source_target_pairs={{0,4},{4,8},{8,12},{12,0},{1,5},{5,9},{9,13},{13,1},{2,6},{6,10},{... | collective-permute-start | bytes 3932168 | tf_op jit(solution)/shard_map/ppermute | solution.py:106
  547.9 191.0 %reduce-scatter.5.cloned.1.call-start = ((), (), s32[]{:S(2)}) async-start(), calls=%async_computation.20 | async-start | bytes 6553600 | tf_op jit(solution)/shard_map/reduce_scatter | solution.py:511
  548.2 22.9 %copy-start.28 = (bf16[2,2,2,192,2560]{4,3,2,1,0:T(8,128)(2,1)S(1)}, bf16[2,2,2,192,2560]{4,3,2,1,0:T(8,128)(2,1)}, u32[]{:S(2)}) copy-start(bf16[2,2,2,192,2560]{4,3,2,1,0:T(8,128)(2,1)} %copy.121) | copy-start | bytes 23592964
  589.0 21.9 %slice-start = ((s8[10485760]{0:T(1024)(128)(4,1)}), s8[2097152]{0:T(1024)(128)(4,1)S(1)}, s32[]{:S(2)}) async-start(s8[10485760]{0:T(1024)(128)(4,1)} %bitcast.194), calls=%async_computation.24 | async-start | bytes 4194304
  590.7 20.3 %slice-start.1 = ((s8[10485760]{0:T(1024)(128)(4,1)}), s8[4194304]{0:T(1024)(128)(4,1)S(1)}, s32[]{:S(2)}) async-start(s8[10485760]{0:T(1024)(128)(4,1)} %bitcast.194), calls=%async_computation.25 | async-start | bytes 8388608
  590.7 20.3 %slice-start.2 = ((s8[10485760]{0:T(1024)(128)(4,1)}), s8[4194304]{0:T(1024)(128)(4,1)S(1)}, s32[]{:S(2)}) async-start(s8[10485760]{0:T(1024)(128)(4,1)} %bitcast.194), calls=%async_computation.26 | async-start | bytes 8388608
  603.1 7.8 collective-permute-start.17
  640.1 28.2 %all-to-all-start.2 = ((bf16[4,192,1280]{2,1,0:T(8,128)(2,1)}), bf16[4,192,1280]{2,1,0:T(8,128)(2,1)}, u32[]{:S(2)}, u32[]{:S(2)}) async-start(bf16[4,192,1280]{2,1,0:T(8,128)(2,1)} %get-tuple-element.145), calls=%async_computation.2 | async-start | bytes 3932160 | tf_op jit(solution)/shard_map/all_to_all | solution.py:141
  645.3 240.7 %reduce-scatter.11.cloned.1.call-start = ((), (), s32[]{:S(2)}) async-start(), calls=%async_computation.23 | async-start | bytes 6553600 | tf_op jit(solution)/shard_map/reduce_scatter | solution.py:511
  685.3 33.4 %all-to-all-start.3 = ((bf16[4,192,1280]{2,1,0:T(8,128)(2,1)}), bf16[4,192,1280]{2,1,0:T(8,128)(2,1)}, u32[]{:S(2)}, u32[]{:S(2)}) async-start(bf16[4,192,1280]{2,1,0:T(8,128)(2,1)} %get-tuple-element.62), calls=%async_computation.3 | async-start | bytes 3932160 | tf_op jit(solution)/shard_map/all_to_all | solution.py:141
  690.0 261.7 %reduce-scatter.9.cloned.1.call-start = ((), (), s32[]{:S(2)}) async-start(), calls=%async_computation.22 | async-start | bytes 6553600 | tf_op jit(solution)/shard_map/reduce_scatter | solution.py:511
  738.9 44.1 %all-to-all-start.4 = ((bf16[4,160,1024]{2,1,0:T(8,128)(2,1)}), bf16[4,160,1024]{2,1,0:T(8,128)(2,1)S(1)}, u32[]{:S(2)}, u32[]{:S(2)}) async-start(bf16[4,160,1024]{2,1,0:T(8,128)(2,1)} %bitcast.218), calls=%async_computation.5 | async-start | bytes 2621440 | tf_op jit(solution)/shard_map/all_to_all | solution.py:141
  785.7 3.6 collective-permute-start.18
  792.3 48.3 %collective-permute-start.19 = (bf16[2,2,192,512]{3,2,1,0:T(8,128)(2,1)}, bf16[2,2,192,512]{3,2,1,0:T(8,128)(2,1)}, u32[]{:S(2)}, u32[]{:S(2)}) collective-permute-start(bf16[2,2,192,512]{3,2,1,0:T(8,128)(2,1)} %dynamic-slice_bitcast_fusion.1), channel_id=1, source_target_pairs={{0,4},{4,0},{1,5},{5,1},{2,6},{6,2},{3,7},{7,3},{8,12},{12,8},{9,1... | collective-permute-start | bytes 2359304 | tf_op jit(solution)/shard_map/ppermute | solution.py:91
  798.0 46.9 %copy-start.26 = (f32[192,2560]{0,1:T(8,128)S(1)}, f32[192,2560]{0,1:T(8,128)}, u32[]{:S(2)}) copy-start(f32[192,2560]{0,1:T(8,128)} %copy.125) | copy-start | bytes 5898244
  798.0 46.9 %copy-start.45 = (f32[192,128]{0,1:T(8,128)S(1)}, f32[192,128]{0,1:T(8,128)}, u32[]{:S(2)}) copy-start(f32[192,128]{0,1:T(8,128)} %copy-done.44) | copy-start | bytes 294916
  798.0 59.9 %collective-permute-start.23 = (bf16[4,160,1024]{2,1,0:T(8,128)(2,1)S(1)}, bf16[4,160,1024]{2,1,0:T(8,128)(2,1)S(1)}, u32[]{:S(2)}, u32[]{:S(2)}) collective-permute-start(bf16[4,160,1024]{2,1,0:T(8,128)(2,1)S(1)} %all-to-all-done.4.refs_1_), channel_id=1, source_target_pairs={{0,16},{16,0},{1,17},{17,1},{2,18},{18,2},{3,19},{19,3},{4,20},{20... | collective-permute-start | bytes 3932168 | tf_op jit(solution)/shard_map/ppermute | solution.py:91
  842.2 6.9 collective-permute-start.22
  843.5 9.0 collective-permute-start.21
  843.8 10.4 collective-permute-start.20
  860.9 19.8 %all-to-all-start.5 = ((bf16[8,192,384]{2,1,0:T(8,128)(2,1)}), bf16[8,192,384]{2,1,0:T(8,128)(2,1)}, u32[]{:S(2)}, u32[]{:S(2)}) async-start(bf16[8,192,384]{2,1,0:T(8,128)(2,1)} %bitcast.207), calls=%async_computation.7 | async-start | bytes 2359296 | tf_op jit(solution)/shard_map/all_to_all | solution.py:141
  880.7 19.5 %all-to-all-start.6 = ((bf16[8,192,320]{2,1,0:T(8,128)(2,1)}), bf16[8,192,320]{2,1,0:T(8,128)(2,1)S(1)}, u32[]{:S(2)}, u32[]{:S(2)}) async-start(bf16[8,192,320]{2,1,0:T(8,128)(2,1)} %bitcast.172), calls=%async_computation.8 | async-start | bytes 2359296 | tf_op jit(solution)/shard_map/all_to_all | solution.py:141
  885.2 250.6 %reduce-scatter.7.cloned.1.call-start = ((), (), s32[]{:S(2)}) async-start(), calls=%async_computation.21 | async-start | bytes 8847360 | tf_op jit(solution)/shard_map/reduce_scatter | solution.py:562
  901.2 19.9 %all-to-all-start.8 = ((bf16[4,160,1024]{2,1,0:T(8,128)(2,1)}), bf16[4,160,1024]{2,1,0:T(8,128)(2,1)S(1)}, u32[]{:S(2)}, u32[]{:S(2)}) async-start(bf16[4,160,1024]{2,1,0:T(8,128)(2,1)} %bitcast.217), calls=%async_computation.12 | async-start | bytes 2621440 | tf_op jit(solution)/shard_map/all_to_all | solution.py:141
  922.2 59.7 %all-to-all-start.7 = ((bf16[16,160,320]{2,1,0:T(8,128)(2,1)}), bf16[16,160,320]{2,1,0:T(8,128)(2,1)}, u32[]{:S(2)}, u32[]{:S(2)}) async-start(bf16[16,160,320]{2,1,0:T(8,128)(2,1)} %bitcast.196), calls=%async_computation.9 | async-start | bytes 3932160 | tf_op jit(solution)/shard_map/all_to_all | solution.py:141
  981.9 33.1 %all-to-all-start.9 = ((bf16[4,160,1024]{2,1,0:T(8,128)(2,1)}), bf16[4,160,1024]{2,1,0:T(8,128)(2,1)S(1)}, u32[]{:S(2)}, u32[]{:S(2)}) async-start(bf16[4,160,1024]{2,1,0:T(8,128)(2,1)} %bitcast.216), calls=%async_computation.13 | async-start | bytes 2621440 | tf_op jit(solution)/shard_map/all_to_all | solution.py:141
  1015.0 79.5 %all-to-all-start.10 = ((bf16[16,160,384]{2,1,0:T(8,128)(2,1)}), bf16[16,160,384]{2,1,0:T(8,128)(2,1)}, u32[]{:S(2)}, u32[]{:S(2)}) async-start(bf16[16,160,384]{2,1,0:T(8,128)(2,1)} %bitcast.215), calls=%async_computation.14 | async-start | bytes 3932160 | tf_op jit(solution)/shard_map/all_to_all | solution.py:141
  1022.9 17.5 %copy-start.1 = (bf16[4,160,1024]{2,1,0:T(8,128)(2,1)S(1)}, bf16[4,160,1024]{2,1,0:T(8,128)(2,1)}, u32[]{:S(2)}) copy-start(bf16[4,160,1024]{2,1,0:T(8,128)(2,1)} %copy-done) | copy-start | bytes 3932164
  1022.9 18.8 %copy-start.32 = (bf16[192,3072]{0,1:T(8,128)(2,1)S(1)}, bf16[192,3072]{0,1:T(8,128)(2,1)}, u32[]{:S(2)}) copy-start(bf16[192,3072]{0,1:T(8,128)(2,1)} %pad_maximum_fusion.7) | copy-start | bytes 3538948
  1040.4 30.1 %collective-permute-start.24 = (bf16[4,160,1024]{2,1,0:T(8,128)(2,1)S(1)}, bf16[4,160,1024]{2,1,0:T(8,128)(2,1)S(1)}, u32[]{:S(2)}, u32[]{:S(2)}) collective-permute-start(bf16[4,160,1024]{2,1,0:T(8,128)(2,1)S(1)} %copy-done.1), channel_id=1, source_target_pairs={{0,16},{16,0},{1,17},{17,1},{2,18},{18,2},{3,19},{19,3},{4,20},{20... | collective-permute-start | bytes 3932168 | tf_op jit(solution)/shard_map/ppermute | solution.py:91
  1047.8 41.0 %collective-permute-start.26 = (bf16[4,160,320]{2,1,0:T(8,128)(2,1)S(1)}, bf16[4,160,320]{2,1,0:T(8,128)(2,1)S(1)}, u32[]{:S(2)}, u32[]{:S(2)}) collective-permute-start(bf16[4,160,320]{2,1,0:T(8,128)(2,1)S(1)} %reduce_sum.132), channel_id=1, source_target_pairs={{0,16},{16,0},{1,17},{17,1},{2,18},{18,2},{3,19},{19,3},{4,20},{20... | collective-permute-start | bytes 1228808 | tf_op jit(solution)/shard_map/ppermute | solution.py:99
  1055.4 53.7 %collective-permute-start.27 = (bf16[4,160,1024]{2,1,0:T(8,128)(2,1)S(1)}, bf16[4,160,1024]{2,1,0:T(8,128)(2,1)S(1)}, u32[]{:S(2)}, u32[]{:S(2)}) collective-permute-start(bf16[4,160,1024]{2,1,0:T(8,128)(2,1)S(1)} %all-to-all-done.9.refs_1_), channel_id=1, source_target_pairs={{0,16},{16,0},{1,17},{17,1},{2,18},{18,2},{3,19},{19,3},{4,20},{20... | collective-permute-start | bytes 3932168 | tf_op jit(solution)/shard_map/ppermute | solution.py:91
  1096.4 31.4 %collective-permute-start.25 = (bf16[4,160,384]{2,1,0:T(8,128)(2,1)S(1)}, bf16[4,160,384]{2,1,0:T(8,128)(2,1)}, u32[]{:S(2)}, u32[]{:S(2)}) collective-permute-start(bf16[4,160,384]{2,1,0:T(8,128)(2,1)S(1)} %reduce_sum.133), channel_id=1, source_target_pairs={{0,16},{16,0},{1,17},{17,1},{2,18},{18,2},{3,19},{19,3},{4,20},{20... | collective-permute-start | bytes 1474568 | tf_op jit(solution)/shard_map/ppermute | solution.py:99
  (57 other events, 226.7 us)
Sparse Core Ops, SparseCore 0:
  11.5 151.2 all-gather.5
  166.2 140.8 all-gather.7
  360.1 52.7 all-gather.9
  414.6 52.1 all-gather.11
  548.0 53.0 all-gather.13
  635.9 93.9 reduce-scatter.4
  732.8 107.0 reduce-scatter.10
  842.7 108.8 reduce-scatter.8
  955.1 93.2 reduce-scatter.6

commit v2 on v1

--- a/solution.py
+++ b/solution.py
@@ -473,10 +473,10 @@
     window_kv = spread_ring(jnp.concatenate([key_low, value_low], axis=1))
     window_kv = doubled(window_kv, "c", 1, 1)
     window_kv = window_kv.reshape(SEQ_LEN, 2 * HEAD_DIM)
-    gate_up_blocks.append(next_plane(after(gate_up_blocks[1], window_kv)))
+    gate_up_blocks.append(next_plane(after(gate_up_blocks[1], projected)))
     for _ in range(planes - 3):
         gate_up_blocks.append(next_plane(gate_up_blocks[-1]))
-    down_blocks.append(next_plane(after(down_blocks[0], window_kv)))
+    down_blocks.append(next_plane(after(down_blocks[0], projected)))
     for _ in range(planes - 2):
         down_blocks.append(next_plane(down_blocks[-1]))
     gate_up_own = joined_planes(gate_up_blocks)
@@ -484,7 +484,7 @@
     incoming_sides = doubled(after(incoming_columns, window_kv), "seq", 1, 0)
     query_pre = projected[:, :width].reshape(tok_rows, head_count, HEAD_DIM)
     queries = low(rotate(query_pre, cosine[:, None, :], sine[:, None, :]) * query_scale)
-    queries = queries.reshape(tok_rows, width)
+    queries = after(queries.reshape(tok_rows, width), gate_up_blocks[2], down_blocks[1])
     incoming_all = doubled(incoming_sides, "c", 1, incoming_sides.ndim - 2)
     incoming_all = incoming_all.reshape(sides * members * tok_rows, width)
     keys_win = window_kv[:, :HEAD_DIM]
@@ -492,12 +492,12 @@
     bias = jnp.where(allowed.T, 0.0, MASKED_SCORE)
     bias = jnp.concatenate([bias, bias], axis=1)
     attn_low, log_total = attend(queries, keys_win, values_win, bias)
-    attn_low = after(attn_low, gate_up_blocks[2], down_blocks[1], incoming_sides)
+    attn_low = after(attn_low, incoming_sides)
     branch = [dot(attn_low, half, (1, 0)) for half in out_halves]
     middle = tokens + jnp.concatenate(branch, axis=1)
 
     factor_two = lax.rsqrt(jnp.mean(middle * middle, axis=-1, keepdims=True) + NORM_EPS)
-    normed_two = low(middle * factor_two)
+    normed_two = after(low(middle * factor_two), gate_up_blocks[3], down_blocks[2])
     normed_two_all = lax.all_gather(normed_two, GROUP, axis=0, tiled=True)
     grad_act = low(dot(incoming_all, down_own, (1, 0)))
     gate_up = dot(normed_two_all, gate_up_own, (1, 0))
@@ -515,30 +515,25 @@
         ours = exchanged(after(term, *others), ("k", "c"))
         return (ours, swapped(ours, "seq"))
 
-    by_core = grad_gate_up.reshape(sides * columns, 2, tok_rows, 2 * piece)
-
-    def core_term(which):
-        rows = lax.dynamic_index_in_dim(by_core, which, 1, keepdims=False)
-        return dot(rows.reshape(-1, 2 * piece), gate_up_own, (1, 1))
-
-    given = swapped(low(core_term(1 - core)), "c")
-    terms = low(core_term(core) + wide(given)).reshape(sides * columns, tok_rows, width)
-    half = width // sides
-    first, second = terms[:, :, :half], terms[:, :, half:]
+    def group_terms(hidden, weight):
+        by_core = hidden.reshape(sides * columns, 2, tok_rows, hidden.shape[1])
+
+        def one_core(which):
+            rows = lax.dynamic_index_in_dim(by_core, which, 1, keepdims=False)
+            return dot(rows.reshape(-1, hidden.shape[1]), weight, (1, 1))
+
+        given = swapped(low(one_core(1 - core)), "c")
+        return low(one_core(core) + wide(given)).reshape(sides * columns, tok_rows, width)
+
+    terms = group_terms(grad_gate_up, gate_up_own)
     down_term = low(dot(incoming_all, after(activated_low, terms), (0, 0)))
     down_term = after(down_term, attn_all, normed_one_all)
-    first = exchanged(first, CHIPS)
-    late = after(grad_gate_up, first)
-    gate_term = low(dot(normed_two_all, late[:, :piece], (0, 0)))
-    second = exchanged(after(second, first), CHIPS)
-    up_term = low(dot(normed_two_all, late[:, piece:], (0, 0)))
-    branch = low(dot(after(activated_low, first), down_own, (1, 1)))
-    grad_normed_two = jnp.sum(wide(jnp.concatenate([first, second], axis=2)), axis=0)
-    grad_normed_two = after(grad_normed_two, gate_term, up_term, branch)
+    late = after(grad_gate_up[:, :piece], terms)
+    gate_term = low(dot(normed_two_all, late, (0, 0)))
+    grad_normed_two = after(ring_sum(terms), down_term, gate_term)
 
     down_rows = to_owners(down_term)
     gate_rows = to_owners(gate_term)
-    up_rows = to_owners(up_term)
     down_pieces = in_plane(down_rows)
     grad_middle = (
         wide(incoming)
@@ -546,26 +541,42 @@
         - middle * factor_two**3 * jnp.mean(grad_normed_two * middle, axis=-1, keepdims=True)
     )
 
+    shares = sides * members
+
+    def by_column(terms):
+        terms = terms.reshape(tok_rows, shares, terms.shape[1] // shares).transpose(1, 0, 2)
+        return exchanged(terms, GROUP).reshape(shares * tok_rows, -1)
+
+    def to_rows(total):
+        total = exchanged(total.reshape(owner_count, own_rows, -1), OWNERS)
+        return low(jnp.sum(wide(total.reshape(planes, members, own_rows, -1)), axis=0))
+
+    def joined(total):
+        total = doubled(total, "seq", 1, 0).reshape(shares, own_rows, -1)
+        return wide(total.transpose(1, 0, 2).reshape(own_rows, -1))
+
     grad_branch_low = low(grad_middle)
+    out_columns = by_column(grad_branch_low)
     half = width // sides
     grad_mixed = sum(
         dot(grad_branch_low[:, index * half : (index + 1) * half], out_halves[index], (1, 1))
         for index in range(sides)
     )
     grad_mixed_low = low(grad_mixed)
+    branch = ring_sum(group_terms(after(activated_low, grad_mixed_low), down_own))
     delta = (wide(grad_mixed_low) * wide(attn_low)).reshape(tok_rows, head_count, HEAD_DIM)
     delta = jnp.sum(delta, axis=-1).T.reshape(log_total.shape)
     grad_query, grad_window = attend_back(
         queries, grad_mixed_low, keys_win, values_win, bias, log_total, delta
     )
-    grad_window = after(low(grad_window), down_pieces[0])
-    branch = lax.psum_scatter(
-        after(branch, grad_window), GROUP, scatter_dimension=0, tiled=True
-    )
+    grad_window = after(low(grad_window), down_pieces[0], out_columns)
+    late = after(grad_gate_up[:, piece:], grad_window)
+    up_term = low(dot(normed_two_all, late, (0, 0)))
+    up_rows = to_owners(up_term)
     grad_window = half_sum(grad_window.reshape(-1, 2, tok_rows, 2 * HEAD_DIM), "c", 1)
     grad_window = grad_window.reshape(sides, -1, columns, tok_rows, 2 * HEAD_DIM)
     grad_window = half_sum(grad_window, "h", 1).reshape(-1, tok_rows, 2 * HEAD_DIM)
-    grad_local = ring_sum(grad_window)
+    grad_local = after(ring_sum(grad_window), up_term)
     grad_query = grad_query.reshape(tok_rows, head_count, HEAD_DIM)
     grad_query_pre = rotate(
         grad_query * query_scale, cosine[:, None, :], -sine[:, None, :]
@@ -577,44 +588,26 @@
 
     grad_proj = after(grad_proj, down_pieces[1])
 
-    shares = sides * members
-
-    def by_column(terms):
-        terms = terms.reshape(tok_rows, shares, terms.shape[1] // shares).transpose(1, 0, 2)
-        return exchanged(terms, GROUP).reshape(shares * tok_rows, -1)
-
-    def to_rows(total):
-        total = exchanged(total.reshape(owner_count, own_rows, -1), OWNERS)
-        return low(jnp.sum(wide(total.reshape(planes, members, own_rows, -1)), axis=0))
-
-    def joined(total):
-        total = doubled(total, "seq", 1, 0).reshape(shares, own_rows, -1)
-        return wide(total.transpose(1, 0, 2).reshape(own_rows, -1))
-
-    out_columns = by_column(grad_branch_low)
     qkv_columns = by_column(grad_proj)
-    out_total = after(low(dot(attn_all, out_columns, (0, 0))), qkv_columns)
     qkv_total = low(dot(normed_one_all, qkv_columns, (0, 0)))
-    out_total = to_rows(out_total)
+    out_total = low(dot(attn_all, after(out_columns, qkv_columns), (0, 0)))
     gate_pieces = in_plane(gate_rows, qkv_columns)
-    up_pieces = in_plane(up_rows, gate_pieces[0])
-    grad_out = joined(out_total)
-    qkv_total = to_rows(after(qkv_total, out_total, up_pieces[0]))
+    qkv_total = to_rows(after(qkv_total, gate_pieces[0]))
+    up_pieces = in_plane(up_rows, qkv_total)
+    grad_out = joined(to_rows(after(out_total, up_pieces[0])))
 
     mlp_states = (mlp_planes, first_mlp.transpose(1, 0, 2), second_mlp.transpose(1, 0, 2))
     mlp_outs = ()
     gain_dots = {}
     rate_main = 2.0 * D ** (-0.5)
     for part, pieces in ((2, down_pieces), (0, gate_pieces), (1, up_pieces)):
-        if part == 1:
-            qkv_total = after(qkv_total, *mlp_outs)
         *mlp_outs, gain_dots[part] = mlp_adam(
             part, side, pieces, mlp_states, gain_two, rate_main, mlp_outs
         )
     grad_mlp, second_new_mlp, new_mlp = mlp_outs
     grad_gain_two = gain_dots[0] + gain_dots[1]
     grad_qkv = joined(qkv_total)
-    hidden_out = low(middle + wide(after(branch, grad_qkv))).reshape(1, 1, tok_rows, width)
+    hidden_out = low(middle + after(branch, grad_qkv)).reshape(1, 1, tok_rows, width)
 
     half = grad_proj.shape[1] // sides
     grad_normed = sum(

time: 1160 us -> 1140 us (0.983)
  waiting for transfers between devices: 588 us -> 558 us
    ppermute x3 -> x9, waiting for transfers between devices: 7.53 us -> 49.1 us  [ring_sum(): term = lax.ppermute(term, CHIPS, traded(CHIPS, step))]
    ppermute x6, waiting for transfers between devices: 55.2 us -> 20.5 us  [doubled(): other = lax.ppermute(value, axis, traded((axis,), step))]
    reduce_scatter x3, waiting for transfers between devices: 21.5 us -> 3.06 us  [to_owners(): return lax.psum_scatter(term, PLANES, scatter_dimension=0, tiled=True)]
    ppermute x6 -> x7, waiting for transfers between devices: 70.5 us -> 54.8 us  [swapped(): return lax.ppermute(value, axis, [(0, 1), (1, 0)])]
    all_to_all x11 -> x9, waiting for transfers between devices: 157 us -> 144 us  [exchanged(): return lax.all_to_all(value, axes, split_axis=0, concat_axis=0, tiled=True)]
    ppermute x6, waiting for transfers between devices: 202 us -> 214 us  [next_plane(): lax.ppermute(block, PLANES, [(one, (one + 1) % count) for one in range(co...]
    all_to_all x11 -> x9, starting transfers between devices: 58.7 us -> 50.2 us  [exchanged(): return lax.all_to_all(value, axes, split_axis=0, concat_axis=0, tiled=True)]
    dot_general x18 -> x19, matrix products: 175 us -> 178 us  [dot(): lax.dot_general(left, right, ((contract[:1], contract[1:]), ((), ())), pr...]
  transfers between devices with their start and end apart: 48 -> 52, of which waited for: 29 -> 27; matrix products, arithmetic and copies ran while one was open for 27% -> 29% of each run, Pallas kernels for 9% -> 10%
where the time goes in v2:
time: 1140 us; the launch traced here: 1120 us
  waiting for transfers between devices  558 us (49%)
  matrix products  178 us (16%)
  Pallas kernels  110 us (10%)
  other arithmetic  88.4 us (8%)
  local copies, waits for them, and re-layouts  87.6 us (8%)
  starting transfers between devices  83.5 us (7%)
  between operations  15.6 us (1%)
    ppermute x6, waiting for transfers between devices, next_plane(): lax.ppermute(block, PLANES, [(one, (one + 1) % count) for one in range(co...  214 us
    dot_general x19, matrix products, dot(): lax.dot_general(left, right, ((contract[:1], contract[1:]), ((), ())), pr...  178 us
    all_to_all x9, waiting for transfers between devices, exchanged(): return lax.all_to_all(value, axes, split_axis=0, concat_axis=0, tiled=True)  144 us
    ppermute x7, waiting for transfers between devices, swapped(): return lax.ppermute(value, axis, [(0, 1), (1, 0)])  54.8 us
    pallas_call x3, Pallas kernels, mlp_adam(): pl.pallas_call(lambda *refs: mlp_adam_kernel(rate, per_side, part < 2, *r...  54.2 us
    all_gather x1, waiting for transfers between devices, on_device(): normed_two_all = lax.all_gather(normed_two, GROUP, axis=0, tiled=True)  53.9 us
    all_to_all x9, starting transfers between devices, exchanged(): return lax.all_to_all(value, axes, split_axis=0, concat_axis=0, tiled=True)  50.2 us
    ppermute x9, waiting for transfers between devices, ring_sum(): term = lax.ppermute(term, CHIPS, traded(CHIPS, step))  49.1 us
  transfers between devices with their start and end apart: 52, of which 27 were waited for; matrix products, arithmetic and copies ran while one was open for 29% of the time, Pallas kernels for 10%

profile of v2, /device:TPU:13, one launch (start us, length us, event | category | flops | bytes accessed | tf_op | source)
XLA Modules:
  0.0 1120.5 jit_solution(7345635701175539908)
XLA Ops:
  12.9 8.1 mlp_chunks.1
  21.0 5.5 all-to-all-start
  27.4 35.6 %all-to-all-done = bf16[4,160,2048]{2,1,0:T(8,128)(2,1)} async-done(((bf16[4,160,2048]{2,1,0:T(8,128)(2,1)}), bf16[4,160,2048]{2,1,0:T(8,128)(2,1)}, u32[]{:S(2)}, u32[]{:S(2)}) %all-to-all-start) | async-done | bytes 2621472 | tf_op jit(solution)/shard_map/all_to_all | solution.py:141
  63.0 6.6 all-to-all-start.1
  71.7 20.5 %collective-permute-done = bf16[192,2560]{1,0:T(8,128)(2,1)} collective-permute-done((bf16[192,2560]{1,0:T(8,128)(2,1)S(1)}, bf16[192,2560]{1,0:T(8,128)(2,1)}, u32[]{:S(2)}, u32[]{:S(2)}) %collective-permute-start) | collective-permute-done | bytes 983072 | tf_op jit(solution)/shard_map/ppermute | solution.py:99
  94.9 25.3 %all-to-all-done.1 = bf16[4,160,1024]{2,1,0:T(8,128)(2,1)} async-done(((bf16[4,160,1024]{2,1,0:T(8,128)(2,1)}), bf16[4,160,1024]{2,1,0:T(8,128)(2,1)}, u32[]{:S(2)}, u32[]{:S(2)}) %all-to-all-start.1) | async-done | bytes 1310752 | tf_op jit(solution)/shard_map/all_to_all | solution.py:141
  120.3 49.9 %collective-permute-done.1 = bf16[640,2048]{1,0:T(8,128)(2,1)} collective-permute-done((bf16[640,2048]{1,0:T(8,128)(2,1)}, bf16[640,2048]{1,0:T(8,128)(2,1)}, u32[]{:S(2)}, u32[]{:S(2)}) %collective-permute-start.1) | collective-permute-done | bytes 2621472 | tf_op jit(solution)/shard_map/ppermute | solution.py:106
  170.2 4.9 fusion.2
  200.4 9.8 collective-permute-done.10
  214.1 5.2 fusion.6
  234.8 109.7 %collective-permute-done.3 = bf16[640,1024]{1,0:T(8,128)(2,1)} collective-permute-done((bf16[640,1024]{1,0:T(8,128)(2,1)}, bf16[640,1024]{1,0:T(8,128)(2,1)}, u32[]{:S(2)}, u32[]{:S(2)}) %collective-permute-start.3) | collective-permute-done | bytes 1310752 | tf_op jit(solution)/shard_map/ppermute | solution.py:106
  354.2 16.3 %attend.1 = (bf16[192,2560]{1,0:T(8,128)(2,1)}, f32[5,1,384]{2,1,0:T(1,128)S(1)}) custom-call(bf16[192,2560]{1,0:T(8,128)(2,1)S(1)} %copy-done.9, bf16[3072,256]{1,0:T(8,128)(2,1)S(1)} %get-tuple-element.159.key_ref, bf16[256,3072]{1,0:T(8,128)(2,1)S(1)} %copy.120.value_t_ref, f32[3072,384]{1,0:T(8,128)} %pad_maximum_fusion.1.bias_ref), custom_call_target="tpu_custom_call" | custom-call | flops 6039797760 | bytes 18087936 | tf_op jit(solution)/shard_map/attend/pallas_call | solution.py:306
  375.4 4.6 fusion.18
  380.1 5.0 fusion.22
  387.2 44.0 %collective-permute-done.13 = bf16[640,2048]{1,0:T(8,128)(2,1)} collective-permute-done((bf16[640,2048]{1,0:T(8,128)(2,1)}, bf16[640,2048]{1,0:T(8,128)(2,1)}, u32[]{:S(2)}, u32[]{:S(2)}) %collective-permute-start.13) | collective-permute-done | bytes 2621472 | tf_op jit(solution)/shard_map/ppermute | solution.py:106
  431.3 53.9 %all-gather.10.cloned.1.call-done = bf16[1536,2560]{1,0:T(8,128)(2,1)} async-done(((bf16[192,2560]{1,0:T(8,128)(2,1)}), bf16[1536,2560]{1,0:T(8,128)(2,1)}) %all-gather.10.cloned.1.call-update) | async-done | bytes 7864336 | tf_op jit(solution)/shard_map/all_gather | solution.py:501
  505.4 10.6 collective-permute-done.16
  520.9 7.3 select_bitcast_fusion.1
  528.3 4.1 pad_maximum_fusion
  532.4 3.7 copy.121
  536.6 23.0 %fusion.92 = f32[1536,2048]{1,0:T(8,128)} fusion(bf16[1536,2560]{1,0:T(8,128)(2,1)} %all-gather.10.cloned.1.call-done, bf16[2560,2048]{1,0:T(8,128)(2,1)} %copy-done.27), kind=kOutput, calls=%fused_computation.218 | convolution fusion | flops 16106127360 | bytes 30932992 | tf_op jit(solution)/shard_map/dot_general | solution.py:80
  559.6 20.8 %fusion.8 = (bf16[1536,1024]{1,0:T(8,128)(2,1)}, bf16[1536,1024]{1,0:T(8,128)(2,1)}, bf16[1536,1024]{1,0:T(8,128)(2,1)S(1)}) fusion(f32[1536,2048]{1,0:T(8,128)} %fusion.92, bf16[1536,2560]{1,0:T(8,128)(2,1)} %bitcast.221, bf16[2560,1024]{1,0:T(8,128)(2,1)} %constant_dynamic-update-slice_fusion), kind=kOutput, calls=%fused_computation.19 | convolution fusion | flops 8097103872 | bytes 35127296 | tf_op jit(solution)/shard_map/dot_general | solution.py:80
  580.4 4.3 fusion.34
  584.7 9.9 convolution_convert_fusion.4
  595.6 6.8 collective-permute-done.17
  602.3 11.8 %add_convert_fusion.1 = bf16[768,2560]{1,0:T(8,128)(2,1)} fusion(bf16[768,2560]{1,0:T(8,128)(2,1)} %collective-permute-done.17, bf16[768,2048]{1,0:T(8,128)(2,1)S(1)} %bitcast.240, bf16[2560,2048]{1,0:T(8,128)(2,1)S(1)} %bitcast.219), kind=kOutput, calls=%fused_computation.4 | convolution fusion | flops 8058961920 | bytes 21495808 | tf_op jit(solution)/shard_map/dot_general | solution.py:80
  614.1 12.3 %convolution_convert_fusion.2 = bf16[2560,1024]{1,0:T(8,128)(2,1)} fusion(bf16[1536,2560]{1,0:T(8,128)(2,1)} %bitcast.222, bf16[1536,1024]{1,0:T(8,128)(2,1)S(1)} %get-tuple-element.71), kind=kOutput, calls=%fused_computation.39 | convolution fusion | flops 8055685120 | bytes 16252928 | tf_op jit(solution)/shard_map/dot_general | solution.py:80
  628.3 12.4 %convolution_convert_fusion.1 = bf16[2560,1024]{1,0:T(8,128)(2,1)} fusion(bf16[1536,2560]{1,0:T(8,128)(2,1)} %all-gather.10.cloned.1.call-done, bf16[1536,1024]{1,0:T(8,128)(2,1)S(1)} %copy-done.37), kind=kOutput, calls=%fused_computation.38 | convolution fusion | flops 8055685120 | bytes 16252928 | tf_op jit(solution)/shard_map/dot_general | solution.py:80
  640.7 3.4 dynamic-slice_bitcast_fusion.6
  648.5 19.8 %collective-permute-done.20 = bf16[192,2560]{1,0:T(8,128)(2,1)} collective-permute-done((bf16[192,2560]{1,0:T(8,128)(2,1)}, bf16[192,2560]{1,0:T(8,128)(2,1)}, u32[]{:S(2)}, u32[]{:S(2)}) %collective-permute-start.20) | collective-permute-done | bytes 983072 | tf_op jit(solution)/shard_map/ppermute | solution.py:135
  668.3 20.5 %collective-permute-done.19 = bf16[192,2560]{1,0:T(8,128)(2,1)} collective-permute-done((bf16[192,2560]{1,0:T(8,128)(2,1)}, bf16[192,2560]{1,0:T(8,128)(2,1)}, u32[]{:S(2)}, u32[]{:S(2)}) %collective-permute-start.19) | collective-permute-done | bytes 983072 | tf_op jit(solution)/shard_map/ppermute | solution.py:135
  697.8 5.2 all-to-all-start.3
  703.0 5.1 fusion.16
  708.2 6.9 convert_multiply_fusion.6
  720.5 4.3 all-to-all-start.2
  728.6 31.3 %attend_back.1 = (f32[192,2560]{1,0:T(8,128)}, f32[3072,512]{1,0:T(8,128)}) custom-call(bf16[192,2560]{1,0:T(8,128)(2,1)S(1)} %copy-done.10, bf16[192,2560]{1,0:T(8,128)(2,1)S(1)} %copy-done.11, bf16[3072,256]{1,0:T(8,128)(2,1)S(1)} %copy-done.5, bf16[256,3072]{1,0:T(8,128)(2,1)S(1)} %copy-done.6, bf16[3072,256]{1,0:T(8,128)(2,1)} %get-tuple-element.156.value_ref, ...), custom_call_target="tpu_custom_call" | custom-call | flops 15099494400 | bytes 22806528 | tf_op jit(solution)/shard_map/attend_back/pallas_call | solution.py:365
  759.9 4.8 convert_element_type.256
  764.7 13.3 %convolution_convert_fusion = bf16[2560,1024]{1,0:T(8,128)(2,1)} fusion(bf16[1536,2560]{1,0:T(8,128)(2,1)} %all-gather.10.cloned.1.call-done, bf16[1536,1024]{1,0:T(8,128)(2,1)} %get-tuple-element.76), kind=kOutput, calls=%fused_computation.37 | convolution fusion | flops 8055685120 | bytes 16252928 | tf_op jit(solution)/shard_map/dot_general | solution.py:80
  785.0 3.5 constant_dynamic-slice_fusion.1
  790.7 8.4 convolution_convert_fusion.3
  800.9 30.4 %collective-permute-done.26 = bf16[2,2,192,512]{3,2,1,0:T(8,128)(2,1)S(1)} collective-permute-done((bf16[2,2,192,512]{3,2,1,0:T(8,128)(2,1)S(1)}, bf16[2,2,192,512]{3,2,1,0:T(8,128)(2,1)S(1)}, u32[]{:S(2)}, u32[]{:S(2)}) %collective-permute-start.26) | collective-permute-done | bytes 786464 | tf_op jit(solution)/shard_map/ppermute | solution.py:91
  838.7 3.3 collective-permute-done.28
  850.5 4.8 all-to-all-start.4
  855.4 14.9 %all-to-all-done.4 = bf16[8,192,384]{2,1,0:T(8,128)(2,1)} async-done(((bf16[8,192,384]{2,1,0:T(8,128)(2,1)}), bf16[8,192,384]{2,1,0:T(8,128)(2,1)}, u32[]{:S(2)}, u32[]{:S(2)}) %all-to-all-start.4) | async-done | bytes 1179680 | tf_op jit(solution)/shard_map/all_to_all | solution.py:141
  870.3 4.6 all-to-all-start.5
  874.9 9.1 convolution_convert_fusion.5
  883.9 6.4 all-to-all-done.5.refs_1_
  891.4 7.7 all-to-all-start.6
  899.1 8.5 add_convert_fusion
  913.1 59.3 %all-to-all-done.6 = bf16[16,160,384]{2,1,0:T(8,128)(2,1)} async-done(((bf16[16,160,384]{2,1,0:T(8,128)(2,1)}), bf16[16,160,384]{2,1,0:T(8,128)(2,1)}, u32[]{:S(2)}, u32[]{:S(2)}) %all-to-all-start.6) | async-done | bytes 1966112 | tf_op jit(solution)/shard_map/all_to_all | solution.py:141
  974.3 4.1 all-to-all-start.7
  978.5 4.0 fusion.49
  982.5 17.4 %mlp_adam.3 = (f32[3,160,7680]{2,1,0:T(8,128)}, f32[3,160,7680]{2,1,0:T(8,128)}, f32[3,160,7680]{2,1,0:T(8,128)}, f32[160,1]{1,0:T(8,128)}) custom-call(s32[1]{0:T(128)} %bitcast.5.refs_0_, bf16[4,160,1024]{2,1,0:T(8,128)(2,1)S(1)} %all-to-all-done.2.refs_1_, bf16[4,160,1024]{2,1,0:T(8,128)(2,1)S(1)} %copy-done.8, f32[3,160,7680]{2,1,0:T(8,128)} %bitcast.200, ...), custom_call_target="tpu_custom_call" | custom-call | flops 24576000 | bytes 31948800 | tf_op jit(solution)/shard_map/mlp_adam/pallas_call | solution.py:239
  999.9 5.4 convolution_convert_fusion.6
  1006.4 3.8 copy.134
  1010.2 7.4 all-to-all-start.8
  1017.6 6.4 fusion
  1024.4 5.2 fusion.47
  1029.6 5.8 collective-permute-done.34.refs_2_
  1035.4 18.4 %mlp_adam.4 = (f32[3,160,7680]{2,1,0:T(8,128)}, f32[3,160,7680]{2,1,0:T(8,128)}, f32[3,160,7680]{2,1,0:T(8,128)}, f32[160,1]{1,0:T(8,128)S(1)}) custom-call(s32[1]{0:T(128)} %bitcast.5.refs_0_, bf16[4,160,1024]{2,1,0:T(8,128)(2,1)S(1)} %copy-done.1, ...), custom_call_target="tpu_custom_call", output_to_operand_aliasing={{0}: (7, {}), {1}: (8, {}), {2}: (9, {})} | custom-call | flops 24576000 | bytes 31948800 | tf_op jit(solution)/shard_map/mlp_adam/pallas_call | solution.py:239
  1064.6 7.6 multiply_subtract_fusion
  1072.2 11.9 %collective-permute-done.33.refs_2_ = bf16[4,160,1024]{2,1,0:T(8,128)(2,1)S(1)} collective-permute-done((bf16[4,160,1024]{2,1,0:T(8,128)(2,1)S(1)}, bf16[4,160,1024]{2,1,0:T(8,128)(2,1)S(1)}, u32[]{:S(2)}, u32[]{:S(2)}) %collective-permute-start.33) | collective-permute-done | bytes 1310752 | tf_op jit(solution)/shard_map/ppermute | solution.py:91
  1084.1 18.4 %mlp_adam.5 = (f32[3,160,7680]{2,1,0:T(8,128)}, f32[3,160,7680]{2,1,0:T(8,128)}, f32[3,160,7680]{2,1,0:T(8,128)}, f32[160,1]{1,0:T(8,128)S(1)}) custom-call(s32[1]{0:T(128)} %bitcast.5.refs_0_, bf16[4,160,1024]{2,1,0:T(8,128)(2,1)S(1)} %all-to-all-done.7.refs_1_, ...), custom_call_target="tpu_custom_call", output_to_operand_aliasing={{0}: (7, {}), {1}: (8, {}), {2}: (9, {})} | custom-call | flops 24576000 | bytes 31948800 | tf_op jit(solution)/shard_map/mlp_adam/pallas_call | solution.py:239
  1107.5 5.8 multiply_subtract_fusion.2
  (324 shorter events, 176.1 us)
Async XLA Ops:
  7.2 163.0 %all-gather.6.cloned.1.call-start = ((), (), s32[]{:S(2)}) async-start(), calls=%async_computation.12 | async-start | bytes 16220160 | tf_op jit(solution)/shard_map/all_gather | solution.py:434
  10.8 364.6 %all-gather.8.cloned.1.call-start = ((), (), s32[]{:S(2)}) async-start(), calls=%async_computation.13 | async-start | bytes 13516800 | tf_op jit(solution)/shard_map/all_gather | solution.py:434
  21.0 42.0 %all-to-all-start = ((bf16[4,160,2048]{2,1,0:T(8,128)(2,1)}), bf16[4,160,2048]{2,1,0:T(8,128)(2,1)}, u32[]{:S(2)}, u32[]{:S(2)}) async-start(bf16[4,160,2048]{2,1,0:T(8,128)(2,1)} %get-tuple-element.55), calls=%async_computation | async-start | bytes 5242880 | tf_op jit(solution)/shard_map/all_to_all | solution.py:141
  26.5 44.5 %copy-start.58 = (s32[2,3]{1,0:T(2,128)S(1)}, s32[2,3]{1,0:T(2,128)}, u32[]{:S(2)}) copy-start(s32[2,3]{1,0:T(2,128)} %param.17) | copy-start | bytes 76
  26.5 65.7 %collective-permute-start = (bf16[192,2560]{1,0:T(8,128)(2,1)S(1)}, bf16[192,2560]{1,0:T(8,128)(2,1)}, u32[]{:S(2)}, u32[]{:S(2)}) collective-permute-start(bf16[192,2560]{1,0:T(8,128)(2,1)S(1)} %bitcast.234), channel_id=1, source_target_pairs={{0,2},{2,0},{1,3},{3,1},{4,6},{6,4},{5,7},{7,5},{8,10},{10,8},{9,1... | collective-permute-start | bytes 2949128 | tf_op jit(solution)/shard_map/ppermute | solution.py:99
  27.4 44.2 %copy-start.43 = (f32[192]{0:T(256)}, f32[192]{0:T(256)S(1)}, u32[]{:S(2)}) copy-start(f32[192]{0:T(256)S(1)} %get-tuple-element.189) | copy-start | bytes 2308
  63.0 57.2 %all-to-all-start.1 = ((bf16[4,160,1024]{2,1,0:T(8,128)(2,1)}), bf16[4,160,1024]{2,1,0:T(8,128)(2,1)}, u32[]{:S(2)}, u32[]{:S(2)}) async-start(bf16[4,160,1024]{2,1,0:T(8,128)(2,1)} %get-tuple-element.56), calls=%async_computation.1 | async-start | bytes 2621440 | tf_op jit(solution)/shard_map/all_to_all | solution.py:141
  69.7 415.6 %all-gather.10.cloned.1.call-start = ((), (), s32[]{:S(2)}) async-start(), calls=%async_computation.14 | async-start | bytes 8847360 | tf_op jit(solution)/shard_map/all_gather | solution.py:501
  69.7 100.5 %collective-permute-start.1 = (bf16[640,2048]{1,0:T(8,128)(2,1)}, bf16[640,2048]{1,0:T(8,128)(2,1)}, u32[]{:S(2)}, u32[]{:S(2)}) collective-permute-start(bf16[640,2048]{1,0:T(8,128)(2,1)} %bitcast.7), channel_id=1, source_target_pairs={{0,4},{4,8},{8,12},{12,0},{1,5},{5,9},{9,13},{13,1},{2,6},{6,10},{... | collective-permute-start | bytes 7864328 | tf_op jit(solution)/shard_map/ppermute | solution.py:106
  71.3 103.8 %copy-start.56 = (f32[128]{0:T(128)}, f32[128]{0:T(128)S(1)}, u32[]{:S(2)}) copy-start(f32[128]{0:T(128)S(1)} %multiply_exponential_fusion) | copy-start | bytes 1540
  71.4 103.7 %copy-start.45 = (f32[192]{0:T(256)}, f32[192]{0:T(256)S(1)}, u32[]{:S(2)}) copy-start(f32[192]{0:T(256)S(1)} %get-tuple-element.138) | copy-start | bytes 2308
  71.7 98.5 %copy-start.33 = (bf16[192,2560]{1,0:T(8,128)(2,1)}, bf16[192,2560]{1,0:T(8,128)(2,1)S(1)}, u32[]{:S(2)}) copy-start(bf16[192,2560]{1,0:T(8,128)(2,1)S(1)} %fusion.43) | copy-start | bytes 2949124
  177.3 7.5 collective-permute-start.4
  177.8 11.9 %collective-permute-start.5 = (bf16[192,512]{1,0:T(8,128)(2,1)S(1)}, bf16[192,512]{1,0:T(8,128)(2,1)S(1)}, u32[]{:S(2)}, u32[]{:S(2)}) collective-permute-start(bf16[192,512]{1,0:T(8,128)(2,1)S(1)} %pad_maximum_fusion.10), channel_id=1, source_target_pairs={{0,4},{2,6},{4,0},{6,2},{16,20},{18,22},{20,16},{22,18},{1,5},{3,7... | collective-permute-start | bytes 589832 | tf_op jit(solution)/shard_map/ppermute | solution.py:123
  180.3 15.6 %collective-permute-start.6 = (bf16[192,512]{1,0:T(8,128)(2,1)S(1)}, bf16[192,512]{1,0:T(8,128)(2,1)S(1)}, u32[]{:S(2)}, u32[]{:S(2)}) collective-permute-start(bf16[192,512]{1,0:T(8,128)(2,1)S(1)} %pad_maximum_fusion.10), channel_id=1, source_target_pairs={{0,6},{2,4},{4,2},{6,0},{16,22},{18,20},{20,18},{22,16},{1,7},{3,5... | collective-permute-start | bytes 589832 | tf_op jit(solution)/shard_map/ppermute | solution.py:123
  181.4 15.3 %collective-permute-start.7 = (bf16[192,512]{1,0:T(8,128)(2,1)S(1)}, bf16[192,512]{1,0:T(8,128)(2,1)S(1)}, u32[]{:S(2)}, u32[]{:S(2)}) collective-permute-start(bf16[192,512]{1,0:T(8,128)(2,1)S(1)} %pad_maximum_fusion.10), channel_id=1, source_target_pairs={{0,16},{2,18},{4,20},{6,22},{16,0},{18,2},{20,4},{22,6},{1,17},{3,... | collective-permute-start | bytes 589832 | tf_op jit(solution)/shard_map/ppermute | solution.py:123
  181.5 15.8 %collective-permute-start.8 = (bf16[192,512]{1,0:T(8,128)(2,1)S(1)}, bf16[192,512]{1,0:T(8,128)(2,1)S(1)}, u32[]{:S(2)}, u32[]{:S(2)}) collective-permute-start(bf16[192,512]{1,0:T(8,128)(2,1)S(1)} %pad_maximum_fusion.10), channel_id=1, source_target_pairs={{0,18},{2,16},{4,22},{6,20},{16,2},{18,0},{20,6},{22,4},{1,19},{3,... | collective-permute-start | bytes 589832 | tf_op jit(solution)/shard_map/ppermute | solution.py:123
  184.8 14.9 %collective-permute-start.9 = (bf16[192,512]{1,0:T(8,128)(2,1)S(1)}, bf16[192,512]{1,0:T(8,128)(2,1)S(1)}, u32[]{:S(2)}, u32[]{:S(2)}) collective-permute-start(bf16[192,512]{1,0:T(8,128)(2,1)S(1)} %pad_maximum_fusion.10), channel_id=1, source_target_pairs={{0,20},{2,22},{4,16},{6,18},{16,4},{18,6},{20,0},{22,2},{1,21},{3,... | collective-permute-start | bytes 589832 | tf_op jit(solution)/shard_map/ppermute | solution.py:123
  189.7 20.5 %collective-permute-start.10 = (bf16[192,512]{1,0:T(8,128)(2,1)S(1)}, bf16[192,512]{1,0:T(8,128)(2,1)S(1)}, u32[]{:S(2)}, u32[]{:S(2)}) collective-permute-start(bf16[192,512]{1,0:T(8,128)(2,1)S(1)} %pad_maximum_fusion.10), channel_id=1, source_target_pairs={{0,22},{2,20},{4,18},{6,16},{16,6},{18,4},{20,2},{22,0},{1,23},{3,... | collective-permute-start | bytes 589832 | tf_op jit(solution)/shard_map/ppermute | solution.py:123
  210.8 12.9 %collective-permute-start.11 = (bf16[8,192,512]{2,1,0:T(8,128)(2,1)}, bf16[8,192,512]{2,1,0:T(8,128)(2,1)}, u32[]{:S(2)}, u32[]{:S(2)}) collective-permute-start(bf16[8,192,512]{2,1,0:T(8,128)(2,1)} %bitcast_dynamic-update-slice_fusion), channel_id=1, source_target_pairs={{0,1},{1,0},{2,3},{3,2},{4,5},{5,4},{6,7},{7,6},{8,9},{9,8},{10,11... | collective-permute-start | bytes 4718600 | tf_op jit(solution)/shard_map/ppermute | solution.py:99
  219.4 130.0 %collective-permute-start.2 = (bf16[640,2048]{1,0:T(8,128)(2,1)}, bf16[640,2048]{1,0:T(8,128)(2,1)}, u32[]{:S(2)}, u32[]{:S(2)}) collective-permute-start(bf16[640,2048]{1,0:T(8,128)(2,1)} %collective-permute-done.1), channel_id=1, source_target_pairs={{0,4},{4,8},{8,12},{12,0},{1,5},{5,9},{9,13},{13,1},{2,6},{6,10},{... | collective-permute-start | bytes 7864328 | tf_op jit(solution)/shard_map/ppermute | solution.py:106
  222.6 122.0 %collective-permute-start.3 = (bf16[640,1024]{1,0:T(8,128)(2,1)}, bf16[640,1024]{1,0:T(8,128)(2,1)}, u32[]{:S(2)}, u32[]{:S(2)}) collective-permute-start(bf16[640,1024]{1,0:T(8,128)(2,1)} %bitcast.8), channel_id=1, source_target_pairs={{0,4},{4,8},{8,12},{12,0},{1,5},{5,9},{9,13},{13,1},{2,6},{6,10},{... | collective-permute-start | bytes 3932168 | tf_op jit(solution)/shard_map/ppermute | solution.py:106
  227.7 142.7 %collective-permute-start.12 = (bf16[2,192,2560]{2,1,0:T(8,128)(2,1)}, bf16[2,192,2560]{2,1,0:T(8,128)(2,1)}, u32[]{:S(2)}, u32[]{:S(2)}) collective-permute-start(bf16[2,192,2560]{2,1,0:T(8,128)(2,1)} %pad_maximum_fusion.5), channel_id=1, source_target_pairs={{0,16},{16,0},{1,17},{17,1},{2,18},{18,2},{3,19},{19,3},{4,20},{20... | collective-permute-start | bytes 5898248 | tf_op jit(solution)/shard_map/ppermute | solution.py:99
  233.5 111.2 %copy-start.25 = (bf16[8,2,192,512]{3,2,1,0:T(8,128)(2,1)S(1)}, bf16[8,2,192,512]{3,2,1,0:T(8,128)(2,1)}, u32[]{:S(2)}) copy-start(bf16[8,2,192,512]{3,2,1,0:T(8,128)(2,1)} %pad_maximum_fusion.3) | copy-start | bytes 9437188
  344.6 42.6 %collective-permute-start.14 = (bf16[640,1024]{1,0:T(8,128)(2,1)}, bf16[640,1024]{1,0:T(8,128)(2,1)}, u32[]{:S(2)}, u32[]{:S(2)}) collective-permute-start(bf16[640,1024]{1,0:T(8,128)(2,1)} %collective-permute-done.3), channel_id=1, source_target_pairs={{0,4},{4,8},{8,12},{12,0},{1,5},{5,9},{9,13},{13,1},{2,6},{6,10},{... | collective-permute-start | bytes 3932168 | tf_op jit(solution)/shard_map/ppermute | solution.py:106
  351.7 79.5 %collective-permute-start.13 = (bf16[640,2048]{1,0:T(8,128)(2,1)}, bf16[640,2048]{1,0:T(8,128)(2,1)}, u32[]{:S(2)}, u32[]{:S(2)}) collective-permute-start(bf16[640,2048]{1,0:T(8,128)(2,1)} %collective-permute-done.2), channel_id=1, source_target_pairs={{0,4},{4,8},{8,12},{12,0},{1,5},{5,9},{9,13},{13,1},{2,6},{6,10},{... | collective-permute-start | bytes 7864328 | tf_op jit(solution)/shard_map/ppermute | solution.py:106
  431.2 195.1 %all-gather.12.cloned.1.call-start = ((), (), s32[]{:S(2)}) async-start(), calls=%async_computation.15 | async-start | bytes 8847360 | tf_op jit(solution)/shard_map/all_gather | solution.py:506
  485.2 141.1 %all-gather.14.cloned.1.call-start = ((), (), s32[]{:S(2)}) async-start(), calls=%async_computation.16 | async-start | bytes 8847360 | tf_op jit(solution)/shard_map/all_gather | solution.py:507
  485.3 35.5 %collective-permute-start.15 = (bf16[2,2,192,2560]{3,2,1,0:T(8,128)(2,1)}, bf16[2,2,192,2560]{3,2,1,0:T(8,128)(2,1)}, u32[]{:S(2)}, u32[]{:S(2)}) collective-permute-start(bf16[2,2,192,2560]{3,2,1,0:T(8,128)(2,1)} %pad_maximum_fusion.2), channel_id=1, source_target_pairs={{0,1},{1,0},{2,3},{3,2},{4,5},{5,4},{6,7},{7,6},{8,9},{9,8},{10,11... | collective-permute-start | bytes 11796488 | tf_op jit(solution)/shard_map/ppermute | solution.py:99
  485.6 30.4 %collective-permute-start.16 = (bf16[640,1024]{1,0:T(8,128)(2,1)}, bf16[640,1024]{1,0:T(8,128)(2,1)}, u32[]{:S(2)}, u32[]{:S(2)}) collective-permute-start(bf16[640,1024]{1,0:T(8,128)(2,1)} %collective-permute-done.14), channel_id=1, source_target_pairs={{0,4},{4,8},{8,12},{12,0},{1,5},{5,9},{9,13},{13,1},{2,6},{6,10},{... | collective-permute-start | bytes 3932168 | tf_op jit(solution)/shard_map/ppermute | solution.py:106
  536.1 184.3 %reduce-scatter.4.cloned.1.call-start = ((), (), s32[]{:S(2)}) async-start(), calls=%async_computation.17 | async-start | bytes 6553600 | tf_op jit(solution)/shard_map/reduce_scatter | solution.py:511
  536.6 48.1 %slice-start = ((s8[10485760]{0:T(1024)(128)(4,1)}), s8[4194304]{0:T(1024)(128)(4,1)S(1)}, s32[]{:S(2)}) async-start(s8[10485760]{0:T(1024)(128)(4,1)} %bitcast.218), calls=%async_computation.20 | async-start | bytes 8388608
  536.6 48.1 %slice-start.1 = ((s8[10485760]{0:T(1024)(128)(4,1)}), s8[4194304]{0:T(1024)(128)(4,1)S(1)}, s32[]{:S(2)}) async-start(s8[10485760]{0:T(1024)(128)(4,1)} %bitcast.218), calls=%async_computation.21 | async-start | bytes 8388608
  594.6 7.8 collective-permute-start.17
  626.4 229.0 %reduce-scatter.6.cloned.1.call-start = ((), (), s32[]{:S(2)}) async-start(), calls=%async_computation.18 | async-start | bytes 6553600 | tf_op jit(solution)/shard_map/reduce_scatter | solution.py:511
  644.1 24.2 %collective-permute-start.20 = (bf16[192,2560]{1,0:T(8,128)(2,1)}, bf16[192,2560]{1,0:T(8,128)(2,1)}, u32[]{:S(2)}, u32[]{:S(2)}) collective-permute-start(bf16[192,2560]{1,0:T(8,128)(2,1)} %get-tuple-element.152), channel_id=1, source_target_pairs={{0,18},{2,16},{16,2},{18,0},{1,19},{3,17},{17,3},{19,1},{4,22},{6,... | collective-permute-start | bytes 2949128 | tf_op jit(solution)/shard_map/ppermute | solution.py:135
  645.7 43.2 %collective-permute-start.19 = (bf16[192,2560]{1,0:T(8,128)(2,1)}, bf16[192,2560]{1,0:T(8,128)(2,1)}, u32[]{:S(2)}, u32[]{:S(2)}) collective-permute-start(bf16[192,2560]{1,0:T(8,128)(2,1)} %get-tuple-element.153), channel_id=1, source_target_pairs={{0,16},{2,18},{16,0},{18,2},{1,17},{3,19},{17,1},{19,3},{4,20},{6,... | collective-permute-start | bytes 2949128 | tf_op jit(solution)/shard_map/ppermute | solution.py:135
  645.9 44.1 %collective-permute-start.18 = (bf16[192,2560]{1,0:T(8,128)(2,1)S(1)}, bf16[192,2560]{1,0:T(8,128)(2,1)}, u32[]{:S(2)}, u32[]{:S(2)}) collective-permute-start(bf16[192,2560]{1,0:T(8,128)(2,1)S(1)} %get-tuple-element.151), channel_id=1, source_target_pairs={{0,2},{2,0},{16,18},{18,16},{1,3},{3,1},{17,19},{19,17},{4,6},{6,4... | collective-permute-start | bytes 2949128 | tf_op jit(solution)/shard_map/ppermute | solution.py:135
  648.5 44.1 %copy-start.14 = (bf16[1,1,192,2560]{3,2,1,0:T(8,128)(2,1)S(1)}, bf16[1,1,192,2560]{3,2,1,0:T(8,128)(2,1)}, u32[]{:S(2)}) copy-start(bf16[1,1,192,2560]{3,2,1,0:T(8,128)(2,1)} %param.15) | copy-start | bytes 2949124
  648.5 44.1 %copy-start.17 = (f32[192,1280]{1,0:T(8,128)S(1)}, f32[192,1280]{1,0:T(8,128)}, u32[]{:S(2)}) copy-start(f32[192,1280]{1,0:T(8,128)} %copy-done.16) | copy-start | bytes 2949124
  648.5 44.1 %copy-start.20 = (f32[192,1280]{1,0:T(8,128)S(1)}, f32[192,1280]{1,0:T(8,128)}, u32[]{:S(2)}) copy-start(f32[192,1280]{1,0:T(8,128)} %copy-done.19) | copy-start | bytes 2949124
  697.8 22.7 %all-to-all-start.3 = ((bf16[8,192,320]{2,1,0:T(8,128)(2,1)}), bf16[8,192,320]{2,1,0:T(8,128)(2,1)}, u32[]{:S(2)}, u32[]{:S(2)}) async-start(bf16[8,192,320]{2,1,0:T(8,128)(2,1)} %bitcast.198), calls=%async_computation.4 | async-start | bytes 2359296 | tf_op jit(solution)/shard_map/all_to_all | solution.py:141
  720.5 44.3 %all-to-all-start.2 = ((bf16[4,160,1024]{2,1,0:T(8,128)(2,1)}), bf16[4,160,1024]{2,1,0:T(8,128)(2,1)S(1)}, u32[]{:S(2)}, u32[]{:S(2)}) async-start(bf16[4,160,1024]{2,1,0:T(8,128)(2,1)} %bitcast.247), calls=%async_computation.3 | async-start | bytes 2621440 | tf_op jit(solution)/shard_map/all_to_all | solution.py:141
  724.8 249.5 %reduce-scatter.8.cloned.1.call-start = ((), (), s32[]{:S(2)}) async-start(), calls=%async_computation.19 | async-start | bytes 6553600 | tf_op jit(solution)/shard_map/reduce_scatter | solution.py:511
  780.7 7.7 collective-permute-start.25
  790.4 40.9 %collective-permute-start.26 = (bf16[2,2,192,512]{3,2,1,0:T(8,128)(2,1)S(1)}, bf16[2,2,192,512]{3,2,1,0:T(8,128)(2,1)S(1)}, u32[]{:S(2)}, u32[]{:S(2)}) collective-permute-start(bf16[2,2,192,512]{3,2,1,0:T(8,128)(2,1)S(1)} %dynamic-slice_bitcast_fusion.7), channel_id=1, source_target_pairs={{0,4},{4,0},{1,5},{5,1},{2,6},{6,2},{3,7},{7,3},{8,12},{12,8},{9,1... | collective-permute-start | bytes 2359304 | tf_op jit(solution)/shard_map/ppermute | solution.py:91
  799.1 35.2 %copy-start.26 = (f32[192,2560]{0,1:T(8,128)S(1)}, f32[192,2560]{0,1:T(8,128)}, u32[]{:S(2)}) copy-start(f32[192,2560]{0,1:T(8,128)} %copy.125) | copy-start | bytes 5898244
  799.1 99.9 %collective-permute-start.21 = (bf16[768,2560]{1,0:T(8,128)(2,1)}, bf16[768,2560]{1,0:T(8,128)(2,1)}, u32[]{:S(2)}, u32[]{:S(2)}) collective-permute-start(bf16[768,2560]{1,0:T(8,128)(2,1)} %convolution_convert_fusion.3), channel_id=1, source_target_pairs={{0,1},{1,0},{2,3},{3,2},{4,5},{5,4},{6,7},{7,6},{8,9},{9,8},{10,11... | collective-permute-start | bytes 11796488 | tf_op jit(solution)/shard_map/ppermute | solution.py:91
  799.7 47.9 %collective-permute-start.30 = (bf16[4,160,1024]{2,1,0:T(8,128)(2,1)S(1)}, bf16[4,160,1024]{2,1,0:T(8,128)(2,1)S(1)}, u32[]{:S(2)}, u32[]{:S(2)}) collective-permute-start(bf16[4,160,1024]{2,1,0:T(8,128)(2,1)S(1)} %all-to-all-done.2.refs_1_), channel_id=1, source_target_pairs={{0,16},{16,0},{1,17},{17,1},{2,18},{18,2},{3,19},{19,3},{4,20},{20... | collective-permute-start | bytes 3932168 | tf_op jit(solution)/shard_map/ppermute | solution.py:91
  831.6 7.1 collective-permute-start.29
  832.8 9.2 collective-permute-start.28
  833.1 10.5 collective-permute-start.27
  850.5 19.8 %all-to-all-start.4 = ((bf16[8,192,384]{2,1,0:T(8,128)(2,1)}), bf16[8,192,384]{2,1,0:T(8,128)(2,1)}, u32[]{:S(2)}, u32[]{:S(2)}) async-start(bf16[8,192,384]{2,1,0:T(8,128)(2,1)} %bitcast.229), calls=%async_computation.5 | async-start | bytes 2359296 | tf_op jit(solution)/shard_map/all_to_all | solution.py:141
  870.3 20.0 %all-to-all-start.5 = ((bf16[4,160,1024]{2,1,0:T(8,128)(2,1)}), bf16[4,160,1024]{2,1,0:T(8,128)(2,1)S(1)}, u32[]{:S(2)}, u32[]{:S(2)}) async-start(bf16[4,160,1024]{2,1,0:T(8,128)(2,1)} %bitcast.245), calls=%async_computation.7 | async-start | bytes 2621440 | tf_op jit(solution)/shard_map/all_to_all | solution.py:141
  891.4 81.0 %all-to-all-start.6 = ((bf16[16,160,384]{2,1,0:T(8,128)(2,1)}), bf16[16,160,384]{2,1,0:T(8,128)(2,1)}, u32[]{:S(2)}, u32[]{:S(2)}) async-start(bf16[16,160,384]{2,1,0:T(8,128)(2,1)} %bitcast.242), calls=%async_computation.8 | async-start | bytes 3932160 | tf_op jit(solution)/shard_map/all_to_all | solution.py:141
  910.4 68.1 %collective-permute-start.24 = (bf16[192,2560]{1,0:T(8,128)(2,1)}, bf16[192,2560]{1,0:T(8,128)(2,1)}, u32[]{:S(2)}, u32[]{:S(2)}) collective-permute-start(bf16[192,2560]{1,0:T(8,128)(2,1)} %get-tuple-element.149), channel_id=1, source_target_pairs={{0,18},{2,16},{16,2},{18,0},{1,19},{3,17},{17,3},{19,1},{4,22},{6,... | collective-permute-start | bytes 2949128 | tf_op jit(solution)/shard_map/ppermute | solution.py:135
  911.6 66.9 %collective-permute-start.23 = (bf16[192,2560]{1,0:T(8,128)(2,1)}, bf16[192,2560]{1,0:T(8,128)(2,1)}, u32[]{:S(2)}, u32[]{:S(2)}) collective-permute-start(bf16[192,2560]{1,0:T(8,128)(2,1)} %get-tuple-element.150), channel_id=1, source_target_pairs={{0,16},{2,18},{16,0},{18,2},{1,17},{3,19},{17,1},{19,3},{4,20},{6,... | collective-permute-start | bytes 2949128 | tf_op jit(solution)/shard_map/ppermute | solution.py:135
  911.9 66.6 %collective-permute-start.22 = (bf16[192,2560]{1,0:T(8,128)(2,1)}, bf16[192,2560]{1,0:T(8,128)(2,1)}, u32[]{:S(2)}, u32[]{:S(2)}) collective-permute-start(bf16[192,2560]{1,0:T(8,128)(2,1)} %get-tuple-element.148), channel_id=1, source_target_pairs={{0,2},{2,0},{16,18},{18,16},{1,3},{3,1},{17,19},{19,17},{4,6},{6,4... | collective-permute-start | bytes 2949128 | tf_op jit(solution)/shard_map/ppermute | solution.py:135
  974.3 32.0 %all-to-all-start.7 = ((bf16[4,160,1024]{2,1,0:T(8,128)(2,1)}), bf16[4,160,1024]{2,1,0:T(8,128)(2,1)S(1)}, u32[]{:S(2)}, u32[]{:S(2)}) async-start(bf16[4,160,1024]{2,1,0:T(8,128)(2,1)} %bitcast.246), calls=%async_computation.10 | async-start | bytes 2621440 | tf_op jit(solution)/shard_map/all_to_all | solution.py:141
  1005.3 30.1 %collective-permute-start.34 = (bf16[4,160,1024]{2,1,0:T(8,128)(2,1)S(1)}, bf16[4,160,1024]{2,1,0:T(8,128)(2,1)}, u32[]{:S(2)}, u32[]{:S(2)}) collective-permute-start(bf16[4,160,1024]{2,1,0:T(8,128)(2,1)S(1)} %copy-done.1), channel_id=1, source_target_pairs={{0,16},{16,0},{1,17},{17,1},{2,18},{18,2},{3,19},{19,3},{4,20},{20... | collective-permute-start | bytes 3932168 | tf_op jit(solution)/shard_map/ppermute | solution.py:91
  1010.2 52.1 %all-to-all-start.8 = ((bf16[16,160,320]{2,1,0:T(8,128)(2,1)}), bf16[16,160,320]{2,1,0:T(8,128)(2,1)}, u32[]{:S(2)}, u32[]{:S(2)}) async-start(bf16[16,160,320]{2,1,0:T(8,128)(2,1)} %bitcast.220), calls=%async_computation.11 | async-start | bytes 3932160 | tf_op jit(solution)/shard_map/all_to_all | solution.py:141
  1024.0 29.8 %collective-permute-start.31 = (bf16[4,160,384]{2,1,0:T(8,128)(2,1)S(1)}, bf16[4,160,384]{2,1,0:T(8,128)(2,1)S(1)}, u32[]{:S(2)}, u32[]{:S(2)}) collective-permute-start(bf16[4,160,384]{2,1,0:T(8,128)(2,1)S(1)} %reduce_sum.122), channel_id=1, source_target_pairs={{0,16},{16,0},{1,17},{17,1},{2,18},{18,2},{3,19},{19,3},{4,20},{20... | collective-permute-start | bytes 1474568 | tf_op jit(solution)/shard_map/ppermute | solution.py:99
  1055.8 28.3 %collective-permute-start.33 = (bf16[4,160,1024]{2,1,0:T(8,128)(2,1)S(1)}, bf16[4,160,1024]{2,1,0:T(8,128)(2,1)S(1)}, u32[]{:S(2)}, u32[]{:S(2)}) collective-permute-start(bf16[4,160,1024]{2,1,0:T(8,128)(2,1)S(1)} %all-to-all-done.7.refs_1_), channel_id=1, source_target_pairs={{0,16},{16,0},{1,17},{17,1},{2,18},{18,2},{3,19},{19,3},{4,20},{20... | collective-permute-start | bytes 3932168 | tf_op jit(solution)/shard_map/ppermute | solution.py:91
  1064.3 38.9 %collective-permute-start.32 = (bf16[4,160,320]{2,1,0:T(8,128)(2,1)S(1)}, bf16[4,160,320]{2,1,0:T(8,128)(2,1)}, u32[]{:S(2)}, u32[]{:S(2)}) collective-permute-start(bf16[4,160,320]{2,1,0:T(8,128)(2,1)S(1)} %reduce_sum.124), channel_id=1, source_target_pairs={{0,16},{16,0},{1,17},{17,1},{2,18},{18,2},{3,19},{19,3},{4,20},{20... | collective-permute-start | bytes 1228808 | tf_op jit(solution)/shard_map/ppermute | solution.py:99
  (52 other events, 360.5 us)
Sparse Core Ops, SparseCore 0:
  11.5 151.2 all-gather.5
  166.2 144.6 all-gather.7
  431.4 53.8 all-gather.9
  487.0 52.1 all-gather.11
  541.5 52.1 all-gather.13
  626.5 93.9 reduce-scatter.3
  723.3 107.0 reduce-scatter.5
  833.3 133.2 reduce-scatter.7

commit v3 on v2

--- a/solution.py
+++ b/solution.py
@@ -27,7 +27,6 @@
 CHIPS = ("seq", "k")
 GROUP = ("seq", "k", "c")
 RING = ("seq", "h", "k")
-EVERY = ("seq", "g", "h", "k", "c")
 
 
 def rotate(values, cosine, sine):
@@ -125,13 +124,15 @@
     return whole
 
 
-def ring_sum(terms):
+def ring_sum(terms, first=None):
     chips = terms.shape[0]
     place = lax.axis_index(CHIPS)
     total = 0.0
     for step in range(chips):
         term = lax.dynamic_index_in_dim(terms, place ^ step, 0, keepdims=False)
-        if step:
+        if step == 1 and first is not None:
+            term = first
+        elif step:
             term = lax.ppermute(term, CHIPS, traded(CHIPS, step))
         total = total + wide(term)
     return total
@@ -428,22 +429,27 @@
     gain_one = gains_low[:, :1]
     gain_two = gains_low[:, 1:]
     qkv_low = wide(low(weight_qkv))
-    def gathered(weight):
+    def regrouped(value, outer, inner):
+        value = value.reshape(value.shape[0], outer, inner, own_rows).transpose(0, 2, 1, 3)
+        return value.reshape(value.shape[0], outer * inner * own_rows)
+
+    mlp_planes = weight_mlp.transpose(1, 0, 2)
+    gate_up_chunks, down_chunks = mlp_chunks(mlp_planes, gain_two, side, members, piece)
+
+    def to_members(chunks):
+        return exchanged(chunks, ("k", "c")).reshape(members * own_rows, chunks.shape[2])
+
+    incoming = cotangent.reshape(tok_rows, width)
+    def gathered(weight, *others):
         half = weight.shape[1] // sides
         weight = lax.dynamic_slice_in_dim(weight, side * half, half, 1)
-        whole = lax.all_gather(weight, EVERY, axis=0, tiled=True)
-        return whole.reshape(sides, owner_count * own_rows, half)
-
-    qkv_halves = gathered(low(qkv_low * gain_one))
-    out_halves = gathered(low(weight_out))
-    mlp_planes = weight_mlp.transpose(1, 0, 2)
-    gate_up_chunks, down_chunks = mlp_chunks(mlp_planes, gain_two, side, members, piece)
-
-    def to_members(chunks):
-        return exchanged(chunks, ("k", "c")).reshape(members * own_rows, chunks.shape[2])
-
-    incoming = cotangent.reshape(tok_rows, width)
+        weight = after(lax.all_gather(weight, PLANES, axis=0, tiled=True), *others)
+        weight = lax.all_gather(weight, GROUP, axis=0, tiled=True)
+        return weight.reshape(sides, owner_count * own_rows, half)
+
     gate_up_blocks = [to_members(gate_up_chunks)]
+    qkv_halves = gathered(low(qkv_low * gain_one), gate_up_chunks)
+    out_halves = gathered(after(low(weight_out), gate_up_blocks[0]))
     gate_up_blocks.append(next_plane(gate_up_blocks[0]))
     down_blocks = [to_members(down_chunks)]
     incoming_columns = doubled(incoming, "k", 1, 0)
@@ -466,7 +472,8 @@
     factor_one = lax.rsqrt(jnp.mean(tokens * tokens, axis=-1, keepdims=True) + NORM_EPS)
     normed_one = low(tokens * factor_one)
     normed_one = after(normed_one, incoming_columns, gate_up_blocks[1], down_blocks[0])
-    projected = jnp.concatenate([dot(normed_one, half, (1, 0)) for half in qkv_halves], axis=1)
+    rows = regrouped(normed_one, planes, members)
+    projected = jnp.concatenate([dot(rows, half, (1, 0)) for half in qkv_halves], axis=1)
     key_pre = projected[:, width : width + HEAD_DIM]
     value_low = low(projected[:, width + HEAD_DIM :])
     key_low = low(rotate(key_pre, cosine, sine))
@@ -493,22 +500,25 @@
     bias = jnp.concatenate([bias, bias], axis=1)
     attn_low, log_total = attend(queries, keys_win, values_win, bias)
     attn_low = after(attn_low, incoming_sides)
-    branch = [dot(attn_low, half, (1, 0)) for half in out_halves]
+    rows = regrouped(attn_low, planes, members)
+    branch = [dot(rows, half, (1, 0)) for half in out_halves]
     middle = tokens + jnp.concatenate(branch, axis=1)
 
     factor_two = lax.rsqrt(jnp.mean(middle * middle, axis=-1, keepdims=True) + NORM_EPS)
-    normed_two = after(low(middle * factor_two), gate_up_blocks[3], down_blocks[2])
+    normed_two = low(middle * factor_two)
     normed_two_all = lax.all_gather(normed_two, GROUP, axis=0, tiled=True)
     grad_act = low(dot(incoming_all, down_own, (1, 0)))
-    gate_up = dot(normed_two_all, gate_up_own, (1, 0))
+    gate_up = dot(after(normed_two_all, down_blocks[2]), gate_up_own, (1, 0))
     activated, glu_back = jax.vjp(glu_values, gate_up[:, :piece], gate_up[:, piece:])
     activated_low = low(activated)
-    attn_all = lax.all_gather(after(attn_low, normed_two_all), GROUP, axis=0, tiled=True)
-    normed_one_all = lax.all_gather(after(normed_one, normed_two_all), GROUP, axis=0, tiled=True)
-    grad_gate, grad_up = glu_back(wide(grad_act))
-    grad_gate_up = low(jnp.concatenate([grad_gate, grad_up], axis=1))
     def to_owners(term):
         return lax.psum_scatter(term, PLANES, scatter_dimension=0, tiled=True)
+
+    attn_all = lax.all_gather(after(attn_low, gate_up), GROUP, axis=0, tiled=True)
+    down_term = after(low(dot(incoming_all, activated_low, (0, 0))), attn_all)
+    down_rows = to_owners(down_term)
+    grad_gate, grad_up = glu_back(wide(after(grad_act, down_term)))
+    grad_gate_up = low(jnp.concatenate([grad_gate, grad_up], axis=1))
 
     def in_plane(term, *others):
         term = term.reshape(members, own_rows, term.shape[1])
@@ -526,15 +536,18 @@
         return low(one_core(core) + wide(given)).reshape(sides * columns, tok_rows, width)
 
     terms = group_terms(grad_gate_up, gate_up_own)
-    down_term = low(dot(incoming_all, after(activated_low, terms), (0, 0)))
-    down_term = after(down_term, attn_all, normed_one_all)
-    late = after(grad_gate_up[:, :piece], terms)
-    gate_term = low(dot(normed_two_all, late, (0, 0)))
-    grad_normed_two = after(ring_sum(terms), down_term, gate_term)
-
-    down_rows = to_owners(down_term)
+    first = lax.ppermute(
+        lax.dynamic_index_in_dim(terms, lax.axis_index(CHIPS) ^ 1, 0, keepdims=False),
+        CHIPS,
+        traded(CHIPS, 1),
+    )
+    late = after(grad_gate_up, first)
+    gate_term = low(dot(normed_two_all, late[:, :piece], (0, 0)))
+    up_term = low(dot(normed_two_all, late[:, piece:], (0, 0)))
+    grad_normed_two = after(ring_sum(terms, first), gate_term, up_term)
+
     gate_rows = to_owners(gate_term)
-    down_pieces = in_plane(down_rows)
+    up_rows = to_owners(up_term)
     grad_middle = (
         wide(incoming)
         + factor_two * grad_normed_two
@@ -562,21 +575,25 @@
         dot(grad_branch_low[:, index * half : (index + 1) * half], out_halves[index], (1, 1))
         for index in range(sides)
     )
-    grad_mixed_low = low(grad_mixed)
-    branch = ring_sum(group_terms(after(activated_low, grad_mixed_low), down_own))
+    grad_mixed_low = regrouped(low(grad_mixed), members, planes)
+    branch_terms = group_terms(after(activated_low, grad_mixed_low), down_own)
     delta = (wide(grad_mixed_low) * wide(attn_low)).reshape(tok_rows, head_count, HEAD_DIM)
     delta = jnp.sum(delta, axis=-1).T.reshape(log_total.shape)
     grad_query, grad_window = attend_back(
         queries, grad_mixed_low, keys_win, values_win, bias, log_total, delta
     )
-    grad_window = after(low(grad_window), down_pieces[0], out_columns)
-    late = after(grad_gate_up[:, piece:], grad_window)
-    up_term = low(dot(normed_two_all, late, (0, 0)))
-    up_rows = to_owners(up_term)
+    out_total = to_rows(low(dot(attn_all, out_columns, (0, 0))))
+    normed_one_columns = doubled(after(normed_one, grad_normed_two), "k", 1, 0)
+    normed_one_sides = doubled(normed_one_columns, "seq", 1, 0)
+    grad_window = after(low(grad_window), out_total, normed_one_sides)
+    down_pieces = in_plane(down_rows, out_total)
     grad_window = half_sum(grad_window.reshape(-1, 2, tok_rows, 2 * HEAD_DIM), "c", 1)
     grad_window = grad_window.reshape(sides, -1, columns, tok_rows, 2 * HEAD_DIM)
-    grad_window = half_sum(grad_window, "h", 1).reshape(-1, tok_rows, 2 * HEAD_DIM)
-    grad_local = after(ring_sum(grad_window), up_term)
+    grad_window = grad_window.swapaxes(1, 2).reshape(sides * columns, -1, tok_rows, 2 * HEAD_DIM)
+    grad_local = wide(half_sum(low(ring_sum(grad_window)), "h", 0))
+    grad_local = after(grad_local, down_pieces[0])
+    normed_one_all = doubled(normed_one_sides, "c", 1, normed_one_sides.ndim - 2)
+    normed_one_all = normed_one_all.reshape(-1, width)
     grad_query = grad_query.reshape(tok_rows, head_count, HEAD_DIM)
     grad_query_pre = rotate(
         grad_query * query_scale, cosine[:, None, :], -sine[:, None, :]
@@ -586,34 +603,34 @@
         jnp.concatenate([grad_query_pre, grad_key_pre, grad_local[:, HEAD_DIM:]], axis=1)
     )
 
-    grad_proj = after(grad_proj, down_pieces[1])
-
-    qkv_columns = by_column(grad_proj)
+    mlp_states = (mlp_planes, first_mlp.transpose(1, 0, 2), second_mlp.transpose(1, 0, 2))
+    rate_main = 2.0 * D ** (-0.5)
+
+    def mlp_updated(part, pieces, outs):
+        *outs, gain_dot = mlp_adam(part, side, pieces, mlp_states, gain_two, rate_main, outs)
+        return outs, gain_dot
+
+    gate_pieces = in_plane(gate_rows, down_pieces[0])
+    qkv_columns = by_column(after(grad_proj, normed_one_all, gate_pieces[0]))
+    branch = ring_sum(after(branch_terms, qkv_columns))
+    mlp_outs, _ = mlp_updated(2, down_pieces, ())
     qkv_total = low(dot(normed_one_all, qkv_columns, (0, 0)))
-    out_total = low(dot(attn_all, after(out_columns, qkv_columns), (0, 0)))
-    gate_pieces = in_plane(gate_rows, qkv_columns)
-    qkv_total = to_rows(after(qkv_total, gate_pieces[0]))
-    up_pieces = in_plane(up_rows, qkv_total)
-    grad_out = joined(to_rows(after(out_total, up_pieces[0])))
-
-    mlp_states = (mlp_planes, first_mlp.transpose(1, 0, 2), second_mlp.transpose(1, 0, 2))
-    mlp_outs = ()
-    gain_dots = {}
-    rate_main = 2.0 * D ** (-0.5)
-    for part, pieces in ((2, down_pieces), (0, gate_pieces), (1, up_pieces)):
-        *mlp_outs, gain_dots[part] = mlp_adam(
-            part, side, pieces, mlp_states, gain_two, rate_main, mlp_outs
-        )
-    grad_mlp, second_new_mlp, new_mlp = mlp_outs
-    grad_gain_two = gain_dots[0] + gain_dots[1]
+    qkv_total = to_rows(qkv_total)
+    mlp_outs, gate_dot = mlp_updated(0, gate_pieces, mlp_outs)
+    up_pieces = in_plane(up_rows, qkv_total, gate_dot, branch)
+    (grad_mlp, second_new_mlp, new_mlp), up_dot = mlp_updated(1, up_pieces, mlp_outs)
+    grad_gain_two = gate_dot + up_dot
+    grad_out = joined(out_total)
+
     grad_qkv = joined(qkv_total)
-    hidden_out = low(middle + after(branch, grad_qkv)).reshape(1, 1, tok_rows, width)
+    hidden_out = low(middle + branch).reshape(1, 1, tok_rows, width)
 
     half = grad_proj.shape[1] // sides
     grad_normed = sum(
         dot(grad_proj[:, index * half : (index + 1) * half], qkv_halves[index], (1, 1))
         for index in range(sides)
     )
+    grad_normed = regrouped(grad_normed, members, planes)
     hidden_grad = (
         grad_middle
         + factor_one * grad_normed

time: 1140 us -> 1140 us (level)
  waiting for transfers between devices: 558 us -> 481 us
  local copies, waits for them, and re-layouts: 87.6 us -> 127 us
  other arithmetic: 88.4 us -> 126 us
    all_gather x4 -> x5, waiting for transfers between devices: 0.01 us -> 79.3 us  [the longest x2 40.1 us: gathered(): weight = lax.all_gather(weight, GROUP, axis=0, tiled=True)]
    all_to_all x9, waiting for transfers between devices: 144 us -> 74.5 us  [exchanged(): return lax.all_to_all(value, axes, split_axis=0, concat_axis=0, tiled=True)]
    all_gather x1, waiting for transfers between devices: 53.9 us -> 0.01 us  [on_device(): normed_two_all = lax.all_gather(normed_two, GROUP, axis=0, tiled=True)]
    ppermute x6, waiting for transfers between devices: 214 us -> 167 us  [next_plane(): lax.ppermute(block, PLANES, [(one, (one + 1) % count) for one in range(co...]
    ppermute x0 -> x1, waiting for transfers between devices: none -> 36.4 us  [on_device(): lax.ppermute(lax.dynamic_index_in_dim(terms, lax.axis_index(CHIPS) ^ 1, 0...]
    another operation x12 -> x18, other arithmetic: 24.6 us -> 45 us  [doubled(): jnp.stack([jnp.where(first, value, other), jnp.where(first, other, value)...]
    ppermute x9 -> x8, waiting for transfers between devices: 49.1 us -> 34.1 us  [ring_sum(): term = lax.ppermute(term, CHIPS, traded(CHIPS, step))]
    another operation x3 -> x4, other arithmetic: 1.05 us -> 12.7 us  [whole(): jax.shard_map(on_device, mesh=split, in_specs=(acts, acts, P()) + (flat,)...]
  transfers between devices with their start and end apart: 52 -> 56, of which waited for: 27 -> 29; matrix products, arithmetic and copies ran while one was open for 29% -> 33% of each run, Pallas kernels for 10% -> 8%
where the time goes in v3:
time: 1140 us; the launch traced here: 1120 us
  waiting for transfers between devices  481 us (42%)
  matrix products  176 us (15%)
  local copies, waits for them, and re-layouts  127 us (11%)
  other arithmetic  126 us (11%)
  Pallas kernels  110 us (10%)
  starting transfers between devices  87.4 us (8%)
  between operations  15.6 us (1%)
    dot_general x19, matrix products, dot(): lax.dot_general(left, right, ((contract[:1], contract[1:]), ((), ())), pr...  176 us
    ppermute x6, waiting for transfers between devices, next_plane(): lax.ppermute(block, PLANES, [(one, (one + 1) % count) for one in range(co...  167 us
    all_to_all x9, waiting for transfers between devices, exchanged(): return lax.all_to_all(value, axes, split_axis=0, concat_axis=0, tiled=True)  74.5 us
    pallas_call x3, Pallas kernels, mlp_adam(): pl.pallas_call(lambda *refs: mlp_adam_kernel(rate, per_side, part < 2, *r...  55.4 us
    all_to_all x9, starting transfers between devices, exchanged(): return lax.all_to_all(value, axes, split_axis=0, concat_axis=0, tiled=True)  52.9 us
    ppermute x7, waiting for transfers between devices, swapped(): return lax.ppermute(value, axis, [(0, 1), (1, 0)])  45.2 us
    another operation x18, other arithmetic, doubled(): jnp.stack([jnp.where(first, value, other), jnp.where(first, other, value)...  45 us
    all_gather x2, waiting for transfers between devices, gathered(): weight = lax.all_gather(weight, GROUP, axis=0, tiled=True)  40.1 us
  transfers between devices with their start and end apart: 56, of which 29 were waited for; matrix products, arithmetic and copies ran while one was open for 33% of the time, Pallas kernels for 8%

profile of v3, /device:TPU:13, one launch (start us, length us, event | category | flops | bytes accessed | tf_op | source)
XLA Modules:
  0.0 1123.1 jit_solution(18350478886560560258)
XLA Ops:
  10.9 8.1 mlp_chunks.1
  19.0 4.5 all-to-all-start
  25.0 28.0 %all-to-all-done = bf16[4,160,2048]{2,1,0:T(8,128)(2,1)S(1)} async-done(((bf16[4,160,2048]{2,1,0:T(8,128)(2,1)}), bf16[4,160,2048]{2,1,0:T(8,128)(2,1)S(1)}, u32[]{:S(2)}, u32[]{:S(2)}) %all-to-all-start) | async-done | bytes 2621472 | tf_op jit(solution)/shard_map/all_to_all | solution.py:142
  54.6 38.9 %all-gather.11.cloned.1.call-done = bf16[640,1280]{1,0:T(8,128)(2,1)} async-done(((bf16[160,1280]{1,0:T(8,128)(2,1)}), bf16[640,1280]{1,0:T(8,128)(2,1)}) %all-gather.11.cloned.1.call-update) | async-done | bytes 1638416 | tf_op jit(solution)/shard_map/all_gather | solution.py:446
  93.9 5.8 all-to-all-start.1
  102.5 22.9 %collective-permute-done = bf16[192,2560]{1,0:T(8,128)(2,1)} collective-permute-done((bf16[192,2560]{1,0:T(8,128)(2,1)}, bf16[192,2560]{1,0:T(8,128)(2,1)}, u32[]{:S(2)}, u32[]{:S(2)}) %collective-permute-start) | collective-permute-done | bytes 983072 | tf_op jit(solution)/shard_map/ppermute | solution.py:98
  128.5 23.0 %all-to-all-done.1 = bf16[4,160,1024]{2,1,0:T(8,128)(2,1)S(1)} async-done(((bf16[4,160,1024]{2,1,0:T(8,128)(2,1)}), bf16[4,160,1024]{2,1,0:T(8,128)(2,1)S(1)}, u32[]{:S(2)}, u32[]{:S(2)}) %all-to-all-start.1) | async-done | bytes 1310752 | tf_op jit(solution)/shard_map/all_to_all | solution.py:142
  151.4 7.6 collective-permute-done.1
  161.8 40.1 %all-gather.9.cloned.1.call-done = bf16[5120,1536]{1,0:T(8,128)(2,1)} async-done(((bf16[640,1536]{1,0:T(8,128)(2,1)}), bf16[5120,1536]{1,0:T(8,128)(2,1)}) %all-gather.9.cloned.1.call-update) | async-done | bytes 15728656 | tf_op jit(solution)/shard_map/all_gather | solution.py:447
  202.0 5.0 fusion.2
  221.4 6.5 collective-permute-done.7
  228.6 11.4 %collective-permute-done.8 = bf16[192,512]{1,0:T(8,128)(2,1)S(1)} collective-permute-done((bf16[192,512]{1,0:T(8,128)(2,1)S(1)}, bf16[192,512]{1,0:T(8,128)(2,1)S(1)}, u32[]{:S(2)}, u32[]{:S(2)}) %collective-permute-start.8) | collective-permute-done | bytes 196640 | tf_op jit(solution)/shard_map/ppermute | solution.py:122
  244.9 5.4 fusion.6
  273.1 64.1 %collective-permute-done.3 = bf16[640,1024]{1,0:T(8,128)(2,1)} collective-permute-done((bf16[640,1024]{1,0:T(8,128)(2,1)}, bf16[640,1024]{1,0:T(8,128)(2,1)}, u32[]{:S(2)}, u32[]{:S(2)}) %collective-permute-start.3) | collective-permute-done | bytes 1310752 | tf_op jit(solution)/shard_map/ppermute | solution.py:105
  340.7 16.5 %attend.1 = (bf16[192,2560]{1,0:T(8,128)(2,1)}, f32[5,1,384]{2,1,0:T(1,128)S(1)}) custom-call(bf16[192,2560]{1,0:T(8,128)(2,1)S(1)} %copy-done.5, bf16[3072,256]{1,0:T(8,128)(2,1)S(1)} %get-tuple-element.162.key_ref, bf16[256,3072]{1,0:T(8,128)(2,1)S(1)} %copy.152.value_t_ref, f32[3072,384]{1,0:T(8,128)} %pad_maximum_fusion.3.bias_ref), custom_call_target="tpu_custom_call" | custom-call | flops 6039797760 | bytes 18087936 | tf_op jit(solution)/shard_map/attend/pallas_call | solution.py:307
  364.9 4.8 fusion.18
  369.8 4.7 fusion.22
  379.8 5.4 broadcast_in_dim.86
  394.2 42.0 %collective-permute-done.14 = bf16[640,2048]{1,0:T(8,128)(2,1)} collective-permute-done((bf16[640,2048]{1,0:T(8,128)(2,1)}, bf16[640,2048]{1,0:T(8,128)(2,1)}, u32[]{:S(2)}, u32[]{:S(2)}) %collective-permute-start.14) | collective-permute-done | bytes 2621472 | tf_op jit(solution)/shard_map/ppermute | solution.py:105
  439.8 24.4 %collective-permute-done.13 = bf16[640,1024]{1,0:T(8,128)(2,1)S(1)} collective-permute-done((bf16[640,1024]{1,0:T(8,128)(2,1)}, bf16[640,1024]{1,0:T(8,128)(2,1)S(1)}, u32[]{:S(2)}, u32[]{:S(2)}) %collective-permute-start.13) | collective-permute-done | bytes 1310752 | tf_op jit(solution)/shard_map/ppermute | solution.py:105
  464.2 22.8 %fusion.97 = f32[1536,2048]{1,0:T(8,128)} fusion(bf16[1536,2560]{1,0:T(8,128)(2,1)} %all-gather.15.cloned.1.call-done, bf16[2560,2048]{1,0:T(8,128)(2,1)} %constant_dynamic-update-slice_fusion.4), kind=kOutput, calls=%fused_computation.232 | convolution fusion | flops 16106127360 | bytes 30932992 | tf_op jit(solution)/shard_map/dot_general | solution.py:79
  492.3 28.7 %collective-permute-done.16 = bf16[640,1024]{1,0:T(8,128)(2,1)} collective-permute-done((bf16[640,1024]{1,0:T(8,128)(2,1)S(1)}, bf16[640,1024]{1,0:T(8,128)(2,1)}, u32[]{:S(2)}, u32[]{:S(2)}) %collective-permute-start.16) | collective-permute-done | bytes 1310752 | tf_op jit(solution)/shard_map/ppermute | solution.py:105
  522.5 5.6 select_bitcast_fusion.3
  528.1 6.2 pad_maximum_fusion
  534.3 7.1 copy.155
  541.4 13.4 %convolution_convert_fusion.7 = bf16[1536,1024]{1,0:T(8,128)(2,1)} fusion(bf16[1536,2560]{1,0:T(8,128)(2,1)} %bitcast.270, bf16[2560,1024]{1,0:T(8,128)(2,1)} %copy-done.41), kind=kOutput, calls=%fused_computation.57 | convolution fusion | flops 8054636544 | bytes 16252928 | tf_op jit(solution)/shard_map/dot_general | solution.py:79
  558.8 10.3 convolution_convert_fusion.2
  569.6 8.7 fusion.8
  581.5 9.8 convolution_convert_fusion.4
  591.9 6.8 collective-permute-done.17
  598.6 12.7 %add_convert_fusion.1 = bf16[768,2560]{1,0:T(8,128)(2,1)S(1)} fusion(bf16[768,2560]{1,0:T(8,128)(2,1)} %collective-permute-done.17, bf16[768,2048]{1,0:T(8,128)(2,1)} %bitcast.292, bf16[2560,2048]{1,0:T(8,128)(2,1)} %constant_dynamic-update-slice_fusion.4), kind=kOutput, calls=%fused_computation.5 | convolution fusion | flops 8058961920 | bytes 21495808 | tf_op jit(solution)/shard_map/dot_general | solution.py:79
  622.1 36.4 %collective-permute-done.18 = bf16[192,2560]{1,0:T(8,128)(2,1)} collective-permute-done((bf16[192,2560]{1,0:T(8,128)(2,1)}, bf16[192,2560]{1,0:T(8,128)(2,1)}, u32[]{:S(2)}, u32[]{:S(2)}) %collective-permute-start.18) | collective-permute-done | bytes 983072 | tf_op jit(solution)/shard_map/ppermute | solution.py:539
  658.5 12.3 %convolution_convert_fusion.1 = bf16[2560,1024]{1,0:T(8,128)(2,1)} fusion(bf16[1536,2560]{1,0:T(8,128)(2,1)} %all-gather.15.cloned.1.call-done, bf16[1536,2048]{1,0:T(8,128)(2,1)S(1)} %pad_maximum_fusion.2), kind=kOutput, calls=%fused_computation.40 | convolution fusion | flops 8055685120 | bytes 16252928 | tf_op jit(solution)/shard_map/dot_general | solution.py:79
  674.1 14.0 %convolution_convert_fusion = bf16[2560,1024]{1,0:T(8,128)(2,1)} fusion(bf16[1536,2560]{1,0:T(8,128)(2,1)} %all-gather.15.cloned.1.call-done, bf16[1536,2048]{1,0:T(8,128)(2,1)} %copy-done.39), kind=kOutput, calls=%fused_computation.39 | convolution fusion | flops 8055685120 | bytes 16252928 | tf_op jit(solution)/shard_map/dot_general | solution.py:79
  696.1 5.5 all-to-all-start.2
  701.7 5.2 fusion.16
  706.9 6.1 fusion.30
  717.3 7.4 convolution_convert_fusion.6
  728.5 10.6 all-to-all-start.3
  752.5 29.9 %attend_back.1 = (f32[192,2560]{1,0:T(8,128)}, f32[3072,512]{1,0:T(8,128)}) custom-call(bf16[192,2560]{1,0:T(8,128)(2,1)S(1)} %copy-done.6, bf16[192,2560]{1,0:T(8,128)(2,1)S(1)} %copy.161.grad_ref, bf16[3072,256]{1,0:T(8,128)(2,1)S(1)} %copy-done.3, bf16[256,3072]{1,0:T(8,128)(2,1)S(1)} %copy-done.4, bf16[3072,256]{1,0:T(8,128)(2,1)} %get-tuple-element.159.value_ref, ...), custom_call_target="tpu_custom_call" | custom-call | flops 15099494400 | bytes 22806528 | tf_op jit(solution)/shard_map/attend_back/pallas_call | solution.py:366
  782.4 5.0 convert_element_type.264
  793.4 14.9 %all-to-all-done.3 = bf16[16,160,320]{2,1,0:T(8,128)(2,1)} async-done(((bf16[16,160,320]{2,1,0:T(8,128)(2,1)}), bf16[16,160,320]{2,1,0:T(8,128)(2,1)}, u32[]{:S(2)}, u32[]{:S(2)}) %all-to-all-start.3) | async-done | bytes 1638432 | tf_op jit(solution)/shard_map/all_to_all | solution.py:142
  820.8 9.3 convolution_convert_fusion.3
  844.2 7.4 collective-permute-done.26
  858.8 7.8 collective-permute-done.28
  874.4 4.5 all-to-all-start.5
  878.8 5.0 select_bitcast_fusion.1
  883.9 6.0 pad_maximum_fusion.1
  889.9 7.0 copy.171
  903.6 10.3 add_convert_fusion
  914.0 4.5 all-to-all-done.6
  918.5 9.1 convolution_convert_fusion.5
  927.6 8.3 all-to-all-start.7
  938.6 6.2 fusion
  950.4 7.3 fusion.24
  970.2 17.6 %mlp_adam.3 = (f32[3,160,7680]{2,1,0:T(8,128)}, f32[3,160,7680]{2,1,0:T(8,128)}, f32[3,160,7680]{2,1,0:T(8,128)}, f32[160,1]{1,0:T(8,128)}) custom-call(s32[1]{0:T(128)} %bitcast.4.refs_0_, bf16[4,160,1024]{2,1,0:T(8,128)(2,1)S(1)} %all-to-all-done.4.refs_1_, bf16[4,160,1024]{2,1,0:T(8,128)(2,1)} %collective-permute-done.36.refs_2_, ...), custom_call_target="tpu_custom_call" | custom-call | flops 24576000 | bytes 31948800 | tf_op jit(solution)/shard_map/mlp_adam/pallas_call | solution.py:240
  987.8 8.7 collective-permute-done.35.refs_2_
  996.6 19.5 %mlp_adam.4 = (f32[3,160,7680]{2,1,0:T(8,128)}, f32[3,160,7680]{2,1,0:T(8,128)}, f32[3,160,7680]{2,1,0:T(8,128)}, f32[160,1]{1,0:T(8,128)S(1)}) custom-call(s32[1]{0:T(128)} %bitcast.4.refs_0_, bf16[4,160,1024]{2,1,0:T(8,128)(2,1)S(1)} %all-to-all-done.5.refs_1_, ...), custom_call_target="tpu_custom_call", output_to_operand_aliasing={{0}: (7, {}), {1}: (8, {}), {2}: (9, {})} | custom-call | flops 24576000 | bytes 31948800 | tf_op jit(solution)/shard_map/mlp_adam/pallas_call | solution.py:240
  1017.6 21.1 %collective-permute-done.31 = bf16[192,2560]{1,0:T(8,128)(2,1)} collective-permute-done((bf16[192,2560]{1,0:T(8,128)(2,1)}, bf16[192,2560]{1,0:T(8,128)(2,1)}, u32[]{:S(2)}, u32[]{:S(2)}) %collective-permute-start.31) | collective-permute-done | bytes 983072 | tf_op jit(solution)/shard_map/ppermute | solution.py:136
  1038.7 5.0 fusion.55
  1045.7 5.2 all-to-all-start.8
  1056.5 5.8 multiply_subtract_fusion.2
  1075.1 21.9 %collective-permute-done.37.refs_2_ = bf16[4,160,1024]{2,1,0:T(8,128)(2,1)S(1)} collective-permute-done((bf16[4,160,1024]{2,1,0:T(8,128)(2,1)S(1)}, bf16[4,160,1024]{2,1,0:T(8,128)(2,1)S(1)}, u32[]{:S(2)}, u32[]{:S(2)}) %collective-permute-start.37) | collective-permute-done | bytes 1310752 | tf_op jit(solution)/shard_map/ppermute | solution.py:90
  1097.1 18.4 %mlp_adam.5 = (f32[3,160,7680]{2,1,0:T(8,128)}, f32[3,160,7680]{2,1,0:T(8,128)}, f32[3,160,7680]{2,1,0:T(8,128)}, f32[160,1]{1,0:T(8,128)S(1)}) custom-call(s32[1]{0:T(128)} %bitcast.4.refs_0_, bf16[4,160,1024]{2,1,0:T(8,128)(2,1)S(1)} %all-to-all-done.8.refs_1_, ...), custom_call_target="tpu_custom_call", output_to_operand_aliasing={{0}: (7, {}), {1}: (8, {}), {2}: (9, {})} | custom-call | flops 24576000 | bytes 31948800 | tf_op jit(solution)/shard_map/mlp_adam/pallas_call | solution.py:240
  (395 shorter events, 243.2 us)
Async XLA Ops:
  7.2 46.9 %all-gather.7.cloned.1.call-start = ((), (), s32[]{:S(2)}) async-start(), calls=%async_computation.12 | async-start | bytes 2457600 | tf_op jit(solution)/shard_map/all_gather | solution.py:446
  19.0 34.0 %all-to-all-start = ((bf16[4,160,2048]{2,1,0:T(8,128)(2,1)}), bf16[4,160,2048]{2,1,0:T(8,128)(2,1)S(1)}, u32[]{:S(2)}, u32[]{:S(2)}) async-start(bf16[4,160,2048]{2,1,0:T(8,128)(2,1)} %get-tuple-element.54), calls=%async_computation | async-start | bytes 5242880 | tf_op jit(solution)/shard_map/all_to_all | solution.py:142
  23.5 70.1 %all-gather.11.cloned.1.call-start = ((), (), s32[]{:S(2)}) async-start(), calls=%async_computation.14 | async-start | bytes 2048000 | tf_op jit(solution)/shard_map/all_gather | solution.py:446
  53.8 148.1 %all-gather.9.cloned.1.call-start = ((), (), s32[]{:S(2)}) async-start(), calls=%async_computation.13 | async-start | bytes 17694720 | tf_op jit(solution)/shard_map/all_gather | solution.py:447
  54.6 310.3 %all-gather.13.cloned.1.call-start = ((), (), s32[]{:S(2)}) async-start(), calls=%async_computation.15 | async-start | bytes 14745600 | tf_op jit(solution)/shard_map/all_gather | solution.py:447
  93.6 31.8 %collective-permute-start = (bf16[192,2560]{1,0:T(8,128)(2,1)}, bf16[192,2560]{1,0:T(8,128)(2,1)}, u32[]{:S(2)}, u32[]{:S(2)}) collective-permute-start(bf16[192,2560]{1,0:T(8,128)(2,1)} %bitcast.291), channel_id=1, source_target_pairs={{0,2},{2,0},{1,3},{3,1},{4,6},{6,4},{5,7},{7,5},{8,10},{10,8},{9,1... | collective-permute-start | bytes 2949128 | tf_op jit(solution)/shard_map/ppermute | solution.py:98
  93.9 57.5 %all-to-all-start.1 = ((bf16[4,160,1024]{2,1,0:T(8,128)(2,1)}), bf16[4,160,1024]{2,1,0:T(8,128)(2,1)S(1)}, u32[]{:S(2)}, u32[]{:S(2)}) async-start(bf16[4,160,1024]{2,1,0:T(8,128)(2,1)} %get-tuple-element.55), calls=%async_computation.1 | async-start | bytes 2621440 | tf_op jit(solution)/shard_map/all_to_all | solution.py:142
  99.7 364.5 %all-gather.15.cloned.1.call-start = ((), (), s32[]{:S(2)}) async-start(), calls=%async_computation.16 | async-start | bytes 8847360 | tf_op jit(solution)/shard_map/all_gather | solution.py:509
  100.6 58.4 %collective-permute-start.1 = (bf16[640,2048]{1,0:T(8,128)(2,1)}, bf16[640,2048]{1,0:T(8,128)(2,1)}, u32[]{:S(2)}, u32[]{:S(2)}) collective-permute-start(bf16[640,2048]{1,0:T(8,128)(2,1)} %bitcast.259), channel_id=1, source_target_pairs={{0,4},{4,8},{8,12},{12,0},{1,5},{5,9},{9,13},{13,1},{2,6},{6,10},{... | collective-permute-start | bytes 7864328 | tf_op jit(solution)/shard_map/ppermute | solution.py:105
  102.1 104.9 %copy-start.75 = (f32[128]{0:T(128)}, f32[128]{0:T(128)S(1)}, u32[]{:S(2)}) copy-start(f32[128]{0:T(128)S(1)} %multiply_exponential_fusion) | copy-start | bytes 1540
  102.2 104.8 %copy-start.65 = (f32[192]{0:T(256)}, f32[192]{0:T(256)S(1)}, u32[]{:S(2)}) copy-start(f32[192]{0:T(256)S(1)} %get-tuple-element.138) | copy-start | bytes 2308
  102.5 56.5 %copy-start.29 = (bf16[192,2560]{1,0:T(8,128)(2,1)}, bf16[192,2560]{1,0:T(8,128)(2,1)S(1)}, u32[]{:S(2)}) copy-start(bf16[192,2560]{1,0:T(8,128)(2,1)S(1)} %fusion.50) | copy-start | bytes 2949124
  161.8 45.1 %copy-start.57 = (bf16[192,4,4,160]{0,3,2,1:T(8,128)(2,1)}, bf16[192,4,4,160]{0,3,2,1:T(8,128)(2,1)S(1)}, u32[]{:S(2)}) copy-start(bf16[192,4,4,160]{0,3,2,1:T(8,128)(2,1)S(1)} %copy.146) | copy-start | bytes 2949124
  209.1 7.1 collective-permute-start.4
  210.3 7.7 collective-permute-start.5
  210.6 10.2 collective-permute-start.6
  212.0 15.9 %collective-permute-start.7 = (bf16[192,512]{1,0:T(8,128)(2,1)S(1)}, bf16[192,512]{1,0:T(8,128)(2,1)S(1)}, u32[]{:S(2)}, u32[]{:S(2)}) collective-permute-start(bf16[192,512]{1,0:T(8,128)(2,1)S(1)} %pad_maximum_fusion.14), channel_id=1, source_target_pairs={{0,16},{2,18},{4,20},{6,22},{16,0},{18,2},{20,4},{22,6},{1,17},{3,... | collective-permute-start | bytes 589832 | tf_op jit(solution)/shard_map/ppermute | solution.py:122
  213.0 27.1 %collective-permute-start.8 = (bf16[192,512]{1,0:T(8,128)(2,1)S(1)}, bf16[192,512]{1,0:T(8,128)(2,1)S(1)}, u32[]{:S(2)}, u32[]{:S(2)}) collective-permute-start(bf16[192,512]{1,0:T(8,128)(2,1)S(1)} %pad_maximum_fusion.14), channel_id=1, source_target_pairs={{0,18},{2,16},{4,22},{6,20},{16,2},{18,0},{20,6},{22,4},{1,19},{3,... | collective-permute-start | bytes 589832 | tf_op jit(solution)/shard_map/ppermute | solution.py:122
  216.1 24.6 %collective-permute-start.9 = (bf16[192,512]{1,0:T(8,128)(2,1)S(1)}, bf16[192,512]{1,0:T(8,128)(2,1)S(1)}, u32[]{:S(2)}, u32[]{:S(2)}) collective-permute-start(bf16[192,512]{1,0:T(8,128)(2,1)S(1)} %pad_maximum_fusion.14), channel_id=1, source_target_pairs={{0,20},{2,22},{4,16},{6,18},{16,4},{18,6},{20,0},{22,2},{1,21},{3,... | collective-permute-start | bytes 589832 | tf_op jit(solution)/shard_map/ppermute | solution.py:122
  218.0 23.5 %collective-permute-start.10 = (bf16[192,512]{1,0:T(8,128)(2,1)S(1)}, bf16[192,512]{1,0:T(8,128)(2,1)S(1)}, u32[]{:S(2)}, u32[]{:S(2)}) collective-permute-start(bf16[192,512]{1,0:T(8,128)(2,1)S(1)} %pad_maximum_fusion.14), channel_id=1, source_target_pairs={{0,22},{2,20},{4,18},{6,16},{16,6},{18,4},{20,2},{22,0},{1,23},{3,... | collective-permute-start | bytes 589832 | tf_op jit(solution)/shard_map/ppermute | solution.py:122
  242.2 12.5 %collective-permute-start.11 = (bf16[8,192,512]{2,1,0:T(8,128)(2,1)}, bf16[8,192,512]{2,1,0:T(8,128)(2,1)}, u32[]{:S(2)}, u32[]{:S(2)}) collective-permute-start(bf16[8,192,512]{2,1,0:T(8,128)(2,1)} %bitcast_dynamic-update-slice_fusion), channel_id=1, source_target_pairs={{0,1},{1,0},{2,3},{3,2},{4,5},{5,4},{6,7},{7,6},{8,9},{9,8},{10,11... | collective-permute-start | bytes 4718600 | tf_op jit(solution)/shard_map/ppermute | solution.py:98
  250.2 87.0 %collective-permute-start.2 = (bf16[640,2048]{1,0:T(8,128)(2,1)}, bf16[640,2048]{1,0:T(8,128)(2,1)}, u32[]{:S(2)}, u32[]{:S(2)}) collective-permute-start(bf16[640,2048]{1,0:T(8,128)(2,1)} %collective-permute-done.1), channel_id=1, source_target_pairs={{0,4},{4,8},{8,12},{12,0},{1,5},{5,9},{9,13},{13,1},{2,6},{6,10},{... | collective-permute-start | bytes 7864328 | tf_op jit(solution)/shard_map/ppermute | solution.py:105
  259.3 98.0 %collective-permute-start.12 = (bf16[2,192,2560]{2,1,0:T(8,128)(2,1)}, bf16[2,192,2560]{2,1,0:T(8,128)(2,1)}, u32[]{:S(2)}, u32[]{:S(2)}) collective-permute-start(bf16[2,192,2560]{2,1,0:T(8,128)(2,1)} %pad_maximum_fusion.8), channel_id=1, source_target_pairs={{0,16},{16,0},{1,17},{17,1},{2,18},{18,2},{3,19},{19,3},{4,20},{20... | collective-permute-start | bytes 5898248 | tf_op jit(solution)/shard_map/ppermute | solution.py:98
  264.3 72.9 %collective-permute-start.3 = (bf16[640,1024]{1,0:T(8,128)(2,1)}, bf16[640,1024]{1,0:T(8,128)(2,1)}, u32[]{:S(2)}, u32[]{:S(2)}) collective-permute-start(bf16[640,1024]{1,0:T(8,128)(2,1)} %bitcast.277), channel_id=1, source_target_pairs={{0,4},{4,8},{8,12},{12,0},{1,5},{5,9},{9,13},{13,1},{2,6},{6,10},{... | collective-permute-start | bytes 3932168 | tf_op jit(solution)/shard_map/ppermute | solution.py:105
  270.8 68.7 %copy-start.2 = (bf16[3072,256]{1,0:T(8,128)(2,1)}, bf16[3072,256]{1,0:T(8,128)(2,1)S(1)}, u32[]{:S(2)}) copy-start(bf16[3072,256]{1,0:T(8,128)(2,1)S(1)} %get-tuple-element.162.key_ref) | copy-start | bytes 4718596
  377.2 191.9 %all-gather.17.cloned.1.call-start = ((), (), s32[]{:S(2)}) async-start(), calls=%async_computation.17 | async-start | bytes 8847360 | tf_op jit(solution)/shard_map/all_gather | solution.py:517
  377.3 58.9 %collective-permute-start.14 = (bf16[640,2048]{1,0:T(8,128)(2,1)}, bf16[640,2048]{1,0:T(8,128)(2,1)}, u32[]{:S(2)}, u32[]{:S(2)}) collective-permute-start(bf16[640,2048]{1,0:T(8,128)(2,1)} %collective-permute-done.2), channel_id=1, source_target_pairs={{0,4},{4,8},{8,12},{12,0},{1,5},{5,9},{9,13},{13,1},{2,6},{6,10},{... | collective-permute-start | bytes 7864328 | tf_op jit(solution)/shard_map/ppermute | solution.py:105
  378.6 85.6 %collective-permute-start.13 = (bf16[640,1024]{1,0:T(8,128)(2,1)}, bf16[640,1024]{1,0:T(8,128)(2,1)S(1)}, u32[]{:S(2)}, u32[]{:S(2)}) collective-permute-start(bf16[640,1024]{1,0:T(8,128)(2,1)} %collective-permute-done.3), channel_id=1, source_target_pairs={{0,4},{4,8},{8,12},{12,0},{1,5},{5,9},{9,13},{13,1},{2,6},{6,10},{... | collective-permute-start | bytes 3932168 | tf_op jit(solution)/shard_map/ppermute | solution.py:105
  487.0 350.1 %reduce-scatter.4.cloned.1.call-start = ((), (), s32[]{:S(2)}) async-start(), calls=%async_computation.18 | async-start | bytes 6553600 | tf_op jit(solution)/shard_map/reduce_scatter | solution.py:515
  487.0 35.5 %collective-permute-start.15 = (bf16[2,2,192,2560]{3,2,1,0:T(8,128)(2,1)}, bf16[2,2,192,2560]{3,2,1,0:T(8,128)(2,1)}, u32[]{:S(2)}, u32[]{:S(2)}) collective-permute-start(bf16[2,2,192,2560]{3,2,1,0:T(8,128)(2,1)} %pad_maximum_fusion.4), channel_id=1, source_target_pairs={{0,1},{1,0},{2,3},{3,2},{4,5},{5,4},{6,7},{7,6},{8,9},{9,8},{10,11... | collective-permute-start | bytes 11796488 | tf_op jit(solution)/shard_map/ppermute | solution.py:98
  488.4 32.6 %collective-permute-start.16 = (bf16[640,1024]{1,0:T(8,128)(2,1)S(1)}, bf16[640,1024]{1,0:T(8,128)(2,1)}, u32[]{:S(2)}, u32[]{:S(2)}) collective-permute-start(bf16[640,1024]{1,0:T(8,128)(2,1)S(1)} %collective-permute-done.13), channel_id=1, source_target_pairs={{0,4},{4,8},{8,12},{12,0},{1,5},{5,9},{9,13},{13,1},{2,6},{6,10},{... | collective-permute-start | bytes 3932168 | tf_op jit(solution)/shard_map/ppermute | solution.py:105
  569.1 305.2 %reduce-scatter.6.cloned.1.call-start = ((), (), s32[]{:S(2)}) async-start(), calls=%async_computation.19 | async-start | bytes 6553600 | tf_op jit(solution)/shard_map/reduce_scatter | solution.py:515
  591.3 7.4 collective-permute-start.17
  614.2 44.4 %collective-permute-start.18 = (bf16[192,2560]{1,0:T(8,128)(2,1)}, bf16[192,2560]{1,0:T(8,128)(2,1)}, u32[]{:S(2)}, u32[]{:S(2)}) collective-permute-start(bf16[192,2560]{1,0:T(8,128)(2,1)} %get-tuple-element.154), channel_id=1, source_target_pairs={{0,2},{2,0},{16,18},{18,16},{1,3},{3,1},{17,19},{19,17},{4,6},{6,4... | collective-permute-start | bytes 2949128 | tf_op jit(solution)/shard_map/ppermute | solution.py:539
  619.4 51.5 %collective-permute-start.20 = (bf16[192,2560]{1,0:T(8,128)(2,1)}, bf16[192,2560]{1,0:T(8,128)(2,1)S(1)}, u32[]{:S(2)}, u32[]{:S(2)}) collective-permute-start(bf16[192,2560]{1,0:T(8,128)(2,1)} %get-tuple-element.155), channel_id=1, source_target_pairs={{0,18},{2,16},{16,2},{18,0},{1,19},{3,17},{17,3},{19,1},{4,22},{6,... | collective-permute-start | bytes 2949128 | tf_op jit(solution)/shard_map/ppermute | solution.py:136
  621.9 49.0 %collective-permute-start.19 = (bf16[192,2560]{1,0:T(8,128)(2,1)}, bf16[192,2560]{1,0:T(8,128)(2,1)S(1)}, u32[]{:S(2)}, u32[]{:S(2)}) collective-permute-start(bf16[192,2560]{1,0:T(8,128)(2,1)} %get-tuple-element.156), channel_id=1, source_target_pairs={{0,16},{2,18},{16,0},{18,2},{1,17},{3,19},{17,1},{19,3},{4,20},{6,... | collective-permute-start | bytes 2949128 | tf_op jit(solution)/shard_map/ppermute | solution.py:136
  696.1 21.2 %all-to-all-start.2 = ((bf16[8,192,320]{2,1,0:T(8,128)(2,1)}), bf16[8,192,320]{2,1,0:T(8,128)(2,1)}, u32[]{:S(2)}, u32[]{:S(2)}) async-start(bf16[8,192,320]{2,1,0:T(8,128)(2,1)} %bitcast.235), calls=%async_computation.2 | async-start | bytes 2359296 | tf_op jit(solution)/shard_map/all_to_all | solution.py:142
  701.6 37.5 %collective-permute-start.22 = (bf16[192,2560]{1,0:T(8,128)(2,1)S(1)}, bf16[192,2560]{1,0:T(8,128)(2,1)}, u32[]{:S(2)}, u32[]{:S(2)}) collective-permute-start(bf16[192,2560]{1,0:T(8,128)(2,1)S(1)} %copy-done.30), channel_id=1, source_target_pairs={{0,2},{2,0},{1,3},{3,1},{4,6},{6,4},{5,7},{7,5},{8,10},{10,8},{9,1... | collective-permute-start | bytes 2949128 | tf_op jit(solution)/shard_map/ppermute | solution.py:98
  728.5 79.7 %all-to-all-start.3 = ((bf16[16,160,320]{2,1,0:T(8,128)(2,1)}), bf16[16,160,320]{2,1,0:T(8,128)(2,1)}, u32[]{:S(2)}, u32[]{:S(2)}) async-start(bf16[16,160,320]{2,1,0:T(8,128)(2,1)} %bitcast.268), calls=%async_computation.3 | async-start | bytes 3932160 | tf_op jit(solution)/shard_map/all_to_all | solution.py:142
  739.1 306.6 %reduce-scatter.8.cloned.1.call-start = ((), (), s32[]{:S(2)}) async-start(), calls=%async_computation.20 | async-start | bytes 6553600 | tf_op jit(solution)/shard_map/reduce_scatter | solution.py:515
  742.4 45.0 %collective-permute-start.23 = (bf16[2,192,2560]{2,1,0:T(8,128)(2,1)}, bf16[2,192,2560]{2,1,0:T(8,128)(2,1)}, u32[]{:S(2)}, u32[]{:S(2)}) collective-permute-start(bf16[2,192,2560]{2,1,0:T(8,128)(2,1)} %pad_maximum_fusion.9), channel_id=1, source_target_pairs={{0,16},{16,0},{1,17},{17,1},{2,18},{18,2},{3,19},{19,3},{4,20},{20... | collective-permute-start | bytes 5898248 | tf_op jit(solution)/shard_map/ppermute | solution.py:98
  813.8 16.7 %collective-permute-start.24 = (bf16[8,192,512]{2,1,0:T(8,128)(2,1)}, bf16[8,192,512]{2,1,0:T(8,128)(2,1)S(1)}, u32[]{:S(2)}, u32[]{:S(2)}) collective-permute-start(bf16[8,192,512]{2,1,0:T(8,128)(2,1)} %dynamic-slice_bitcast_fusion), channel_id=1, source_target_pairs={{0,1},{1,0},{2,3},{3,2},{4,5},{5,4},{6,7},{7,6},{8,9},{9,8},{10,11... | collective-permute-start | bytes 4718600 | tf_op jit(solution)/shard_map/ppermute | solution.py:90
  816.8 62.0 %collective-permute-start.29 = (bf16[2,2,192,2560]{3,2,1,0:T(8,128)(2,1)}, bf16[2,2,192,2560]{3,2,1,0:T(8,128)(2,1)}, u32[]{:S(2)}, u32[]{:S(2)}) collective-permute-start(bf16[2,2,192,2560]{3,2,1,0:T(8,128)(2,1)} %pad_maximum_fusion.5), channel_id=1, source_target_pairs={{0,1},{1,0},{2,3},{3,2},{4,5},{5,4},{6,7},{7,6},{8,9},{9,8},{10,11... | collective-permute-start | bytes 11796488 | tf_op jit(solution)/shard_map/ppermute | solution.py:98
  830.1 73.5 %collective-permute-start.21 = (bf16[768,2560]{1,0:T(8,128)(2,1)}, bf16[768,2560]{1,0:T(8,128)(2,1)}, u32[]{:S(2)}, u32[]{:S(2)}) collective-permute-start(bf16[768,2560]{1,0:T(8,128)(2,1)} %convolution_convert_fusion.3), channel_id=1, source_target_pairs={{0,1},{1,0},{2,3},{3,2},{4,5},{5,4},{6,7},{7,6},{8,9},{9,8},{10,11... | collective-permute-start | bytes 11796488 | tf_op jit(solution)/shard_map/ppermute | solution.py:90
  832.2 11.9 %collective-permute-start.27 = (bf16[2,192,512]{2,1,0:T(8,128)(2,1)}, bf16[2,192,512]{2,1,0:T(8,128)(2,1)}, u32[]{:S(2)}, u32[]{:S(2)}) collective-permute-start(bf16[2,192,512]{2,1,0:T(8,128)(2,1)} %get-tuple-element.176), channel_id=1, source_target_pairs={{0,18},{2,16},{16,2},{18,0},{1,19},{3,17},{17,3},{19,1},{4,22},{6,... | collective-permute-start | bytes 1179656 | tf_op jit(solution)/shard_map/ppermute | solution.py:136
  832.2 19.3 %collective-permute-start.26 = (bf16[2,192,512]{2,1,0:T(8,128)(2,1)}, bf16[2,192,512]{2,1,0:T(8,128)(2,1)}, u32[]{:S(2)}, u32[]{:S(2)}) collective-permute-start(bf16[2,192,512]{2,1,0:T(8,128)(2,1)} %get-tuple-element.177), channel_id=1, source_target_pairs={{0,16},{2,18},{16,0},{18,2},{1,17},{3,19},{17,1},{19,3},{4,20},{6,... | collective-permute-start | bytes 1179656 | tf_op jit(solution)/shard_map/ppermute | solution.py:136
  833.4 19.5 %collective-permute-start.25 = (bf16[2,192,512]{2,1,0:T(8,128)(2,1)}, bf16[2,192,512]{2,1,0:T(8,128)(2,1)}, u32[]{:S(2)}, u32[]{:S(2)}) collective-permute-start(bf16[2,192,512]{2,1,0:T(8,128)(2,1)} %get-tuple-element.175), channel_id=1, source_target_pairs={{0,2},{2,0},{16,18},{18,16},{1,3},{3,1},{17,19},{19,17},{4,6},{6,4... | collective-permute-start | bytes 1179656 | tf_op jit(solution)/shard_map/ppermute | solution.py:136
  837.1 29.9 %all-to-all-start.4 = ((bf16[4,160,1024]{2,1,0:T(8,128)(2,1)}), bf16[4,160,1024]{2,1,0:T(8,128)(2,1)S(1)}, u32[]{:S(2)}, u32[]{:S(2)}) async-start(bf16[4,160,1024]{2,1,0:T(8,128)(2,1)} %bitcast.297), calls=%async_computation.5 | async-start | bytes 2621440 | tf_op jit(solution)/shard_map/all_to_all | solution.py:142
  854.4 12.2 %collective-permute-start.28 = (bf16[192,512]{1,0:T(8,128)(2,1)S(1)}, bf16[192,512]{1,0:T(8,128)(2,1)S(1)}, u32[]{:S(2)}, u32[]{:S(2)}) collective-permute-start(bf16[192,512]{1,0:T(8,128)(2,1)S(1)} %dynamic-slice_bitcast_fusion.10), channel_id=1, source_target_pairs={{0,4},{4,0},{1,5},{5,1},{2,6},{6,2},{3,7},{7,3},{8,12},{12,8},{9,1... | collective-permute-start | bytes 589832 | tf_op jit(solution)/shard_map/ppermute | solution.py:90
  857.7 78.3 %collective-permute-start.34 = (bf16[4,160,320]{2,1,0:T(8,128)(2,1)S(1)}, bf16[4,160,320]{2,1,0:T(8,128)(2,1)}, u32[]{:S(2)}, u32[]{:S(2)}) collective-permute-start(bf16[4,160,320]{2,1,0:T(8,128)(2,1)S(1)} %copy-done.54), channel_id=1, source_target_pairs={{0,16},{16,0},{1,17},{17,1},{2,18},{18,2},{3,19},{19,3},{4,20},{20... | collective-permute-start | bytes 1228808 | tf_op jit(solution)/shard_map/ppermute | solution.py:98
  874.4 22.5 %all-to-all-start.5 = ((bf16[4,160,1024]{2,1,0:T(8,128)(2,1)}), bf16[4,160,1024]{2,1,0:T(8,128)(2,1)S(1)}, u32[]{:S(2)}, u32[]{:S(2)}) async-start(bf16[4,160,1024]{2,1,0:T(8,128)(2,1)} %bitcast.299), calls=%async_computation.7 | async-start | bytes 2621440 | tf_op jit(solution)/shard_map/all_to_all | solution.py:142
  899.4 19.1 %all-to-all-start.6 = ((bf16[8,192,384]{2,1,0:T(8,128)(2,1)}), bf16[8,192,384]{2,1,0:T(8,128)(2,1)}, u32[]{:S(2)}, u32[]{:S(2)}) async-start(bf16[8,192,384]{2,1,0:T(8,128)(2,1)} %bitcast.286), calls=%async_computation.8 | async-start | bytes 2359296 | tf_op jit(solution)/shard_map/all_to_all | solution.py:142
  927.6 116.1 %all-to-all-start.7 = ((bf16[16,160,384]{2,1,0:T(8,128)(2,1)}), bf16[16,160,384]{2,1,0:T(8,128)(2,1)}, u32[]{:S(2)}, u32[]{:S(2)}) async-start(bf16[16,160,384]{2,1,0:T(8,128)(2,1)} %bitcast.294), calls=%async_computation.9 | async-start | bytes 3932160 | tf_op jit(solution)/shard_map/all_to_all | solution.py:142
  938.4 31.9 %collective-permute-start.36 = (bf16[4,160,1024]{2,1,0:T(8,128)(2,1)S(1)}, bf16[4,160,1024]{2,1,0:T(8,128)(2,1)}, u32[]{:S(2)}, u32[]{:S(2)}) collective-permute-start(bf16[4,160,1024]{2,1,0:T(8,128)(2,1)S(1)} %all-to-all-done.4.refs_1_), channel_id=1, source_target_pairs={{0,16},{16,0},{1,17},{17,1},{2,18},{18,2},{3,19},{19,3},{4,20},{20... | collective-permute-start | bytes 3932168 | tf_op jit(solution)/shard_map/ppermute | solution.py:90
  944.8 51.7 %collective-permute-start.35 = (bf16[4,160,1024]{2,1,0:T(8,128)(2,1)S(1)}, bf16[4,160,1024]{2,1,0:T(8,128)(2,1)}, u32[]{:S(2)}, u32[]{:S(2)}) collective-permute-start(bf16[4,160,1024]{2,1,0:T(8,128)(2,1)S(1)} %all-to-all-done.5.refs_1_), channel_id=1, source_target_pairs={{0,16},{16,0},{1,17},{17,1},{2,18},{18,2},{3,19},{19,3},{4,20},{20... | collective-permute-start | bytes 3932168 | tf_op jit(solution)/shard_map/ppermute | solution.py:90
  947.7 69.9 %collective-permute-start.32 = (bf16[192,2560]{1,0:T(8,128)(2,1)}, bf16[192,2560]{1,0:T(8,128)(2,1)}, u32[]{:S(2)}, u32[]{:S(2)}) collective-permute-start(bf16[192,2560]{1,0:T(8,128)(2,1)} %get-tuple-element.150), channel_id=1, source_target_pairs={{0,18},{2,16},{16,2},{18,0},{1,19},{3,17},{17,3},{19,1},{4,22},{6,... | collective-permute-start | bytes 2949128 | tf_op jit(solution)/shard_map/ppermute | solution.py:136
  948.0 90.7 %collective-permute-start.31 = (bf16[192,2560]{1,0:T(8,128)(2,1)}, bf16[192,2560]{1,0:T(8,128)(2,1)}, u32[]{:S(2)}, u32[]{:S(2)}) collective-permute-start(bf16[192,2560]{1,0:T(8,128)(2,1)} %get-tuple-element.151), channel_id=1, source_target_pairs={{0,16},{2,18},{16,0},{18,2},{1,17},{3,19},{17,1},{19,3},{4,20},{6,... | collective-permute-start | bytes 2949128 | tf_op jit(solution)/shard_map/ppermute | solution.py:136
  949.2 89.5 %collective-permute-start.30 = (bf16[192,2560]{1,0:T(8,128)(2,1)}, bf16[192,2560]{1,0:T(8,128)(2,1)}, u32[]{:S(2)}, u32[]{:S(2)}) collective-permute-start(bf16[192,2560]{1,0:T(8,128)(2,1)} %get-tuple-element.149), channel_id=1, source_target_pairs={{0,2},{2,0},{16,18},{18,16},{1,3},{3,1},{17,19},{19,17},{4,6},{6,4... | collective-permute-start | bytes 2949128 | tf_op jit(solution)/shard_map/ppermute | solution.py:136
  996.6 42.2 %copy-start.36 = (f32[192,2560]{1,0:T(8,128)S(1)}, f32[192,2560]{1,0:T(8,128)}, u32[]{:S(2)}) copy-start(f32[192,2560]{1,0:T(8,128)} %copy.175) | copy-start | bytes 5898244
  996.6 42.2 %copy-start.64 = (f32[192]{0:T(256)S(1)}, f32[192]{0:T(256)}, u32[]{:S(2)}) copy-start(f32[192]{0:T(256)} %copy-done.63) | copy-start | bytes 2308
  996.6 42.2 %copy-start.71 = (f32[192]{0:T(256)S(1)}, f32[192]{0:T(256)}, u32[]{:S(2)}) copy-start(f32[192]{0:T(256)} %get-tuple-element.192) | copy-start | bytes 2308
  1045.7 20.5 %all-to-all-start.8 = ((bf16[4,160,1024]{2,1,0:T(8,128)(2,1)}), bf16[4,160,1024]{2,1,0:T(8,128)(2,1)S(1)}, u32[]{:S(2)}, u32[]{:S(2)}) async-start(bf16[4,160,1024]{2,1,0:T(8,128)(2,1)} %bitcast.298), calls=%async_computation.11 | async-start | bytes 2621440 | tf_op jit(solution)/shard_map/all_to_all | solution.py:142
  1056.3 12.4 %collective-permute-start.33 = (bf16[4,160,384]{2,1,0:T(8,128)(2,1)S(1)}, bf16[4,160,384]{2,1,0:T(8,128)(2,1)S(1)}, u32[]{:S(2)}, u32[]{:S(2)}) collective-permute-start(bf16[4,160,384]{2,1,0:T(8,128)(2,1)S(1)} %reduce_sum.124), channel_id=1, source_target_pairs={{0,16},{16,0},{1,17},{17,1},{2,18},{18,2},{3,19},{19,3},{4,20},{20... | collective-permute-start | bytes 1474568 | tf_op jit(solution)/shard_map/ppermute | solution.py:98
  1066.2 30.8 %collective-permute-start.37 = (bf16[4,160,1024]{2,1,0:T(8,128)(2,1)S(1)}, bf16[4,160,1024]{2,1,0:T(8,128)(2,1)S(1)}, u32[]{:S(2)}, u32[]{:S(2)}) collective-permute-start(bf16[4,160,1024]{2,1,0:T(8,128)(2,1)S(1)} %all-to-all-done.8.refs_1_), channel_id=1, source_target_pairs={{0,16},{16,0},{1,17},{17,1},{2,18},{18,2},{3,19},{19,3},{4,20},{20... | collective-permute-start | bytes 3932168 | tf_op jit(solution)/shard_map/ppermute | solution.py:90
  (75 other events, 723.3 us)
Sparse Core Ops, SparseCore 0:
  10.9 43.1 all-gather.6
  56.3 37.2 all-gather.10
  95.4 106.4 all-gather.8
  203.7 121.2 all-gather.12
  377.4 53.3 all-gather.14
  487.1 54.1 all-gather.16
  569.2 95.0 reduce-scatter.3
  671.0 129.6 reduce-scatter.5
  820.9 95.6 reduce-scatter.7

commit v4 on v3

--- a/solution.py
+++ b/solution.py
@@ -124,15 +124,13 @@
     return whole
 
 
-def ring_sum(terms, first=None):
+def ring_sum(terms):
     chips = terms.shape[0]
     place = lax.axis_index(CHIPS)
     total = 0.0
     for step in range(chips):
         term = lax.dynamic_index_in_dim(terms, place ^ step, 0, keepdims=False)
-        if step == 1 and first is not None:
-            term = first
-        elif step:
+        if step:
             term = lax.ppermute(term, CHIPS, traded(CHIPS, step))
         total = total + wide(term)
     return total
@@ -449,9 +447,9 @@
 
     gate_up_blocks = [to_members(gate_up_chunks)]
     qkv_halves = gathered(low(qkv_low * gain_one), gate_up_chunks)
-    out_halves = gathered(after(low(weight_out), gate_up_blocks[0]))
     gate_up_blocks.append(next_plane(gate_up_blocks[0]))
     down_blocks = [to_members(down_chunks)]
+    out_halves = gathered(after(low(weight_out), gate_up_blocks[1]))
     incoming_columns = doubled(incoming, "k", 1, 0)
 
     tokens = wide(hidden_in.reshape(tok_rows, width))
@@ -508,7 +506,7 @@
     normed_two = low(middle * factor_two)
     normed_two_all = lax.all_gather(normed_two, GROUP, axis=0, tiled=True)
     grad_act = low(dot(incoming_all, down_own, (1, 0)))
-    gate_up = dot(after(normed_two_all, down_blocks[2]), gate_up_own, (1, 0))
+    gate_up = dot(after(normed_two_all, down_blocks[2], incoming_all), gate_up_own, (1, 0))
     activated, glu_back = jax.vjp(glu_values, gate_up[:, :piece], gate_up[:, piece:])
     activated_low = low(activated)
     def to_owners(term):
@@ -536,15 +534,19 @@
         return low(one_core(core) + wide(given)).reshape(sides * columns, tok_rows, width)
 
     terms = group_terms(grad_gate_up, gate_up_own)
-    first = lax.ppermute(
-        lax.dynamic_index_in_dim(terms, lax.axis_index(CHIPS) ^ 1, 0, keepdims=False),
-        CHIPS,
-        traded(CHIPS, 1),
-    )
-    late = after(grad_gate_up, first)
+    place = lax.axis_index(CHIPS)
+    grad_normed_two = wide(lax.dynamic_index_in_dim(terms, place, 0, keepdims=False))
+    arrived = []
+    for step in range(1, sides * columns):
+        term = lax.dynamic_index_in_dim(terms, place ^ step, 0, keepdims=False)
+        if step == sides * columns - 1:
+            term = after(term, *arrived)
+        arrived.append(lax.ppermute(term, CHIPS, traded(CHIPS, step)))
+    late = after(grad_gate_up, *arrived[:-1])
     gate_term = low(dot(normed_two_all, late[:, :piece], (0, 0)))
     up_term = low(dot(normed_two_all, late[:, piece:], (0, 0)))
-    grad_normed_two = after(ring_sum(terms, first), gate_term, up_term)
+    grad_normed_two = grad_normed_two + sum(wide(term) for term in arrived)
+    grad_normed_two = after(grad_normed_two, gate_term, up_term)
 
     gate_rows = to_owners(gate_term)
     up_rows = to_owners(up_term)
@@ -576,24 +578,23 @@
         for index in range(sides)
     )
     grad_mixed_low = regrouped(low(grad_mixed), members, planes)
-    branch_terms = group_terms(after(activated_low, grad_mixed_low), down_own)
     delta = (wide(grad_mixed_low) * wide(attn_low)).reshape(tok_rows, head_count, HEAD_DIM)
     delta = jnp.sum(delta, axis=-1).T.reshape(log_total.shape)
     grad_query, grad_window = attend_back(
         queries, grad_mixed_low, keys_win, values_win, bias, log_total, delta
     )
-    out_total = to_rows(low(dot(attn_all, out_columns, (0, 0))))
     normed_one_columns = doubled(after(normed_one, grad_normed_two), "k", 1, 0)
     normed_one_sides = doubled(normed_one_columns, "seq", 1, 0)
-    grad_window = after(low(grad_window), out_total, normed_one_sides)
-    down_pieces = in_plane(down_rows, out_total)
+    branch_terms = group_terms(after(activated_low, grad_window), down_own)
+    down_pieces = in_plane(down_rows, out_columns)
+    grad_window = after(low(grad_window), normed_one_sides, down_pieces[1])
+    out_total = to_rows(low(dot(attn_all, after(out_columns, grad_window), (0, 0))))
+    normed_one_others = swapped(normed_one_sides, "c")
+    gate_pieces = in_plane(gate_rows, out_total)
     grad_window = half_sum(grad_window.reshape(-1, 2, tok_rows, 2 * HEAD_DIM), "c", 1)
     grad_window = grad_window.reshape(sides, -1, columns, tok_rows, 2 * HEAD_DIM)
     grad_window = grad_window.swapaxes(1, 2).reshape(sides * columns, -1, tok_rows, 2 * HEAD_DIM)
     grad_local = wide(half_sum(low(ring_sum(grad_window)), "h", 0))
-    grad_local = after(grad_local, down_pieces[0])
-    normed_one_all = doubled(normed_one_sides, "c", 1, normed_one_sides.ndim - 2)
-    normed_one_all = normed_one_all.reshape(-1, width)
     grad_query = grad_query.reshape(tok_rows, head_count, HEAD_DIM)
     grad_query_pre = rotate(
         grad_query * query_scale, cosine[:, None, :], -sine[:, None, :]
@@ -610,16 +611,23 @@
         *outs, gain_dot = mlp_adam(part, side, pieces, mlp_states, gain_two, rate_main, outs)
         return outs, gain_dot
 
-    gate_pieces = in_plane(gate_rows, down_pieces[0])
-    qkv_columns = by_column(after(grad_proj, normed_one_all, gate_pieces[0]))
-    branch = ring_sum(after(branch_terms, qkv_columns))
+    qkv_columns = by_column(after(grad_proj, gate_pieces[0], normed_one_others))
     mlp_outs, _ = mlp_updated(2, down_pieces, ())
-    qkv_total = low(dot(normed_one_all, qkv_columns, (0, 0)))
-    qkv_total = to_rows(qkv_total)
+    by_core = after(qkv_columns, *mlp_outs).reshape(sides * columns, 2, tok_rows, -1)
+
+    def one_core_total(rows, which):
+        columns_there = lax.dynamic_index_in_dim(by_core, which, 1, keepdims=False)
+        return dot(rows.reshape(-1, width), columns_there.reshape(-1, by_core.shape[3]), (0, 0))
+
+    qkv_total = one_core_total(normed_one_sides, core)
+    qkv_total = low(qkv_total + one_core_total(normed_one_others, 1 - core))
+    up_pieces = in_plane(up_rows, qkv_columns, gate_pieces[1])
     mlp_outs, gate_dot = mlp_updated(0, gate_pieces, mlp_outs)
-    up_pieces = in_plane(up_rows, qkv_total, gate_dot, branch)
+    qkv_total = to_rows(after(qkv_total, up_pieces[0], gate_dot))
+    branch = ring_sum(after(branch_terms, up_pieces[0]))
     (grad_mlp, second_new_mlp, new_mlp), up_dot = mlp_updated(1, up_pieces, mlp_outs)
     grad_gain_two = gate_dot + up_dot
+    qkv_total = after(qkv_total, up_dot)
     grad_out = joined(out_total)
 
     grad_qkv = joined(qkv_total)

time: 1140 us -> 1190 us (1.044)
  waiting for transfers between devices: 481 us -> 573 us
  other arithmetic: 126 us -> 106 us
  local copies, waits for them, and re-layouts: 127 us -> 115 us
    ppermute x6, waiting for transfers between devices: 167 us -> 213 us  [next_plane(): lax.ppermute(block, PLANES, [(one, (one + 1) % count) for one in range(co...]
    all_to_all x9, waiting for transfers between devices: 74.5 us -> 109 us  [exchanged(): return lax.all_to_all(value, axes, split_axis=0, concat_axis=0, tiled=True)]
    another operation x18 -> x16, other arithmetic: 45 us -> 28.9 us  [doubled(): jnp.stack([jnp.where(first, value, other), jnp.where(first, other, value)...]
    ppermute x9 -> x8, waiting for transfers between devices: 25.1 us -> 36.4 us  [doubled(): other = lax.ppermute(value, axis, traded((axis,), step))]
    ppermute x1 -> x3, waiting for transfers between devices: 36.4 us -> 27.7 us  [on_device(): arrived.append(lax.ppermute(term, CHIPS, traded(CHIPS, step)))]
    dot_general x19 -> x20, matrix products: 176 us -> 168 us  [dot(): lax.dot_general(left, right, ((contract[:1], contract[1:]), ((), ())), pr...]
    ppermute x8 -> x6, waiting for transfers between devices: 34.1 us -> 39.4 us  [ring_sum(): term = lax.ppermute(term, CHIPS, traded(CHIPS, step))]
    ppermute x7 -> x8, waiting for transfers between devices: 45.2 us -> 41.2 us  [swapped(): return lax.ppermute(value, axis, [(0, 1), (1, 0)])]
  transfers between devices with their start and end apart: 56 -> 56, of which waited for: 29 -> 29; matrix products, arithmetic and copies ran while one was open for 33% -> 28% of each run, Pallas kernels for 8% -> 9%
where the time goes in v4:
time: 1190 us; the launch traced here: 1180 us
  waiting for transfers between devices  573 us (48%)
  matrix products  168 us (14%)
  local copies, waits for them, and re-layouts  115 us (10%)
  Pallas kernels  109 us (9%)
  other arithmetic  106 us (9%)
  starting transfers between devices  91.8 us (8%)
  between operations  15.8 us (1%)
    ppermute x6, waiting for transfers between devices, next_plane(): lax.ppermute(block, PLANES, [(one, (one + 1) % count) for one in range(co...  213 us
    dot_general x20, matrix products, dot(): lax.dot_general(left, right, ((contract[:1], contract[1:]), ((), ())), pr...  168 us
    all_to_all x9, waiting for transfers between devices, exchanged(): return lax.all_to_all(value, axes, split_axis=0, concat_axis=0, tiled=True)  109 us
    all_to_all x9, starting transfers between devices, exchanged(): return lax.all_to_all(value, axes, split_axis=0, concat_axis=0, tiled=True)  55.2 us
    pallas_call x3, Pallas kernels, mlp_adam(): pl.pallas_call(lambda *refs: mlp_adam_kernel(rate, per_side, part < 2, *r...  54.2 us
    all_gather x2, waiting for transfers between devices, gathered(): weight = lax.all_gather(weight, GROUP, axis=0, tiled=True)  49.9 us
    ppermute x8, waiting for transfers between devices, swapped(): return lax.ppermute(value, axis, [(0, 1), (1, 0)])  41.2 us
    ppermute x6, waiting for transfers between devices, ring_sum(): term = lax.ppermute(term, CHIPS, traded(CHIPS, step))  39.4 us
  transfers between devices with their start and end apart: 56, of which 29 were waited for; matrix products, arithmetic and copies ran while one was open for 28% of the time, Pallas kernels for 9%

profile of v4, /device:TPU:13, one launch (start us, length us, event | category | flops | bytes accessed | tf_op | source)
XLA Modules:
  0.0 1178.1 jit_solution(2211669929067240813)
XLA Ops:
  8.1 8.1 mlp_chunks.1
  16.2 4.4 all-to-all-start
  23.5 26.7 %all-to-all-done = bf16[4,160,2048]{2,1,0:T(8,128)(2,1)S(1)} async-done(((bf16[4,160,2048]{2,1,0:T(8,128)(2,1)}), bf16[4,160,2048]{2,1,0:T(8,128)(2,1)S(1)}, u32[]{:S(2)}, u32[]{:S(2)}) %all-to-all-start) | async-done | bytes 2621472 | tf_op jit(solution)/shard_map/all_to_all | solution.py:140
  53.0 68.0 %collective-permute-done.1 = bf16[640,2048]{1,0:T(8,128)(2,1)} collective-permute-done((bf16[640,2048]{1,0:T(8,128)(2,1)S(1)}, bf16[640,2048]{1,0:T(8,128)(2,1)}, u32[]{:S(2)}, u32[]{:S(2)}) %collective-permute-start.1) | collective-permute-done | bytes 2621472 | tf_op jit(solution)/shard_map/ppermute | solution.py:105
  122.6 37.3 %all-gather.11.cloned.1.call-done = bf16[640,1280]{1,0:T(8,128)(2,1)} async-done(((bf16[160,1280]{1,0:T(8,128)(2,1)}), bf16[640,1280]{1,0:T(8,128)(2,1)}) %all-gather.11.cloned.1.call-update) | async-done | bytes 1638416 | tf_op jit(solution)/shard_map/all_gather | solution.py:444
  160.2 6.5 all-to-all-start.1
  168.4 23.2 %collective-permute-done = bf16[192,2560]{1,0:T(8,128)(2,1)} collective-permute-done((bf16[192,2560]{1,0:T(8,128)(2,1)}, bf16[192,2560]{1,0:T(8,128)(2,1)}, u32[]{:S(2)}, u32[]{:S(2)}) %collective-permute-start) | collective-permute-done | bytes 983072 | tf_op jit(solution)/shard_map/ppermute | solution.py:98
  194.4 23.3 %all-to-all-done.1 = bf16[4,160,1024]{2,1,0:T(8,128)(2,1)} async-done(((bf16[4,160,1024]{2,1,0:T(8,128)(2,1)}), bf16[4,160,1024]{2,1,0:T(8,128)(2,1)}, u32[]{:S(2)}, u32[]{:S(2)}) %all-to-all-start.1) | async-done | bytes 1310752 | tf_op jit(solution)/shard_map/all_to_all | solution.py:140
  218.4 49.9 %all-gather.9.cloned.1.call-done = bf16[5120,1536]{1,0:T(8,128)(2,1)} async-done(((bf16[640,1536]{1,0:T(8,128)(2,1)}), bf16[5120,1536]{1,0:T(8,128)(2,1)}) %all-gather.9.cloned.1.call-update) | async-done | bytes 15728656 | tf_op jit(solution)/shard_map/all_gather | solution.py:445
  268.3 4.9 fusion.2
  288.5 17.7 %collective-permute-done.8 = bf16[192,512]{1,0:T(8,128)(2,1)S(1)} collective-permute-done((bf16[192,512]{1,0:T(8,128)(2,1)S(1)}, bf16[192,512]{1,0:T(8,128)(2,1)S(1)}, u32[]{:S(2)}, u32[]{:S(2)}) %collective-permute-start.8) | collective-permute-done | bytes 196640 | tf_op jit(solution)/shard_map/ppermute | solution.py:122
  311.2 5.4 fusion.6
  339.4 64.1 %collective-permute-done.3 = bf16[640,1024]{1,0:T(8,128)(2,1)} collective-permute-done((bf16[640,1024]{1,0:T(8,128)(2,1)}, bf16[640,1024]{1,0:T(8,128)(2,1)}, u32[]{:S(2)}, u32[]{:S(2)}) %collective-permute-start.3) | collective-permute-done | bytes 1310752 | tf_op jit(solution)/shard_map/ppermute | solution.py:105
  407.0 16.3 %attend.1 = (bf16[192,2560]{1,0:T(8,128)(2,1)}, f32[5,1,384]{2,1,0:T(1,128)S(1)}) custom-call(bf16[192,2560]{1,0:T(8,128)(2,1)S(1)} %copy-done.7, bf16[3072,256]{1,0:T(8,128)(2,1)S(1)} %get-tuple-element.170.key_ref, bf16[256,3072]{1,0:T(8,128)(2,1)S(1)} %copy.150.value_t_ref, f32[3072,384]{1,0:T(8,128)} %pad_maximum_fusion.2.bias_ref), custom_call_target="tpu_custom_call" | custom-call | flops 6039797760 | bytes 18087936 | tf_op jit(solution)/shard_map/attend/pallas_call | solution.py:305
  430.9 4.8 fusion.18
  435.8 4.7 fusion.22
  444.8 5.4 broadcast_in_dim.86
  460.9 42.2 %collective-permute-done.15 = bf16[640,2048]{1,0:T(8,128)(2,1)} collective-permute-done((bf16[640,2048]{1,0:T(8,128)(2,1)}, bf16[640,2048]{1,0:T(8,128)(2,1)}, u32[]{:S(2)}, u32[]{:S(2)}) %collective-permute-start.15) | collective-permute-done | bytes 2621472 | tf_op jit(solution)/shard_map/ppermute | solution.py:105
  506.7 5.1 select_bitcast_fusion.1
  511.8 4.0 pad_maximum_fusion
  519.5 11.6 collective-permute-done.13
  531.1 22.8 %fusion.98 = f32[1536,2048]{1,0:T(8,128)} fusion(bf16[1536,2560]{1,0:T(8,128)(2,1)} %all-gather.15.cloned.1.call-done, bf16[2560,2048]{1,0:T(8,128)(2,1)} %constant_dynamic-update-slice_fusion.4), kind=kOutput, calls=%fused_computation.230 | convolution fusion | flops 16106127360 | bytes 30932992 | tf_op jit(solution)/shard_map/dot_general | solution.py:79
  558.7 26.8 %collective-permute-done.16 = bf16[640,1024]{1,0:T(8,128)(2,1)S(1)} collective-permute-done((bf16[640,1024]{1,0:T(8,128)(2,1)S(1)}, bf16[640,1024]{1,0:T(8,128)(2,1)S(1)}, u32[]{:S(2)}, u32[]{:S(2)}) %collective-permute-start.16) | collective-permute-done | bytes 1310752 | tf_op jit(solution)/shard_map/ppermute | solution.py:105
  585.7 9.6 convolution_convert_fusion.6
  599.2 10.4 convolution_convert_fusion.2
  609.8 8.7 fusion.8
  621.7 9.8 convolution_convert_fusion.4
  632.8 6.8 collective-permute-done.17
  639.6 12.7 %add_convert_fusion.1 = bf16[768,2560]{1,0:T(8,128)(2,1)S(1)} fusion(bf16[768,2560]{1,0:T(8,128)(2,1)} %collective-permute-done.17, bf16[768,2048]{1,0:T(8,128)(2,1)} %bitcast.292, bf16[2560,2048]{1,0:T(8,128)(2,1)} %constant_dynamic-update-slice_fusion.4), kind=kOutput, calls=%fused_computation.4 | convolution fusion | flops 8058961920 | bytes 21495808 | tf_op jit(solution)/shard_map/dot_general | solution.py:79
  658.0 21.0 %collective-permute-done.18 = bf16[192,2560]{1,0:T(8,128)(2,1)} collective-permute-done((bf16[192,2560]{1,0:T(8,128)(2,1)}, bf16[192,2560]{1,0:T(8,128)(2,1)}, u32[]{:S(2)}, u32[]{:S(2)}) %collective-permute-start.18) | collective-permute-done | bytes 983072 | tf_op jit(solution)/shard_map/ppermute | solution.py:544
  679.0 12.2 %convolution_convert_fusion.1 = bf16[2560,1024]{1,0:T(8,128)(2,1)} fusion(bf16[1536,2560]{1,0:T(8,128)(2,1)} %all-gather.15.cloned.1.call-done, bf16[1536,2048]{1,0:T(8,128)(2,1)S(1)} %pad_maximum_fusion.1), kind=kOutput, calls=%fused_computation.39 | convolution fusion | flops 8055685120 | bytes 16252928 | tf_op jit(solution)/shard_map/dot_general | solution.py:79
  696.7 14.0 %convolution_convert_fusion = bf16[2560,1024]{1,0:T(8,128)(2,1)} fusion(bf16[1536,2560]{1,0:T(8,128)(2,1)} %all-gather.15.cloned.1.call-done, bf16[1536,2048]{1,0:T(8,128)(2,1)} %copy-done.35), kind=kOutput, calls=%fused_computation.38 | convolution fusion | flops 8055685120 | bytes 16252928 | tf_op jit(solution)/shard_map/dot_general | solution.py:79
  710.8 6.7 collective-permute-done.20
  725.4 5.1 fusion.16
  730.5 5.2 fusion.31
  740.4 6.6 all-to-all-start.2
  762.9 5.3 all-to-all-start.3
  771.1 30.0 %attend_back.1 = (f32[192,2560]{1,0:T(8,128)}, f32[3072,512]{1,0:T(8,128)}) custom-call(bf16[192,2560]{1,0:T(8,128)(2,1)S(1)} %copy-done.8, bf16[192,2560]{1,0:T(8,128)(2,1)S(1)} %copy.159.grad_ref, bf16[3072,256]{1,0:T(8,128)(2,1)S(1)} %copy-done.3, bf16[256,3072]{1,0:T(8,128)(2,1)S(1)} %copy-done.4, bf16[3072,256]{1,0:T(8,128)(2,1)} %get-tuple-element.167.value_ref, ...), custom_call_target="tpu_custom_call" | custom-call | flops 15099494400 | bytes 22806528 | tf_op jit(solution)/shard_map/attend_back/pallas_call | solution.py:364
  801.8 4.1 constant_dynamic-slice_fusion.2
  813.6 18.5 %collective-permute-done.24.refs_2_ = bf16[4,160,1024]{2,1,0:T(8,128)(2,1)S(1)} collective-permute-done((bf16[4,160,1024]{2,1,0:T(8,128)(2,1)S(1)}, bf16[4,160,1024]{2,1,0:T(8,128)(2,1)S(1)}, u32[]{:S(2)}, u32[]{:S(2)}) %collective-permute-start.24) | collective-permute-done | bytes 1310752 | tf_op jit(solution)/shard_map/ppermute | solution.py:90
  840.3 8.4 all-to-all-start.4
  848.7 9.2 convolution_convert_fusion.3
  868.7 9.5 collective-permute-done.28
  878.2 4.9 collective-permute-done.27
  883.1 4.0 collective-permute-done.26
  889.4 48.7 %all-to-all-done.4 = bf16[16,160,320]{2,1,0:T(8,128)(2,1)} async-done(((bf16[16,160,320]{2,1,0:T(8,128)(2,1)}), bf16[16,160,320]{2,1,0:T(8,128)(2,1)}, u32[]{:S(2)}, u32[]{:S(2)}) %all-to-all-start.4) | async-done | bytes 1638432 | tf_op jit(solution)/shard_map/all_to_all | solution.py:140
  953.5 5.7 all-to-all-done.5.refs_1_
  965.3 6.7 all-to-all-start.6
  972.0 10.3 add_convert_fusion
  982.4 17.2 %mlp_adam.3 = (f32[3,160,7680]{2,1,0:T(8,128)}, f32[3,160,7680]{2,1,0:T(8,128)}, f32[3,160,7680]{2,1,0:T(8,128)}, f32[160,1]{1,0:T(8,128)}) custom-call(s32[1]{0:T(128)} %bitcast.4.refs_0_, bf16[4,160,1024]{2,1,0:T(8,128)(2,1)S(1)} %all-to-all-done.3.refs_1_, bf16[4,160,1024]{2,1,0:T(8,128)(2,1)S(1)} %copy-done.6, f32[3,160,7680]{2,1,0:T(8,128)} %bitcast.239, ...), custom_call_target="tpu_custom_call" | custom-call | flops 24576000 | bytes 31948800 | tf_op jit(solution)/shard_map/mlp_adam/pallas_call | solution.py:238
  1004.0 6.0 all-to-all-start.7
  1009.9 4.6 fusion.99
  1014.5 5.7 fusion.24
  1020.3 18.4 %mlp_adam.4 = (f32[3,160,7680]{2,1,0:T(8,128)}, f32[3,160,7680]{2,1,0:T(8,128)}, f32[3,160,7680]{2,1,0:T(8,128)}, f32[160,1]{1,0:T(8,128)S(1)}) custom-call(s32[1]{0:T(128)} %bitcast.4.refs_0_, bf16[4,160,1024]{2,1,0:T(8,128)(2,1)S(1)} %all-to-all-done.5.refs_1_, ...), custom_call_target="tpu_custom_call", output_to_operand_aliasing={{0}: (7, {}), {1}: (8, {}), {2}: (9, {})} | custom-call | flops 24576000 | bytes 31948800 | tf_op jit(solution)/shard_map/mlp_adam/pallas_call | solution.py:238
  1038.7 7.6 all-to-all-start.8
  1046.3 6.3 fusion
  1052.6 7.3 fusion.25
  1072.8 9.2 collective-permute-done.37
  1092.3 5.8 multiply_subtract_fusion.2
  1098.1 13.4 %collective-permute-done.35.refs_2_ = bf16[4,160,1024]{2,1,0:T(8,128)(2,1)S(1)} collective-permute-done((bf16[4,160,1024]{2,1,0:T(8,128)(2,1)S(1)}, bf16[4,160,1024]{2,1,0:T(8,128)(2,1)S(1)}, u32[]{:S(2)}, u32[]{:S(2)}) %collective-permute-start.35) | collective-permute-done | bytes 1310752 | tf_op jit(solution)/shard_map/ppermute | solution.py:90
  1111.5 18.6 %mlp_adam.5 = (f32[3,160,7680]{2,1,0:T(8,128)}, f32[3,160,7680]{2,1,0:T(8,128)}, f32[3,160,7680]{2,1,0:T(8,128)}, f32[160,1]{1,0:T(8,128)S(1)}) custom-call(s32[1]{0:T(128)} %bitcast.4.refs_0_, bf16[4,160,1024]{2,1,0:T(8,128)(2,1)S(1)} %all-to-all-done.7.refs_1_, ...), custom_call_target="tpu_custom_call", output_to_operand_aliasing={{0}: (7, {}), {1}: (8, {}), {2}: (9, {})} | custom-call | flops 24576000 | bytes 31948800 | tf_op jit(solution)/shard_map/mlp_adam/pallas_call | solution.py:238
  1132.6 21.0 %collective-permute-done.33 = bf16[192,2560]{1,0:T(8,128)(2,1)} collective-permute-done((bf16[192,2560]{1,0:T(8,128)(2,1)}, bf16[192,2560]{1,0:T(8,128)(2,1)}, u32[]{:S(2)}, u32[]{:S(2)}) %collective-permute-start.33) | collective-permute-done | bytes 983072 | tf_op jit(solution)/shard_map/ppermute | solution.py:134
  1153.7 6.4 fusion.54
  1160.2 3.9 collective-permute-done.36
  (404 shorter events, 233.6 us)
Async XLA Ops:
  16.2 34.0 %all-to-all-start = ((bf16[4,160,2048]{2,1,0:T(8,128)(2,1)}), bf16[4,160,2048]{2,1,0:T(8,128)(2,1)S(1)}, u32[]{:S(2)}, u32[]{:S(2)}) async-start(bf16[4,160,2048]{2,1,0:T(8,128)(2,1)} %get-tuple-element.58), calls=%async_computation | async-start | bytes 5242880 | tf_op jit(solution)/shard_map/all_to_all | solution.py:140
  20.6 101.2 %all-gather.7.cloned.1.call-start = ((), (), s32[]{:S(2)}) async-start(), calls=%async_computation.12 | async-start | bytes 2457600 | tf_op jit(solution)/shard_map/all_gather | solution.py:444
  23.4 136.4 %all-gather.11.cloned.1.call-start = ((), (), s32[]{:S(2)}) async-start(), calls=%async_computation.14 | async-start | bytes 2048000 | tf_op jit(solution)/shard_map/all_gather | solution.py:444
  50.1 72.4 %copy-start.26 = (bf16[4,160,2048]{2,1,0:T(8,128)(2,1)}, bf16[4,160,2048]{2,1,0:T(8,128)(2,1)S(1)}, u32[]{:S(2)}) copy-start(bf16[4,160,2048]{2,1,0:T(8,128)(2,1)S(1)} %all-to-all-done) | copy-start | bytes 7864324
  50.1 70.9 %collective-permute-start.1 = (bf16[640,2048]{1,0:T(8,128)(2,1)S(1)}, bf16[640,2048]{1,0:T(8,128)(2,1)}, u32[]{:S(2)}, u32[]{:S(2)}) collective-permute-start(bf16[640,2048]{1,0:T(8,128)(2,1)S(1)} %bitcast.261), channel_id=1, source_target_pairs={{0,4},{4,8},{8,12},{12,0},{1,5},{5,9},{9,13},{13,1},{2,6},{6,10},{... | collective-permute-start | bytes 7864328 | tf_op jit(solution)/shard_map/ppermute | solution.py:105
  121.8 146.5 %all-gather.9.cloned.1.call-start = ((), (), s32[]{:S(2)}) async-start(), calls=%async_computation.13 | async-start | bytes 17694720 | tf_op jit(solution)/shard_map/all_gather | solution.py:445
  122.6 308.4 %all-gather.13.cloned.1.call-start = ((), (), s32[]{:S(2)}) async-start(), calls=%async_computation.15 | async-start | bytes 14745600 | tf_op jit(solution)/shard_map/all_gather | solution.py:445
  159.9 31.7 %collective-permute-start = (bf16[192,2560]{1,0:T(8,128)(2,1)}, bf16[192,2560]{1,0:T(8,128)(2,1)}, u32[]{:S(2)}, u32[]{:S(2)}) collective-permute-start(bf16[192,2560]{1,0:T(8,128)(2,1)} %bitcast.291), channel_id=1, source_target_pairs={{0,2},{2,0},{1,3},{3,1},{4,6},{6,4},{5,7},{7,5},{8,10},{10,8},{9,1... | collective-permute-start | bytes 2949128 | tf_op jit(solution)/shard_map/ppermute | solution.py:98
  160.2 57.5 %all-to-all-start.1 = ((bf16[4,160,1024]{2,1,0:T(8,128)(2,1)}), bf16[4,160,1024]{2,1,0:T(8,128)(2,1)}, u32[]{:S(2)}, u32[]{:S(2)}) async-start(bf16[4,160,1024]{2,1,0:T(8,128)(2,1)} %get-tuple-element.59), calls=%async_computation.1 | async-start | bytes 2621440 | tf_op jit(solution)/shard_map/all_to_all | solution.py:140
  166.8 364.4 %all-gather.15.cloned.1.call-start = ((), (), s32[]{:S(2)}) async-start(), calls=%async_computation.16 | async-start | bytes 8847360 | tf_op jit(solution)/shard_map/all_gather | solution.py:507
  168.0 105.3 %copy-start.74 = (f32[128]{0:T(128)}, f32[128]{0:T(128)S(1)}, u32[]{:S(2)}) copy-start(f32[128]{0:T(128)S(1)} %multiply_exponential_fusion) | copy-start | bytes 1540
  168.1 105.2 %copy-start.63 = (f32[192]{0:T(256)}, f32[192]{0:T(256)S(1)}, u32[]{:S(2)}) copy-start(f32[192]{0:T(256)S(1)} %get-tuple-element.146) | copy-start | bytes 2308
  168.4 49.4 %copy-start.28 = (bf16[192,2560]{1,0:T(8,128)(2,1)}, bf16[192,2560]{1,0:T(8,128)(2,1)S(1)}, u32[]{:S(2)}) copy-start(bf16[192,2560]{1,0:T(8,128)(2,1)S(1)} %fusion.51) | copy-start | bytes 2949124
  218.4 54.8 %copy-start.52 = (bf16[192,4,4,160]{0,3,2,1:T(8,128)(2,1)}, bf16[192,4,4,160]{0,3,2,1:T(8,128)(2,1)S(1)}, u32[]{:S(2)}) copy-start(bf16[192,4,4,160]{0,3,2,1:T(8,128)(2,1)S(1)} %copy.144) | copy-start | bytes 2949124
  275.4 7.1 collective-permute-start.4
  276.6 7.7 collective-permute-start.5
  276.9 10.1 collective-permute-start.6
  278.3 9.5 collective-permute-start.7
  279.3 27.0 %collective-permute-start.8 = (bf16[192,512]{1,0:T(8,128)(2,1)S(1)}, bf16[192,512]{1,0:T(8,128)(2,1)S(1)}, u32[]{:S(2)}, u32[]{:S(2)}) collective-permute-start(bf16[192,512]{1,0:T(8,128)(2,1)S(1)} %pad_maximum_fusion.13), channel_id=1, source_target_pairs={{0,18},{2,16},{4,22},{6,20},{16,2},{18,0},{20,6},{22,4},{1,19},{3,... | collective-permute-start | bytes 589832 | tf_op jit(solution)/shard_map/ppermute | solution.py:122
  282.5 24.5 %collective-permute-start.9 = (bf16[192,512]{1,0:T(8,128)(2,1)S(1)}, bf16[192,512]{1,0:T(8,128)(2,1)S(1)}, u32[]{:S(2)}, u32[]{:S(2)}) collective-permute-start(bf16[192,512]{1,0:T(8,128)(2,1)S(1)} %pad_maximum_fusion.13), channel_id=1, source_target_pairs={{0,20},{2,22},{4,16},{6,18},{16,4},{18,6},{20,0},{22,2},{1,21},{3,... | collective-permute-start | bytes 589832 | tf_op jit(solution)/shard_map/ppermute | solution.py:122
  284.3 23.3 %collective-permute-start.10 = (bf16[192,512]{1,0:T(8,128)(2,1)S(1)}, bf16[192,512]{1,0:T(8,128)(2,1)S(1)}, u32[]{:S(2)}, u32[]{:S(2)}) collective-permute-start(bf16[192,512]{1,0:T(8,128)(2,1)S(1)} %pad_maximum_fusion.13), channel_id=1, source_target_pairs={{0,22},{2,20},{4,18},{6,16},{16,6},{18,4},{20,2},{22,0},{1,23},{3,... | collective-permute-start | bytes 589832 | tf_op jit(solution)/shard_map/ppermute | solution.py:122
  308.4 12.5 %collective-permute-start.11 = (bf16[8,192,512]{2,1,0:T(8,128)(2,1)}, bf16[8,192,512]{2,1,0:T(8,128)(2,1)}, u32[]{:S(2)}, u32[]{:S(2)}) collective-permute-start(bf16[8,192,512]{2,1,0:T(8,128)(2,1)} %bitcast_dynamic-update-slice_fusion), channel_id=1, source_target_pairs={{0,1},{1,0},{2,3},{3,2},{4,5},{5,4},{6,7},{7,6},{8,9},{9,8},{10,11... | collective-permute-start | bytes 4718600 | tf_op jit(solution)/shard_map/ppermute | solution.py:98
  316.5 87.0 %collective-permute-start.2 = (bf16[640,2048]{1,0:T(8,128)(2,1)}, bf16[640,2048]{1,0:T(8,128)(2,1)}, u32[]{:S(2)}, u32[]{:S(2)}) collective-permute-start(bf16[640,2048]{1,0:T(8,128)(2,1)} %collective-permute-done.1), channel_id=1, source_target_pairs={{0,4},{4,8},{8,12},{12,0},{1,5},{5,9},{9,13},{13,1},{2,6},{6,10},{... | collective-permute-start | bytes 7864328 | tf_op jit(solution)/shard_map/ppermute | solution.py:105
  325.3 98.0 %collective-permute-start.12 = (bf16[2,192,2560]{2,1,0:T(8,128)(2,1)}, bf16[2,192,2560]{2,1,0:T(8,128)(2,1)}, u32[]{:S(2)}, u32[]{:S(2)}) collective-permute-start(bf16[2,192,2560]{2,1,0:T(8,128)(2,1)} %pad_maximum_fusion.7), channel_id=1, source_target_pairs={{0,16},{16,0},{1,17},{17,1},{2,18},{18,2},{3,19},{19,3},{4,20},{20... | collective-permute-start | bytes 5898248 | tf_op jit(solution)/shard_map/ppermute | solution.py:98
  328.1 75.4 %collective-permute-start.3 = (bf16[640,1024]{1,0:T(8,128)(2,1)}, bf16[640,1024]{1,0:T(8,128)(2,1)}, u32[]{:S(2)}, u32[]{:S(2)}) collective-permute-start(bf16[640,1024]{1,0:T(8,128)(2,1)} %bitcast.7), channel_id=1, source_target_pairs={{0,4},{4,8},{8,12},{12,0},{1,5},{5,9},{9,13},{13,1},{2,6},{6,10},{... | collective-permute-start | bytes 3932168 | tf_op jit(solution)/shard_map/ppermute | solution.py:105
  337.1 68.7 %copy-start.2 = (bf16[3072,256]{1,0:T(8,128)(2,1)}, bf16[3072,256]{1,0:T(8,128)(2,1)S(1)}, u32[]{:S(2)}) copy-start(bf16[3072,256]{1,0:T(8,128)(2,1)S(1)} %get-tuple-element.170.key_ref) | copy-start | bytes 4718596
  442.7 166.8 %all-gather.17.cloned.1.call-start = ((), (), s32[]{:S(2)}) async-start(), calls=%async_computation.17 | async-start | bytes 8847360 | tf_op jit(solution)/shard_map/all_gather | solution.py:515
  442.7 64.0 %collective-permute-start.14 = (bf16[2,2,192,2560]{3,2,1,0:T(8,128)(2,1)}, bf16[2,2,192,2560]{3,2,1,0:T(8,128)(2,1)}, u32[]{:S(2)}, u32[]{:S(2)}) collective-permute-start(bf16[2,2,192,2560]{3,2,1,0:T(8,128)(2,1)} %pad_maximum_fusion.3), channel_id=1, source_target_pairs={{0,1},{1,0},{2,3},{3,2},{4,5},{5,4},{6,7},{7,6},{8,9},{9,8},{10,11... | collective-permute-start | bytes 11796488 | tf_op jit(solution)/shard_map/ppermute | solution.py:98
  443.6 59.6 %collective-permute-start.15 = (bf16[640,2048]{1,0:T(8,128)(2,1)}, bf16[640,2048]{1,0:T(8,128)(2,1)}, u32[]{:S(2)}, u32[]{:S(2)}) collective-permute-start(bf16[640,2048]{1,0:T(8,128)(2,1)} %collective-permute-done.2), channel_id=1, source_target_pairs={{0,4},{4,8},{8,12},{12,0},{1,5},{5,9},{9,13},{13,1},{2,6},{6,10},{... | collective-permute-start | bytes 7864328 | tf_op jit(solution)/shard_map/ppermute | solution.py:105
  455.7 75.4 %collective-permute-start.13 = (bf16[640,1024]{1,0:T(8,128)(2,1)}, bf16[640,1024]{1,0:T(8,128)(2,1)S(1)}, u32[]{:S(2)}, u32[]{:S(2)}) collective-permute-start(bf16[640,1024]{1,0:T(8,128)(2,1)} %collective-permute-done.3), channel_id=1, source_target_pairs={{0,4},{4,8},{8,12},{12,0},{1,5},{5,9},{9,13},{13,1},{2,6},{6,10},{... | collective-permute-start | bytes 3932168 | tf_op jit(solution)/shard_map/ppermute | solution.py:105
  460.9 45.8 %copy-start.22 = (bf16[1,2,192,2560]{3,2,1,0:T(8,128)(2,1)S(1)}, bf16[1,2,192,2560]{3,2,1,0:T(8,128)(2,1)}, u32[]{:S(2)}) copy-start(bf16[1,2,192,2560]{3,2,1,0:T(8,128)(2,1)} %copy-done.21) | copy-start | bytes 5898244
  553.9 207.9 %reduce-scatter.6.cloned.1.call-start = ((), (), s32[]{:S(2)}) async-start(), calls=%async_computation.19 | async-start | bytes 6553600 | tf_op jit(solution)/shard_map/reduce_scatter | solution.py:513
  554.0 31.5 %collective-permute-start.16 = (bf16[640,1024]{1,0:T(8,128)(2,1)S(1)}, bf16[640,1024]{1,0:T(8,128)(2,1)S(1)}, u32[]{:S(2)}, u32[]{:S(2)}) collective-permute-start(bf16[640,1024]{1,0:T(8,128)(2,1)S(1)} %collective-permute-done.13), channel_id=1, source_target_pairs={{0,4},{4,8},{8,12},{12,0},{1,5},{5,9},{9,13},{13,1},{2,6},{6,10},{... | collective-permute-start | bytes 3932168 | tf_op jit(solution)/shard_map/ppermute | solution.py:105
  554.4 31.2 %slice-start.6 = ((s8[7864320]{0:T(1024)(128)(4,1)}), s8[4194304]{0:T(1024)(128)(4,1)S(1)}, s32[]{:S(2)}) async-start(s8[7864320]{0:T(1024)(128)(4,1)} %bitcast.270), calls=%async_computation.27 | async-start | bytes 8388608
  609.6 330.5 %reduce-scatter.8.cloned.1.call-start = ((), (), s32[]{:S(2)}) async-start(), calls=%async_computation.20 | async-start | bytes 6553600 | tf_op jit(solution)/shard_map/reduce_scatter | solution.py:513
  631.5 8.0 collective-permute-start.17
  655.7 23.3 %collective-permute-start.18 = (bf16[192,2560]{1,0:T(8,128)(2,1)}, bf16[192,2560]{1,0:T(8,128)(2,1)}, u32[]{:S(2)}, u32[]{:S(2)}) collective-permute-start(bf16[192,2560]{1,0:T(8,128)(2,1)} %get-tuple-element.162), channel_id=1, source_target_pairs={{0,2},{2,0},{16,18},{18,16},{1,3},{3,1},{17,19},{19,17},{4,6},{6,4... | collective-permute-start | bytes 2949128 | tf_op jit(solution)/shard_map/ppermute | solution.py:544
  655.7 23.3 %collective-permute-start.19 = (bf16[192,2560]{1,0:T(8,128)(2,1)}, bf16[192,2560]{1,0:T(8,128)(2,1)}, u32[]{:S(2)}, u32[]{:S(2)}) collective-permute-start(bf16[192,2560]{1,0:T(8,128)(2,1)} %get-tuple-element.160), channel_id=1, source_target_pairs={{0,16},{2,18},{16,0},{18,2},{1,17},{3,19},{17,1},{19,3},{4,20},{6,... | collective-permute-start | bytes 2949128 | tf_op jit(solution)/shard_map/ppermute | solution.py:544
  691.2 312.8 %reduce-scatter.4.cloned.1.call-start = ((), (), s32[]{:S(2)}) async-start(), calls=%async_computation.18 | async-start | bytes 6553600 | tf_op jit(solution)/shard_map/reduce_scatter | solution.py:513
  694.5 23.0 %collective-permute-start.20 = (bf16[192,2560]{1,0:T(8,128)(2,1)S(1)}, bf16[192,2560]{1,0:T(8,128)(2,1)S(1)}, u32[]{:S(2)}, u32[]{:S(2)}) collective-permute-start(bf16[192,2560]{1,0:T(8,128)(2,1)S(1)} %copy-done.58), channel_id=1, source_target_pairs={{0,18},{2,16},{16,2},{18,0},{1,19},{3,17},{17,3},{19,1},{4,22},{6,... | collective-permute-start | bytes 2949128 | tf_op jit(solution)/shard_map/ppermute | solution.py:544
  721.0 26.0 %collective-permute-start.22 = (bf16[192,2560]{1,0:T(8,128)(2,1)S(1)}, bf16[192,2560]{1,0:T(8,128)(2,1)}, u32[]{:S(2)}, u32[]{:S(2)}) collective-permute-start(bf16[192,2560]{1,0:T(8,128)(2,1)S(1)} %copy-done.29), channel_id=1, source_target_pairs={{0,2},{2,0},{1,3},{3,1},{4,6},{6,4},{5,7},{7,5},{8,10},{10,8},{9,1... | collective-permute-start | bytes 2949128 | tf_op jit(solution)/shard_map/ppermute | solution.py:98
  740.4 21.5 %all-to-all-start.2 = ((bf16[8,192,320]{2,1,0:T(8,128)(2,1)}), bf16[8,192,320]{2,1,0:T(8,128)(2,1)S(1)}, u32[]{:S(2)}, u32[]{:S(2)}) async-start(bf16[8,192,320]{2,1,0:T(8,128)(2,1)} %bitcast.237), calls=%async_computation.4 | async-start | bytes 2359296 | tf_op jit(solution)/shard_map/all_to_all | solution.py:140
  750.3 56.8 %collective-permute-start.23 = (bf16[2,192,2560]{2,1,0:T(8,128)(2,1)}, bf16[2,192,2560]{2,1,0:T(8,128)(2,1)}, u32[]{:S(2)}, u32[]{:S(2)}) collective-permute-start(bf16[2,192,2560]{2,1,0:T(8,128)(2,1)} %pad_maximum_fusion.8), channel_id=1, source_target_pairs={{0,16},{16,0},{1,17},{17,1},{2,18},{18,2},{3,19},{19,3},{4,20},{20... | collective-permute-start | bytes 5898248 | tf_op jit(solution)/shard_map/ppermute | solution.py:98
  762.9 38.2 %all-to-all-start.3 = ((bf16[4,160,1024]{2,1,0:T(8,128)(2,1)}), bf16[4,160,1024]{2,1,0:T(8,128)(2,1)S(1)}, u32[]{:S(2)}, u32[]{:S(2)}) async-start(bf16[4,160,1024]{2,1,0:T(8,128)(2,1)} %bitcast.299), calls=%async_computation.5 | async-start | bytes 2621440 | tf_op jit(solution)/shard_map/all_to_all | solution.py:140
  801.1 31.0 %collective-permute-start.24 = (bf16[4,160,1024]{2,1,0:T(8,128)(2,1)S(1)}, bf16[4,160,1024]{2,1,0:T(8,128)(2,1)S(1)}, u32[]{:S(2)}, u32[]{:S(2)}) collective-permute-start(bf16[4,160,1024]{2,1,0:T(8,128)(2,1)S(1)} %all-to-all-done.3.refs_1_), channel_id=1, source_target_pairs={{0,16},{16,0},{1,17},{17,1},{2,18},{18,2},{3,19},{19,3},{4,20},{20... | collective-permute-start | bytes 3932168 | tf_op jit(solution)/shard_map/ppermute | solution.py:90
  813.0 149.8 %collective-permute-start.30 = (bf16[2,2,192,2560]{3,2,1,0:T(8,128)(2,1)}, bf16[2,2,192,2560]{3,2,1,0:T(8,128)(2,1)}, u32[]{:S(2)}, u32[]{:S(2)}) collective-permute-start(bf16[2,2,192,2560]{3,2,1,0:T(8,128)(2,1)} %pad_maximum_fusion.4), channel_id=1, source_target_pairs={{0,1},{1,0},{2,3},{3,2},{4,5},{5,4},{6,7},{7,6},{8,9},{9,8},{10,11... | collective-permute-start | bytes 11796488 | tf_op jit(solution)/shard_map/ppermute | solution.py:90
  834.5 25.8 %collective-permute-start.25 = (bf16[8,192,512]{2,1,0:T(8,128)(2,1)}, bf16[8,192,512]{2,1,0:T(8,128)(2,1)}, u32[]{:S(2)}, u32[]{:S(2)}) collective-permute-start(bf16[8,192,512]{2,1,0:T(8,128)(2,1)} %dynamic-slice_bitcast_fusion), channel_id=1, source_target_pairs={{0,1},{1,0},{2,3},{3,2},{4,5},{5,4},{6,7},{7,6},{8,9},{9,8},{10,11... | collective-permute-start | bytes 4718600 | tf_op jit(solution)/shard_map/ppermute | solution.py:90
  840.3 97.8 %all-to-all-start.4 = ((bf16[16,160,320]{2,1,0:T(8,128)(2,1)}), bf16[16,160,320]{2,1,0:T(8,128)(2,1)}, u32[]{:S(2)}, u32[]{:S(2)}) async-start(bf16[16,160,320]{2,1,0:T(8,128)(2,1)} %bitcast.80), calls=%async_computation.7 | async-start | bytes 3932160 | tf_op jit(solution)/shard_map/all_to_all | solution.py:140
  857.9 114.1 %collective-permute-start.21 = (bf16[768,2560]{1,0:T(8,128)(2,1)}, bf16[768,2560]{1,0:T(8,128)(2,1)}, u32[]{:S(2)}, u32[]{:S(2)}) collective-permute-start(bf16[768,2560]{1,0:T(8,128)(2,1)} %convolution_convert_fusion.3), channel_id=1, source_target_pairs={{0,1},{1,0},{2,3},{3,2},{4,5},{5,4},{6,7},{7,6},{8,9},{9,8},{10,11... | collective-permute-start | bytes 11796488 | tf_op jit(solution)/shard_map/ppermute | solution.py:90
  863.8 14.5 %collective-permute-start.28 = (bf16[2,192,512]{2,1,0:T(8,128)(2,1)}, bf16[2,192,512]{2,1,0:T(8,128)(2,1)}, u32[]{:S(2)}, u32[]{:S(2)}) collective-permute-start(bf16[2,192,512]{2,1,0:T(8,128)(2,1)} %get-tuple-element.182), channel_id=1, source_target_pairs={{0,18},{2,16},{16,2},{18,0},{1,19},{3,17},{17,3},{19,1},{4,22},{6,... | collective-permute-start | bytes 1179656 | tf_op jit(solution)/shard_map/ppermute | solution.py:134
  864.0 19.2 %collective-permute-start.27 = (bf16[2,192,512]{2,1,0:T(8,128)(2,1)}, bf16[2,192,512]{2,1,0:T(8,128)(2,1)}, u32[]{:S(2)}, u32[]{:S(2)}) collective-permute-start(bf16[2,192,512]{2,1,0:T(8,128)(2,1)} %get-tuple-element.183), channel_id=1, source_target_pairs={{0,16},{2,18},{16,0},{18,2},{1,17},{3,19},{17,1},{19,3},{4,20},{6,... | collective-permute-start | bytes 1179656 | tf_op jit(solution)/shard_map/ppermute | solution.py:134
  865.2 21.8 %collective-permute-start.26 = (bf16[2,192,512]{2,1,0:T(8,128)(2,1)}, bf16[2,192,512]{2,1,0:T(8,128)(2,1)}, u32[]{:S(2)}, u32[]{:S(2)}) collective-permute-start(bf16[2,192,512]{2,1,0:T(8,128)(2,1)} %get-tuple-element.181), channel_id=1, source_target_pairs={{0,2},{2,0},{16,18},{18,16},{1,3},{3,1},{17,19},{19,17},{4,6},{6,4... | collective-permute-start | bytes 1179656 | tf_op jit(solution)/shard_map/ppermute | solution.py:134
  940.1 19.0 %all-to-all-start.5 = ((bf16[4,160,1024]{2,1,0:T(8,128)(2,1)}), bf16[4,160,1024]{2,1,0:T(8,128)(2,1)S(1)}, u32[]{:S(2)}, u32[]{:S(2)}) async-start(bf16[4,160,1024]{2,1,0:T(8,128)(2,1)} %bitcast.298), calls=%async_computation.8 | async-start | bytes 2621440 | tf_op jit(solution)/shard_map/all_to_all | solution.py:140
  944.7 6.1 collective-permute-start.29
  959.1 44.8 %collective-permute-start.31 = (bf16[4,160,1024]{2,1,0:T(8,128)(2,1)S(1)}, bf16[4,160,1024]{2,1,0:T(8,128)(2,1)}, u32[]{:S(2)}, u32[]{:S(2)}) collective-permute-start(bf16[4,160,1024]{2,1,0:T(8,128)(2,1)S(1)} %all-to-all-done.5.refs_1_), channel_id=1, source_target_pairs={{0,16},{16,0},{1,17},{17,1},{2,18},{18,2},{3,19},{19,3},{4,20},{20... | collective-permute-start | bytes 3932168 | tf_op jit(solution)/shard_map/ppermute | solution.py:90
  965.3 36.3 %all-to-all-start.6 = ((bf16[8,192,384]{2,1,0:T(8,128)(2,1)}), bf16[8,192,384]{2,1,0:T(8,128)(2,1)}, u32[]{:S(2)}, u32[]{:S(2)}) async-start(bf16[8,192,384]{2,1,0:T(8,128)(2,1)} %bitcast.286), calls=%async_computation.9 | async-start | bytes 2359296 | tf_op jit(solution)/shard_map/all_to_all | solution.py:140
  1004.0 34.7 %all-to-all-start.7 = ((bf16[4,160,1024]{2,1,0:T(8,128)(2,1)}), bf16[4,160,1024]{2,1,0:T(8,128)(2,1)S(1)}, u32[]{:S(2)}, u32[]{:S(2)}) async-start(bf16[4,160,1024]{2,1,0:T(8,128)(2,1)} %bitcast.297), calls=%async_computation.10 | async-start | bytes 2621440 | tf_op jit(solution)/shard_map/all_to_all | solution.py:140
  1038.7 91.5 %all-to-all-start.8 = ((bf16[16,160,384]{2,1,0:T(8,128)(2,1)}), bf16[16,160,384]{2,1,0:T(8,128)(2,1)}, u32[]{:S(2)}, u32[]{:S(2)}) async-start(bf16[16,160,384]{2,1,0:T(8,128)(2,1)} %bitcast.294), calls=%async_computation.11 | async-start | bytes 3932160 | tf_op jit(solution)/shard_map/all_to_all | solution.py:140
  1069.5 12.4 %collective-permute-start.37 = (bf16[4,160,320]{2,1,0:T(8,128)(2,1)S(1)}, bf16[4,160,320]{2,1,0:T(8,128)(2,1)S(1)}, u32[]{:S(2)}, u32[]{:S(2)}) collective-permute-start(bf16[4,160,320]{2,1,0:T(8,128)(2,1)S(1)} %reduce_sum.122), channel_id=1, source_target_pairs={{0,16},{16,0},{1,17},{17,1},{2,18},{18,2},{3,19},{19,3},{4,20},{20... | collective-permute-start | bytes 1228808 | tf_op jit(solution)/shard_map/ppermute | solution.py:98
  1082.3 29.3 %collective-permute-start.35 = (bf16[4,160,1024]{2,1,0:T(8,128)(2,1)S(1)}, bf16[4,160,1024]{2,1,0:T(8,128)(2,1)S(1)}, u32[]{:S(2)}, u32[]{:S(2)}) collective-permute-start(bf16[4,160,1024]{2,1,0:T(8,128)(2,1)S(1)} %all-to-all-done.7.refs_1_), channel_id=1, source_target_pairs={{0,16},{16,0},{1,17},{17,1},{2,18},{18,2},{3,19},{19,3},{4,20},{20... | collective-permute-start | bytes 3932168 | tf_op jit(solution)/shard_map/ppermute | solution.py:90
  1084.3 48.3 %collective-permute-start.34 = (bf16[192,2560]{1,0:T(8,128)(2,1)}, bf16[192,2560]{1,0:T(8,128)(2,1)}, u32[]{:S(2)}, u32[]{:S(2)}) collective-permute-start(bf16[192,2560]{1,0:T(8,128)(2,1)} %get-tuple-element.156), channel_id=1, source_target_pairs={{0,18},{2,16},{16,2},{18,0},{1,19},{3,17},{17,3},{19,1},{4,22},{6,... | collective-permute-start | bytes 2949128 | tf_op jit(solution)/shard_map/ppermute | solution.py:134
  1085.4 68.2 %collective-permute-start.33 = (bf16[192,2560]{1,0:T(8,128)(2,1)}, bf16[192,2560]{1,0:T(8,128)(2,1)}, u32[]{:S(2)}, u32[]{:S(2)}) collective-permute-start(bf16[192,2560]{1,0:T(8,128)(2,1)} %get-tuple-element.157), channel_id=1, source_target_pairs={{0,16},{2,18},{16,0},{18,2},{1,17},{3,19},{17,1},{19,3},{4,20},{6,... | collective-permute-start | bytes 2949128 | tf_op jit(solution)/shard_map/ppermute | solution.py:134
  1085.8 67.9 %collective-permute-start.32 = (bf16[192,2560]{1,0:T(8,128)(2,1)}, bf16[192,2560]{1,0:T(8,128)(2,1)}, u32[]{:S(2)}, u32[]{:S(2)}) collective-permute-start(bf16[192,2560]{1,0:T(8,128)(2,1)} %get-tuple-element.155), channel_id=1, source_target_pairs={{0,2},{2,0},{16,18},{18,16},{1,3},{3,1},{17,19},{19,17},{4,6},{6,4... | collective-permute-start | bytes 2949128 | tf_op jit(solution)/shard_map/ppermute | solution.py:134
  1132.2 31.9 %collective-permute-start.36 = (bf16[4,160,384]{2,1,0:T(8,128)(2,1)S(1)}, bf16[4,160,384]{2,1,0:T(8,128)(2,1)S(1)}, u32[]{:S(2)}, u32[]{:S(2)}) collective-permute-start(bf16[4,160,384]{2,1,0:T(8,128)(2,1)S(1)} %reduce_sum.124), channel_id=1, source_target_pairs={{0,16},{16,0},{1,17},{17,1},{2,18},{18,2},{3,19},{19,3},{4,20},{20... | collective-permute-start | bytes 1474568 | tf_op jit(solution)/shard_map/ppermute | solution.py:98
  (79 other events, 594.2 us)
Sparse Core Ops, SparseCore 0:
  23.6 53.6 all-gather.6
  121.9 37.8 all-gather.10
  161.8 106.5 all-gather.8
  270.1 121.5 all-gather.12
  442.8 53.3 all-gather.14
  554.0 53.5 all-gather.16
  609.9 95.5 reduce-scatter.5
  708.4 94.2 reduce-scatter.7
  805.0 136.3 reduce-scatter.3

commit v5 on v4

--- a/solution.py
+++ b/solution.py
@@ -438,18 +438,23 @@
         return exchanged(chunks, ("k", "c")).reshape(members * own_rows, chunks.shape[2])
 
     incoming = cotangent.reshape(tok_rows, width)
-    def gathered(weight, *others):
+    def own_half(weight):
         half = weight.shape[1] // sides
-        weight = lax.dynamic_slice_in_dim(weight, side * half, half, 1)
-        weight = after(lax.all_gather(weight, PLANES, axis=0, tiled=True), *others)
+        return lax.dynamic_slice_in_dim(weight, side * half, half, 1)
+
+    def gathered_group(weight):
+        half = weight.shape[1]
         weight = lax.all_gather(weight, GROUP, axis=0, tiled=True)
         return weight.reshape(sides, owner_count * own_rows, half)
 
     gate_up_blocks = [to_members(gate_up_chunks)]
-    qkv_halves = gathered(low(qkv_low * gain_one), gate_up_chunks)
-    gate_up_blocks.append(next_plane(gate_up_blocks[0]))
+    qkv_rows = lax.all_gather(own_half(low(qkv_low * gain_one)), PLANES, axis=0, tiled=True)
+    qkv_halves = gathered_group(after(qkv_rows, gate_up_chunks))
+    gate_up_blocks.append(next_plane(after(gate_up_blocks[0], qkv_rows)))
     down_blocks = [to_members(down_chunks)]
-    out_halves = gathered(after(low(weight_out), gate_up_blocks[1]))
+    down_blocks.append(next_plane(down_blocks[0]))
+    out_rows = own_half(after(low(weight_out), qkv_halves))
+    out_halves = gathered_group(lax.all_gather(out_rows, PLANES, axis=0, tiled=True))
     incoming_columns = doubled(incoming, "k", 1, 0)
 
     tokens = wide(hidden_in.reshape(tok_rows, width))
@@ -469,7 +474,7 @@
 
     factor_one = lax.rsqrt(jnp.mean(tokens * tokens, axis=-1, keepdims=True) + NORM_EPS)
     normed_one = low(tokens * factor_one)
-    normed_one = after(normed_one, incoming_columns, gate_up_blocks[1], down_blocks[0])
+    normed_one = after(normed_one, incoming_columns, gate_up_blocks[1], down_blocks[1])
     rows = regrouped(normed_one, planes, members)
     projected = jnp.concatenate([dot(rows, half, (1, 0)) for half in qkv_halves], axis=1)
     key_pre = projected[:, width : width + HEAD_DIM]
@@ -481,15 +486,15 @@
     gate_up_blocks.append(next_plane(after(gate_up_blocks[1], projected)))
     for _ in range(planes - 3):
         gate_up_blocks.append(next_plane(gate_up_blocks[-1]))
-    down_blocks.append(next_plane(after(down_blocks[0], projected)))
-    for _ in range(planes - 2):
+    down_blocks.append(next_plane(after(down_blocks[1], projected)))
+    for _ in range(planes - 3):
         down_blocks.append(next_plane(down_blocks[-1]))
     gate_up_own = joined_planes(gate_up_blocks)
     down_own = joined_planes(down_blocks)
     incoming_sides = doubled(after(incoming_columns, window_kv), "seq", 1, 0)
     query_pre = projected[:, :width].reshape(tok_rows, head_count, HEAD_DIM)
     queries = low(rotate(query_pre, cosine[:, None, :], sine[:, None, :]) * query_scale)
-    queries = after(queries.reshape(tok_rows, width), gate_up_blocks[2], down_blocks[1])
+    queries = after(queries.reshape(tok_rows, width), gate_up_blocks[2], down_blocks[2])
     incoming_all = doubled(incoming_sides, "c", 1, incoming_sides.ndim - 2)
     incoming_all = incoming_all.reshape(sides * members * tok_rows, width)
     keys_win = window_kv[:, :HEAD_DIM]
@@ -506,7 +511,7 @@
     normed_two = low(middle * factor_two)
     normed_two_all = lax.all_gather(normed_two, GROUP, axis=0, tiled=True)
     grad_act = low(dot(incoming_all, down_own, (1, 0)))
-    gate_up = dot(after(normed_two_all, down_blocks[2], incoming_all), gate_up_own, (1, 0))
+    gate_up = dot(after(normed_two_all, down_own, incoming_all), gate_up_own, (1, 0))
     activated, glu_back = jax.vjp(glu_values, gate_up[:, :piece], gate_up[:, piece:])
     activated_low = low(activated)
     def to_owners(term):
@@ -586,11 +591,10 @@
     normed_one_columns = doubled(after(normed_one, grad_normed_two), "k", 1, 0)
     normed_one_sides = doubled(normed_one_columns, "seq", 1, 0)
     branch_terms = group_terms(after(activated_low, grad_window), down_own)
-    down_pieces = in_plane(down_rows, out_columns)
-    grad_window = after(low(grad_window), normed_one_sides, down_pieces[1])
-    out_total = to_rows(low(dot(attn_all, after(out_columns, grad_window), (0, 0))))
+    down_pieces = in_plane(down_rows, grad_window)
+    out_total = to_rows(low(dot(attn_all, out_columns, (0, 0))))
+    grad_window = after(low(grad_window), normed_one_sides, out_total)
     normed_one_others = swapped(normed_one_sides, "c")
-    gate_pieces = in_plane(gate_rows, out_total)
     grad_window = half_sum(grad_window.reshape(-1, 2, tok_rows, 2 * HEAD_DIM), "c", 1)
     grad_window = grad_window.reshape(sides, -1, columns, tok_rows, 2 * HEAD_DIM)
     grad_window = grad_window.swapaxes(1, 2).reshape(sides * columns, -1, tok_rows, 2 * HEAD_DIM)
@@ -611,7 +615,7 @@
         *outs, gain_dot = mlp_adam(part, side, pieces, mlp_states, gain_two, rate_main, outs)
         return outs, gain_dot
 
-    qkv_columns = by_column(after(grad_proj, gate_pieces[0], normed_one_others))
+    qkv_columns = by_column(after(grad_proj, down_pieces[0], normed_one_others))
     mlp_outs, _ = mlp_updated(2, down_pieces, ())
     by_core = after(qkv_columns, *mlp_outs).reshape(sides * columns, 2, tok_rows, -1)
 
@@ -621,10 +625,12 @@
 
     qkv_total = one_core_total(normed_one_sides, core)
     qkv_total = low(qkv_total + one_core_total(normed_one_others, 1 - core))
-    up_pieces = in_plane(up_rows, qkv_columns, gate_pieces[1])
+    branch = ring_sum(after(branch_terms, qkv_columns))
+    gate_pieces = in_plane(gate_rows, qkv_columns)
+    up_pieces = in_plane(up_rows, gate_pieces[0])
+    qkv_total = to_rows(after(qkv_total, up_pieces[0], gate_pieces[1]))
+    gate_pieces = lax.optimization_barrier((*gate_pieces, branch))[:2]
     mlp_outs, gate_dot = mlp_updated(0, gate_pieces, mlp_outs)
-    qkv_total = to_rows(after(qkv_total, up_pieces[0], gate_dot))
-    branch = ring_sum(after(branch_terms, up_pieces[0]))
     (grad_mlp, second_new_mlp, new_mlp), up_dot = mlp_updated(1, up_pieces, mlp_outs)
     grad_gain_two = gate_dot + up_dot
     qkv_total = after(qkv_total, up_dot)

time: 1190 us -> 1180 us (level)
  waiting for transfers between devices: 573 us -> 550 us
    all_to_all x9, waiting for transfers between devices: 109 us -> 156 us  [exchanged(): return lax.all_to_all(value, axes, split_axis=0, concat_axis=0, tiled=True)]
    ppermute x6, waiting for transfers between devices: 213 us -> 166 us  [next_plane(): lax.ppermute(block, PLANES, [(one, (one + 1) % count) for one in range(co...]
    ppermute x8, waiting for transfers between devices: 36.4 us -> 7.89 us  [doubled(): other = lax.ppermute(value, axis, traded((axis,), step))]
    all_gather x1, waiting for transfers between devices: 0.01 us -> 25.4 us  [on_device(): lax.all_gather(after(attn_low, gate_up), GROUP, axis=0, tiled=True)]
    all_gather x4, waiting for transfers between devices: 87.1 us -> 72.9 us  [the longest x1 39.3 us: on_device(): lax.all_gather(out_rows, PLANES, axis=0, tiled=True)]
    ppermute x8, waiting for transfers between devices: 41.2 us -> 27.6 us  [swapped(): return lax.ppermute(value, axis, [(0, 1), (1, 0)])]
  transfers between devices with their start and end apart: 56 -> 56, of which waited for: 29 -> 30; matrix products, arithmetic and copies ran while one was open for 28% -> 29% of each run, Pallas kernels for 9% -> 9%
where the time goes in v5:
time: 1180 us; the launch traced here: 1170 us
  waiting for transfers between devices  550 us (47%)
  matrix products  177 us (15%)
  local copies, waits for them, and re-layouts  114 us (10%)
  other arithmetic  113 us (10%)
  Pallas kernels  109 us (9%)
  starting transfers between devices  86.6 us (7%)
  between operations  15.3 us (1%)
    dot_general x20, matrix products, dot(): lax.dot_general(left, right, ((contract[:1], contract[1:]), ((), ())), pr...  177 us
    ppermute x6, waiting for transfers between devices, next_plane(): lax.ppermute(block, PLANES, [(one, (one + 1) % count) for one in range(co...  166 us
    all_to_all x9, waiting for transfers between devices, exchanged(): return lax.all_to_all(value, axes, split_axis=0, concat_axis=0, tiled=True)  156 us
    all_to_all x9, starting transfers between devices, exchanged(): return lax.all_to_all(value, axes, split_axis=0, concat_axis=0, tiled=True)  55.6 us
    pallas_call x3, Pallas kernels, mlp_adam(): pl.pallas_call(lambda *refs: mlp_adam_kernel(rate, per_side, part < 2, *r...  54.7 us
    ppermute x6, waiting for transfers between devices, ring_sum(): term = lax.ppermute(term, CHIPS, traded(CHIPS, step))  49.9 us
    all_gather x1, waiting for transfers between devices, on_device(): lax.all_gather(out_rows, PLANES, axis=0, tiled=True)  39.3 us
    all_gather x1, waiting for transfers between devices, on_device(): lax.all_gather(own_half(low(qkv_low * gain_one)), PLANES, axis=0, tiled=T...  33.5 us
  transfers between devices with their start and end apart: 56, of which 30 were waited for; matrix products, arithmetic and copies ran while one was open for 29% of the time, Pallas kernels for 9%

profile of v5, /device:TPU:13, one launch (start us, length us, event | category | flops | bytes accessed | tf_op | source)
XLA Modules:
  0.0 1165.9 jit_solution(8900358658849351119)
XLA Ops:
  14.5 8.0 mlp_chunks.1
  23.2 33.5 %all-gather.7.cloned.1.call-done = bf16[640,1536]{1,0:T(8,128)(2,1)} async-done(((bf16[160,1536]{1,0:T(8,128)(2,1)}), bf16[640,1536]{1,0:T(8,128)(2,1)}) %all-gather.7.cloned.1.call-update) | async-done | bytes 1966096 | tf_op jit(solution)/shard_map/all_gather | solution.py:451
  56.8 39.3 %all-gather.11.cloned.1.call-done = bf16[640,1280]{1,0:T(8,128)(2,1)} async-done(((bf16[160,1280]{1,0:T(8,128)(2,1)}), bf16[640,1280]{1,0:T(8,128)(2,1)}) %all-gather.11.cloned.1.call-update) | async-done | bytes 1638416 | tf_op jit(solution)/shard_map/all_gather | solution.py:457
  96.2 5.7 all-to-all-start
  102.9 49.6 %all-to-all-done = bf16[4,160,2048]{2,1,0:T(8,128)(2,1)} async-done(((bf16[4,160,2048]{2,1,0:T(8,128)(2,1)}), bf16[4,160,2048]{2,1,0:T(8,128)(2,1)}, u32[]{:S(2)}, u32[]{:S(2)}) %all-to-all-start) | async-done | bytes 2621472 | tf_op jit(solution)/shard_map/all_to_all | solution.py:140
  152.5 5.9 all-to-all-start.1
  160.2 55.3 %all-to-all-done.1 = bf16[4,160,1024]{2,1,0:T(8,128)(2,1)S(1)} async-done(((bf16[4,160,1024]{2,1,0:T(8,128)(2,1)}), bf16[4,160,1024]{2,1,0:T(8,128)(2,1)S(1)}, u32[]{:S(2)}, u32[]{:S(2)}) %all-to-all-start.1) | async-done | bytes 1310752 | tf_op jit(solution)/shard_map/all_to_all | solution.py:140
  219.7 26.7 %collective-permute-done.2 = bf16[640,1024]{1,0:T(8,128)(2,1)} collective-permute-done((bf16[640,1024]{1,0:T(8,128)(2,1)S(1)}, bf16[640,1024]{1,0:T(8,128)(2,1)}, u32[]{:S(2)}, u32[]{:S(2)}) %collective-permute-start.2) | collective-permute-done | bytes 1310752 | tf_op jit(solution)/shard_map/ppermute | solution.py:105
  247.1 5.4 fusion.2
  262.5 11.2 collective-permute-done.5
  288.7 5.4 fusion.6
  313.6 67.5 %collective-permute-done.4 = bf16[640,1024]{1,0:T(8,128)(2,1)} collective-permute-done((bf16[640,1024]{1,0:T(8,128)(2,1)}, bf16[640,1024]{1,0:T(8,128)(2,1)}, u32[]{:S(2)}, u32[]{:S(2)}) %collective-permute-start.4) | collective-permute-done | bytes 1310752 | tf_op jit(solution)/shard_map/ppermute | solution.py:105
  384.7 16.5 %attend.1 = (bf16[192,2560]{1,0:T(8,128)(2,1)}, f32[5,1,384]{2,1,0:T(1,128)S(1)}) custom-call(bf16[192,2560]{1,0:T(8,128)(2,1)S(1)} %copy-done.5, bf16[3072,256]{1,0:T(8,128)(2,1)S(1)} %get-tuple-element.174.key_ref, bf16[256,3072]{1,0:T(8,128)(2,1)S(1)} %copy.150.value_t_ref, f32[3072,384]{1,0:T(8,128)} %pad_maximum_fusion.2.bias_ref), custom_call_target="tpu_custom_call" | custom-call | flops 6039797760 | bytes 18087936 | tf_op jit(solution)/shard_map/attend/pallas_call | solution.py:305
  408.8 4.8 fusion.18
  413.7 4.7 fusion.22
  438.5 71.6 %collective-permute-done.14 = bf16[640,1024]{1,0:T(8,128)(2,1)S(1)} collective-permute-done((bf16[640,1024]{1,0:T(8,128)(2,1)}, bf16[640,1024]{1,0:T(8,128)(2,1)S(1)}, u32[]{:S(2)}, u32[]{:S(2)}) %collective-permute-start.14) | collective-permute-done | bytes 1310752 | tf_op jit(solution)/shard_map/ppermute | solution.py:105
  523.5 6.0 pad_maximum_fusion
  529.5 7.0 copy.153
  536.5 22.8 %fusion.97 = f32[1536,2048]{1,0:T(8,128)} fusion(bf16[1536,2560]{1,0:T(8,128)(2,1)} %all-gather.15.cloned.1.call-done, bf16[2560,2048]{1,0:T(8,128)(2,1)} %copy-done.23), kind=kOutput, calls=%fused_computation.229 | convolution fusion | flops 16106127360 | bytes 30932992 | tf_op jit(solution)/shard_map/dot_general | solution.py:79
  559.8 13.4 %convolution_convert_fusion.6 = bf16[1536,1024]{1,0:T(8,128)(2,1)} fusion(bf16[1536,2560]{1,0:T(8,128)(2,1)} %bitcast.268, bf16[2560,1024]{1,0:T(8,128)(2,1)} %constant_dynamic-update-slice_fusion.4), kind=kOutput, calls=%fused_computation.55 | convolution fusion | flops 8054636544 | bytes 16252928 | tf_op jit(solution)/shard_map/dot_general | solution.py:79
  577.1 10.3 convolution_convert_fusion.2
  587.5 25.4 %all-gather.17.cloned.1.call-done = bf16[1536,2560]{1,0:T(8,128)(2,1)} async-done(((bf16[192,2560]{1,0:T(8,128)(2,1)}), bf16[1536,2560]{1,0:T(8,128)(2,1)}) %all-gather.17.cloned.1.call-update) | async-done | bytes 7864336 | tf_op jit(solution)/shard_map/all_gather | solution.py:520
  613.2 8.7 fusion.8
  625.1 9.8 convolution_convert_fusion.4
  635.2 6.9 collective-permute-done.17
  642.1 12.7 %add_convert_fusion.1 = bf16[768,2560]{1,0:T(8,128)(2,1)S(1)} fusion(bf16[768,2560]{1,0:T(8,128)(2,1)} %collective-permute-done.17, bf16[768,2048]{1,0:T(8,128)(2,1)} %bitcast.290, bf16[2560,2048]{1,0:T(8,128)(2,1)} %copy-done.23), kind=kOutput, calls=%fused_computation.4 | convolution fusion | flops 8058961920 | bytes 21495808 | tf_op jit(solution)/shard_map/dot_general | solution.py:79
  660.6 20.9 %collective-permute-done.18 = bf16[192,2560]{1,0:T(8,128)(2,1)} collective-permute-done((bf16[192,2560]{1,0:T(8,128)(2,1)}, bf16[192,2560]{1,0:T(8,128)(2,1)}, u32[]{:S(2)}, u32[]{:S(2)}) %collective-permute-start.18) | collective-permute-done | bytes 983072 | tf_op jit(solution)/shard_map/ppermute | solution.py:549
  681.8 12.6 %convolution_convert_fusion.1 = bf16[2560,1024]{1,0:T(8,128)(2,1)} fusion(bf16[1536,2560]{1,0:T(8,128)(2,1)} %all-gather.15.cloned.1.call-done, bf16[1536,2048]{1,0:T(8,128)(2,1)S(1)} %pad_maximum_fusion.1), kind=kOutput, calls=%fused_computation.39 | convolution fusion | flops 8055685120 | bytes 16252928 | tf_op jit(solution)/shard_map/dot_general | solution.py:79
  698.9 13.9 %convolution_convert_fusion = bf16[2560,1024]{1,0:T(8,128)(2,1)} fusion(bf16[1536,2560]{1,0:T(8,128)(2,1)} %all-gather.15.cloned.1.call-done, bf16[1536,2048]{1,0:T(8,128)(2,1)} %copy-done.34), kind=kOutput, calls=%fused_computation.38 | convolution fusion | flops 8055685120 | bytes 16252928 | tf_op jit(solution)/shard_map/dot_general | solution.py:79
  712.9 7.5 collective-permute-done.20
  729.9 7.5 all-to-all-start.2
  737.4 5.1 fusion.16
  742.5 6.2 fusion.31
  753.0 5.9 all-to-all-done.2
  758.9 7.5 convolution_convert_fusion.5
  770.2 7.8 all-to-all-start.3
  790.9 29.9 %attend_back.1 = (f32[192,2560]{1,0:T(8,128)}, f32[3072,512]{1,0:T(8,128)}) custom-call(bf16[192,2560]{1,0:T(8,128)(2,1)S(1)} %copy-done.6, bf16[192,2560]{1,0:T(8,128)(2,1)S(1)} %copy.159.grad_ref, bf16[3072,256]{1,0:T(8,128)(2,1)S(1)} %copy-done.3, bf16[256,3072]{1,0:T(8,128)(2,1)S(1)} %copy-done.4, bf16[3072,256]{1,0:T(8,128)(2,1)} %get-tuple-element.171.value_ref, ...), custom_call_target="tpu_custom_call" | custom-call | flops 15099494400 | bytes 22806528 | tf_op jit(solution)/shard_map/attend_back/pallas_call | solution.py:364
  829.7 18.0 %all-to-all-done.3 = bf16[16,160,320]{2,1,0:T(8,128)(2,1)} async-done(((bf16[16,160,320]{2,1,0:T(8,128)(2,1)}), bf16[16,160,320]{2,1,0:T(8,128)(2,1)}, u32[]{:S(2)}, u32[]{:S(2)}) %all-to-all-start.3) | async-done | bytes 1638432 | tf_op jit(solution)/shard_map/all_to_all | solution.py:140
  856.4 8.3 convolution_convert_fusion.3
  874.2 5.7 collective-permute-done.27
  879.8 7.5 collective-permute-done.26
  892.3 4.6 all-to-all-start.4
  898.3 5.4 collective-permute-done.28
  907.0 5.4 all-to-all-done.4.refs_1_
  914.9 6.0 all-to-all-start.5
  924.2 11.6 all-to-all-done.5
  935.8 5.0 all-to-all-start.6
  940.9 10.3 add_convert_fusion
  951.2 5.2 all-to-all-done.6.refs_1_
  959.1 15.3 %collective-permute-done.33.refs_2_ = bf16[4,160,1024]{2,1,0:T(8,128)(2,1)} collective-permute-done((bf16[4,160,1024]{2,1,0:T(8,128)(2,1)S(1)}, bf16[4,160,1024]{2,1,0:T(8,128)(2,1)}, u32[]{:S(2)}, u32[]{:S(2)}) %collective-permute-start.33) | collective-permute-done | bytes 1310752 | tf_op jit(solution)/shard_map/ppermute | solution.py:90
  974.5 17.6 %mlp_adam.3 = (f32[3,160,7680]{2,1,0:T(8,128)}, f32[3,160,7680]{2,1,0:T(8,128)}, f32[3,160,7680]{2,1,0:T(8,128)}, f32[160,1]{1,0:T(8,128)}) custom-call(s32[1]{0:T(128)} %bitcast.4.refs_0_, bf16[4,160,1024]{2,1,0:T(8,128)(2,1)S(1)} %all-to-all-done.4.refs_1_, bf16[4,160,1024]{2,1,0:T(8,128)(2,1)} %collective-permute-done.33.refs_2_, ...), custom_call_target="tpu_custom_call" | custom-call | flops 24576000 | bytes 31948800 | tf_op jit(solution)/shard_map/mlp_adam/pallas_call | solution.py:238
  994.2 5.0 all-to-all-start.7
  1003.8 5.7 fusion.24
  1009.5 5.1 all-to-all-done.7.refs_1_
  1014.6 8.0 all-to-all-start.8
  1029.2 6.4 fusion
  1039.9 7.3 fusion.25
  1058.4 13.1 %collective-permute-done.32 = bf16[192,2560]{1,0:T(8,128)(2,1)} collective-permute-done((bf16[192,2560]{1,0:T(8,128)(2,1)}, bf16[192,2560]{1,0:T(8,128)(2,1)}, u32[]{:S(2)}, u32[]{:S(2)}) %collective-permute-start.32) | collective-permute-done | bytes 983072 | tf_op jit(solution)/shard_map/ppermute | solution.py:134
  1071.5 19.3 %collective-permute-done.31 = bf16[192,2560]{1,0:T(8,128)(2,1)} collective-permute-done((bf16[192,2560]{1,0:T(8,128)(2,1)}, bf16[192,2560]{1,0:T(8,128)(2,1)}, u32[]{:S(2)}, u32[]{:S(2)}) %collective-permute-start.31) | collective-permute-done | bytes 983072 | tf_op jit(solution)/shard_map/ppermute | solution.py:134
  1093.8 7.1 fusion.54
  1100.8 18.5 %mlp_adam.4 = (f32[3,160,7680]{2,1,0:T(8,128)}, f32[3,160,7680]{2,1,0:T(8,128)}, f32[3,160,7680]{2,1,0:T(8,128)}, f32[160,1]{1,0:T(8,128)S(1)}) custom-call(s32[1]{0:T(128)} %bitcast.4.refs_0_, bf16[4,160,1024]{2,1,0:T(8,128)(2,1)S(1)} %all-to-all-done.6.refs_1_, ...), custom_call_target="tpu_custom_call", output_to_operand_aliasing={{0}: (7, {}), {1}: (8, {}), {2}: (9, {})} | custom-call | flops 24576000 | bytes 31948800 | tf_op jit(solution)/shard_map/mlp_adam/pallas_call | solution.py:238
  1119.3 18.7 %mlp_adam.5 = (f32[3,160,7680]{2,1,0:T(8,128)}, f32[3,160,7680]{2,1,0:T(8,128)}, f32[3,160,7680]{2,1,0:T(8,128)}, f32[160,1]{1,0:T(8,128)S(1)}) custom-call(s32[1]{0:T(128)} %bitcast.4.refs_0_, bf16[4,160,1024]{2,1,0:T(8,128)(2,1)S(1)} %all-to-all-done.7.refs_1_, ...), custom_call_target="tpu_custom_call", output_to_operand_aliasing={{0}: (7, {}), {1}: (8, {}), {2}: (9, {})} | custom-call | flops 24576000 | bytes 31948800 | tf_op jit(solution)/shard_map/mlp_adam/pallas_call | solution.py:238
  1140.3 5.3 multiply_subtract_fusion.2
  1145.7 6.4 collective-permute-done.36
  (381 shorter events, 239.8 us)
Async XLA Ops:
  7.2 49.6 %all-gather.7.cloned.1.call-start = ((), (), s32[]{:S(2)}) async-start(), calls=%async_computation.12 | async-start | bytes 2457600 | tf_op jit(solution)/shard_map/all_gather | solution.py:451
  13.4 82.7 %all-gather.11.cloned.1.call-start = ((), (), s32[]{:S(2)}) async-start(), calls=%async_computation.14 | async-start | bytes 2048000 | tf_op jit(solution)/shard_map/all_gather | solution.py:457
  14.4 232.7 %all-gather.9.cloned.1.call-start = ((), (), s32[]{:S(2)}) async-start(), calls=%async_computation.13 | async-start | bytes 17694720 | tf_op jit(solution)/shard_map/all_gather | solution.py:447
  56.8 352.1 %all-gather.13.cloned.1.call-start = ((), (), s32[]{:S(2)}) async-start(), calls=%async_computation.15 | async-start | bytes 14745600 | tf_op jit(solution)/shard_map/all_gather | solution.py:447
  96.2 56.3 %all-to-all-start = ((bf16[4,160,2048]{2,1,0:T(8,128)(2,1)}), bf16[4,160,2048]{2,1,0:T(8,128)(2,1)}, u32[]{:S(2)}, u32[]{:S(2)}) async-start(bf16[4,160,2048]{2,1,0:T(8,128)(2,1)} %get-tuple-element.59), calls=%async_computation | async-start | bytes 5242880 | tf_op jit(solution)/shard_map/all_to_all | solution.py:140
  101.9 57.6 %copy-start.73 = (s32[2,3]{1,0:T(2,128)S(1)}, s32[2,3]{1,0:T(2,128)}, u32[]{:S(2)}) copy-start(s32[2,3]{1,0:T(2,128)} %param.17) | copy-start | bytes 76
  101.9 114.7 %collective-permute-start = (bf16[192,2560]{1,0:T(8,128)(2,1)}, bf16[192,2560]{1,0:T(8,128)(2,1)}, u32[]{:S(2)}, u32[]{:S(2)}) collective-permute-start(bf16[192,2560]{1,0:T(8,128)(2,1)} %bitcast.1), channel_id=1, source_target_pairs={{0,2},{2,0},{1,3},{3,1},{4,6},{6,4},{5,7},{7,5},{8,10},{10,8},{9,1... | collective-permute-start | bytes 2949128 | tf_op jit(solution)/shard_map/ppermute | solution.py:98
  102.9 57.2 %copy-start.58 = (f32[192]{0:T(256)}, f32[192]{0:T(256)S(1)}, u32[]{:S(2)}) copy-start(f32[192]{0:T(256)S(1)} %get-tuple-element.205) | copy-start | bytes 2308
  152.5 62.9 %all-to-all-start.1 = ((bf16[4,160,1024]{2,1,0:T(8,128)(2,1)}), bf16[4,160,1024]{2,1,0:T(8,128)(2,1)S(1)}, u32[]{:S(2)}, u32[]{:S(2)}) async-start(bf16[4,160,1024]{2,1,0:T(8,128)(2,1)} %get-tuple-element.61), calls=%async_computation.1 | async-start | bytes 2621440 | tf_op jit(solution)/shard_map/all_to_all | solution.py:140
  158.4 378.1 %all-gather.15.cloned.1.call-start = ((), (), s32[]{:S(2)}) async-start(), calls=%async_computation.16 | async-start | bytes 8847360 | tf_op jit(solution)/shard_map/all_gather | solution.py:512
  158.4 88.0 %collective-permute-start.1 = (bf16[640,2048]{1,0:T(8,128)(2,1)}, bf16[640,2048]{1,0:T(8,128)(2,1)}, u32[]{:S(2)}, u32[]{:S(2)}) collective-permute-start(bf16[640,2048]{1,0:T(8,128)(2,1)} %bitcast.6), channel_id=1, source_target_pairs={{0,4},{4,8},{8,12},{12,0},{1,5},{5,9},{9,13},{13,1},{2,6},{6,10},{... | collective-permute-start | bytes 7864328 | tf_op jit(solution)/shard_map/ppermute | solution.py:105
  160.1 86.2 %copy-start.24 = (bf16[192,2560]{1,0:T(8,128)(2,1)}, bf16[192,2560]{1,0:T(8,128)(2,1)S(1)}, u32[]{:S(2)}) copy-start(bf16[192,2560]{1,0:T(8,128)(2,1)S(1)} %fusion.49) | copy-start | bytes 2949124
  215.4 30.9 %collective-permute-start.2 = (bf16[640,1024]{1,0:T(8,128)(2,1)S(1)}, bf16[640,1024]{1,0:T(8,128)(2,1)}, u32[]{:S(2)}, u32[]{:S(2)}) collective-permute-start(bf16[640,1024]{1,0:T(8,128)(2,1)S(1)} %bitcast.275), channel_id=1, source_target_pairs={{0,4},{4,8},{8,12},{12,0},{1,5},{5,9},{9,13},{13,1},{2,6},{6,10},{... | collective-permute-start | bytes 3932168 | tf_op jit(solution)/shard_map/ppermute | solution.py:105
  216.5 36.1 %copy-start.60 = (f32[192]{0:T(256)}, f32[192]{0:T(256)S(1)}, u32[]{:S(2)}) copy-start(f32[192]{0:T(256)S(1)} %get-tuple-element.150) | copy-start | bytes 2308
  216.6 36.0 %copy-start.71 = (f32[128]{0:T(128)}, f32[128]{0:T(128)S(1)}, u32[]{:S(2)}) copy-start(f32[128]{0:T(128)S(1)} %multiply_exponential_fusion) | copy-start | bytes 1540
  254.7 19.0 %collective-permute-start.5 = (bf16[192,512]{1,0:T(8,128)(2,1)S(1)}, bf16[192,512]{1,0:T(8,128)(2,1)S(1)}, u32[]{:S(2)}, u32[]{:S(2)}) collective-permute-start(bf16[192,512]{1,0:T(8,128)(2,1)S(1)} %pad_maximum_fusion.13), channel_id=1, source_target_pairs={{0,2},{2,0},{4,6},{6,4},{16,18},{18,16},{20,22},{22,20},{1,3},{3,1... | collective-permute-start | bytes 589832 | tf_op jit(solution)/shard_map/ppermute | solution.py:122
  254.9 21.4 %collective-permute-start.6 = (bf16[192,512]{1,0:T(8,128)(2,1)S(1)}, bf16[192,512]{1,0:T(8,128)(2,1)S(1)}, u32[]{:S(2)}, u32[]{:S(2)}) collective-permute-start(bf16[192,512]{1,0:T(8,128)(2,1)S(1)} %pad_maximum_fusion.13), channel_id=1, source_target_pairs={{0,4},{2,6},{4,0},{6,2},{16,20},{18,22},{20,16},{22,18},{1,5},{3,7... | collective-permute-start | bytes 589832 | tf_op jit(solution)/shard_map/ppermute | solution.py:122
  257.9 19.7 %collective-permute-start.7 = (bf16[192,512]{1,0:T(8,128)(2,1)S(1)}, bf16[192,512]{1,0:T(8,128)(2,1)S(1)}, u32[]{:S(2)}, u32[]{:S(2)}) collective-permute-start(bf16[192,512]{1,0:T(8,128)(2,1)S(1)} %pad_maximum_fusion.13), channel_id=1, source_target_pairs={{0,6},{2,4},{4,2},{6,0},{16,22},{18,20},{20,18},{22,16},{1,7},{3,5... | collective-permute-start | bytes 589832 | tf_op jit(solution)/shard_map/ppermute | solution.py:122
  259.2 19.2 %collective-permute-start.8 = (bf16[192,512]{1,0:T(8,128)(2,1)S(1)}, bf16[192,512]{1,0:T(8,128)(2,1)S(1)}, u32[]{:S(2)}, u32[]{:S(2)}) collective-permute-start(bf16[192,512]{1,0:T(8,128)(2,1)S(1)} %pad_maximum_fusion.13), channel_id=1, source_target_pairs={{0,16},{2,18},{4,20},{6,22},{16,0},{18,2},{20,4},{22,6},{1,17},{3,... | collective-permute-start | bytes 589832 | tf_op jit(solution)/shard_map/ppermute | solution.py:122
  260.1 19.0 %collective-permute-start.9 = (bf16[192,512]{1,0:T(8,128)(2,1)S(1)}, bf16[192,512]{1,0:T(8,128)(2,1)S(1)}, u32[]{:S(2)}, u32[]{:S(2)}) collective-permute-start(bf16[192,512]{1,0:T(8,128)(2,1)S(1)} %pad_maximum_fusion.13), channel_id=1, source_target_pairs={{0,18},{2,16},{4,22},{6,20},{16,2},{18,0},{20,6},{22,4},{1,19},{3,... | collective-permute-start | bytes 589832 | tf_op jit(solution)/shard_map/ppermute | solution.py:122
  273.7 6.1 collective-permute-start.10
  276.3 8.7 collective-permute-start.11
  285.7 11.6 collective-permute-start.12
  294.2 87.0 %collective-permute-start.3 = (bf16[640,2048]{1,0:T(8,128)(2,1)}, bf16[640,2048]{1,0:T(8,128)(2,1)}, u32[]{:S(2)}, u32[]{:S(2)}) collective-permute-start(bf16[640,2048]{1,0:T(8,128)(2,1)} %collective-permute-done.1), channel_id=1, source_target_pairs={{0,4},{4,8},{8,12},{12,0},{1,5},{5,9},{9,13},{13,1},{2,6},{6,10},{... | collective-permute-start | bytes 7864328 | tf_op jit(solution)/shard_map/ppermute | solution.py:105
  301.4 99.8 %collective-permute-start.13 = (bf16[2,192,2560]{2,1,0:T(8,128)(2,1)}, bf16[2,192,2560]{2,1,0:T(8,128)(2,1)}, u32[]{:S(2)}, u32[]{:S(2)}) collective-permute-start(bf16[2,192,2560]{2,1,0:T(8,128)(2,1)} %pad_maximum_fusion.7), channel_id=1, source_target_pairs={{0,16},{16,0},{1,17},{17,1},{2,18},{18,2},{3,19},{19,3},{4,20},{20... | collective-permute-start | bytes 5898248 | tf_op jit(solution)/shard_map/ppermute | solution.py:98
  306.0 75.2 %collective-permute-start.4 = (bf16[640,1024]{1,0:T(8,128)(2,1)}, bf16[640,1024]{1,0:T(8,128)(2,1)}, u32[]{:S(2)}, u32[]{:S(2)}) collective-permute-start(bf16[640,1024]{1,0:T(8,128)(2,1)} %collective-permute-done.2), channel_id=1, source_target_pairs={{0,4},{4,8},{8,12},{12,0},{1,5},{5,9},{9,13},{13,1},{2,6},{6,10},{... | collective-permute-start | bytes 3932168 | tf_op jit(solution)/shard_map/ppermute | solution.py:105
  311.4 72.1 %copy-start.2 = (bf16[3072,256]{1,0:T(8,128)(2,1)}, bf16[3072,256]{1,0:T(8,128)(2,1)S(1)}, u32[]{:S(2)}) copy-start(bf16[3072,256]{1,0:T(8,128)(2,1)S(1)} %get-tuple-element.174.key_ref) | copy-start | bytes 4718596
  421.2 191.7 %all-gather.17.cloned.1.call-start = ((), (), s32[]{:S(2)}) async-start(), calls=%async_computation.17 | async-start | bytes 8847360 | tf_op jit(solution)/shard_map/all_gather | solution.py:520
  421.2 98.6 %collective-permute-start.15 = (bf16[2,2,192,2560]{3,2,1,0:T(8,128)(2,1)}, bf16[2,2,192,2560]{3,2,1,0:T(8,128)(2,1)}, u32[]{:S(2)}, u32[]{:S(2)}) collective-permute-start(bf16[2,2,192,2560]{3,2,1,0:T(8,128)(2,1)} %pad_maximum_fusion.3), channel_id=1, source_target_pairs={{0,1},{1,0},{2,3},{3,2},{4,5},{5,4},{6,7},{7,6},{8,9},{9,8},{10,11... | collective-permute-start | bytes 11796488 | tf_op jit(solution)/shard_map/ppermute | solution.py:98
  422.0 91.4 %collective-permute-start.16 = (bf16[640,2048]{1,0:T(8,128)(2,1)}, bf16[640,2048]{1,0:T(8,128)(2,1)}, u32[]{:S(2)}, u32[]{:S(2)}) collective-permute-start(bf16[640,2048]{1,0:T(8,128)(2,1)} %collective-permute-done.3), channel_id=1, source_target_pairs={{0,4},{4,8},{8,12},{12,0},{1,5},{5,9},{9,13},{13,1},{2,6},{6,10},{... | collective-permute-start | bytes 7864328 | tf_op jit(solution)/shard_map/ppermute | solution.py:105
  422.0 88.1 %collective-permute-start.14 = (bf16[640,1024]{1,0:T(8,128)(2,1)}, bf16[640,1024]{1,0:T(8,128)(2,1)S(1)}, u32[]{:S(2)}, u32[]{:S(2)}) collective-permute-start(bf16[640,1024]{1,0:T(8,128)(2,1)} %collective-permute-done.4), channel_id=1, source_target_pairs={{0,4},{4,8},{8,12},{12,0},{1,5},{5,9},{9,13},{13,1},{2,6},{6,10},{... | collective-permute-start | bytes 3932168 | tf_op jit(solution)/shard_map/ppermute | solution.py:105
  559.3 333.0 %reduce-scatter.4.cloned.1.call-start = ((), (), s32[]{:S(2)}) async-start(), calls=%async_computation.18 | async-start | bytes 6553600 | tf_op jit(solution)/shard_map/reduce_scatter | solution.py:518
  612.9 322.9 %reduce-scatter.8.cloned.1.call-start = ((), (), s32[]{:S(2)}) async-start(), calls=%async_computation.20 | async-start | bytes 6553600 | tf_op jit(solution)/shard_map/reduce_scatter | solution.py:518
  634.9 7.1 collective-permute-start.17
  658.1 23.4 %collective-permute-start.18 = (bf16[192,2560]{1,0:T(8,128)(2,1)}, bf16[192,2560]{1,0:T(8,128)(2,1)}, u32[]{:S(2)}, u32[]{:S(2)}) collective-permute-start(bf16[192,2560]{1,0:T(8,128)(2,1)} %get-tuple-element.166), channel_id=1, source_target_pairs={{0,2},{2,0},{16,18},{18,16},{1,3},{3,1},{17,19},{19,17},{4,6},{6,4... | collective-permute-start | bytes 2949128 | tf_op jit(solution)/shard_map/ppermute | solution.py:549
  658.7 23.1 %collective-permute-start.19 = (bf16[192,2560]{1,0:T(8,128)(2,1)}, bf16[192,2560]{1,0:T(8,128)(2,1)}, u32[]{:S(2)}, u32[]{:S(2)}) collective-permute-start(bf16[192,2560]{1,0:T(8,128)(2,1)} %get-tuple-element.164), channel_id=1, source_target_pairs={{0,16},{2,18},{16,0},{18,2},{1,17},{3,19},{17,1},{19,3},{4,20},{6,... | collective-permute-start | bytes 2949128 | tf_op jit(solution)/shard_map/ppermute | solution.py:549
  694.4 299.8 %reduce-scatter.6.cloned.1.call-start = ((), (), s32[]{:S(2)}) async-start(), calls=%async_computation.19 | async-start | bytes 6553600 | tf_op jit(solution)/shard_map/reduce_scatter | solution.py:518
  697.6 22.8 %collective-permute-start.20 = (bf16[192,2560]{1,0:T(8,128)(2,1)S(1)}, bf16[192,2560]{1,0:T(8,128)(2,1)S(1)}, u32[]{:S(2)}, u32[]{:S(2)}) collective-permute-start(bf16[192,2560]{1,0:T(8,128)(2,1)S(1)} %copy-done.56), channel_id=1, source_target_pairs={{0,18},{2,16},{16,2},{18,0},{1,19},{3,17},{17,3},{19,1},{4,22},{6,... | collective-permute-start | bytes 2949128 | tf_op jit(solution)/shard_map/ppermute | solution.py:549
  723.9 54.1 %collective-permute-start.22 = (bf16[192,2560]{1,0:T(8,128)(2,1)S(1)}, bf16[192,2560]{1,0:T(8,128)(2,1)}, u32[]{:S(2)}, u32[]{:S(2)}) collective-permute-start(bf16[192,2560]{1,0:T(8,128)(2,1)S(1)} %copy-done.25), channel_id=1, source_target_pairs={{0,2},{2,0},{1,3},{3,1},{4,6},{6,4},{5,7},{7,5},{8,10},{10,8},{9,1... | collective-permute-start | bytes 2949128 | tf_op jit(solution)/shard_map/ppermute | solution.py:98
  729.9 29.0 %all-to-all-start.2 = ((bf16[8,192,320]{2,1,0:T(8,128)(2,1)}), bf16[8,192,320]{2,1,0:T(8,128)(2,1)}, u32[]{:S(2)}, u32[]{:S(2)}) async-start(bf16[8,192,320]{2,1,0:T(8,128)(2,1)} %bitcast.238), calls=%async_computation.2 | async-start | bytes 2359296 | tf_op jit(solution)/shard_map/all_to_all | solution.py:140
  770.2 77.5 %all-to-all-start.3 = ((bf16[16,160,320]{2,1,0:T(8,128)(2,1)}), bf16[16,160,320]{2,1,0:T(8,128)(2,1)}, u32[]{:S(2)}, u32[]{:S(2)}) async-start(bf16[16,160,320]{2,1,0:T(8,128)(2,1)} %bitcast.267), calls=%async_computation.3 | async-start | bytes 3932160 | tf_op jit(solution)/shard_map/all_to_all | solution.py:140
  781.3 44.4 %collective-permute-start.23 = (bf16[2,192,2560]{2,1,0:T(8,128)(2,1)}, bf16[2,192,2560]{2,1,0:T(8,128)(2,1)}, u32[]{:S(2)}, u32[]{:S(2)}) collective-permute-start(bf16[2,192,2560]{2,1,0:T(8,128)(2,1)} %pad_maximum_fusion.8), channel_id=1, source_target_pairs={{0,16},{16,0},{1,17},{17,1},{2,18},{18,2},{3,19},{19,3},{4,20},{20... | collective-permute-start | bytes 5898248 | tf_op jit(solution)/shard_map/ppermute | solution.py:98
  852.3 12.7 %collective-permute-start.24 = (bf16[8,192,512]{2,1,0:T(8,128)(2,1)}, bf16[8,192,512]{2,1,0:T(8,128)(2,1)}, u32[]{:S(2)}, u32[]{:S(2)}) collective-permute-start(bf16[8,192,512]{2,1,0:T(8,128)(2,1)} %dynamic-slice_bitcast_fusion), channel_id=1, source_target_pairs={{0,1},{1,0},{2,3},{3,2},{4,5},{5,4},{6,7},{7,6},{8,9},{9,8},{10,11... | collective-permute-start | bytes 4718600 | tf_op jit(solution)/shard_map/ppermute | solution.py:90
  852.9 59.5 %collective-permute-start.29 = (bf16[2,2,192,2560]{3,2,1,0:T(8,128)(2,1)}, bf16[2,2,192,2560]{3,2,1,0:T(8,128)(2,1)}, u32[]{:S(2)}, u32[]{:S(2)}) collective-permute-start(bf16[2,2,192,2560]{3,2,1,0:T(8,128)(2,1)} %pad_maximum_fusion.4), channel_id=1, source_target_pairs={{0,1},{1,0},{2,3},{3,2},{4,5},{5,4},{6,7},{7,6},{8,9},{9,8},{10,11... | collective-permute-start | bytes 11796488 | tf_op jit(solution)/shard_map/ppermute | solution.py:90
  864.6 76.2 %collective-permute-start.21 = (bf16[768,2560]{1,0:T(8,128)(2,1)}, bf16[768,2560]{1,0:T(8,128)(2,1)}, u32[]{:S(2)}, u32[]{:S(2)}) collective-permute-start(bf16[768,2560]{1,0:T(8,128)(2,1)} %convolution_convert_fusion.3), channel_id=1, source_target_pairs={{0,1},{1,0},{2,3},{3,2},{4,5},{5,4},{6,7},{7,6},{8,9},{9,8},{10,11... | collective-permute-start | bytes 11796488 | tf_op jit(solution)/shard_map/ppermute | solution.py:90
  868.0 11.8 %collective-permute-start.27 = (bf16[2,192,512]{2,1,0:T(8,128)(2,1)}, bf16[2,192,512]{2,1,0:T(8,128)(2,1)}, u32[]{:S(2)}, u32[]{:S(2)}) collective-permute-start(bf16[2,192,512]{2,1,0:T(8,128)(2,1)} %get-tuple-element.186), channel_id=1, source_target_pairs={{0,18},{2,16},{16,2},{18,0},{1,19},{3,17},{17,3},{19,1},{4,22},{6,... | collective-permute-start | bytes 1179656 | tf_op jit(solution)/shard_map/ppermute | solution.py:134
  868.0 19.3 %collective-permute-start.26 = (bf16[2,192,512]{2,1,0:T(8,128)(2,1)}, bf16[2,192,512]{2,1,0:T(8,128)(2,1)}, u32[]{:S(2)}, u32[]{:S(2)}) collective-permute-start(bf16[2,192,512]{2,1,0:T(8,128)(2,1)} %get-tuple-element.187), channel_id=1, source_target_pairs={{0,16},{2,18},{16,0},{18,2},{1,17},{3,19},{17,1},{19,3},{4,20},{6,... | collective-permute-start | bytes 1179656 | tf_op jit(solution)/shard_map/ppermute | solution.py:134
  869.2 19.5 %collective-permute-start.25 = (bf16[2,192,512]{2,1,0:T(8,128)(2,1)S(1)}, bf16[2,192,512]{2,1,0:T(8,128)(2,1)}, u32[]{:S(2)}, u32[]{:S(2)}) collective-permute-start(bf16[2,192,512]{2,1,0:T(8,128)(2,1)S(1)} %get-tuple-element.185), channel_id=1, source_target_pairs={{0,2},{2,0},{16,18},{18,16},{1,3},{3,1},{17,19},{19,17},{4,6},{6,4... | collective-permute-start | bytes 1179656 | tf_op jit(solution)/shard_map/ppermute | solution.py:134
  891.0 12.7 %collective-permute-start.28 = (bf16[192,512]{1,0:T(8,128)(2,1)}, bf16[192,512]{1,0:T(8,128)(2,1)}, u32[]{:S(2)}, u32[]{:S(2)}) collective-permute-start(bf16[192,512]{1,0:T(8,128)(2,1)} %dynamic-slice_bitcast_fusion.10), channel_id=1, source_target_pairs={{0,4},{4,0},{1,5},{5,1},{2,6},{6,2},{3,7},{7,3},{8,12},{12,8},{9,1... | collective-permute-start | bytes 589832 | tf_op jit(solution)/shard_map/ppermute | solution.py:90
  892.3 20.1 %all-to-all-start.4 = ((bf16[4,160,1024]{2,1,0:T(8,128)(2,1)}), bf16[4,160,1024]{2,1,0:T(8,128)(2,1)S(1)}, u32[]{:S(2)}, u32[]{:S(2)}) async-start(bf16[4,160,1024]{2,1,0:T(8,128)(2,1)} %bitcast.295), calls=%async_computation.5 | async-start | bytes 2621440 | tf_op jit(solution)/shard_map/all_to_all | solution.py:140
  914.9 20.9 %all-to-all-start.5 = ((bf16[8,192,384]{2,1,0:T(8,128)(2,1)}), bf16[8,192,384]{2,1,0:T(8,128)(2,1)}, u32[]{:S(2)}, u32[]{:S(2)}) async-start(bf16[8,192,384]{2,1,0:T(8,128)(2,1)} %bitcast.284), calls=%async_computation.6 | async-start | bytes 2359296 | tf_op jit(solution)/shard_map/all_to_all | solution.py:140
  922.7 34.3 %collective-permute-start.37 = (bf16[4,160,320]{2,1,0:T(8,128)(2,1)S(1)}, bf16[4,160,320]{2,1,0:T(8,128)(2,1)}, u32[]{:S(2)}, u32[]{:S(2)}) collective-permute-start(bf16[4,160,320]{2,1,0:T(8,128)(2,1)S(1)} %copy-done.46), channel_id=1, source_target_pairs={{0,16},{16,0},{1,17},{17,1},{2,18},{18,2},{3,19},{19,3},{4,20},{20... | collective-permute-start | bytes 1228808 | tf_op jit(solution)/shard_map/ppermute | solution.py:98
  923.9 50.5 %collective-permute-start.33 = (bf16[4,160,1024]{2,1,0:T(8,128)(2,1)S(1)}, bf16[4,160,1024]{2,1,0:T(8,128)(2,1)}, u32[]{:S(2)}, u32[]{:S(2)}) collective-permute-start(bf16[4,160,1024]{2,1,0:T(8,128)(2,1)S(1)} %all-to-all-done.4.refs_1_), channel_id=1, source_target_pairs={{0,16},{16,0},{1,17},{17,1},{2,18},{18,2},{3,19},{19,3},{4,20},{20... | collective-permute-start | bytes 3932168 | tf_op jit(solution)/shard_map/ppermute | solution.py:90
  935.8 20.5 %all-to-all-start.6 = ((bf16[4,160,1024]{2,1,0:T(8,128)(2,1)}), bf16[4,160,1024]{2,1,0:T(8,128)(2,1)S(1)}, u32[]{:S(2)}, u32[]{:S(2)}) async-start(bf16[4,160,1024]{2,1,0:T(8,128)(2,1)} %bitcast.297), calls=%async_computation.9 | async-start | bytes 2621440 | tf_op jit(solution)/shard_map/all_to_all | solution.py:140
  956.4 58.3 %collective-permute-start.34 = (bf16[4,160,1024]{2,1,0:T(8,128)(2,1)S(1)}, bf16[4,160,1024]{2,1,0:T(8,128)(2,1)}, u32[]{:S(2)}, u32[]{:S(2)}) collective-permute-start(bf16[4,160,1024]{2,1,0:T(8,128)(2,1)S(1)} %all-to-all-done.6.refs_1_), channel_id=1, source_target_pairs={{0,16},{16,0},{1,17},{17,1},{2,18},{18,2},{3,19},{19,3},{4,20},{20... | collective-permute-start | bytes 3932168 | tf_op jit(solution)/shard_map/ppermute | solution.py:90
  994.2 20.4 %all-to-all-start.7 = ((bf16[4,160,1024]{2,1,0:T(8,128)(2,1)}), bf16[4,160,1024]{2,1,0:T(8,128)(2,1)S(1)}, u32[]{:S(2)}, u32[]{:S(2)}) async-start(bf16[4,160,1024]{2,1,0:T(8,128)(2,1)} %bitcast.296), calls=%async_computation.10 | async-start | bytes 2621440 | tf_op jit(solution)/shard_map/all_to_all | solution.py:140
  1014.6 123.4 %all-to-all-start.8 = ((bf16[16,160,384]{2,1,0:T(8,128)(2,1)}), bf16[16,160,384]{2,1,0:T(8,128)(2,1)}, u32[]{:S(2)}, u32[]{:S(2)}) async-start(bf16[16,160,384]{2,1,0:T(8,128)(2,1)} %bitcast.292), calls=%async_computation.11 | async-start | bytes 3932160 | tf_op jit(solution)/shard_map/all_to_all | solution.py:140
  1037.3 34.3 %collective-permute-start.32 = (bf16[192,2560]{1,0:T(8,128)(2,1)}, bf16[192,2560]{1,0:T(8,128)(2,1)}, u32[]{:S(2)}, u32[]{:S(2)}) collective-permute-start(bf16[192,2560]{1,0:T(8,128)(2,1)} %get-tuple-element.160), channel_id=1, source_target_pairs={{0,18},{2,16},{16,2},{18,0},{1,19},{3,17},{17,3},{19,1},{4,22},{6,... | collective-permute-start | bytes 2949128 | tf_op jit(solution)/shard_map/ppermute | solution.py:134
  1037.3 53.6 %collective-permute-start.31 = (bf16[192,2560]{1,0:T(8,128)(2,1)}, bf16[192,2560]{1,0:T(8,128)(2,1)}, u32[]{:S(2)}, u32[]{:S(2)}) collective-permute-start(bf16[192,2560]{1,0:T(8,128)(2,1)} %get-tuple-element.161), channel_id=1, source_target_pairs={{0,16},{2,18},{16,0},{18,2},{1,17},{3,19},{17,1},{19,3},{4,20},{6,... | collective-permute-start | bytes 2949128 | tf_op jit(solution)/shard_map/ppermute | solution.py:134
  1038.7 55.0 %collective-permute-start.30 = (bf16[192,2560]{1,0:T(8,128)(2,1)}, bf16[192,2560]{1,0:T(8,128)(2,1)}, u32[]{:S(2)}, u32[]{:S(2)}) collective-permute-start(bf16[192,2560]{1,0:T(8,128)(2,1)} %get-tuple-element.159), channel_id=1, source_target_pairs={{0,2},{2,0},{16,18},{18,16},{1,3},{3,1},{17,19},{19,17},{4,6},{6,4... | collective-permute-start | bytes 2949128 | tf_op jit(solution)/shard_map/ppermute | solution.py:134
  1050.3 69.0 %collective-permute-start.35 = (bf16[4,160,1024]{2,1,0:T(8,128)(2,1)S(1)}, bf16[4,160,1024]{2,1,0:T(8,128)(2,1)}, u32[]{:S(2)}, u32[]{:S(2)}) collective-permute-start(bf16[4,160,1024]{2,1,0:T(8,128)(2,1)S(1)} %all-to-all-done.7.refs_1_), channel_id=1, source_target_pairs={{0,16},{16,0},{1,17},{17,1},{2,18},{18,2},{3,19},{19,3},{4,20},{20... | collective-permute-start | bytes 3932168 | tf_op jit(solution)/shard_map/ppermute | solution.py:90
  1055.3 38.4 %copy-start.59 = (f32[192]{0:T(256)S(1)}, f32[192]{0:T(256)}, u32[]{:S(2)}) copy-start(f32[192]{0:T(256)} %copy-done.58) | copy-start | bytes 2308
  1055.3 38.4 %copy-start.67 = (f32[192]{0:T(256)S(1)}, f32[192]{0:T(256)}, u32[]{:S(2)}) copy-start(f32[192]{0:T(256)} %get-tuple-element.204) | copy-start | bytes 2308
  1140.0 12.1 %collective-permute-start.36 = (bf16[4,160,384]{2,1,0:T(8,128)(2,1)S(1)}, bf16[4,160,384]{2,1,0:T(8,128)(2,1)S(1)}, u32[]{:S(2)}, u32[]{:S(2)}) collective-permute-start(bf16[4,160,384]{2,1,0:T(8,128)(2,1)S(1)} %reduce_sum.124), channel_id=1, source_target_pairs={{0,16},{16,0},{1,17},{17,1},{2,18},{18,2},{3,19},{19,3},{4,20},{20... | collective-permute-start | bytes 1474568 | tf_op jit(solution)/shard_map/ppermute | solution.py:98
  (69 other events, 334.1 us)
Sparse Core Ops, SparseCore 0:
  13.6 43.1 all-gather.6
  58.9 37.2 all-gather.10
  98.1 134.4 all-gather.8
  234.3 105.4 all-gather.12
  421.3 52.8 all-gather.14
  559.4 53.4 all-gather.16
  615.8 93.7 reduce-scatter.3
  712.4 127.5 reduce-scatter.7
  842.3 95.5 reduce-scatter.5

commit v6 on v5

--- a/solution.py
+++ b/solution.py
@@ -449,12 +449,10 @@
 
     gate_up_blocks = [to_members(gate_up_chunks)]
     qkv_rows = lax.all_gather(own_half(low(qkv_low * gain_one)), PLANES, axis=0, tiled=True)
-    qkv_halves = gathered_group(after(qkv_rows, gate_up_chunks))
+    qkv_halves = gathered_group(after(qkv_rows, gate_up_blocks[0]))
     gate_up_blocks.append(next_plane(after(gate_up_blocks[0], qkv_rows)))
     down_blocks = [to_members(down_chunks)]
     down_blocks.append(next_plane(down_blocks[0]))
-    out_rows = own_half(after(low(weight_out), qkv_halves))
-    out_halves = gathered_group(lax.all_gather(out_rows, PLANES, axis=0, tiled=True))
     incoming_columns = doubled(incoming, "k", 1, 0)
 
     tokens = wide(hidden_in.reshape(tok_rows, width))
@@ -477,6 +475,8 @@
     normed_one = after(normed_one, incoming_columns, gate_up_blocks[1], down_blocks[1])
     rows = regrouped(normed_one, planes, members)
     projected = jnp.concatenate([dot(rows, half, (1, 0)) for half in qkv_halves], axis=1)
+    out_rows = own_half(low(after(weight_out, projected)))
+    out_halves = gathered_group(lax.all_gather(out_rows, PLANES, axis=0, tiled=True))
     key_pre = projected[:, width : width + HEAD_DIM]
     value_low = low(projected[:, width + HEAD_DIM :])
     key_low = low(rotate(key_pre, cosine, sine))
@@ -517,9 +517,9 @@
     def to_owners(term):
         return lax.psum_scatter(term, PLANES, scatter_dimension=0, tiled=True)
 
-    attn_all = lax.all_gather(after(attn_low, gate_up), GROUP, axis=0, tiled=True)
-    down_term = after(low(dot(incoming_all, activated_low, (0, 0))), attn_all)
+    down_term = low(dot(incoming_all, activated_low, (0, 0)))
     down_rows = to_owners(down_term)
+    attn_all = lax.all_gather(after(attn_low, down_term), GROUP, axis=0, tiled=True)
     grad_gate, grad_up = glu_back(wide(after(grad_act, down_term)))
     grad_gate_up = low(jnp.concatenate([grad_gate, grad_up], axis=1))
 
@@ -563,20 +563,19 @@
 
     shares = sides * members
 
-    def by_column(terms):
-        terms = terms.reshape(tok_rows, shares, terms.shape[1] // shares).transpose(1, 0, 2)
-        return exchanged(terms, GROUP).reshape(shares * tok_rows, -1)
+    def by_column(*terms):
+        terms = [term.reshape(tok_rows, shares, term.shape[1] // shares) for term in terms]
+        terms = jnp.concatenate(terms, axis=2).transpose(1, 0, 2)
+        return exchanged(terms, GROUP)
 
     def to_rows(total):
         total = exchanged(total.reshape(owner_count, own_rows, -1), OWNERS)
         return low(jnp.sum(wide(total.reshape(planes, members, own_rows, -1)), axis=0))
 
     def joined(total):
-        total = doubled(total, "seq", 1, 0).reshape(shares, own_rows, -1)
         return wide(total.transpose(1, 0, 2).reshape(own_rows, -1))
 
     grad_branch_low = low(grad_middle)
-    out_columns = by_column(grad_branch_low)
     half = width // sides
     grad_mixed = sum(
         dot(grad_branch_low[:, index * half : (index + 1) * half], out_halves[index], (1, 1))
@@ -590,15 +589,24 @@
     )
     normed_one_columns = doubled(after(normed_one, grad_normed_two), "k", 1, 0)
     normed_one_sides = doubled(normed_one_columns, "seq", 1, 0)
-    branch_terms = group_terms(after(activated_low, grad_window), down_own)
-    down_pieces = in_plane(down_rows, grad_window)
-    out_total = to_rows(low(dot(attn_all, out_columns, (0, 0))))
-    grad_window = after(low(grad_window), normed_one_sides, out_total)
+    down_pieces = in_plane(down_rows)
+    grad_window = after(low(grad_window), normed_one_sides, down_pieces[0])
+    branch = low(dot(after(activated_low, grad_window), down_own, (1, 1)))
     normed_one_others = swapped(normed_one_sides, "c")
     grad_window = half_sum(grad_window.reshape(-1, 2, tok_rows, 2 * HEAD_DIM), "c", 1)
     grad_window = grad_window.reshape(sides, -1, columns, tok_rows, 2 * HEAD_DIM)
     grad_window = grad_window.swapaxes(1, 2).reshape(sides * columns, -1, tok_rows, 2 * HEAD_DIM)
     grad_local = wide(half_sum(low(ring_sum(grad_window)), "h", 0))
+
+    mlp_states = (mlp_planes, first_mlp.transpose(1, 0, 2), second_mlp.transpose(1, 0, 2))
+    rate_main = 2.0 * D ** (-0.5)
+
+    def mlp_updated(part, pieces, outs):
+        *outs, gain_dot = mlp_adam(part, side, pieces, mlp_states, gain_two, rate_main, outs)
+        return outs, gain_dot
+
+    mlp_outs, down_dot = mlp_updated(2, down_pieces, ())
+    grad_local = after(grad_local, down_dot)
     grad_query = grad_query.reshape(tok_rows, head_count, HEAD_DIM)
     grad_query_pre = rotate(
         grad_query * query_scale, cosine[:, None, :], -sine[:, None, :]
@@ -608,36 +616,32 @@
         jnp.concatenate([grad_query_pre, grad_key_pre, grad_local[:, HEAD_DIM:]], axis=1)
     )
 
-    mlp_states = (mlp_planes, first_mlp.transpose(1, 0, 2), second_mlp.transpose(1, 0, 2))
-    rate_main = 2.0 * D ** (-0.5)
-
-    def mlp_updated(part, pieces, outs):
-        *outs, gain_dot = mlp_adam(part, side, pieces, mlp_states, gain_two, rate_main, outs)
-        return outs, gain_dot
-
-    qkv_columns = by_column(after(grad_proj, down_pieces[0], normed_one_others))
-    mlp_outs, _ = mlp_updated(2, down_pieces, ())
-    by_core = after(qkv_columns, *mlp_outs).reshape(sides * columns, 2, tok_rows, -1)
+    all_columns = by_column(after(grad_proj, normed_one_others), grad_branch_low)
+    qkv_share = grad_proj.shape[1] // shares
+    by_core = all_columns.reshape(sides * columns, 2, tok_rows, -1)[:, :, :, :qkv_share]
 
     def one_core_total(rows, which):
         columns_there = lax.dynamic_index_in_dim(by_core, which, 1, keepdims=False)
-        return dot(rows.reshape(-1, width), columns_there.reshape(-1, by_core.shape[3]), (0, 0))
+        return dot(rows.reshape(-1, width), columns_there.reshape(-1, qkv_share), (0, 0))
 
     qkv_total = one_core_total(normed_one_sides, core)
     qkv_total = low(qkv_total + one_core_total(normed_one_others, 1 - core))
-    branch = ring_sum(after(branch_terms, qkv_columns))
-    gate_pieces = in_plane(gate_rows, qkv_columns)
+    out_columns = all_columns.reshape(shares * tok_rows, -1)[:, qkv_share:]
+    out_total = low(dot(attn_all, out_columns, (0, 0)))
+    gate_pieces = in_plane(gate_rows, all_columns)
     up_pieces = in_plane(up_rows, gate_pieces[0])
-    qkv_total = to_rows(after(qkv_total, up_pieces[0], gate_pieces[1]))
-    gate_pieces = lax.optimization_barrier((*gate_pieces, branch))[:2]
+    total = jnp.concatenate([qkv_total, out_total], axis=1)
+    total = to_rows(after(total, up_pieces[0]))
+    branch = lax.psum_scatter(
+        after(branch, all_columns), GROUP, scatter_dimension=0, tiled=True
+    )
     mlp_outs, gate_dot = mlp_updated(0, gate_pieces, mlp_outs)
     (grad_mlp, second_new_mlp, new_mlp), up_dot = mlp_updated(1, up_pieces, mlp_outs)
     grad_gain_two = gate_dot + up_dot
-    qkv_total = after(qkv_total, up_dot)
-    grad_out = joined(out_total)
-
-    grad_qkv = joined(qkv_total)
-    hidden_out = low(middle + branch).reshape(1, 1, tok_rows, width)
+    total = doubled(total, "seq", 1, 0).reshape(shares, own_rows, -1)
+    grad_qkv = joined(total[:, :, :qkv_share])
+    grad_out = joined(total[:, :, qkv_share:])
+    hidden_out = low(middle + wide(branch)).reshape(1, 1, tok_rows, width)
 
     half = grad_proj.shape[1] // sides
     grad_normed = sum(

time: 1180 us -> 1120 us (0.949)
  waiting for transfers between devices: 550 us -> 473 us
  blocking collectives: 0 us -> 33.5 us
    all_to_all x9 -> x6, waiting for transfers between devices: 156 us -> 66.7 us  [exchanged(): return lax.all_to_all(value, axes, split_axis=0, concat_axis=0, tiled=True)]
    all_to_all x0 -> x1, blocking collectives: none -> 33.5 us  [exchanged(): return lax.all_to_all(value, axes, split_axis=0, concat_axis=0, tiled=True)]
    all_gather x1, waiting for transfers between devices: 33.5 us -> 2.47 us  [on_device(): lax.all_gather(own_half(low(qkv_low * gain_one)), PLANES, axis=0, tiled=T...]
    ppermute x8 -> x7, waiting for transfers between devices: 7.89 us -> 35.3 us  [doubled(): other = lax.ppermute(value, axis, traded((axis,), step))]
    ppermute x8 -> x7, waiting for transfers between devices: 27.6 us -> 54.1 us  [swapped(): return lax.ppermute(value, axis, [(0, 1), (1, 0)])]
    all_gather x1, waiting for transfers between devices: 25.4 us -> 0.01 us  [on_device(): lax.all_gather(after(attn_low, down_term), GROUP, axis=0, tiled=True)]
    reduce_scatter x3, waiting for transfers between devices: 0.01 us -> 25.4 us  [to_owners(): return lax.psum_scatter(term, PLANES, scatter_dimension=0, tiled=True)]
    ppermute x6 -> x3, waiting for transfers between devices: 49.9 us -> 25.4 us  [ring_sum(): term = lax.ppermute(term, CHIPS, traded(CHIPS, step))]
  transfers between devices with their start and end apart: 56 -> 49, of which waited for: 30 -> 25; matrix products, arithmetic and copies ran while one was open for 29% -> 28% of each run, Pallas kernels for 9% -> 10%
where the time goes in v6:
time: 1120 us; the launch traced here: 1110 us
  waiting for transfers between devices  473 us (42%)
  matrix products  171 us (15%)
  other arithmetic  114 us (10%)
  local copies, waits for them, and re-layouts  111 us (10%)
  Pallas kernels  109 us (10%)
  starting transfers between devices  83.6 us (7%)
  blocking collectives  33.5 us (3%)
  between operations  15.9 us (1%)
    dot_general x19, matrix products, dot(): lax.dot_general(left, right, ((contract[:1], contract[1:]), ((), ())), pr...  171 us
    ppermute x6, waiting for transfers between devices, next_plane(): lax.ppermute(block, PLANES, [(one, (one + 1) % count) for one in range(co...  161 us
    all_to_all x6, waiting for transfers between devices, exchanged(): return lax.all_to_all(value, axes, split_axis=0, concat_axis=0, tiled=True)  66.7 us
    pallas_call x3, Pallas kernels, mlp_adam(): pl.pallas_call(lambda *refs: mlp_adam_kernel(rate, per_side, part < 2, *r...  55.3 us
    ppermute x7, waiting for transfers between devices, swapped(): return lax.ppermute(value, axis, [(0, 1), (1, 0)])  54.1 us
    all_gather x1, waiting for transfers between devices, on_device(): lax.all_gather(out_rows, PLANES, axis=0, tiled=True)  37.2 us
    all_to_all x6, starting transfers between devices, exchanged(): return lax.all_to_all(value, axes, split_axis=0, concat_axis=0, tiled=True)  35.6 us
    ppermute x7, waiting for transfers between devices, doubled(): other = lax.ppermute(value, axis, traded((axis,), step))  35.3 us
  transfers between devices with their start and end apart: 49, of which 25 were waited for; matrix products, arithmetic and copies ran while one was open for 28% of the time, Pallas kernels for 10%

profile of v6, /device:TPU:13, one launch (start us, length us, event | category | flops | bytes accessed | tf_op | source)
XLA Modules:
  0.0 1112.8 jit_solution(12691021537036758725)
XLA Ops:
  11.0 7.2 mlp_chunks.1
  18.1 33.5 %all_to_all.35 = bf16[4,160,2048]{2,1,0:T(8,128)(2,1)} all-to-all(bf16[4,160,2048]{2,1,0:T(8,128)(2,1)S(1)} %get-tuple-element.54), channel_id=1, replica_groups=mesh['seq'=2,'g'=2,'h'=2,'k'=2,'c'=2] {'k','c'}, dimensions={0} | all-to-all | bytes 5242880 | tf_op jit(solution)/shard_map/all_to_all | solution.py:140
  54.2 4.7 all-to-all-start.1
  61.2 19.5 %all-to-all-done.1 = bf16[4,160,1024]{2,1,0:T(8,128)(2,1)S(1)} async-done(((bf16[4,160,1024]{2,1,0:T(8,128)(2,1)}), bf16[4,160,1024]{2,1,0:T(8,128)(2,1)S(1)}, u32[]{:S(2)}, u32[]{:S(2)}) %all-to-all-start.1) | async-done | bytes 1310752 | tf_op jit(solution)/shard_map/all_to_all | solution.py:140
  82.4 34.1 %collective-permute-done = bf16[192,2560]{1,0:T(8,128)(2,1)} collective-permute-done((bf16[192,2560]{1,0:T(8,128)(2,1)}, bf16[192,2560]{1,0:T(8,128)(2,1)}, u32[]{:S(2)}, u32[]{:S(2)}) %collective-permute-start) | collective-permute-done | bytes 983072 | tf_op jit(solution)/shard_map/ppermute | solution.py:98
  120.2 25.4 %collective-permute-done.2 = bf16[640,1024]{1,0:T(8,128)(2,1)} collective-permute-done((bf16[640,1024]{1,0:T(8,128)(2,1)S(1)}, bf16[640,1024]{1,0:T(8,128)(2,1)}, u32[]{:S(2)}, u32[]{:S(2)}) %collective-permute-start.2) | collective-permute-done | bytes 1310752 | tf_op jit(solution)/shard_map/ppermute | solution.py:105
  146.3 16.5 %all-gather.9.cloned.1.call-done = bf16[5120,1536]{1,0:T(8,128)(2,1)} async-done(((bf16[640,1536]{1,0:T(8,128)(2,1)}), bf16[5120,1536]{1,0:T(8,128)(2,1)}) %all-gather.9.cloned.1.call-update) | async-done | bytes 15728656 | tf_op jit(solution)/shard_map/all_gather | solution.py:447
  162.8 4.9 fusion.2
  167.7 6.0 fusion.6
  175.7 37.2 %all-gather.11.cloned.1.call-done = bf16[640,1280]{1,0:T(8,128)(2,1)} async-done(((bf16[160,1280]{1,0:T(8,128)(2,1)}), bf16[640,1280]{1,0:T(8,128)(2,1)}) %all-gather.11.cloned.1.call-update) | async-done | bytes 1638416 | tf_op jit(solution)/shard_map/all_gather | solution.py:479
  222.0 8.9 collective-permute-done.6
  231.8 8.6 collective-permute-done.8
  268.0 64.1 %collective-permute-done.4 = bf16[640,1024]{1,0:T(8,128)(2,1)} collective-permute-done((bf16[640,1024]{1,0:T(8,128)(2,1)}, bf16[640,1024]{1,0:T(8,128)(2,1)}, u32[]{:S(2)}, u32[]{:S(2)}) %collective-permute-start.4) | collective-permute-done | bytes 1310752 | tf_op jit(solution)/shard_map/ppermute | solution.py:105
  335.7 16.5 %attend.1 = (bf16[192,2560]{1,0:T(8,128)(2,1)}, f32[5,1,384]{2,1,0:T(1,128)S(1)}) custom-call(bf16[192,2560]{1,0:T(8,128)(2,1)S(1)} %copy-done.5, bf16[3072,256]{1,0:T(8,128)(2,1)S(1)} %get-tuple-element.169.key_ref, bf16[256,3072]{1,0:T(8,128)(2,1)S(1)} %copy.196.value_t_ref, f32[3072,384]{1,0:T(8,128)} %pad_maximum_fusion.2.bias_ref), custom_call_target="tpu_custom_call" | custom-call | flops 6039797760 | bytes 18087936 | tf_op jit(solution)/shard_map/attend/pallas_call | solution.py:305
  359.8 4.8 fusion.18
  364.7 4.7 fusion.22
  374.6 5.4 broadcast_in_dim.87
  388.6 71.2 %collective-permute-done.14 = bf16[640,1024]{1,0:T(8,128)(2,1)S(1)} collective-permute-done((bf16[640,1024]{1,0:T(8,128)(2,1)}, bf16[640,1024]{1,0:T(8,128)(2,1)S(1)}, u32[]{:S(2)}, u32[]{:S(2)}) %collective-permute-start.14) | collective-permute-done | bytes 1310752 | tf_op jit(solution)/shard_map/ppermute | solution.py:105
  460.0 5.5 constant_dynamic-update-slice_fusion.1
  473.3 6.1 pad_maximum_fusion
  479.4 7.1 copy.199
  486.6 11.9 %convolution_convert_fusion.6 = bf16[1536,1024]{1,0:T(8,128)(2,1)} fusion(bf16[1536,2560]{1,0:T(8,128)(2,1)} %bitcast.237, bf16[2560,1024]{1,0:T(8,128)(2,1)S(1)} %bitcast.247), kind=kOutput, calls=%fused_computation.54 | convolution fusion | flops 8054636544 | bytes 16252928 | tf_op jit(solution)/shard_map/dot_general | solution.py:79
  498.4 20.6 %fusion.94 = f32[1536,2048]{1,0:T(8,128)S(1)} fusion(bf16[1536,2560]{1,0:T(8,128)(2,1)} %all-gather.15.cloned.1.call-done, bf16[2560,2048]{1,0:T(8,128)(2,1)} %constant_dynamic-update-slice_fusion), kind=kOutput, calls=%fused_computation.220 | convolution fusion | flops 16106127360 | bytes 30932992 | tf_op jit(solution)/shard_map/dot_general | solution.py:79
  519.1 4.8 copy-done.11
  527.7 10.3 convolution_convert_fusion.3
  538.1 8.8 fusion.8
  550.4 9.8 convolution_convert_fusion.4
  561.1 6.8 collective-permute-done.17
  567.9 12.7 %add_convert_fusion = bf16[768,2560]{1,0:T(8,128)(2,1)S(1)} fusion(bf16[768,2560]{1,0:T(8,128)(2,1)} %collective-permute-done.17, bf16[768,2048]{1,0:T(8,128)(2,1)} %bitcast.260, bf16[2560,2048]{1,0:T(8,128)(2,1)} %constant_dynamic-update-slice_fusion), kind=kOutput, calls=%fused_computation.4 | convolution fusion | flops 8058961920 | bytes 21495808 | tf_op jit(solution)/shard_map/dot_general | solution.py:79
  584.0 4.7 collective-permute-start.19
  589.4 21.4 %collective-permute-done.19 = bf16[192,2560]{1,0:T(8,128)(2,1)} collective-permute-done((bf16[192,2560]{1,0:T(8,128)(2,1)}, bf16[192,2560]{1,0:T(8,128)(2,1)}, u32[]{:S(2)}, u32[]{:S(2)}) %collective-permute-start.19) | collective-permute-done | bytes 983072 | tf_op jit(solution)/shard_map/ppermute | solution.py:549
  611.7 12.4 %convolution_convert_fusion.2 = bf16[2560,1024]{1,0:T(8,128)(2,1)} fusion(bf16[1536,2560]{1,0:T(8,128)(2,1)} %all-gather.15.cloned.1.call-done, bf16[1536,2048]{1,0:T(8,128)(2,1)S(1)} %pad_maximum_fusion.1), kind=kOutput, calls=%fused_computation.39 | convolution fusion | flops 8055685120 | bytes 16252928 | tf_op jit(solution)/shard_map/dot_general | solution.py:79
  627.4 13.9 %convolution_convert_fusion.1 = bf16[2560,1024]{1,0:T(8,128)(2,1)} fusion(bf16[1536,2560]{1,0:T(8,128)(2,1)} %all-gather.15.cloned.1.call-done, bf16[1536,2048]{1,0:T(8,128)(2,1)} %copy-done.32), kind=kOutput, calls=%fused_computation.38 | convolution fusion | flops 8055685120 | bytes 16252928 | tf_op jit(solution)/shard_map/dot_general | solution.py:79
  641.4 8.4 collective-permute-done.20
  657.1 5.5 fusion.16
  662.5 6.2 fusion.31
  687.0 30.4 %attend_back.1 = (f32[192,2560]{1,0:T(8,128)}, f32[3072,512]{1,0:T(8,128)}) custom-call(bf16[192,2560]{1,0:T(8,128)(2,1)S(1)} %copy-done.6, bf16[192,2560]{1,0:T(8,128)(2,1)S(1)} %copy.205.grad_ref, bf16[3072,256]{1,0:T(8,128)(2,1)S(1)} %copy-done.3, bf16[256,3072]{1,0:T(8,128)(2,1)S(1)} %copy-done.4, bf16[3072,256]{1,0:T(8,128)(2,1)} %get-tuple-element.166.value_ref, ...), custom_call_target="tpu_custom_call" | custom-call | flops 15099494400 | bytes 22806528 | tf_op jit(solution)/shard_map/attend_back/pallas_call | solution.py:364
  717.3 4.8 convert_element_type.235
  722.2 7.1 all-to-all-start.2
  733.4 11.3 %all-to-all-done.2.refs_1_ = bf16[4,160,1024]{2,1,0:T(8,128)(2,1)S(1)} async-done(((bf16[4,160,1024]{2,1,0:T(8,128)(2,1)}), bf16[4,160,1024]{2,1,0:T(8,128)(2,1)S(1)}, u32[]{:S(2)}, u32[]{:S(2)}) %all-to-all-start.2) | async-done | bytes 1310752 | tf_op jit(solution)/shard_map/all_to_all | solution.py:140
  748.8 4.7 collective-permute-done.23
  761.4 20.1 %collective-permute-done.24 = bf16[2,192,512]{2,1,0:T(8,128)(2,1)} collective-permute-done((bf16[2,192,512]{2,1,0:T(8,128)(2,1)}, bf16[2,192,512]{2,1,0:T(8,128)(2,1)}, u32[]{:S(2)}, u32[]{:S(2)}) %collective-permute-start.24) | collective-permute-done | bytes 393248 | tf_op jit(solution)/shard_map/ppermute | solution.py:134
  781.5 5.3 collective-permute-done.25
  789.2 13.7 %collective-permute-start.27 = (bf16[192,512]{1,0:T(8,128)(2,1)}, bf16[192,512]{1,0:T(8,128)(2,1)}, u32[]{:S(2)}, u32[]{:S(2)}) collective-permute-start(bf16[192,512]{1,0:T(8,128)(2,1)} %dynamic-slice_bitcast_fusion.7), channel_id=1, source_target_pairs={{0,4},{4,0},{1,5},{5,1},{2,6},{6,2},{3,7},{7,3},{8,12},{12,8},{9,1... | collective-permute-start | bytes 589832 | tf_op jit(solution)/shard_map/ppermute | solution.py:90
  818.8 7.6 all-to-all-start.3
  826.4 13.5 %convolution_convert_fusion = bf16[1536,2560]{1,0:T(8,128)(2,1)} fusion(bf16[1536,1024]{1,0:T(8,128)(2,1)} %copy-done.44, bf16[2560,1024]{1,0:T(8,128)(2,1)} %copy-done.37), kind=kOutput, calls=%fused_computation | convolution fusion | flops 8056995840 | bytes 16252928 | tf_op jit(solution)/shard_map/dot_general | solution.py:79
  839.8 14.0 %all-to-all-done.3 = bf16[8,192,704]{2,1,0:T(8,128)(2,1)} async-done(((bf16[8,192,704]{2,1,0:T(8,128)(2,1)}), bf16[8,192,704]{2,1,0:T(8,128)(2,1)}, u32[]{:S(2)}, u32[]{:S(2)}) %all-to-all-start.3) | async-done | bytes 2162720 | tf_op jit(solution)/shard_map/all_to_all | solution.py:140
  860.8 6.0 fusion.95
  866.8 7.5 convolution_convert_fusion.5
  874.3 25.4 %reduce-scatter.9.cloned.1.call-done = bf16[640,1024]{1,0:T(8,128)(2,1)} async-done(((bf16[2560,1024]{1,0:T(8,128)(2,1)}), bf16[640,1024]{1,0:T(8,128)(2,1)}) %reduce-scatter.9.cloned.1.call-update) | async-done | bytes 1310736 | tf_op jit(solution)/shard_map/reduce_scatter | solution.py:518
  899.7 5.1 all-to-all-start.5
  904.8 5.1 fusion.24
  912.0 8.3 all-to-all-done.5.refs_1_
  920.3 6.1 copy.220
  926.4 6.5 all-to-all-start.6
  936.9 42.7 %collective-permute-done.32.refs_2_ = bf16[4,160,1024]{2,1,0:T(8,128)(2,1)} collective-permute-done((bf16[4,160,1024]{2,1,0:T(8,128)(2,1)S(1)}, bf16[4,160,1024]{2,1,0:T(8,128)(2,1)}, u32[]{:S(2)}, u32[]{:S(2)}) %collective-permute-start.32) | collective-permute-done | bytes 1310752 | tf_op jit(solution)/shard_map/ppermute | solution.py:90
  979.6 17.8 %mlp_adam.3 = (f32[3,160,7680]{2,1,0:T(8,128)}, f32[3,160,7680]{2,1,0:T(8,128)}, f32[3,160,7680]{2,1,0:T(8,128)}, f32[160,1]{1,0:T(8,128)}) custom-call(s32[1]{0:T(128)} %bitcast.4.refs_0_, bf16[4,160,1024]{2,1,0:T(8,128)(2,1)S(1)} %all-to-all-done.2.refs_1_, bf16[4,160,1024]{2,1,0:T(8,128)(2,1)} %collective-permute-done.32.refs_2_, ...), custom_call_target="tpu_custom_call" | custom-call | flops 24576000 | bytes 31948800 | tf_op jit(solution)/shard_map/mlp_adam/pallas_call | solution.py:238
  998.9 7.4 fusion
  1006.3 13.7 %all-to-all-done.6 = bf16[16,160,704]{2,1,0:T(8,128)(2,1)} async-done(((bf16[16,160,704]{2,1,0:T(8,128)(2,1)}), bf16[16,160,704]{2,1,0:T(8,128)(2,1)}, u32[]{:S(2)}, u32[]{:S(2)}) %all-to-all-start.6) | async-done | bytes 3604512 | tf_op jit(solution)/shard_map/all_to_all | solution.py:140
  1025.1 8.1 fusion.25
  1045.8 18.5 %mlp_adam.4 = (f32[3,160,7680]{2,1,0:T(8,128)}, f32[3,160,7680]{2,1,0:T(8,128)}, f32[3,160,7680]{2,1,0:T(8,128)}, f32[160,1]{1,0:T(8,128)S(1)}) custom-call(s32[1]{0:T(128)} %bitcast.4.refs_0_, bf16[4,160,1024]{2,1,0:T(8,128)(2,1)S(1)} %all-to-all-done.4.refs_1_, ...), custom_call_target="tpu_custom_call", output_to_operand_aliasing={{0}: (7, {}), {1}: (8, {}), {2}: (9, {})} | custom-call | flops 24576000 | bytes 31948800 | tf_op jit(solution)/shard_map/mlp_adam/pallas_call | solution.py:238
  1064.3 19.0 %mlp_adam.5 = (f32[3,160,7680]{2,1,0:T(8,128)}, f32[3,160,7680]{2,1,0:T(8,128)}, f32[3,160,7680]{2,1,0:T(8,128)}, f32[160,1]{1,0:T(8,128)S(1)}) custom-call(s32[1]{0:T(128)} %bitcast.4.refs_0_, bf16[4,160,1024]{2,1,0:T(8,128)(2,1)} %all-to-all-done.5.refs_1_, ...), custom_call_target="tpu_custom_call", output_to_operand_aliasing={{0}: (7, {}), {1}: (8, {}), {2}: (9, {})} | custom-call | flops 24576000 | bytes 31948800 | tf_op jit(solution)/shard_map/mlp_adam/pallas_call | solution.py:238
  1089.6 7.5 multiply_subtract_fusion
  1100.7 4.7 fusion.50
  (376 shorter events, 204.6 us)
Async XLA Ops:
  7.2 47.0 %all-gather.7.cloned.1.call-start = ((), (), s32[]{:S(2)}) async-start(), calls=%async_computation.11 | async-start | bytes 2457600 | tf_op jit(solution)/shard_map/all_gather | solution.py:451
  10.8 151.9 %all-gather.9.cloned.1.call-start = ((), (), s32[]{:S(2)}) async-start(), calls=%async_computation.12 | async-start | bytes 17694720 | tf_op jit(solution)/shard_map/all_gather | solution.py:447
  54.2 26.5 %all-to-all-start.1 = ((bf16[4,160,1024]{2,1,0:T(8,128)(2,1)}), bf16[4,160,1024]{2,1,0:T(8,128)(2,1)S(1)}, u32[]{:S(2)}, u32[]{:S(2)}) async-start(bf16[4,160,1024]{2,1,0:T(8,128)(2,1)} %get-tuple-element.56), calls=%async_computation.1 | async-start | bytes 2621440 | tf_op jit(solution)/shard_map/all_to_all | solution.py:140
  58.9 154.1 %all-gather.11.cloned.1.call-start = ((), (), s32[]{:S(2)}) async-start(), calls=%async_computation.13 | async-start | bytes 2048000 | tf_op jit(solution)/shard_map/all_gather | solution.py:479
  58.9 86.7 %collective-permute-start.1 = (bf16[640,2048]{1,0:T(8,128)(2,1)}, bf16[640,2048]{1,0:T(8,128)(2,1)}, u32[]{:S(2)}, u32[]{:S(2)}) collective-permute-start(bf16[640,2048]{1,0:T(8,128)(2,1)} %bitcast.228), channel_id=1, source_target_pairs={{0,4},{4,8},{8,12},{12,0},{1,5},{5,9},{9,13},{13,1},{2,6},{6,10},{... | collective-permute-start | bytes 7864328 | tf_op jit(solution)/shard_map/ppermute | solution.py:105
  60.3 56.2 %collective-permute-start = (bf16[192,2560]{1,0:T(8,128)(2,1)}, bf16[192,2560]{1,0:T(8,128)(2,1)}, u32[]{:S(2)}, u32[]{:S(2)}) collective-permute-start(bf16[192,2560]{1,0:T(8,128)(2,1)} %bitcast.1), channel_id=1, source_target_pairs={{0,2},{2,0},{1,3},{3,1},{4,6},{6,4},{5,7},{7,5},{8,10},{10,8},{9,1... | collective-permute-start | bytes 2949128 | tf_op jit(solution)/shard_map/ppermute | solution.py:98
  61.2 57.6 %copy-start.61 = (f32[192]{0:T(256)}, f32[192]{0:T(256)S(1)}, u32[]{:S(2)}) copy-start(f32[192]{0:T(256)S(1)} %get-tuple-element.199) | copy-start | bytes 2308
  80.6 38.1 %copy-start.38 = (bf16[4,160,1024]{2,1,0:T(8,128)(2,1)}, bf16[4,160,1024]{2,1,0:T(8,128)(2,1)S(1)}, u32[]{:S(2)}) copy-start(bf16[4,160,1024]{2,1,0:T(8,128)(2,1)S(1)} %all-to-all-done.1) | copy-start | bytes 3932164
  80.7 65.0 %collective-permute-start.2 = (bf16[640,1024]{1,0:T(8,128)(2,1)S(1)}, bf16[640,1024]{1,0:T(8,128)(2,1)}, u32[]{:S(2)}, u32[]{:S(2)}) collective-permute-start(bf16[640,1024]{1,0:T(8,128)(2,1)S(1)} %bitcast.248), channel_id=1, source_target_pairs={{0,4},{4,8},{8,12},{12,0},{1,5},{5,9},{9,13},{13,1},{2,6},{6,10},{... | collective-permute-start | bytes 3932168 | tf_op jit(solution)/shard_map/ppermute | solution.py:105
  82.4 63.2 %copy-start.24 = (bf16[192,2560]{1,0:T(8,128)(2,1)}, bf16[192,2560]{1,0:T(8,128)(2,1)S(1)}, u32[]{:S(2)}) copy-start(bf16[192,2560]{1,0:T(8,128)(2,1)S(1)} %fusion.47) | copy-start | bytes 2949124
  173.7 39.4 %copy-start.76 = (s32[2,3]{1,0:T(2,128)S(1)}, s32[2,3]{1,0:T(2,128)}, u32[]{:S(2)}) copy-start(s32[2,3]{1,0:T(2,128)} %param.17) | copy-start | bytes 76
  175.7 184.2 %all-gather.13.cloned.1.call-start = ((), (), s32[]{:S(2)}) async-start(), calls=%async_computation.14 | async-start | bytes 14745600 | tf_op jit(solution)/shard_map/all_gather | solution.py:447
  213.0 285.4 %all-gather.15.cloned.1.call-start = ((), (), s32[]{:S(2)}) async-start(), calls=%async_computation.15 | async-start | bytes 8847360 | tf_op jit(solution)/shard_map/all_gather | solution.py:512
  213.3 18.4 %copy-start.74 = (f32[128]{0:T(128)}, f32[128]{0:T(128)S(1)}, u32[]{:S(2)}) copy-start(f32[128]{0:T(128)S(1)} %multiply_exponential_fusion) | copy-start | bytes 1540
  213.4 18.3 %copy-start.63 = (f32[192]{0:T(256)}, f32[192]{0:T(256)S(1)}, u32[]{:S(2)}) copy-start(f32[192]{0:T(256)S(1)} %get-tuple-element.150) | copy-start | bytes 2308
  214.6 5.6 collective-permute-start.5
  214.9 25.5 %collective-permute-start.10 = (bf16[192,512]{1,0:T(8,128)(2,1)S(1)}, bf16[192,512]{1,0:T(8,128)(2,1)S(1)}, u32[]{:S(2)}, u32[]{:S(2)}) collective-permute-start(bf16[192,512]{1,0:T(8,128)(2,1)S(1)} %pad_maximum_fusion.13), channel_id=1, source_target_pairs={{0,20},{2,22},{4,16},{6,18},{16,4},{18,6},{20,0},{22,2},{1,21},{3,... | collective-permute-start | bytes 589832 | tf_op jit(solution)/shard_map/ppermute | solution.py:122
  217.3 23.1 %collective-permute-start.9 = (bf16[192,512]{1,0:T(8,128)(2,1)S(1)}, bf16[192,512]{1,0:T(8,128)(2,1)S(1)}, u32[]{:S(2)}, u32[]{:S(2)}) collective-permute-start(bf16[192,512]{1,0:T(8,128)(2,1)S(1)} %pad_maximum_fusion.13), channel_id=1, source_target_pairs={{0,18},{2,16},{4,22},{6,20},{16,2},{18,0},{20,6},{22,4},{1,19},{3,... | collective-permute-start | bytes 589832 | tf_op jit(solution)/shard_map/ppermute | solution.py:122
  218.5 21.9 %collective-permute-start.8 = (bf16[192,512]{1,0:T(8,128)(2,1)S(1)}, bf16[192,512]{1,0:T(8,128)(2,1)S(1)}, u32[]{:S(2)}, u32[]{:S(2)}) collective-permute-start(bf16[192,512]{1,0:T(8,128)(2,1)S(1)} %pad_maximum_fusion.13), channel_id=1, source_target_pairs={{0,16},{2,18},{4,20},{6,22},{16,0},{18,2},{20,4},{22,6},{1,17},{3,... | collective-permute-start | bytes 589832 | tf_op jit(solution)/shard_map/ppermute | solution.py:122
  219.7 12.1 %collective-permute-start.7 = (bf16[192,512]{1,0:T(8,128)(2,1)S(1)}, bf16[192,512]{1,0:T(8,128)(2,1)S(1)}, u32[]{:S(2)}, u32[]{:S(2)}) collective-permute-start(bf16[192,512]{1,0:T(8,128)(2,1)S(1)} %pad_maximum_fusion.13), channel_id=1, source_target_pairs={{0,6},{2,4},{4,2},{6,0},{16,22},{18,20},{20,18},{22,16},{1,7},{3,5... | collective-permute-start | bytes 589832 | tf_op jit(solution)/shard_map/ppermute | solution.py:122
  220.1 10.8 collective-permute-start.6
  230.9 9.5 collective-permute-start.11
  240.5 7.8 collective-permute-start.12
  245.2 86.9 %collective-permute-start.3 = (bf16[640,2048]{1,0:T(8,128)(2,1)}, bf16[640,2048]{1,0:T(8,128)(2,1)}, u32[]{:S(2)}, u32[]{:S(2)}) collective-permute-start(bf16[640,2048]{1,0:T(8,128)(2,1)} %collective-permute-done.1), channel_id=1, source_target_pairs={{0,4},{4,8},{8,12},{12,0},{1,5},{5,9},{9,13},{13,1},{2,6},{6,10},{... | collective-permute-start | bytes 7864328 | tf_op jit(solution)/shard_map/ppermute | solution.py:105
  251.9 100.3 %collective-permute-start.13 = (bf16[2,192,2560]{2,1,0:T(8,128)(2,1)}, bf16[2,192,2560]{2,1,0:T(8,128)(2,1)}, u32[]{:S(2)}, u32[]{:S(2)}) collective-permute-start(bf16[2,192,2560]{2,1,0:T(8,128)(2,1)} %pad_maximum_fusion.8), channel_id=1, source_target_pairs={{0,16},{16,0},{1,17},{17,1},{2,18},{18,2},{3,19},{19,3},{4,20},{20... | collective-permute-start | bytes 5898248 | tf_op jit(solution)/shard_map/ppermute | solution.py:98
  259.5 72.6 %collective-permute-start.4 = (bf16[640,1024]{1,0:T(8,128)(2,1)}, bf16[640,1024]{1,0:T(8,128)(2,1)}, u32[]{:S(2)}, u32[]{:S(2)}) collective-permute-start(bf16[640,1024]{1,0:T(8,128)(2,1)} %collective-permute-done.2), channel_id=1, source_target_pairs={{0,4},{4,8},{8,12},{12,0},{1,5},{5,9},{9,13},{13,1},{2,6},{6,10},{... | collective-permute-start | bytes 3932168 | tf_op jit(solution)/shard_map/ppermute | solution.py:105
  265.7 68.8 %copy-start.2 = (bf16[3072,256]{1,0:T(8,128)(2,1)}, bf16[3072,256]{1,0:T(8,128)(2,1)S(1)}, u32[]{:S(2)}) copy-start(bf16[3072,256]{1,0:T(8,128)(2,1)S(1)} %get-tuple-element.169.key_ref) | copy-start | bytes 4718596
  372.2 350.0 %reduce-scatter.5.cloned.1.call-start = ((), (), s32[]{:S(2)}) async-start(), calls=%async_computation.16 | async-start | bytes 6553600 | tf_op jit(solution)/shard_map/reduce_scatter | solution.py:518
  372.2 96.9 %collective-permute-start.15 = (bf16[2,2,192,2560]{3,2,1,0:T(8,128)(2,1)}, bf16[2,2,192,2560]{3,2,1,0:T(8,128)(2,1)}, u32[]{:S(2)}, u32[]{:S(2)}) collective-permute-start(bf16[2,2,192,2560]{3,2,1,0:T(8,128)(2,1)} %pad_maximum_fusion.3), channel_id=1, source_target_pairs={{0,1},{1,0},{2,3},{3,2},{4,5},{5,4},{6,7},{7,6},{8,9},{9,8},{10,11... | collective-permute-start | bytes 11796488 | tf_op jit(solution)/shard_map/ppermute | solution.py:98
  373.1 92.3 %collective-permute-start.16 = (bf16[640,2048]{1,0:T(8,128)(2,1)}, bf16[640,2048]{1,0:T(8,128)(2,1)}, u32[]{:S(2)}, u32[]{:S(2)}) collective-permute-start(bf16[640,2048]{1,0:T(8,128)(2,1)} %collective-permute-done.3), channel_id=1, source_target_pairs={{0,4},{4,8},{8,12},{12,0},{1,5},{5,9},{9,13},{13,1},{2,6},{6,10},{... | collective-permute-start | bytes 7864328 | tf_op jit(solution)/shard_map/ppermute | solution.py:105
  373.1 86.7 %collective-permute-start.14 = (bf16[640,1024]{1,0:T(8,128)(2,1)}, bf16[640,1024]{1,0:T(8,128)(2,1)S(1)}, u32[]{:S(2)}, u32[]{:S(2)}) collective-permute-start(bf16[640,1024]{1,0:T(8,128)(2,1)} %collective-permute-done.4), channel_id=1, source_target_pairs={{0,4},{4,8},{8,12},{12,0},{1,5},{5,9},{9,13},{13,1},{2,6},{6,10},{... | collective-permute-start | bytes 3932168 | tf_op jit(solution)/shard_map/ppermute | solution.py:105
  538.0 301.8 %reduce-scatter.11.cloned.1.call-start = ((), (), s32[]{:S(2)}) async-start(), calls=%async_computation.20 | async-start | bytes 6553600 | tf_op jit(solution)/shard_map/reduce_scatter | solution.py:518
  560.3 7.6 collective-permute-start.17
  584.0 26.9 %collective-permute-start.19 = (bf16[192,2560]{1,0:T(8,128)(2,1)}, bf16[192,2560]{1,0:T(8,128)(2,1)}, u32[]{:S(2)}, u32[]{:S(2)}) collective-permute-start(bf16[192,2560]{1,0:T(8,128)(2,1)} %get-tuple-element.161), channel_id=1, source_target_pairs={{0,16},{2,18},{16,0},{18,2},{1,17},{3,19},{17,1},{19,3},{4,20},{6,... | collective-permute-start | bytes 2949128 | tf_op jit(solution)/shard_map/ppermute | solution.py:549
  588.7 23.0 %collective-permute-start.18 = (bf16[192,2560]{1,0:T(8,128)(2,1)}, bf16[192,2560]{1,0:T(8,128)(2,1)}, u32[]{:S(2)}, u32[]{:S(2)}) collective-permute-start(bf16[192,2560]{1,0:T(8,128)(2,1)} %get-tuple-element.163), channel_id=1, source_target_pairs={{0,2},{2,0},{16,18},{18,16},{1,3},{3,1},{17,19},{19,17},{4,6},{6,4... | collective-permute-start | bytes 2949128 | tf_op jit(solution)/shard_map/ppermute | solution.py:549
  589.4 22.2 %copy-start.32 = (bf16[1536,2048]{1,0:T(8,128)(2,1)}, bf16[1536,2048]{1,0:T(8,128)(2,1)S(1)}, u32[]{:S(2)}) copy-start(bf16[1536,2048]{1,0:T(8,128)(2,1)S(1)} %pad_maximum_fusion.1) | copy-start | bytes 18874372
  624.1 242.7 %all-gather.17.cloned.1.call-start = ((), (), s32[]{:S(2)}) async-start(), calls=%async_computation.18 | async-start | bytes 8847360 | tf_op jit(solution)/shard_map/all_gather | solution.py:522
  624.8 274.9 %reduce-scatter.9.cloned.1.call-start = ((), (), s32[]{:S(2)}) async-start(), calls=%async_computation.19 | async-start | bytes 6553600 | tf_op jit(solution)/shard_map/reduce_scatter | solution.py:518
  627.2 22.6 %collective-permute-start.20 = (bf16[192,2560]{1,0:T(8,128)(2,1)S(1)}, bf16[192,2560]{1,0:T(8,128)(2,1)S(1)}, u32[]{:S(2)}, u32[]{:S(2)}) collective-permute-start(bf16[192,2560]{1,0:T(8,128)(2,1)S(1)} %copy-done.58), channel_id=1, source_target_pairs={{0,18},{2,16},{16,2},{18,0},{1,19},{3,17},{17,3},{19,1},{4,22},{6,... | collective-permute-start | bytes 2949128 | tf_op jit(solution)/shard_map/ppermute | solution.py:549
  653.3 20.9 %collective-permute-start.21 = (bf16[192,2560]{1,0:T(8,128)(2,1)S(1)}, bf16[192,2560]{1,0:T(8,128)(2,1)}, u32[]{:S(2)}, u32[]{:S(2)}) collective-permute-start(bf16[192,2560]{1,0:T(8,128)(2,1)S(1)} %copy-done.25), channel_id=1, source_target_pairs={{0,2},{2,0},{1,3},{3,1},{4,6},{6,4},{5,7},{7,5},{8,10},{10,8},{9,1... | collective-permute-start | bytes 2949128 | tf_op jit(solution)/shard_map/ppermute | solution.py:98
  677.5 51.9 %collective-permute-start.22 = (bf16[2,192,2560]{2,1,0:T(8,128)(2,1)}, bf16[2,192,2560]{2,1,0:T(8,128)(2,1)}, u32[]{:S(2)}, u32[]{:S(2)}) collective-permute-start(bf16[2,192,2560]{2,1,0:T(8,128)(2,1)} %pad_maximum_fusion.9), channel_id=1, source_target_pairs={{0,16},{16,0},{1,17},{17,1},{2,18},{18,2},{3,19},{19,3},{4,20},{20... | collective-permute-start | bytes 5898248 | tf_op jit(solution)/shard_map/ppermute | solution.py:98
  722.2 22.5 %all-to-all-start.2 = ((bf16[4,160,1024]{2,1,0:T(8,128)(2,1)}), bf16[4,160,1024]{2,1,0:T(8,128)(2,1)S(1)}, u32[]{:S(2)}, u32[]{:S(2)}) async-start(bf16[4,160,1024]{2,1,0:T(8,128)(2,1)} %bitcast.264), calls=%async_computation.3 | async-start | bytes 2621440 | tf_op jit(solution)/shard_map/all_to_all | solution.py:140
  733.4 14.7 %copy-start.60 = (f32[192,128]{1,0:T(8,128)S(1)}, f32[192,128]{1,0:T(8,128)}, u32[]{:S(2)}) copy-start(f32[192,128]{1,0:T(8,128)} %get-tuple-element.193) | copy-start | bytes 294916
  747.5 6.0 collective-permute-start.23
  748.1 65.9 %collective-permute-start.28 = (bf16[2,2,192,2560]{3,2,1,0:T(8,128)(2,1)}, bf16[2,2,192,2560]{3,2,1,0:T(8,128)(2,1)}, u32[]{:S(2)}, u32[]{:S(2)}) collective-permute-start(bf16[2,2,192,2560]{3,2,1,0:T(8,128)(2,1)} %pad_maximum_fusion.4), channel_id=1, source_target_pairs={{0,1},{1,0},{2,3},{3,2},{4,5},{5,4},{6,7},{7,6},{8,9},{9,8},{10,11... | collective-permute-start | bytes 11796488 | tf_op jit(solution)/shard_map/ppermute | solution.py:90
  756.5 25.0 %collective-permute-start.24 = (bf16[2,192,512]{2,1,0:T(8,128)(2,1)}, bf16[2,192,512]{2,1,0:T(8,128)(2,1)}, u32[]{:S(2)}, u32[]{:S(2)}) collective-permute-start(bf16[2,192,512]{2,1,0:T(8,128)(2,1)} %get-tuple-element.182), channel_id=1, source_target_pairs={{0,2},{2,0},{16,18},{18,16},{1,3},{3,1},{17,19},{19,17},{4,6},{6,4... | collective-permute-start | bytes 1179656 | tf_op jit(solution)/shard_map/ppermute | solution.py:134
  758.0 23.5 %collective-permute-start.26 = (bf16[2,192,512]{2,1,0:T(8,128)(2,1)}, bf16[2,192,512]{2,1,0:T(8,128)(2,1)}, u32[]{:S(2)}, u32[]{:S(2)}) collective-permute-start(bf16[2,192,512]{2,1,0:T(8,128)(2,1)} %get-tuple-element.183), channel_id=1, source_target_pairs={{0,18},{2,16},{16,2},{18,0},{1,19},{3,17},{17,3},{19,1},{4,22},{6,... | collective-permute-start | bytes 1179656 | tf_op jit(solution)/shard_map/ppermute | solution.py:134
  758.9 27.9 %collective-permute-start.25 = (bf16[2,192,512]{2,1,0:T(8,128)(2,1)}, bf16[2,192,512]{2,1,0:T(8,128)(2,1)}, u32[]{:S(2)}, u32[]{:S(2)}) collective-permute-start(bf16[2,192,512]{2,1,0:T(8,128)(2,1)} %get-tuple-element.184), channel_id=1, source_target_pairs={{0,16},{2,18},{16,0},{18,2},{1,17},{3,19},{17,1},{19,3},{4,20},{6,... | collective-permute-start | bytes 1179656 | tf_op jit(solution)/shard_map/ppermute | solution.py:134
  761.4 41.5 %copy-start.56 = (f32[192,128]{0,1:T(8,128)S(1)}, f32[192,128]{0,1:T(8,128)}, u32[]{:S(2)}) copy-start(f32[192,128]{0,1:T(8,128)} %copy-done.55) | copy-start | bytes 294916
  761.4 41.5 %copy-start.59 = (f32[192,128]{0,1:T(8,128)S(1)}, f32[192,128]{0,1:T(8,128)}, u32[]{:S(2)}) copy-start(f32[192,128]{0,1:T(8,128)} %copy.208) | copy-start | bytes 294916
  788.4 14.5 %copy-start.52 = (bf16[2,192,512]{2,1,0:T(8,128)(2,1)}, bf16[2,192,512]{2,1,0:T(8,128)(2,1)S(1)}, u32[]{:S(2)}) copy-start(bf16[2,192,512]{2,1,0:T(8,128)(2,1)S(1)} %fusion.59) | copy-start | bytes 1179652
  789.2 20.9 %collective-permute-start.27 = (bf16[192,512]{1,0:T(8,128)(2,1)}, bf16[192,512]{1,0:T(8,128)(2,1)}, u32[]{:S(2)}, u32[]{:S(2)}) collective-permute-start(bf16[192,512]{1,0:T(8,128)(2,1)} %dynamic-slice_bitcast_fusion.7), channel_id=1, source_target_pairs={{0,4},{4,0},{1,5},{5,1},{2,6},{6,2},{3,7},{7,3},{8,12},{12,8},{9,1... | collective-permute-start | bytes 589832 | tf_op jit(solution)/shard_map/ppermute | solution.py:90
  818.8 35.1 %all-to-all-start.3 = ((bf16[8,192,704]{2,1,0:T(8,128)(2,1)}), bf16[8,192,704]{2,1,0:T(8,128)(2,1)}, u32[]{:S(2)}, u32[]{:S(2)}) async-start(bf16[8,192,704]{2,1,0:T(8,128)(2,1)} %maximum_bitcast_fusion), calls=%async_computation.4 | async-start | bytes 4718592 | tf_op jit(solution)/shard_map/all_to_all | solution.py:140
  853.9 45.9 %all-to-all-start.4 = ((bf16[4,160,1024]{2,1,0:T(8,128)(2,1)}), bf16[4,160,1024]{2,1,0:T(8,128)(2,1)S(1)}, u32[]{:S(2)}, u32[]{:S(2)}) async-start(bf16[4,160,1024]{2,1,0:T(8,128)(2,1)} %bitcast.262), calls=%async_computation.8 | async-start | bytes 2621440 | tf_op jit(solution)/shard_map/all_to_all | solution.py:140
  858.4 242.3 %reduce-scatter.7.cloned.1.call-start = ((), (), s32[]{:S(2)}) async-start(), calls=%async_computation.17 | async-start | bytes 8847360 | tf_op jit(solution)/shard_map/reduce_scatter | solution.py:635
  899.7 20.6 %all-to-all-start.5 = ((bf16[4,160,1024]{2,1,0:T(8,128)(2,1)}), bf16[4,160,1024]{2,1,0:T(8,128)(2,1)}, u32[]{:S(2)}, u32[]{:S(2)}) async-start(bf16[4,160,1024]{2,1,0:T(8,128)(2,1)} %bitcast.263), calls=%async_computation.9 | async-start | bytes 2621440 | tf_op jit(solution)/shard_map/all_to_all | solution.py:140
  926.4 93.6 %all-to-all-start.6 = ((bf16[16,160,704]{2,1,0:T(8,128)(2,1)}), bf16[16,160,704]{2,1,0:T(8,128)(2,1)}, u32[]{:S(2)}, u32[]{:S(2)}) async-start(bf16[16,160,704]{2,1,0:T(8,128)(2,1)} %bitcast.224), calls=%async_computation.10 | async-start | bytes 7864320 | tf_op jit(solution)/shard_map/all_to_all | solution.py:140
  932.9 46.7 %copy-start.1 = (f32[160,1]{1,0:T(8,128)S(1)}, f32[160,1]{1,0:T(8,128)}, u32[]{:S(2)}) copy-start(f32[160,1]{1,0:T(8,128)} %copy-done) | copy-start | bytes 1924
  932.9 46.7 %collective-permute-start.32 = (bf16[4,160,1024]{2,1,0:T(8,128)(2,1)S(1)}, bf16[4,160,1024]{2,1,0:T(8,128)(2,1)}, u32[]{:S(2)}, u32[]{:S(2)}) collective-permute-start(bf16[4,160,1024]{2,1,0:T(8,128)(2,1)S(1)} %all-to-all-done.2.refs_1_), channel_id=1, source_target_pairs={{0,16},{16,0},{1,17},{17,1},{2,18},{18,2},{3,19},{19,3},{4,20},{20... | collective-permute-start | bytes 3932168 | tf_op jit(solution)/shard_map/ppermute | solution.py:90
  979.6 19.3 %copy-start.36 = (bf16[192,3072]{0,1:T(8,128)(2,1)S(1)}, bf16[192,3072]{0,1:T(8,128)(2,1)}, u32[]{:S(2)}) copy-start(bf16[192,3072]{0,1:T(8,128)(2,1)} %copy-done.35) | copy-start | bytes 3538948
  997.4 48.4 %collective-permute-start.31 = (bf16[4,160,1024]{2,1,0:T(8,128)(2,1)S(1)}, bf16[4,160,1024]{2,1,0:T(8,128)(2,1)}, u32[]{:S(2)}, u32[]{:S(2)}) collective-permute-start(bf16[4,160,1024]{2,1,0:T(8,128)(2,1)S(1)} %all-to-all-done.4.refs_1_), channel_id=1, source_target_pairs={{0,16},{16,0},{1,17},{17,1},{2,18},{18,2},{3,19},{19,3},{4,20},{20... | collective-permute-start | bytes 3932168 | tf_op jit(solution)/shard_map/ppermute | solution.py:90
  997.8 66.5 %collective-permute-start.30 = (bf16[4,160,1024]{2,1,0:T(8,128)(2,1)}, bf16[4,160,1024]{2,1,0:T(8,128)(2,1)S(1)}, u32[]{:S(2)}, u32[]{:S(2)}) collective-permute-start(bf16[4,160,1024]{2,1,0:T(8,128)(2,1)} %all-to-all-done.5.refs_1_), channel_id=1, source_target_pairs={{0,16},{16,0},{1,17},{17,1},{2,18},{18,2},{3,19},{19,3},{4,20},{20... | collective-permute-start | bytes 3932168 | tf_op jit(solution)/shard_map/ppermute | solution.py:90
  1023.9 59.5 %collective-permute-start.29 = (bf16[4,160,704]{2,1,0:T(8,128)(2,1)}, bf16[4,160,704]{2,1,0:T(8,128)(2,1)}, u32[]{:S(2)}, u32[]{:S(2)}) collective-permute-start(bf16[4,160,704]{2,1,0:T(8,128)(2,1)} %reduce_sum.111), channel_id=1, source_target_pairs={{0,16},{16,0},{1,17},{17,1},{2,18},{18,2},{3,19},{19,3},{4,20},{20... | collective-permute-start | bytes 2703368 | tf_op jit(solution)/shard_map/ppermute | solution.py:98
  1064.3 19.1 %copy-start.41 = (bf16[4,160,704]{2,1,0:T(8,128)(2,1)S(1)}, bf16[4,160,704]{2,1,0:T(8,128)(2,1)}, u32[]{:S(2)}) copy-start(bf16[4,160,704]{2,1,0:T(8,128)(2,1)} %reduce_sum.111) | copy-start | bytes 2703364
  (67 other events, 314.4 us)
Sparse Core Ops, SparseCore 0:
  10.9 43.1 all-gather.6
  56.0 106.7 all-gather.8
  175.8 37.1 all-gather.10
  214.7 119.5 all-gather.12
  372.3 55.5 all-gather.14
  538.2 98.9 reduce-scatter.4
  640.1 94.2 reduce-scatter.10
  736.3 64.0 all-gather.16
  803.3 96.4 reduce-scatter.8
  903.0 105.4 reduce-scatter.6

commit v7 on v6

--- a/solution.py
+++ b/solution.py
@@ -106,11 +106,14 @@
 
 
 def joined_planes(blocks):
-    count, rows = len(blocks), blocks[0].shape[0]
-    whole = jnp.zeros((count * rows, blocks[0].shape[1]), blocks[0].dtype)
+    count, (rows, width) = len(blocks), blocks[0].shape
+    whole = jnp.zeros((count * rows, width), blocks[0].dtype)
     for step, block in enumerate(blocks):
         start = lax.rem(lax.axis_index(PLANES) + (count - step), count) * rows
-        whole = lax.dynamic_update_slice_in_dim(whole, block, start, 0)
+        column = 0
+        for part in block if isinstance(block, list) else [block]:
+            whole = lax.dynamic_update_slice(whole, part, (start, column))
+            column += part.shape[1]
     return whole
 
 
@@ -475,43 +478,44 @@
     normed_one = after(normed_one, incoming_columns, gate_up_blocks[1], down_blocks[1])
     rows = regrouped(normed_one, planes, members)
     projected = jnp.concatenate([dot(rows, half, (1, 0)) for half in qkv_halves], axis=1)
-    out_rows = own_half(low(after(weight_out, projected)))
-    out_halves = gathered_group(lax.all_gather(out_rows, PLANES, axis=0, tiled=True))
     key_pre = projected[:, width : width + HEAD_DIM]
     value_low = low(projected[:, width + HEAD_DIM :])
     key_low = low(rotate(key_pre, cosine, sine))
     window_kv = spread_ring(jnp.concatenate([key_low, value_low], axis=1))
     window_kv = doubled(window_kv, "c", 1, 1)
     window_kv = window_kv.reshape(SEQ_LEN, 2 * HEAD_DIM)
+    out_rows = own_half(low(after(weight_out, window_kv)))
+    out_halves = gathered_group(lax.all_gather(out_rows, PLANES, axis=0, tiled=True))
     gate_up_blocks.append(next_plane(after(gate_up_blocks[1], projected)))
-    for _ in range(planes - 3):
+    for _ in range(planes - 4):
         gate_up_blocks.append(next_plane(gate_up_blocks[-1]))
+    last = gate_up_blocks[-1]
+    gate_up_blocks.append([next_plane(last[:, :piece]), next_plane(last[:, piece:])])
     down_blocks.append(next_plane(after(down_blocks[1], projected)))
     for _ in range(planes - 3):
         down_blocks.append(next_plane(down_blocks[-1]))
     gate_up_own = joined_planes(gate_up_blocks)
     down_own = joined_planes(down_blocks)
-    incoming_sides = doubled(after(incoming_columns, window_kv), "seq", 1, 0)
+    incoming_sides = doubled(after(incoming_columns, projected), "seq", 1, 0)
     query_pre = projected[:, :width].reshape(tok_rows, head_count, HEAD_DIM)
     queries = low(rotate(query_pre, cosine[:, None, :], sine[:, None, :]) * query_scale)
-    queries = after(queries.reshape(tok_rows, width), gate_up_blocks[2], down_blocks[2])
     incoming_all = doubled(incoming_sides, "c", 1, incoming_sides.ndim - 2)
     incoming_all = incoming_all.reshape(sides * members * tok_rows, width)
+    queries = after(queries.reshape(tok_rows, width), gate_up_blocks[2], down_blocks[2], incoming_all)
     keys_win = window_kv[:, :HEAD_DIM]
     values_win = window_kv[:, HEAD_DIM:]
     bias = jnp.where(allowed.T, 0.0, MASKED_SCORE)
     bias = jnp.concatenate([bias, bias], axis=1)
     attn_low, log_total = attend(queries, keys_win, values_win, bias)
-    attn_low = after(attn_low, incoming_sides)
     rows = regrouped(attn_low, planes, members)
     branch = [dot(rows, half, (1, 0)) for half in out_halves]
     middle = tokens + jnp.concatenate(branch, axis=1)
 
     factor_two = lax.rsqrt(jnp.mean(middle * middle, axis=-1, keepdims=True) + NORM_EPS)
-    normed_two = low(middle * factor_two)
+    normed_two = after(low(middle * factor_two), gate_up_blocks[-1][0])
     normed_two_all = lax.all_gather(normed_two, GROUP, axis=0, tiled=True)
     grad_act = low(dot(incoming_all, down_own, (1, 0)))
-    gate_up = dot(after(normed_two_all, down_own, incoming_all), gate_up_own, (1, 0))
+    gate_up = dot(after(normed_two_all, down_own), gate_up_own, (1, 0))
     activated, glu_back = jax.vjp(glu_values, gate_up[:, :piece], gate_up[:, piece:])
     activated_low = low(activated)
     def to_owners(term):
@@ -581,7 +585,9 @@
         dot(grad_branch_low[:, index * half : (index + 1) * half], out_halves[index], (1, 1))
         for index in range(sides)
     )
+    down_pieces = in_plane(down_rows)
     grad_mixed_low = regrouped(low(grad_mixed), members, planes)
+    grad_mixed_low = after(grad_mixed_low, down_pieces[0])
     delta = (wide(grad_mixed_low) * wide(attn_low)).reshape(tok_rows, head_count, HEAD_DIM)
     delta = jnp.sum(delta, axis=-1).T.reshape(log_total.shape)
     grad_query, grad_window = attend_back(
@@ -589,8 +595,7 @@
     )
     normed_one_columns = doubled(after(normed_one, grad_normed_two), "k", 1, 0)
     normed_one_sides = doubled(normed_one_columns, "seq", 1, 0)
-    down_pieces = in_plane(down_rows)
-    grad_window = after(low(grad_window), normed_one_sides, down_pieces[0])
+    grad_window = after(low(grad_window), normed_one_sides)
     branch = low(dot(after(activated_low, grad_window), down_own, (1, 1)))
     normed_one_others = swapped(normed_one_sides, "c")
     grad_window = half_sum(grad_window.reshape(-1, 2, tok_rows, 2 * HEAD_DIM), "c", 1)
@@ -629,9 +634,9 @@
     out_columns = all_columns.reshape(shares * tok_rows, -1)[:, qkv_share:]
     out_total = low(dot(attn_all, out_columns, (0, 0)))
     gate_pieces = in_plane(gate_rows, all_columns)
-    up_pieces = in_plane(up_rows, gate_pieces[0])
     total = jnp.concatenate([qkv_total, out_total], axis=1)
-    total = to_rows(after(total, up_pieces[0]))
+    total = to_rows(after(total, gate_pieces[0]))
+    up_pieces = in_plane(up_rows, total)
     branch = lax.psum_scatter(
         after(branch, all_columns), GROUP, scatter_dimension=0, tiled=True
     )

time: 1120 us -> 1140 us (1.018)
    ppermute x7, waiting for transfers between devices: 35.3 us -> 107 us  [doubled(): other = lax.ppermute(value, axis, traded((axis,), step))]
    ppermute x6 -> x7, waiting for transfers between devices: 161 us -> 120 us  [next_plane(): lax.ppermute(block, PLANES, [(one, (one + 1) % count) for one in range(co...]
    reduce_scatter x3, waiting for transfers between devices: 25.4 us -> 0.02 us  [to_owners(): return lax.psum_scatter(term, PLANES, scatter_dimension=0, tiled=True)]
    all_to_all x6, waiting for transfers between devices: 66.7 us -> 88.7 us  [exchanged(): return lax.all_to_all(value, axes, split_axis=0, concat_axis=0, tiled=True)]
    unnamed x164 -> x170, local copies, waits for them, and re-layouts: 17.9 us -> 25.4 us
  transfers between devices with their start and end apart: 49 -> 50, of which waited for: 25 -> 28; matrix products, arithmetic and copies ran while one was open for 28% -> 29% of each run, Pallas kernels for 10% -> 10%
where the time goes in v7:
time: 1140 us; the launch traced here: 1130 us
  waiting for transfers between devices  480 us (42%)
  matrix products  168 us (15%)
  local copies, waits for them, and re-layouts  122 us (11%)
  other arithmetic  117 us (10%)
  Pallas kernels  108 us (9%)
  starting transfers between devices  87 us (8%)
  blocking collectives  33.5 us (3%)
  between operations  15.9 us (1%)
    dot_general x19, matrix products, dot(): lax.dot_general(left, right, ((contract[:1], contract[1:]), ((), ())), pr...  168 us
    ppermute x7, waiting for transfers between devices, next_plane(): lax.ppermute(block, PLANES, [(one, (one + 1) % count) for one in range(co...  120 us
    ppermute x7, waiting for transfers between devices, doubled(): other = lax.ppermute(value, axis, traded((axis,), step))  107 us
    all_to_all x6, waiting for transfers between devices, exchanged(): return lax.all_to_all(value, axes, split_axis=0, concat_axis=0, tiled=True)  88.7 us
    pallas_call x3, Pallas kernels, mlp_adam(): pl.pallas_call(lambda *refs: mlp_adam_kernel(rate, per_side, part < 2, *r...  54.7 us
    ppermute x7, waiting for transfers between devices, swapped(): return lax.ppermute(value, axis, [(0, 1), (1, 0)])  47 us
    all_to_all x6, starting transfers between devices, exchanged(): return lax.all_to_all(value, axes, split_axis=0, concat_axis=0, tiled=True)  45.6 us
    all_gather x1, waiting for transfers between devices, on_device(): lax.all_gather(out_rows, PLANES, axis=0, tiled=True)  36.7 us
  transfers between devices with their start and end apart: 50, of which 28 were waited for; matrix products, arithmetic and copies ran while one was open for 29% of the time, Pallas kernels for 10%

profile of v7, /device:TPU:13, one launch (start us, length us, event | category | flops | bytes accessed | tf_op | source)
XLA Modules:
  0.0 1131.4 jit_solution(5073387560707691035)
XLA Ops:
  11.0 7.2 mlp_chunks.1
  18.1 33.5 %all_to_all.35 = bf16[4,160,2048]{2,1,0:T(8,128)(2,1)} all-to-all(bf16[4,160,2048]{2,1,0:T(8,128)(2,1)S(1)} %get-tuple-element.55), channel_id=1, replica_groups=mesh['seq'=2,'g'=2,'h'=2,'k'=2,'c'=2] {'k','c'}, dimensions={0} | all-to-all | bytes 5242880 | tf_op jit(solution)/shard_map/all_to_all | solution.py:143
  54.5 5.8 all-to-all-start.1
  64.5 47.3 %all-to-all-done.1 = bf16[4,160,1024]{2,1,0:T(8,128)(2,1)S(1)} async-done(((bf16[4,160,1024]{2,1,0:T(8,128)(2,1)}), bf16[4,160,1024]{2,1,0:T(8,128)(2,1)S(1)}, u32[]{:S(2)}, u32[]{:S(2)}) %all-to-all-start.1) | async-done | bytes 1310752 | tf_op jit(solution)/shard_map/all_to_all | solution.py:143
  115.2 32.1 %collective-permute-done.2 = bf16[640,1024]{1,0:T(8,128)(2,1)} collective-permute-done((bf16[640,1024]{1,0:T(8,128)(2,1)S(1)}, bf16[640,1024]{1,0:T(8,128)(2,1)}, u32[]{:S(2)}, u32[]{:S(2)}) %collective-permute-start.2) | collective-permute-done | bytes 1310752 | tf_op jit(solution)/shard_map/ppermute | solution.py:105
  150.1 12.7 %all-gather.9.cloned.1.call-done = bf16[5120,1536]{1,0:T(8,128)(2,1)} async-done(((bf16[640,1536]{1,0:T(8,128)(2,1)}), bf16[5120,1536]{1,0:T(8,128)(2,1)}) %all-gather.9.cloned.1.call-update) | async-done | bytes 15728656 | tf_op jit(solution)/shard_map/all_gather | solution.py:450
  162.8 5.4 fusion.2
  179.1 9.7 collective-permute-done.8
  190.5 5.3 collective-permute-done.13
  207.1 36.7 %all-gather.11.cloned.1.call-done = bf16[640,1280]{1,0:T(8,128)(2,1)} async-done(((bf16[160,1280]{1,0:T(8,128)(2,1)}), bf16[640,1280]{1,0:T(8,128)(2,1)}) %all-gather.11.cloned.1.call-update) | async-done | bytes 1638416 | tf_op jit(solution)/shard_map/all_gather | solution.py:488
  243.8 6.0 fusion.6
  251.0 70.5 %collective-permute-done.5 = bf16[2,192,2560]{2,1,0:T(8,128)(2,1)} collective-permute-done((bf16[2,192,2560]{2,1,0:T(8,128)(2,1)S(1)}, bf16[2,192,2560]{2,1,0:T(8,128)(2,1)}, u32[]{:S(2)}, u32[]{:S(2)}) %collective-permute-start.5) | collective-permute-done | bytes 1966112 | tf_op jit(solution)/shard_map/ppermute | solution.py:98
  326.6 4.6 collective-permute-start.6
  348.2 43.4 %collective-permute-done.3 = bf16[640,2048]{1,0:T(8,128)(2,1)} collective-permute-done((bf16[640,2048]{1,0:T(8,128)(2,1)}, bf16[640,2048]{1,0:T(8,128)(2,1)}, u32[]{:S(2)}, u32[]{:S(2)}) %collective-permute-start.3) | collective-permute-done | bytes 2621472 | tf_op jit(solution)/shard_map/ppermute | solution.py:105
  398.9 6.0 pad_maximum_fusion
  404.9 7.0 copy.194
  411.9 7.8 collective-permute-done.4
  423.3 16.5 %attend.1 = (bf16[192,2560]{1,0:T(8,128)(2,1)}, f32[5,1,384]{2,1,0:T(1,128)S(1)}) custom-call(bf16[192,2560]{1,0:T(8,128)(2,1)S(1)} %copy-done.5, bf16[3072,256]{1,0:T(8,128)(2,1)S(1)} %get-tuple-element.171.key_ref, bf16[256,3072]{1,0:T(8,128)(2,1)S(1)} %copy.197.value_t_ref, f32[3072,384]{1,0:T(8,128)} %pad_maximum_fusion.2.bias_ref), custom_call_target="tpu_custom_call" | custom-call | flops 6039797760 | bytes 18087936 | tf_op jit(solution)/shard_map/attend/pallas_call | solution.py:308
  441.5 4.3 fusion.18
  445.8 4.7 fusion.22
  455.7 5.4 broadcast_in_dim.87
  476.0 8.6 collective-permute-done.16
  484.6 28.1 %collective-permute-done.17 = bf16[640,1024]{1,0:T(8,128)(2,1)S(1)} collective-permute-done((bf16[640,1024]{1,0:T(8,128)(2,1)S(1)}, bf16[640,1024]{1,0:T(8,128)(2,1)S(1)}, u32[]{:S(2)}, u32[]{:S(2)}) %collective-permute-start.17) | collective-permute-done | bytes 1310752 | tf_op jit(solution)/shard_map/ppermute | solution.py:105
  516.4 10.1 convolution_convert_fusion.6
  526.5 20.6 %fusion.95 = f32[1536,2048]{1,0:T(8,128)S(1)} fusion(bf16[1536,2560]{1,0:T(8,128)(2,1)} %all-gather.15.cloned.1.call-done, bf16[2560,2048]{1,0:T(8,128)(2,1)} %get-tuple-element.209), kind=kOutput, calls=%fused_computation.222 | convolution fusion | flops 16106127360 | bytes 30932992 | tf_op jit(solution)/shard_map/dot_general | solution.py:79
  547.1 4.8 copy-done.10
  555.8 12.2 %convolution_convert_fusion.3 = bf16[2560,1024]{1,0:T(8,128)(2,1)} fusion(bf16[1536,2560]{1,0:T(8,128)(2,1)} %bitcast.237, bf16[1536,1024]{1,0:T(8,128)(2,1)S(1)} %multiply_convert_fusion), kind=kOutput, calls=%fused_computation.40 | convolution fusion | flops 8055685120 | bytes 16252928 | tf_op jit(solution)/shard_map/dot_general | solution.py:79
  568.1 8.8 fusion.8
  580.3 9.8 convolution_convert_fusion.4
  591.8 6.8 collective-permute-done.18
  598.6 12.7 %add_convert_fusion = bf16[768,2560]{1,0:T(8,128)(2,1)S(1)} fusion(bf16[768,2560]{1,0:T(8,128)(2,1)} %collective-permute-done.18, bf16[768,2048]{1,0:T(8,128)(2,1)} %bitcast.260, bf16[2560,2048]{1,0:T(8,128)(2,1)} %get-tuple-element.209), kind=kOutput, calls=%fused_computation.4 | convolution fusion | flops 8058961920 | bytes 21495808 | tf_op jit(solution)/shard_map/dot_general | solution.py:79
  617.9 20.9 %collective-permute-done.20 = bf16[192,2560]{1,0:T(8,128)(2,1)} collective-permute-done((bf16[192,2560]{1,0:T(8,128)(2,1)}, bf16[192,2560]{1,0:T(8,128)(2,1)}, u32[]{:S(2)}, u32[]{:S(2)}) %collective-permute-start.20) | collective-permute-done | bytes 983072 | tf_op jit(solution)/shard_map/ppermute | solution.py:553
  639.7 12.4 %convolution_convert_fusion.2 = bf16[2560,1024]{1,0:T(8,128)(2,1)} fusion(bf16[1536,2560]{1,0:T(8,128)(2,1)} %all-gather.15.cloned.1.call-done, bf16[1536,2048]{1,0:T(8,128)(2,1)S(1)} %pad_maximum_fusion.1), kind=kOutput, calls=%fused_computation.39 | convolution fusion | flops 8055685120 | bytes 16252928 | tf_op jit(solution)/shard_map/dot_general | solution.py:79
  653.8 13.9 %convolution_convert_fusion.1 = bf16[2560,1024]{1,0:T(8,128)(2,1)} fusion(bf16[1536,2560]{1,0:T(8,128)(2,1)} %all-gather.15.cloned.1.call-done, bf16[1536,2048]{1,0:T(8,128)(2,1)} %copy-done.31), kind=kOutput, calls=%fused_computation.38 | convolution fusion | flops 8055685120 | bytes 16252928 | tf_op jit(solution)/shard_map/dot_general | solution.py:79
  667.7 8.2 collective-permute-done.21
  685.4 15.4 %collective-permute-done.22 = bf16[192,2560]{1,0:T(8,128)(2,1)} collective-permute-done((bf16[192,2560]{1,0:T(8,128)(2,1)}, bf16[192,2560]{1,0:T(8,128)(2,1)}, u32[]{:S(2)}, u32[]{:S(2)}) %collective-permute-start.22) | collective-permute-done | bytes 983072 | tf_op jit(solution)/shard_map/ppermute | solution.py:98
  707.9 5.5 fusion.16
  713.4 5.1 fusion.31
  720.3 7.4 all-to-all-start.2
  727.7 18.2 %collective-permute-done.23 = bf16[2,192,2560]{2,1,0:T(8,128)(2,1)} collective-permute-done((bf16[2,192,2560]{2,1,0:T(8,128)(2,1)}, bf16[2,192,2560]{2,1,0:T(8,128)(2,1)}, u32[]{:S(2)}, u32[]{:S(2)}) %collective-permute-start.23) | collective-permute-done | bytes 1966112 | tf_op jit(solution)/shard_map/ppermute | solution.py:98
  762.4 29.9 %attend_back.1 = (f32[192,2560]{1,0:T(8,128)}, f32[3072,512]{1,0:T(8,128)}) custom-call(bf16[192,2560]{1,0:T(8,128)(2,1)S(1)} %copy-done.6, bf16[192,2560]{1,0:T(8,128)(2,1)S(1)} %copy.205.grad_ref, bf16[3072,256]{1,0:T(8,128)(2,1)S(1)} %copy-done.3, bf16[256,3072]{1,0:T(8,128)(2,1)S(1)} %copy-done.4, bf16[3072,256]{1,0:T(8,128)(2,1)} %get-tuple-element.168.value_ref, ...), custom_call_target="tpu_custom_call" | custom-call | flops 15099494400 | bytes 22806528 | tf_op jit(solution)/shard_map/attend_back/pallas_call | solution.py:367
  792.3 3.9 convert_element_type.235
  814.5 16.5 %collective-permute-done.25 = bf16[2,192,512]{2,1,0:T(8,128)(2,1)} collective-permute-done((bf16[2,192,512]{2,1,0:T(8,128)(2,1)}, bf16[2,192,512]{2,1,0:T(8,128)(2,1)}, u32[]{:S(2)}, u32[]{:S(2)}) %collective-permute-start.25) | collective-permute-done | bytes 393248 | tf_op jit(solution)/shard_map/ppermute | solution.py:137
  846.7 13.6 %all-to-all-start.3 = ((bf16[8,192,704]{2,1,0:T(8,128)(2,1)}), bf16[8,192,704]{2,1,0:T(8,128)(2,1)}, u32[]{:S(2)}, u32[]{:S(2)}) async-start(bf16[8,192,704]{2,1,0:T(8,128)(2,1)} %maximum_bitcast_fusion), calls=%async_computation.4 | async-start | bytes 4718592 | tf_op jit(solution)/shard_map/all_to_all | solution.py:143
  860.3 13.5 %convolution_convert_fusion = bf16[1536,2560]{1,0:T(8,128)(2,1)} fusion(bf16[1536,1024]{1,0:T(8,128)(2,1)} %copy-done.46, bf16[2560,1024]{1,0:T(8,128)(2,1)} %copy-done.36), kind=kOutput, calls=%fused_computation | convolution fusion | flops 8056995840 | bytes 16252928 | tf_op jit(solution)/shard_map/dot_general | solution.py:79
  873.8 14.0 %all-to-all-done.3 = bf16[8,192,704]{2,1,0:T(8,128)(2,1)} async-done(((bf16[8,192,704]{2,1,0:T(8,128)(2,1)}), bf16[8,192,704]{2,1,0:T(8,128)(2,1)}, u32[]{:S(2)}, u32[]{:S(2)}) %all-to-all-start.3) | async-done | bytes 2162720 | tf_op jit(solution)/shard_map/all_to_all | solution.py:143
  887.8 4.6 all-to-all-start.4
  894.8 5.9 fusion.96
  900.7 6.4 convolution_convert_fusion.5
  907.1 3.9 fusion.24
  913.0 6.1 copy.220
  919.1 10.5 all-to-all-start.5
  933.6 28.1 %collective-permute-done.33.refs_2_ = bf16[4,160,1024]{2,1,0:T(8,128)(2,1)} collective-permute-done((bf16[4,160,1024]{2,1,0:T(8,128)(2,1)S(1)}, bf16[4,160,1024]{2,1,0:T(8,128)(2,1)}, u32[]{:S(2)}, u32[]{:S(2)}) %collective-permute-start.33) | collective-permute-done | bytes 1310752 | tf_op jit(solution)/shard_map/ppermute | solution.py:90
  961.8 17.7 %mlp_adam.3 = (f32[3,160,7680]{2,1,0:T(8,128)}, f32[3,160,7680]{2,1,0:T(8,128)}, f32[3,160,7680]{2,1,0:T(8,128)}, f32[160,1]{1,0:T(8,128)}) custom-call(s32[1]{0:T(128)} %bitcast.4.refs_0_, bf16[4,160,1024]{2,1,0:T(8,128)(2,1)S(1)} %all-to-all-done.2.refs_1_, bf16[4,160,1024]{2,1,0:T(8,128)(2,1)} %collective-permute-done.33.refs_2_, ...), custom_call_target="tpu_custom_call" | custom-call | flops 24576000 | bytes 31948800 | tf_op jit(solution)/shard_map/mlp_adam/pallas_call | solution.py:241
  982.0 7.3 fusion
  989.3 27.4 %all-to-all-done.5 = bf16[16,160,704]{2,1,0:T(8,128)(2,1)} async-done(((bf16[16,160,704]{2,1,0:T(8,128)(2,1)}), bf16[16,160,704]{2,1,0:T(8,128)(2,1)}, u32[]{:S(2)}, u32[]{:S(2)}) %all-to-all-start.5) | async-done | bytes 3604512 | tf_op jit(solution)/shard_map/all_to_all | solution.py:143
  1016.7 4.0 reduce_sum.111
  1022.0 7.9 fusion.25
  1046.3 18.6 %mlp_adam.4 = (f32[3,160,7680]{2,1,0:T(8,128)}, f32[3,160,7680]{2,1,0:T(8,128)}, f32[3,160,7680]{2,1,0:T(8,128)}, f32[160,1]{1,0:T(8,128)S(1)}) custom-call(s32[1]{0:T(128)} %bitcast.4.refs_0_, bf16[4,160,1024]{2,1,0:T(8,128)(2,1)S(1)} %all-to-all-done.4.refs_1_, ...), custom_call_target="tpu_custom_call", output_to_operand_aliasing={{0}: (7, {}), {1}: (8, {}), {2}: (9, {})} | custom-call | flops 24576000 | bytes 31948800 | tf_op jit(solution)/shard_map/mlp_adam/pallas_call | solution.py:241
  1069.5 7.5 multiply_subtract_fusion
  1082.3 5.8 multiply_subtract_fusion.2
  1088.1 11.2 collective-permute-done.31.refs_2_
  1099.4 18.4 %mlp_adam.5 = (f32[3,160,7680]{2,1,0:T(8,128)}, f32[3,160,7680]{2,1,0:T(8,128)}, f32[3,160,7680]{2,1,0:T(8,128)}, f32[160,1]{1,0:T(8,128)S(1)}) custom-call(s32[1]{0:T(128)} %bitcast.4.refs_0_, bf16[4,160,1024]{2,1,0:T(8,128)(2,1)S(1)} %all-to-all-done.6.refs_1_, ...), custom_call_target="tpu_custom_call", output_to_operand_aliasing={{0}: (7, {}), {1}: (8, {}), {2}: (9, {})} | custom-call | flops 24576000 | bytes 31948800 | tf_op jit(solution)/shard_map/mlp_adam/pallas_call | solution.py:241
  1118.5 5.6 fusion.50
  (385 shorter events, 225.6 us)
Async XLA Ops:
  7.2 47.0 %all-gather.7.cloned.1.call-start = ((), (), s32[]{:S(2)}) async-start(), calls=%async_computation.11 | async-start | bytes 2457600 | tf_op jit(solution)/shard_map/all_gather | solution.py:454
  10.8 151.9 %all-gather.9.cloned.1.call-start = ((), (), s32[]{:S(2)}) async-start(), calls=%async_computation.12 | async-start | bytes 17694720 | tf_op jit(solution)/shard_map/all_gather | solution.py:450
  54.2 59.5 %collective-permute-start = (bf16[192,2560]{1,0:T(8,128)(2,1)S(1)}, bf16[192,2560]{1,0:T(8,128)(2,1)}, u32[]{:S(2)}, u32[]{:S(2)}) collective-permute-start(bf16[192,2560]{1,0:T(8,128)(2,1)S(1)} %bitcast.259), channel_id=1, source_target_pairs={{0,2},{2,0},{1,3},{3,1},{4,6},{6,4},{5,7},{7,5},{8,10},{10,8},{9,1... | collective-permute-start | bytes 2949128 | tf_op jit(solution)/shard_map/ppermute | solution.py:98
  54.5 57.3 %all-to-all-start.1 = ((bf16[4,160,1024]{2,1,0:T(8,128)(2,1)}), bf16[4,160,1024]{2,1,0:T(8,128)(2,1)S(1)}, u32[]{:S(2)}, u32[]{:S(2)}) async-start(bf16[4,160,1024]{2,1,0:T(8,128)(2,1)} %get-tuple-element.57), calls=%async_computation.1 | async-start | bytes 2621440 | tf_op jit(solution)/shard_map/all_to_all | solution.py:143
  60.3 183.4 %all-gather.11.cloned.1.call-start = ((), (), s32[]{:S(2)}) async-start(), calls=%async_computation.13 | async-start | bytes 2048000 | tf_op jit(solution)/shard_map/all_gather | solution.py:488
  60.6 86.8 %collective-permute-start.1 = (bf16[640,2048]{1,0:T(8,128)(2,1)}, bf16[640,2048]{1,0:T(8,128)(2,1)}, u32[]{:S(2)}, u32[]{:S(2)}) collective-permute-start(bf16[640,2048]{1,0:T(8,128)(2,1)} %bitcast.228), channel_id=1, source_target_pairs={{0,4},{4,8},{8,12},{12,0},{1,5},{5,9},{9,13},{13,1},{2,6},{6,10},{... | collective-permute-start | bytes 7864328 | tf_op jit(solution)/shard_map/ppermute | solution.py:105
  111.8 35.5 %collective-permute-start.2 = (bf16[640,1024]{1,0:T(8,128)(2,1)S(1)}, bf16[640,1024]{1,0:T(8,128)(2,1)}, u32[]{:S(2)}, u32[]{:S(2)}) collective-permute-start(bf16[640,1024]{1,0:T(8,128)(2,1)S(1)} %bitcast.248), channel_id=1, source_target_pairs={{0,4},{4,8},{8,12},{12,0},{1,5},{5,9},{9,13},{13,1},{2,6},{6,10},{... | collective-permute-start | bytes 3932168 | tf_op jit(solution)/shard_map/ppermute | solution.py:105
  113.7 54.5 %copy-start.65 = (f32[192]{0:T(256)}, f32[192]{0:T(256)S(1)}, u32[]{:S(2)}) copy-start(f32[192]{0:T(256)S(1)} %get-tuple-element.152) | copy-start | bytes 2308
  113.7 54.5 %copy-start.76 = (f32[128]{0:T(128)}, f32[128]{0:T(128)S(1)}, u32[]{:S(2)}) copy-start(f32[128]{0:T(128)S(1)} %multiply_exponential_fusion) | copy-start | bytes 1540
  171.0 6.8 collective-permute-start.7
  172.0 18.5 %collective-permute-start.12 = (bf16[192,512]{1,0:T(8,128)(2,1)}, bf16[192,512]{1,0:T(8,128)(2,1)S(1)}, u32[]{:S(2)}, u32[]{:S(2)}) collective-permute-start(bf16[192,512]{1,0:T(8,128)(2,1)} %pad_maximum_fusion.13), channel_id=1, source_target_pairs={{0,20},{2,22},{4,16},{6,18},{16,4},{18,6},{20,0},{22,2},{1,21},{3,... | collective-permute-start | bytes 589832 | tf_op jit(solution)/shard_map/ppermute | solution.py:125
  173.2 17.3 %collective-permute-start.11 = (bf16[192,512]{1,0:T(8,128)(2,1)}, bf16[192,512]{1,0:T(8,128)(2,1)S(1)}, u32[]{:S(2)}, u32[]{:S(2)}) collective-permute-start(bf16[192,512]{1,0:T(8,128)(2,1)} %pad_maximum_fusion.13), channel_id=1, source_target_pairs={{0,18},{2,16},{4,22},{6,20},{16,2},{18,0},{20,6},{22,4},{1,19},{3,... | collective-permute-start | bytes 589832 | tf_op jit(solution)/shard_map/ppermute | solution.py:125
  173.7 16.8 %collective-permute-start.10 = (bf16[192,512]{1,0:T(8,128)(2,1)}, bf16[192,512]{1,0:T(8,128)(2,1)S(1)}, u32[]{:S(2)}, u32[]{:S(2)}) collective-permute-start(bf16[192,512]{1,0:T(8,128)(2,1)} %pad_maximum_fusion.13), channel_id=1, source_target_pairs={{0,16},{2,18},{4,20},{6,22},{16,0},{18,2},{20,4},{22,6},{1,17},{3,... | collective-permute-start | bytes 589832 | tf_op jit(solution)/shard_map/ppermute | solution.py:125
  174.6 14.3 %collective-permute-start.9 = (bf16[192,512]{1,0:T(8,128)(2,1)}, bf16[192,512]{1,0:T(8,128)(2,1)S(1)}, u32[]{:S(2)}, u32[]{:S(2)}) collective-permute-start(bf16[192,512]{1,0:T(8,128)(2,1)} %pad_maximum_fusion.13), channel_id=1, source_target_pairs={{0,6},{2,4},{4,2},{6,0},{16,22},{18,20},{20,18},{22,16},{1,7},{3,5... | collective-permute-start | bytes 589832 | tf_op jit(solution)/shard_map/ppermute | solution.py:125
  177.8 11.0 collective-permute-start.8
  188.8 7.0 collective-permute-start.13
  195.9 5.5 collective-permute-start.14
  205.0 38.9 %copy-start.51 = (bf16[192,4,4,160]{0,3,2,1:T(8,128)(2,1)S(1)}, bf16[192,4,4,160]{0,3,2,1:T(8,128)(2,1)}, u32[]{:S(2)}) copy-start(bf16[192,4,4,160]{0,3,2,1:T(8,128)(2,1)} %copy.190) | copy-start | bytes 2949124
  207.0 234.4 %all-gather.13.cloned.1.call-start = ((), (), s32[]{:S(2)}) async-start(), calls=%async_computation.14 | async-start | bytes 14745600 | tf_op jit(solution)/shard_map/all_gather | solution.py:450
  243.8 282.7 %all-gather.15.cloned.1.call-start = ((), (), s32[]{:S(2)}) async-start(), calls=%async_computation.15 | async-start | bytes 8847360 | tf_op jit(solution)/shard_map/all_gather | solution.py:516
  249.8 71.7 %collective-permute-start.5 = (bf16[2,192,2560]{2,1,0:T(8,128)(2,1)S(1)}, bf16[2,192,2560]{2,1,0:T(8,128)(2,1)}, u32[]{:S(2)}, u32[]{:S(2)}) collective-permute-start(bf16[2,192,2560]{2,1,0:T(8,128)(2,1)S(1)} %pad_maximum_fusion.8), channel_id=1, source_target_pairs={{0,16},{16,0},{1,17},{17,1},{2,18},{18,2},{3,19},{19,3},{4,20},{20... | collective-permute-start | bytes 5898248 | tf_op jit(solution)/shard_map/ppermute | solution.py:98
  326.6 68.6 %collective-permute-start.6 = (bf16[2,2,192,2560]{3,2,1,0:T(8,128)(2,1)}, bf16[2,2,192,2560]{3,2,1,0:T(8,128)(2,1)}, u32[]{:S(2)}, u32[]{:S(2)}) collective-permute-start(bf16[2,2,192,2560]{3,2,1,0:T(8,128)(2,1)} %pad_maximum_fusion.3), channel_id=1, source_target_pairs={{0,1},{1,0},{2,3},{3,2},{4,5},{5,4},{6,7},{7,6},{8,9},{9,8},{10,11... | collective-permute-start | bytes 11796488 | tf_op jit(solution)/shard_map/ppermute | solution.py:98
  331.5 60.1 %collective-permute-start.3 = (bf16[640,2048]{1,0:T(8,128)(2,1)}, bf16[640,2048]{1,0:T(8,128)(2,1)}, u32[]{:S(2)}, u32[]{:S(2)}) collective-permute-start(bf16[640,2048]{1,0:T(8,128)(2,1)} %collective-permute-done.1), channel_id=1, source_target_pairs={{0,4},{4,8},{8,12},{12,0},{1,5},{5,9},{9,13},{13,1},{2,6},{6,10},{... | collective-permute-start | bytes 7864328 | tf_op jit(solution)/shard_map/ppermute | solution.py:105
  340.5 79.2 %collective-permute-start.4 = (bf16[640,1024]{1,0:T(8,128)(2,1)}, bf16[640,1024]{1,0:T(8,128)(2,1)}, u32[]{:S(2)}, u32[]{:S(2)}) collective-permute-start(bf16[640,1024]{1,0:T(8,128)(2,1)} %collective-permute-done.2), channel_id=1, source_target_pairs={{0,4},{4,8},{8,12},{12,0},{1,5},{5,9},{9,13},{13,1},{2,6},{6,10},{... | collective-permute-start | bytes 3932168 | tf_op jit(solution)/shard_map/ppermute | solution.py:105
  345.9 76.2 %copy-start.2 = (bf16[3072,256]{1,0:T(8,128)(2,1)}, bf16[3072,256]{1,0:T(8,128)(2,1)S(1)}, u32[]{:S(2)}) copy-start(bf16[3072,256]{1,0:T(8,128)(2,1)S(1)} %get-tuple-element.171.key_ref) | copy-start | bytes 4718596
  348.2 46.9 %copy-start.19 = (bf16[1,2,192,2560]{3,2,1,0:T(8,128)(2,1)S(1)}, bf16[1,2,192,2560]{3,2,1,0:T(8,128)(2,1)}, u32[]{:S(2)}) copy-start(bf16[1,2,192,2560]{3,2,1,0:T(8,128)(2,1)} %copy-done.18) | copy-start | bytes 5898244
  348.2 46.9 %copy-start.21 = (bf16[1,2,192,2560]{3,2,1,0:T(8,128)(2,1)S(1)}, bf16[1,2,192,2560]{3,2,1,0:T(8,128)(2,1)}, u32[]{:S(2)}) copy-start(bf16[1,2,192,2560]{3,2,1,0:T(8,128)(2,1)} %copy-done.20) | copy-start | bytes 5898244
  395.1 58.2 %collective-permute-start.15 = (bf16[640,1024]{1,0:T(8,128)(2,1)}, bf16[640,1024]{1,0:T(8,128)(2,1)}, u32[]{:S(2)}, u32[]{:S(2)}) collective-permute-start(bf16[640,1024]{1,0:T(8,128)(2,1)} %get-tuple-element.179), channel_id=1, source_target_pairs={{0,4},{4,8},{8,12},{12,0},{1,5},{5,9},{9,13},{13,1},{2,6},{6,10},{... | collective-permute-start | bytes 3932168 | tf_op jit(solution)/shard_map/ppermute | solution.py:105
  453.3 267.0 %reduce-scatter.5.cloned.1.call-start = ((), (), s32[]{:S(2)}) async-start(), calls=%async_computation.16 | async-start | bytes 6553600 | tf_op jit(solution)/shard_map/reduce_scatter | solution.py:522
  453.4 31.3 %collective-permute-start.16 = (bf16[640,1024]{1,0:T(8,128)(2,1)}, bf16[640,1024]{1,0:T(8,128)(2,1)S(1)}, u32[]{:S(2)}, u32[]{:S(2)}) collective-permute-start(bf16[640,1024]{1,0:T(8,128)(2,1)} %collective-permute-done.4), channel_id=1, source_target_pairs={{0,4},{4,8},{8,12},{12,0},{1,5},{5,9},{9,13},{13,1},{2,6},{6,10},{... | collective-permute-start | bytes 3932168 | tf_op jit(solution)/shard_map/ppermute | solution.py:105
  453.7 59.1 %collective-permute-start.17 = (bf16[640,1024]{1,0:T(8,128)(2,1)S(1)}, bf16[640,1024]{1,0:T(8,128)(2,1)S(1)}, u32[]{:S(2)}, u32[]{:S(2)}) collective-permute-start(bf16[640,1024]{1,0:T(8,128)(2,1)S(1)} %copy-done.50), channel_id=1, source_target_pairs={{0,4},{4,8},{8,12},{12,0},{1,5},{5,9},{9,13},{13,1},{2,6},{6,10},{... | collective-permute-start | bytes 3932168 | tf_op jit(solution)/shard_map/ppermute | solution.py:105
  468.2 48.2 %slice-start.3 = ((s8[7864320]{0:T(1024)(128)(4,1)}), s8[4194304]{0:T(1024)(128)(4,1)S(1)}, s32[]{:S(2)}) async-start(s8[7864320]{0:T(1024)(128)(4,1)} %bitcast.238), calls=%async_computation.24 | async-start | bytes 8388608
  473.4 43.0 %slice-start.4 = ((s8[7864320]{0:T(1024)(128)(4,1)}), s8[3670016]{0:T(1024)(128)(4,1)S(1)}, s32[]{:S(2)}) async-start(s8[7864320]{0:T(1024)(128)(4,1)} %bitcast.238), calls=%async_computation.25 | async-start | bytes 7340032
  568.1 305.8 %reduce-scatter.9.cloned.1.call-start = ((), (), s32[]{:S(2)}) async-start(), calls=%async_computation.19 | async-start | bytes 6553600 | tf_op jit(solution)/shard_map/reduce_scatter | solution.py:522
  590.1 8.5 collective-permute-start.18
  614.7 24.2 %collective-permute-start.20 = (bf16[192,2560]{1,0:T(8,128)(2,1)}, bf16[192,2560]{1,0:T(8,128)(2,1)}, u32[]{:S(2)}, u32[]{:S(2)}) collective-permute-start(bf16[192,2560]{1,0:T(8,128)(2,1)} %get-tuple-element.163), channel_id=1, source_target_pairs={{0,16},{2,18},{16,0},{18,2},{1,17},{3,19},{17,1},{19,3},{4,20},{6,... | collective-permute-start | bytes 2949128 | tf_op jit(solution)/shard_map/ppermute | solution.py:553
  616.7 23.0 %collective-permute-start.19 = (bf16[192,2560]{1,0:T(8,128)(2,1)}, bf16[192,2560]{1,0:T(8,128)(2,1)}, u32[]{:S(2)}, u32[]{:S(2)}) collective-permute-start(bf16[192,2560]{1,0:T(8,128)(2,1)} %get-tuple-element.165), channel_id=1, source_target_pairs={{0,2},{2,0},{16,18},{18,16},{1,3},{3,1},{17,19},{19,17},{4,6},{6,4... | collective-permute-start | bytes 2949128 | tf_op jit(solution)/shard_map/ppermute | solution.py:553
  617.9 21.8 %copy-start.31 = (bf16[1536,2048]{1,0:T(8,128)(2,1)}, bf16[1536,2048]{1,0:T(8,128)(2,1)S(1)}, u32[]{:S(2)}) copy-start(bf16[1536,2048]{1,0:T(8,128)(2,1)S(1)} %pad_maximum_fusion.1) | copy-start | bytes 18874372
  652.1 248.6 %all-gather.17.cloned.1.call-start = ((), (), s32[]{:S(2)}) async-start(), calls=%async_computation.18 | async-start | bytes 8847360 | tf_op jit(solution)/shard_map/all_gather | solution.py:526
  652.8 389.7 %reduce-scatter.11.cloned.1.call-start = ((), (), s32[]{:S(2)}) async-start(), calls=%async_computation.20 | async-start | bytes 6553600 | tf_op jit(solution)/shard_map/reduce_scatter | solution.py:522
  653.3 22.6 %collective-permute-start.21 = (bf16[192,2560]{1,0:T(8,128)(2,1)S(1)}, bf16[192,2560]{1,0:T(8,128)(2,1)S(1)}, u32[]{:S(2)}, u32[]{:S(2)}) collective-permute-start(bf16[192,2560]{1,0:T(8,128)(2,1)S(1)} %copy-done.55), channel_id=1, source_target_pairs={{0,18},{2,16},{16,2},{18,0},{1,19},{3,17},{17,3},{19,1},{4,22},{6,... | collective-permute-start | bytes 2949128 | tf_op jit(solution)/shard_map/ppermute | solution.py:553
  679.6 21.3 %collective-permute-start.22 = (bf16[192,2560]{1,0:T(8,128)(2,1)}, bf16[192,2560]{1,0:T(8,128)(2,1)}, u32[]{:S(2)}, u32[]{:S(2)}) collective-permute-start(bf16[192,2560]{1,0:T(8,128)(2,1)} %fusion.47), channel_id=1, source_target_pairs={{0,2},{2,0},{1,3},{3,1},{4,6},{6,4},{5,7},{7,5},{8,10},{10,8},{9,1... | collective-permute-start | bytes 2949128 | tf_op jit(solution)/shard_map/ppermute | solution.py:98
  704.5 41.4 %collective-permute-start.23 = (bf16[2,192,2560]{2,1,0:T(8,128)(2,1)}, bf16[2,192,2560]{2,1,0:T(8,128)(2,1)}, u32[]{:S(2)}, u32[]{:S(2)}) collective-permute-start(bf16[2,192,2560]{2,1,0:T(8,128)(2,1)} %pad_maximum_fusion.9), channel_id=1, source_target_pairs={{0,16},{16,0},{1,17},{17,1},{2,18},{18,2},{3,19},{19,3},{4,20},{20... | collective-permute-start | bytes 5898248 | tf_op jit(solution)/shard_map/ppermute | solution.py:98
  720.3 25.6 %copy-start.26 = (bf16[1,192,2560]{2,1,0:T(8,128)(2,1)S(1)}, bf16[1,192,2560]{2,1,0:T(8,128)(2,1)}, u32[]{:S(2)}) copy-start(bf16[1,192,2560]{2,1,0:T(8,128)(2,1)} %copy-done.25) | copy-start | bytes 2949124
  720.3 25.6 %copy-start.28 = (bf16[1,192,2560]{2,1,0:T(8,128)(2,1)S(1)}, bf16[1,192,2560]{2,1,0:T(8,128)(2,1)}, u32[]{:S(2)}) copy-start(bf16[1,192,2560]{2,1,0:T(8,128)(2,1)} %copy-done.27) | copy-start | bytes 2949124
  720.3 29.7 %all-to-all-start.2 = ((bf16[4,160,1024]{2,1,0:T(8,128)(2,1)}), bf16[4,160,1024]{2,1,0:T(8,128)(2,1)S(1)}, u32[]{:S(2)}, u32[]{:S(2)}) async-start(bf16[4,160,1024]{2,1,0:T(8,128)(2,1)} %bitcast.266), calls=%async_computation.3 | async-start | bytes 2621440 | tf_op jit(solution)/shard_map/all_to_all | solution.py:143
  799.2 6.9 collective-permute-start.24
  802.7 39.1 %collective-permute-start.29 = (bf16[2,2,192,2560]{3,2,1,0:T(8,128)(2,1)}, bf16[2,2,192,2560]{3,2,1,0:T(8,128)(2,1)}, u32[]{:S(2)}, u32[]{:S(2)}) collective-permute-start(bf16[2,2,192,2560]{3,2,1,0:T(8,128)(2,1)} %pad_maximum_fusion.4), channel_id=1, source_target_pairs={{0,1},{1,0},{2,3},{3,2},{4,5},{5,4},{6,7},{7,6},{8,9},{9,8},{10,11... | collective-permute-start | bytes 11796488 | tf_op jit(solution)/shard_map/ppermute | solution.py:90
  809.6 21.4 %collective-permute-start.25 = (bf16[2,192,512]{2,1,0:T(8,128)(2,1)}, bf16[2,192,512]{2,1,0:T(8,128)(2,1)}, u32[]{:S(2)}, u32[]{:S(2)}) collective-permute-start(bf16[2,192,512]{2,1,0:T(8,128)(2,1)} %get-tuple-element.186), channel_id=1, source_target_pairs={{0,2},{2,0},{16,18},{18,16},{1,3},{3,1},{17,19},{19,17},{4,6},{6,4... | collective-permute-start | bytes 1179656 | tf_op jit(solution)/shard_map/ppermute | solution.py:137
  809.9 21.1 %collective-permute-start.27 = (bf16[2,192,512]{2,1,0:T(8,128)(2,1)}, bf16[2,192,512]{2,1,0:T(8,128)(2,1)}, u32[]{:S(2)}, u32[]{:S(2)}) collective-permute-start(bf16[2,192,512]{2,1,0:T(8,128)(2,1)} %get-tuple-element.187), channel_id=1, source_target_pairs={{0,18},{2,16},{16,2},{18,0},{1,19},{3,17},{17,3},{19,1},{4,22},{6,... | collective-permute-start | bytes 1179656 | tf_op jit(solution)/shard_map/ppermute | solution.py:137
  812.3 19.6 %collective-permute-start.26 = (bf16[2,192,512]{2,1,0:T(8,128)(2,1)}, bf16[2,192,512]{2,1,0:T(8,128)(2,1)}, u32[]{:S(2)}, u32[]{:S(2)}) collective-permute-start(bf16[2,192,512]{2,1,0:T(8,128)(2,1)} %get-tuple-element.188), channel_id=1, source_target_pairs={{0,16},{2,18},{16,0},{18,2},{1,17},{3,19},{17,1},{19,3},{4,20},{6,... | collective-permute-start | bytes 1179656 | tf_op jit(solution)/shard_map/ppermute | solution.py:137
  814.5 21.1 %copy-start.53 = (f32[192,128]{0,1:T(8,128)S(1)}, f32[192,128]{0,1:T(8,128)}, u32[]{:S(2)}) copy-start(f32[192,128]{0,1:T(8,128)} %copy-done.52) | copy-start | bytes 294916
  814.5 21.1 %copy-start.57 = (f32[192,128]{0,1:T(8,128)S(1)}, f32[192,128]{0,1:T(8,128)}, u32[]{:S(2)}) copy-start(f32[192,128]{0,1:T(8,128)} %copy.208) | copy-start | bytes 294916
  833.4 5.9 collective-permute-start.28
  846.7 41.1 %all-to-all-start.3 = ((bf16[8,192,704]{2,1,0:T(8,128)(2,1)}), bf16[8,192,704]{2,1,0:T(8,128)(2,1)}, u32[]{:S(2)}, u32[]{:S(2)}) async-start(bf16[8,192,704]{2,1,0:T(8,128)(2,1)} %maximum_bitcast_fusion), calls=%async_computation.4 | async-start | bytes 4718592 | tf_op jit(solution)/shard_map/all_to_all | solution.py:143
  887.8 25.2 %all-to-all-start.4 = ((bf16[4,160,1024]{2,1,0:T(8,128)(2,1)}), bf16[4,160,1024]{2,1,0:T(8,128)(2,1)S(1)}, u32[]{:S(2)}, u32[]{:S(2)}) async-start(bf16[4,160,1024]{2,1,0:T(8,128)(2,1)} %bitcast.263), calls=%async_computation.7 | async-start | bytes 2621440 | tf_op jit(solution)/shard_map/all_to_all | solution.py:143
  892.4 226.1 %reduce-scatter.7.cloned.1.call-start = ((), (), s32[]{:S(2)}) async-start(), calls=%async_computation.17 | async-start | bytes 8847360 | tf_op jit(solution)/shard_map/reduce_scatter | solution.py:640
  919.1 97.6 %all-to-all-start.5 = ((bf16[16,160,704]{2,1,0:T(8,128)(2,1)}), bf16[16,160,704]{2,1,0:T(8,128)(2,1)}, u32[]{:S(2)}, u32[]{:S(2)}) async-start(bf16[16,160,704]{2,1,0:T(8,128)(2,1)} %bitcast.224), calls=%async_computation.8 | async-start | bytes 7864320 | tf_op jit(solution)/shard_map/all_to_all | solution.py:143
  929.5 32.2 %copy-start.1 = (f32[160,1]{1,0:T(8,128)S(1)}, f32[160,1]{1,0:T(8,128)}, u32[]{:S(2)}) copy-start(f32[160,1]{1,0:T(8,128)} %copy-done) | copy-start | bytes 1924
  929.6 32.2 %collective-permute-start.33 = (bf16[4,160,1024]{2,1,0:T(8,128)(2,1)S(1)}, bf16[4,160,1024]{2,1,0:T(8,128)(2,1)}, u32[]{:S(2)}, u32[]{:S(2)}) collective-permute-start(bf16[4,160,1024]{2,1,0:T(8,128)(2,1)S(1)} %all-to-all-done.2.refs_1_), channel_id=1, source_target_pairs={{0,16},{16,0},{1,17},{17,1},{2,18},{18,2},{3,19},{19,3},{4,20},{20... | collective-permute-start | bytes 3932168 | tf_op jit(solution)/shard_map/ppermute | solution.py:90
  979.5 66.8 %collective-permute-start.32 = (bf16[4,160,1024]{2,1,0:T(8,128)(2,1)S(1)}, bf16[4,160,1024]{2,1,0:T(8,128)(2,1)}, u32[]{:S(2)}, u32[]{:S(2)}) collective-permute-start(bf16[4,160,1024]{2,1,0:T(8,128)(2,1)S(1)} %all-to-all-done.4.refs_1_), channel_id=1, source_target_pairs={{0,16},{16,0},{1,17},{17,1},{2,18},{18,2},{3,19},{19,3},{4,20},{20... | collective-permute-start | bytes 3932168 | tf_op jit(solution)/shard_map/ppermute | solution.py:90
  1020.7 44.2 %collective-permute-start.30 = (bf16[4,160,704]{2,1,0:T(8,128)(2,1)}, bf16[4,160,704]{2,1,0:T(8,128)(2,1)}, u32[]{:S(2)}, u32[]{:S(2)}) collective-permute-start(bf16[4,160,704]{2,1,0:T(8,128)(2,1)} %reduce_sum.111), channel_id=1, source_target_pairs={{0,16},{16,0},{1,17},{17,1},{2,18},{18,2},{3,19},{19,3},{4,20},{20... | collective-permute-start | bytes 2703368 | tf_op jit(solution)/shard_map/ppermute | solution.py:98
  1042.5 26.7 %all-to-all-start.6 = ((bf16[4,160,1024]{2,1,0:T(8,128)(2,1)}), bf16[4,160,1024]{2,1,0:T(8,128)(2,1)S(1)}, u32[]{:S(2)}, u32[]{:S(2)}) async-start(bf16[4,160,1024]{2,1,0:T(8,128)(2,1)} %bitcast.262), calls=%async_computation.10 | async-start | bytes 2621440 | tf_op jit(solution)/shard_map/all_to_all | solution.py:143
  1069.2 30.1 %collective-permute-start.31 = (bf16[4,160,1024]{2,1,0:T(8,128)(2,1)S(1)}, bf16[4,160,1024]{2,1,0:T(8,128)(2,1)S(1)}, u32[]{:S(2)}, u32[]{:S(2)}) collective-permute-start(bf16[4,160,1024]{2,1,0:T(8,128)(2,1)S(1)} %all-to-all-done.6.refs_1_), channel_id=1, source_target_pairs={{0,16},{16,0},{1,17},{17,1},{2,18},{18,2},{3,19},{19,3},{4,20},{20... | collective-permute-start | bytes 3932168 | tf_op jit(solution)/shard_map/ppermute | solution.py:90
  (71 other events, 360.5 us)
Sparse Core Ops, SparseCore 0:
  11.0 43.1 all-gather.6
  56.0 106.7 all-gather.8
  207.1 36.5 all-gather.10
  245.5 103.6 all-gather.12
  453.4 54.5 all-gather.14
  568.2 96.9 reduce-scatter.4
  668.1 94.2 reduce-scatter.8
  764.3 62.2 all-gather.16
  828.9 97.2 reduce-scatter.10
  929.5 93.7 reduce-scatter.6

commit v8 on v7

--- a/solution.py
+++ b/solution.py
@@ -451,9 +451,14 @@
         return weight.reshape(sides, owner_count * own_rows, half)
 
     gate_up_blocks = [to_members(gate_up_chunks)]
-    qkv_rows = lax.all_gather(own_half(low(qkv_low * gain_one)), PLANES, axis=0, tiled=True)
-    qkv_halves = gathered_group(after(qkv_rows, gate_up_blocks[0]))
-    gate_up_blocks.append(next_plane(after(gate_up_blocks[0], qkv_rows)))
+    plane_rows = [own_half(low(qkv_low * gain_one)), own_half(low(weight_out))]
+    split = plane_rows[0].shape[1]
+    plane_rows = jnp.concatenate(plane_rows, axis=1)
+    plane_rows = lax.all_gather(plane_rows, PLANES, axis=0, tiled=True)
+    plane_rows = after(plane_rows, gate_up_blocks[0])
+    qkv_halves = gathered_group(plane_rows[:, :split])
+    out_halves = gathered_group(plane_rows[:, split:])
+    gate_up_blocks.append(next_plane(after(gate_up_blocks[0], plane_rows)))
     down_blocks = [to_members(down_chunks)]
     down_blocks.append(next_plane(down_blocks[0]))
     incoming_columns = doubled(incoming, "k", 1, 0)
@@ -484,8 +489,6 @@
     window_kv = spread_ring(jnp.concatenate([key_low, value_low], axis=1))
     window_kv = doubled(window_kv, "c", 1, 1)
     window_kv = window_kv.reshape(SEQ_LEN, 2 * HEAD_DIM)
-    out_rows = own_half(low(after(weight_out, window_kv)))
-    out_halves = gathered_group(lax.all_gather(out_rows, PLANES, axis=0, tiled=True))
     gate_up_blocks.append(next_plane(after(gate_up_blocks[1], projected)))
     for _ in range(planes - 4):
         gate_up_blocks.append(next_plane(gate_up_blocks[-1]))
@@ -496,17 +499,18 @@
         down_blocks.append(next_plane(down_blocks[-1]))
     gate_up_own = joined_planes(gate_up_blocks)
     down_own = joined_planes(down_blocks)
-    incoming_sides = doubled(after(incoming_columns, projected), "seq", 1, 0)
+    incoming_sides = doubled(after(incoming_columns, window_kv), "seq", 1, 0)
     query_pre = projected[:, :width].reshape(tok_rows, head_count, HEAD_DIM)
     queries = low(rotate(query_pre, cosine[:, None, :], sine[:, None, :]) * query_scale)
     incoming_all = doubled(incoming_sides, "c", 1, incoming_sides.ndim - 2)
     incoming_all = incoming_all.reshape(sides * members * tok_rows, width)
-    queries = after(queries.reshape(tok_rows, width), gate_up_blocks[2], down_blocks[2], incoming_all)
+    queries = after(queries.reshape(tok_rows, width), gate_up_blocks[2], down_blocks[2])
     keys_win = window_kv[:, :HEAD_DIM]
     values_win = window_kv[:, HEAD_DIM:]
     bias = jnp.where(allowed.T, 0.0, MASKED_SCORE)
     bias = jnp.concatenate([bias, bias], axis=1)
     attn_low, log_total = attend(queries, keys_win, values_win, bias)
+    attn_low = after(attn_low, incoming_sides)
     rows = regrouped(attn_low, planes, members)
     branch = [dot(rows, half, (1, 0)) for half in out_halves]
     middle = tokens + jnp.concatenate(branch, axis=1)
@@ -515,7 +519,7 @@
     normed_two = after(low(middle * factor_two), gate_up_blocks[-1][0])
     normed_two_all = lax.all_gather(normed_two, GROUP, axis=0, tiled=True)
     grad_act = low(dot(incoming_all, down_own, (1, 0)))
-    gate_up = dot(after(normed_two_all, down_own), gate_up_own, (1, 0))
+    gate_up = dot(after(normed_two_all, down_own, incoming_all), gate_up_own, (1, 0))
     activated, glu_back = jax.vjp(glu_values, gate_up[:, :piece], gate_up[:, piece:])
     activated_low = low(activated)
     def to_owners(term):
@@ -587,7 +591,6 @@
     )
     down_pieces = in_plane(down_rows)
     grad_mixed_low = regrouped(low(grad_mixed), members, planes)
-    grad_mixed_low = after(grad_mixed_low, down_pieces[0])
     delta = (wide(grad_mixed_low) * wide(attn_low)).reshape(tok_rows, head_count, HEAD_DIM)
     delta = jnp.sum(delta, axis=-1).T.reshape(log_total.shape)
     grad_query, grad_window = attend_back(
@@ -621,7 +624,7 @@
         jnp.concatenate([grad_query_pre, grad_key_pre, grad_local[:, HEAD_DIM:]], axis=1)
     )
 
-    all_columns = by_column(after(grad_proj, normed_one_others), grad_branch_low)
+    all_columns = by_column(after(grad_proj, normed_one_others, down_pieces[0]), grad_branch_low)
     qkv_share = grad_proj.shape[1] // shares
     by_core = all_columns.reshape(sides * columns, 2, tok_rows, -1)[:, :, :, :qkv_share]
 
@@ -635,8 +638,8 @@
     out_total = low(dot(attn_all, out_columns, (0, 0)))
     gate_pieces = in_plane(gate_rows, all_columns)
     total = jnp.concatenate([qkv_total, out_total], axis=1)
-    total = to_rows(after(total, gate_pieces[0]))
-    up_pieces = in_plane(up_rows, total)
+    up_pieces = in_plane(up_rows, gate_pieces[0])
+    total = to_rows(after(total, up_pieces[0]))
     branch = lax.psum_scatter(
         after(branch, all_columns), GROUP, scatter_dimension=0, tiled=True
     )

time: 1140 us -> 1110 us (0.974)
  waiting for transfers between devices: 480 us -> 455 us
    ppermute x7, waiting for transfers between devices: 107 us -> 1.22 us  [doubled(): other = lax.ppermute(value, axis, traded((axis,), step))]
    all_to_all x6, waiting for transfers between devices: 88.7 us -> 166 us  [exchanged(): return lax.all_to_all(value, axes, split_axis=0, concat_axis=0, tiled=True)]
    reduce_scatter x3, waiting for transfers between devices: 0.02 us -> 40.8 us  [to_owners(): return lax.psum_scatter(term, PLANES, scatter_dimension=0, tiled=True)]
    ppermute x7, waiting for transfers between devices: 47 us -> 10 us  [swapped(): return lax.ppermute(value, axis, [(0, 1), (1, 0)])]
    all_to_all x6, starting transfers between devices: 45.6 us -> 33.7 us  [exchanged(): return lax.all_to_all(value, axes, split_axis=0, concat_axis=0, tiled=True)]
    all_gather x2 -> x1, waiting for transfers between devices: 39.2 us -> 29.1 us  [on_device(): plane_rows = lax.all_gather(plane_rows, PLANES, axis=0, tiled=True)]
    unnamed x170 -> x166, local copies, waits for them, and re-layouts: 25.4 us -> 15.9 us
  transfers between devices with their start and end apart: 50 -> 49, of which waited for: 28 -> 22; matrix products, arithmetic and copies ran while one was open for 29% -> 32% of each run, Pallas kernels for 10% -> 10%
where the time goes in v8:
time: 1110 us; the launch traced here: 1100 us
  waiting for transfers between devices  455 us (41%)
  matrix products  173 us (16%)
  local copies, waits for them, and re-layouts  123 us (11%)
  other arithmetic  116 us (10%)
  Pallas kernels  109 us (10%)
  starting transfers between devices  79.4 us (7%)
  blocking collectives  33.5 us (3%)
  between operations  15.3 us (1%)
    dot_general x19, matrix products, dot(): lax.dot_general(left, right, ((contract[:1], contract[1:]), ((), ())), pr...  173 us
    all_to_all x6, waiting for transfers between devices, exchanged(): return lax.all_to_all(value, axes, split_axis=0, concat_axis=0, tiled=True)  166 us
    ppermute x7, waiting for transfers between devices, next_plane(): lax.ppermute(block, PLANES, [(one, (one + 1) % count) for one in range(co...  130 us
    pallas_call x3, Pallas kernels, mlp_adam(): pl.pallas_call(lambda *refs: mlp_adam_kernel(rate, per_side, part < 2, *r...  55.4 us
    reduce_scatter x3, waiting for transfers between devices, to_owners(): return lax.psum_scatter(term, PLANES, scatter_dimension=0, tiled=True)  40.8 us
    all_to_all x6, starting transfers between devices, exchanged(): return lax.all_to_all(value, axes, split_axis=0, concat_axis=0, tiled=True)  33.7 us
    all_to_all x1, blocking collectives, exchanged(): return lax.all_to_all(value, axes, split_axis=0, concat_axis=0, tiled=True)  33.5 us
    ppermute x3, waiting for transfers between devices, on_device(): arrived.append(lax.ppermute(term, CHIPS, traded(CHIPS, step)))  30.8 us
  transfers between devices with their start and end apart: 49, of which 22 were waited for; matrix products, arithmetic and copies ran while one was open for 32% of the time, Pallas kernels for 10%

profile of v8, /device:TPU:13, one launch (start us, length us, event | category | flops | bytes accessed | tf_op | source)
XLA Modules:
  0.0 1103.8 jit_solution(12269310521728062652)
XLA Ops:
  12.4 7.2 mlp_chunks.1
  19.5 33.5 %all_to_all.35 = bf16[4,160,2048]{2,1,0:T(8,128)(2,1)} all-to-all(bf16[4,160,2048]{2,1,0:T(8,128)(2,1)S(1)} %get-tuple-element.54), channel_id=1, replica_groups=mesh['seq'=2,'g'=2,'h'=2,'k'=2,'c'=2] {'k','c'}, dimensions={0} | all-to-all | bytes 5242880 | tf_op jit(solution)/shard_map/all_to_all | solution.py:143
  53.0 29.1 %all-gather.6.cloned.1.call-done = bf16[640,2816]{1,0:T(8,128)(2,1)} async-done(((bf16[160,2816]{1,0:T(8,128)(2,1)}), bf16[640,2816]{1,0:T(8,128)(2,1)}) %all-gather.6.cloned.1.call-update) | async-done | bytes 3604496 | tf_op jit(solution)/shard_map/all_gather | solution.py:457
  88.2 5.7 all-to-all-start.1
  98.7 47.2 %all-to-all-done.1 = bf16[4,160,1024]{2,1,0:T(8,128)(2,1)S(1)} async-done(((bf16[4,160,1024]{2,1,0:T(8,128)(2,1)}), bf16[4,160,1024]{2,1,0:T(8,128)(2,1)S(1)}, u32[]{:S(2)}, u32[]{:S(2)}) %all-to-all-start.1) | async-done | bytes 1310752 | tf_op jit(solution)/shard_map/all_to_all | solution.py:143
  152.7 30.2 %collective-permute-done.2 = bf16[640,1024]{1,0:T(8,128)(2,1)} collective-permute-done((bf16[640,1024]{1,0:T(8,128)(2,1)S(1)}, bf16[640,1024]{1,0:T(8,128)(2,1)}, u32[]{:S(2)}, u32[]{:S(2)}) %collective-permute-start.2) | collective-permute-done | bytes 1310752 | tf_op jit(solution)/shard_map/ppermute | solution.py:105
  183.5 9.1 all-gather.8.cloned.1.call-done
  192.6 5.0 fusion.2
  211.0 6.6 collective-permute-done.6
  219.9 9.8 collective-permute-done.8
  232.8 6.0 fusion.6
  260.9 65.6 %collective-permute-done.4 = bf16[640,1024]{1,0:T(8,128)(2,1)} collective-permute-done((bf16[640,1024]{1,0:T(8,128)(2,1)}, bf16[640,1024]{1,0:T(8,128)(2,1)}, u32[]{:S(2)}, u32[]{:S(2)}) %collective-permute-start.4) | collective-permute-done | bytes 1310752 | tf_op jit(solution)/shard_map/ppermute | solution.py:105
  328.8 3.5 fusion.94
  333.6 16.5 %attend.1 = (bf16[192,2560]{1,0:T(8,128)(2,1)}, f32[5,1,384]{2,1,0:T(1,128)S(1)}) custom-call(bf16[192,2560]{1,0:T(8,128)(2,1)S(1)} %copy-done.5, bf16[3072,256]{1,0:T(8,128)(2,1)S(1)} %get-tuple-element.169.key_ref, bf16[256,3072]{1,0:T(8,128)(2,1)S(1)} %copy.196.value_t_ref, f32[3072,384]{1,0:T(8,128)} %pad_maximum_fusion.2.bias_ref), custom_call_target="tpu_custom_call" | custom-call | flops 6039797760 | bytes 18087936 | tf_op jit(solution)/shard_map/attend/pallas_call | solution.py:308
  357.8 4.8 fusion.18
  362.7 4.7 fusion.22
  376.4 5.4 broadcast_in_dim.87
  385.1 3.6 constant_dynamic-update-slice_fusion.2
  390.2 3.6 constant_dynamic-update-slice_fusion.1
  396.2 5.8 collective-permute-done.15
  402.0 28.2 %collective-permute-done.17 = bf16[640,1024]{1,0:T(8,128)(2,1)} collective-permute-done((bf16[640,1024]{1,0:T(8,128)(2,1)S(1)}, bf16[640,1024]{1,0:T(8,128)(2,1)}, u32[]{:S(2)}, u32[]{:S(2)}) %collective-permute-start.17) | collective-permute-done | bytes 1310752 | tf_op jit(solution)/shard_map/ppermute | solution.py:105
  435.1 3.9 select_bitcast_fusion.1
  439.1 6.1 pad_maximum_fusion
  445.2 7.1 copy.199
  452.3 11.9 %convolution_convert_fusion.6 = bf16[1536,1024]{1,0:T(8,128)(2,1)} fusion(bf16[1536,2560]{1,0:T(8,128)(2,1)} %bitcast.237, bf16[2560,1024]{1,0:T(8,128)(2,1)S(1)} %bitcast.247), kind=kOutput, calls=%fused_computation.54 | convolution fusion | flops 8054636544 | bytes 16252928 | tf_op jit(solution)/shard_map/dot_general | solution.py:79
  464.2 20.6 %fusion.95 = f32[1536,2048]{1,0:T(8,128)S(1)} fusion(bf16[1536,2560]{1,0:T(8,128)(2,1)} %all-gather.12.cloned.1.call-done, bf16[2560,2048]{1,0:T(8,128)(2,1)} %get-tuple-element.207), kind=kOutput, calls=%fused_computation.223 | convolution fusion | flops 16106127360 | bytes 30932992 | tf_op jit(solution)/shard_map/dot_general | solution.py:79
  484.8 4.8 copy-done.11
  493.5 10.3 convolution_convert_fusion.3
  503.9 9.2 fusion.8
  516.4 9.8 convolution_convert_fusion.4
  527.1 6.8 collective-permute-done.18
  533.8 12.7 %add_convert_fusion = bf16[768,2560]{1,0:T(8,128)(2,1)S(1)} fusion(bf16[768,2560]{1,0:T(8,128)(2,1)} %collective-permute-done.18, bf16[768,2048]{1,0:T(8,128)(2,1)} %bitcast.259, bf16[2560,2048]{1,0:T(8,128)(2,1)} %get-tuple-element.207), kind=kOutput, calls=%fused_computation.4 | convolution fusion | flops 8058961920 | bytes 21495808 | tf_op jit(solution)/shard_map/dot_general | solution.py:79
  552.7 21.4 %collective-permute-done.20 = bf16[192,2560]{1,0:T(8,128)(2,1)} collective-permute-done((bf16[192,2560]{1,0:T(8,128)(2,1)}, bf16[192,2560]{1,0:T(8,128)(2,1)}, u32[]{:S(2)}, u32[]{:S(2)}) %collective-permute-start.20) | collective-permute-done | bytes 983072 | tf_op jit(solution)/shard_map/ppermute | solution.py:557
  574.9 12.3 %convolution_convert_fusion.2 = bf16[2560,1024]{1,0:T(8,128)(2,1)} fusion(bf16[1536,2560]{1,0:T(8,128)(2,1)} %all-gather.12.cloned.1.call-done, bf16[1536,2048]{1,0:T(8,128)(2,1)S(1)} %pad_maximum_fusion.1), kind=kOutput, calls=%fused_computation.39 | convolution fusion | flops 8055685120 | bytes 16252928 | tf_op jit(solution)/shard_map/dot_general | solution.py:79
  590.6 13.8 %convolution_convert_fusion.1 = bf16[2560,1024]{1,0:T(8,128)(2,1)} fusion(bf16[1536,2560]{1,0:T(8,128)(2,1)} %all-gather.12.cloned.1.call-done, bf16[1536,2048]{1,0:T(8,128)(2,1)} %copy-done.31), kind=kOutput, calls=%fused_computation.38 | convolution fusion | flops 8055685120 | bytes 16252928 | tf_op jit(solution)/shard_map/dot_general | solution.py:79
  604.5 8.6 collective-permute-done.21
  620.3 5.5 fusion.16
  625.8 6.1 fusion.31
  650.3 30.1 %attend_back.1 = (f32[192,2560]{1,0:T(8,128)}, f32[3072,512]{1,0:T(8,128)}) custom-call(bf16[192,2560]{1,0:T(8,128)(2,1)S(1)} %copy-done.6, bf16[192,2560]{1,0:T(8,128)(2,1)S(1)} %copy.205.grad_ref, bf16[3072,256]{1,0:T(8,128)(2,1)S(1)} %copy-done.3, bf16[256,3072]{1,0:T(8,128)(2,1)S(1)} %copy-done.4, bf16[3072,256]{1,0:T(8,128)(2,1)} %get-tuple-element.166.value_ref, ...), custom_call_target="tpu_custom_call" | custom-call | flops 15099494400 | bytes 22806528 | tf_op jit(solution)/shard_map/attend_back/pallas_call | solution.py:367
  705.1 19.1 %collective-permute-done.25 = bf16[2,192,512]{2,1,0:T(8,128)(2,1)} collective-permute-done((bf16[2,192,512]{2,1,0:T(8,128)(2,1)}, bf16[2,192,512]{2,1,0:T(8,128)(2,1)}, u32[]{:S(2)}, u32[]{:S(2)}) %collective-permute-start.25) | collective-permute-done | bytes 393248 | tf_op jit(solution)/shard_map/ppermute | solution.py:137
  728.5 6.5 collective-permute-start.28
  739.3 5.9 all-to-all-start.2
  749.9 24.0 %all-to-all-done.2.refs_1_ = bf16[4,160,1024]{2,1,0:T(8,128)(2,1)S(1)} async-done(((bf16[4,160,1024]{2,1,0:T(8,128)(2,1)}), bf16[4,160,1024]{2,1,0:T(8,128)(2,1)S(1)}, u32[]{:S(2)}, u32[]{:S(2)}) %all-to-all-start.2) | async-done | bytes 1310752 | tf_op jit(solution)/shard_map/all_to_all | solution.py:143
  778.8 5.8 all-to-all-start.3
  784.6 14.8 %convolution_convert_fusion = bf16[1536,2560]{1,0:T(8,128)(2,1)} fusion(bf16[1536,1024]{1,0:T(8,128)(2,1)} %copy-done.41, bf16[2560,1024]{1,0:T(8,128)(2,1)} %copy-done.35), kind=kOutput, calls=%fused_computation | convolution fusion | flops 8056995840 | bytes 16252928 | tf_op jit(solution)/shard_map/dot_general | solution.py:79
  799.5 12.7 %all-to-all-done.3 = bf16[8,192,704]{2,1,0:T(8,128)(2,1)} async-done(((bf16[8,192,704]{2,1,0:T(8,128)(2,1)}), bf16[8,192,704]{2,1,0:T(8,128)(2,1)}, u32[]{:S(2)}, u32[]{:S(2)}) %all-to-all-start.3) | async-done | bytes 2162720 | tf_op jit(solution)/shard_map/all_to_all | solution.py:143
  814.6 4.6 all-to-all-start.4
  819.2 5.9 fusion.96
  825.1 7.5 convolution_convert_fusion.5
  832.5 40.8 %reduce-scatter.9.cloned.1.call-done = bf16[640,1024]{1,0:T(8,128)(2,1)} async-done(((bf16[2560,1024]{1,0:T(8,128)(2,1)}), bf16[640,1024]{1,0:T(8,128)(2,1)}) %reduce-scatter.9.cloned.1.call-update) | async-done | bytes 1310736 | tf_op jit(solution)/shard_map/reduce_scatter | solution.py:526
  873.3 5.1 all-to-all-start.5
  878.5 5.2 fusion.24
  885.7 8.2 all-to-all-done.5.refs_1_
  893.9 6.1 copy.220
  900.1 6.5 all-to-all-start.6
  912.0 7.5 fusion
  919.6 74.1 %all-to-all-done.6 = bf16[16,160,704]{2,1,0:T(8,128)(2,1)} async-done(((bf16[16,160,704]{2,1,0:T(8,128)(2,1)}), bf16[16,160,704]{2,1,0:T(8,128)(2,1)}, u32[]{:S(2)}, u32[]{:S(2)}) %all-to-all-start.6) | async-done | bytes 3604512 | tf_op jit(solution)/shard_map/all_to_all | solution.py:143
  993.6 4.0 reduce_sum.111
  998.8 8.1 fusion.25
  1019.5 17.6 %mlp_adam.3 = (f32[3,160,7680]{2,1,0:T(8,128)}, f32[3,160,7680]{2,1,0:T(8,128)}, f32[3,160,7680]{2,1,0:T(8,128)}, f32[160,1]{1,0:T(8,128)}) custom-call(s32[1]{0:T(128)} %bitcast.4.refs_0_, bf16[4,160,1024]{2,1,0:T(8,128)(2,1)S(1)} %all-to-all-done.2.refs_1_, bf16[4,160,1024]{2,1,0:T(8,128)(2,1)} %collective-permute-done.33.refs_2_, ...), custom_call_target="tpu_custom_call" | custom-call | flops 24576000 | bytes 31948800 | tf_op jit(solution)/shard_map/mlp_adam/pallas_call | solution.py:241
  1037.1 18.5 %mlp_adam.4 = (f32[3,160,7680]{2,1,0:T(8,128)}, f32[3,160,7680]{2,1,0:T(8,128)}, f32[3,160,7680]{2,1,0:T(8,128)}, f32[160,1]{1,0:T(8,128)S(1)}) custom-call(s32[1]{0:T(128)} %bitcast.4.refs_0_, bf16[4,160,1024]{2,1,0:T(8,128)(2,1)S(1)} %all-to-all-done.4.refs_1_, ...), custom_call_target="tpu_custom_call", output_to_operand_aliasing={{0}: (7, {}), {1}: (8, {}), {2}: (9, {})} | custom-call | flops 24576000 | bytes 31948800 | tf_op jit(solution)/shard_map/mlp_adam/pallas_call | solution.py:241
  1055.6 19.3 %mlp_adam.5 = (f32[3,160,7680]{2,1,0:T(8,128)}, f32[3,160,7680]{2,1,0:T(8,128)}, f32[3,160,7680]{2,1,0:T(8,128)}, f32[160,1]{1,0:T(8,128)S(1)}) custom-call(s32[1]{0:T(128)} %bitcast.4.refs_0_, bf16[4,160,1024]{2,1,0:T(8,128)(2,1)} %all-to-all-done.5.refs_1_, ...), custom_call_target="tpu_custom_call", output_to_operand_aliasing={{0}: (7, {}), {1}: (8, {}), {2}: (9, {})} | custom-call | flops 24576000 | bytes 31948800 | tf_op jit(solution)/shard_map/mlp_adam/pallas_call | solution.py:241
  1081.1 7.5 multiply_subtract_fusion
  1092.3 4.7 fusion.50
  (381 shorter events, 216.3 us)
Async XLA Ops:
  7.2 75.0 %all-gather.6.cloned.1.call-start = ((), (), s32[]{:S(2)}) async-start(), calls=%async_computation.11 | async-start | bytes 4505600 | tf_op jit(solution)/shard_map/all_gather | solution.py:457
  12.2 180.4 %all-gather.8.cloned.1.call-start = ((), (), s32[]{:S(2)}) async-start(), calls=%async_computation.12 | async-start | bytes 17694720 | tf_op jit(solution)/shard_map/all_gather | solution.py:450
  85.1 272.7 %all-gather.10.cloned.1.call-start = ((), (), s32[]{:S(2)}) async-start(), calls=%async_computation.13 | async-start | bytes 14745600 | tf_op jit(solution)/shard_map/all_gather | solution.py:450
  87.9 61.7 %collective-permute-start = (bf16[192,2560]{1,0:T(8,128)(2,1)}, bf16[192,2560]{1,0:T(8,128)(2,1)}, u32[]{:S(2)}, u32[]{:S(2)}) collective-permute-start(bf16[192,2560]{1,0:T(8,128)(2,1)} %bitcast.1), channel_id=1, source_target_pairs={{0,2},{2,0},{1,3},{3,1},{4,6},{6,4},{5,7},{7,5},{8,10},{10,8},{9,1... | collective-permute-start | bytes 2949128 | tf_op jit(solution)/shard_map/ppermute | solution.py:98
  88.2 57.8 %all-to-all-start.1 = ((bf16[4,160,1024]{2,1,0:T(8,128)(2,1)}), bf16[4,160,1024]{2,1,0:T(8,128)(2,1)S(1)}, u32[]{:S(2)}, u32[]{:S(2)}) async-start(bf16[4,160,1024]{2,1,0:T(8,128)(2,1)} %get-tuple-element.57), calls=%async_computation.1 | async-start | bytes 2621440 | tf_op jit(solution)/shard_map/all_to_all | solution.py:143
  93.9 370.3 %all-gather.12.cloned.1.call-start = ((), (), s32[]{:S(2)}) async-start(), calls=%async_computation.14 | async-start | bytes 8847360 | tf_op jit(solution)/shard_map/all_gather | solution.py:520
  94.7 51.3 %copy-start.60 = (f32[192]{0:T(256)}, f32[192]{0:T(256)S(1)}, u32[]{:S(2)}) copy-start(f32[192]{0:T(256)S(1)} %get-tuple-element.201) | copy-start | bytes 2308
  94.8 88.1 %collective-permute-start.1 = (bf16[640,2048]{1,0:T(8,128)(2,1)}, bf16[640,2048]{1,0:T(8,128)(2,1)}, u32[]{:S(2)}, u32[]{:S(2)}) collective-permute-start(bf16[640,2048]{1,0:T(8,128)(2,1)} %bitcast.228), channel_id=1, source_target_pairs={{0,4},{4,8},{8,12},{12,0},{1,5},{5,9},{9,13},{13,1},{2,6},{6,10},{... | collective-permute-start | bytes 7864328 | tf_op jit(solution)/shard_map/ppermute | solution.py:105
  98.4 99.3 %copy-start.62 = (f32[192]{0:T(256)}, f32[192]{0:T(256)S(1)}, u32[]{:S(2)}) copy-start(f32[192]{0:T(256)S(1)} %get-tuple-element.150) | copy-start | bytes 2308
  98.7 84.1 %copy-start.23 = (bf16[192,2560]{1,0:T(8,128)(2,1)}, bf16[192,2560]{1,0:T(8,128)(2,1)S(1)}, u32[]{:S(2)}) copy-start(bf16[192,2560]{1,0:T(8,128)(2,1)S(1)} %fusion.47) | copy-start | bytes 2949124
  146.0 36.9 %collective-permute-start.2 = (bf16[640,1024]{1,0:T(8,128)(2,1)S(1)}, bf16[640,1024]{1,0:T(8,128)(2,1)}, u32[]{:S(2)}, u32[]{:S(2)}) collective-permute-start(bf16[640,1024]{1,0:T(8,128)(2,1)S(1)} %bitcast.248), channel_id=1, source_target_pairs={{0,4},{4,8},{8,12},{12,0},{1,5},{5,9},{9,13},{13,1},{2,6},{6,10},{... | collective-permute-start | bytes 3932168 | tf_op jit(solution)/shard_map/ppermute | solution.py:105
  183.5 14.1 %copy-start.52 = (bf16[192,4,4,160]{0,3,2,1:T(8,128)(2,1)}, bf16[192,4,4,160]{0,3,2,1:T(8,128)(2,1)S(1)}, u32[]{:S(2)}) copy-start(bf16[192,4,4,160]{0,3,2,1:T(8,128)(2,1)S(1)} %copy.190) | copy-start | bytes 2949124
  199.5 8.7 collective-permute-start.5
  201.4 29.6 %collective-permute-start.10 = (bf16[192,512]{1,0:T(8,128)(2,1)}, bf16[192,512]{1,0:T(8,128)(2,1)S(1)}, u32[]{:S(2)}, u32[]{:S(2)}) collective-permute-start(bf16[192,512]{1,0:T(8,128)(2,1)} %pad_maximum_fusion.14), channel_id=1, source_target_pairs={{0,20},{2,22},{4,16},{6,18},{16,4},{18,6},{20,0},{22,2},{1,21},{3,... | collective-permute-start | bytes 589832 | tf_op jit(solution)/shard_map/ppermute | solution.py:125
  203.6 26.8 %collective-permute-start.9 = (bf16[192,512]{1,0:T(8,128)(2,1)}, bf16[192,512]{1,0:T(8,128)(2,1)S(1)}, u32[]{:S(2)}, u32[]{:S(2)}) collective-permute-start(bf16[192,512]{1,0:T(8,128)(2,1)} %pad_maximum_fusion.14), channel_id=1, source_target_pairs={{0,18},{2,16},{4,22},{6,20},{16,2},{18,0},{20,6},{22,4},{1,19},{3,... | collective-permute-start | bytes 589832 | tf_op jit(solution)/shard_map/ppermute | solution.py:125
  204.8 24.9 %collective-permute-start.8 = (bf16[192,512]{1,0:T(8,128)(2,1)}, bf16[192,512]{1,0:T(8,128)(2,1)S(1)}, u32[]{:S(2)}, u32[]{:S(2)}) collective-permute-start(bf16[192,512]{1,0:T(8,128)(2,1)} %pad_maximum_fusion.14), channel_id=1, source_target_pairs={{0,16},{2,18},{4,20},{6,22},{16,0},{18,2},{20,4},{22,6},{1,17},{3,... | collective-permute-start | bytes 589832 | tf_op jit(solution)/shard_map/ppermute | solution.py:125
  205.9 13.3 %collective-permute-start.7 = (bf16[192,512]{1,0:T(8,128)(2,1)}, bf16[192,512]{1,0:T(8,128)(2,1)S(1)}, u32[]{:S(2)}, u32[]{:S(2)}) collective-permute-start(bf16[192,512]{1,0:T(8,128)(2,1)} %pad_maximum_fusion.14), channel_id=1, source_target_pairs={{0,6},{2,4},{4,2},{6,0},{16,22},{18,20},{20,18},{22,16},{1,7},{3,5... | collective-permute-start | bytes 589832 | tf_op jit(solution)/shard_map/ppermute | solution.py:125
  207.5 25.3 %copy-start.53 = (bf16[192,4,4,160]{0,3,2,1:T(8,128)(2,1)S(1)}, bf16[192,4,4,160]{0,3,2,1:T(8,128)(2,1)}, u32[]{:S(2)}) copy-start(bf16[192,4,4,160]{0,3,2,1:T(8,128)(2,1)} %copy-done.52) | copy-start | bytes 2949124
  208.2 9.4 collective-permute-start.6
  217.6 14.1 %collective-permute-start.11 = (bf16[192,512]{1,0:T(8,128)(2,1)}, bf16[192,512]{1,0:T(8,128)(2,1)S(1)}, u32[]{:S(2)}, u32[]{:S(2)}) collective-permute-start(bf16[192,512]{1,0:T(8,128)(2,1)} %pad_maximum_fusion.14), channel_id=1, source_target_pairs={{0,22},{2,20},{4,18},{6,16},{16,6},{18,4},{20,2},{22,0},{1,23},{3,... | collective-permute-start | bytes 589832 | tf_op jit(solution)/shard_map/ppermute | solution.py:125
  232.4 18.6 %collective-permute-start.12 = (bf16[8,192,512]{2,1,0:T(8,128)(2,1)}, bf16[8,192,512]{2,1,0:T(8,128)(2,1)}, u32[]{:S(2)}, u32[]{:S(2)}) collective-permute-start(bf16[8,192,512]{2,1,0:T(8,128)(2,1)} %bitcast_dynamic-update-slice_fusion), channel_id=1, source_target_pairs={{0,1},{1,0},{2,3},{3,2},{4,5},{5,4},{6,7},{7,6},{8,9},{9,8},{10,11... | collective-permute-start | bytes 4718600 | tf_op jit(solution)/shard_map/ppermute | solution.py:98
  238.8 87.6 %collective-permute-start.3 = (bf16[640,2048]{1,0:T(8,128)(2,1)}, bf16[640,2048]{1,0:T(8,128)(2,1)}, u32[]{:S(2)}, u32[]{:S(2)}) collective-permute-start(bf16[640,2048]{1,0:T(8,128)(2,1)} %collective-permute-done.1), channel_id=1, source_target_pairs={{0,4},{4,8},{8,12},{12,0},{1,5},{5,9},{9,13},{13,1},{2,6},{6,10},{... | collective-permute-start | bytes 7864328 | tf_op jit(solution)/shard_map/ppermute | solution.py:105
  249.6 76.8 %collective-permute-start.4 = (bf16[640,1024]{1,0:T(8,128)(2,1)}, bf16[640,1024]{1,0:T(8,128)(2,1)}, u32[]{:S(2)}, u32[]{:S(2)}) collective-permute-start(bf16[640,1024]{1,0:T(8,128)(2,1)} %collective-permute-done.2), channel_id=1, source_target_pairs={{0,4},{4,8},{8,12},{12,0},{1,5},{5,9},{9,13},{13,1},{2,6},{6,10},{... | collective-permute-start | bytes 3932168 | tf_op jit(solution)/shard_map/ppermute | solution.py:105
  253.5 96.6 %collective-permute-start.13 = (bf16[2,192,2560]{2,1,0:T(8,128)(2,1)}, bf16[2,192,2560]{2,1,0:T(8,128)(2,1)}, u32[]{:S(2)}, u32[]{:S(2)}) collective-permute-start(bf16[2,192,2560]{2,1,0:T(8,128)(2,1)} %pad_maximum_fusion.8), channel_id=1, source_target_pairs={{0,16},{16,0},{1,17},{17,1},{2,18},{18,2},{3,19},{19,3},{4,20},{20... | collective-permute-start | bytes 5898248 | tf_op jit(solution)/shard_map/ppermute | solution.py:98
  258.6 75.0 %copy-start.2 = (bf16[3072,256]{1,0:T(8,128)(2,1)}, bf16[3072,256]{1,0:T(8,128)(2,1)S(1)}, u32[]{:S(2)}) copy-start(bf16[3072,256]{1,0:T(8,128)(2,1)S(1)} %get-tuple-element.169.key_ref) | copy-start | bytes 4718596
  332.3 37.8 %collective-permute-start.14 = (bf16[640,1024]{1,0:T(8,128)(2,1)}, bf16[640,1024]{1,0:T(8,128)(2,1)}, u32[]{:S(2)}, u32[]{:S(2)}) collective-permute-start(bf16[640,1024]{1,0:T(8,128)(2,1)} %get-tuple-element.177), channel_id=1, source_target_pairs={{0,4},{4,8},{8,12},{12,0},{1,5},{5,9},{9,13},{13,1},{2,6},{6,10},{... | collective-permute-start | bytes 3932168 | tf_op jit(solution)/shard_map/ppermute | solution.py:105
  370.1 369.2 %reduce-scatter.5.cloned.1.call-start = ((), (), s32[]{:S(2)}) async-start(), calls=%async_computation.15 | async-start | bytes 6553600 | tf_op jit(solution)/shard_map/reduce_scatter | solution.py:526
  370.2 65.0 %collective-permute-start.16 = (bf16[2,2,192,2560]{3,2,1,0:T(8,128)(2,1)}, bf16[2,2,192,2560]{3,2,1,0:T(8,128)(2,1)}, u32[]{:S(2)}, u32[]{:S(2)}) collective-permute-start(bf16[2,2,192,2560]{3,2,1,0:T(8,128)(2,1)} %pad_maximum_fusion.3), channel_id=1, source_target_pairs={{0,1},{1,0},{2,3},{3,2},{4,5},{5,4},{6,7},{7,6},{8,9},{9,8},{10,11... | collective-permute-start | bytes 11796488 | tf_op jit(solution)/shard_map/ppermute | solution.py:98
  371.4 30.6 %collective-permute-start.15 = (bf16[640,1024]{1,0:T(8,128)(2,1)}, bf16[640,1024]{1,0:T(8,128)(2,1)S(1)}, u32[]{:S(2)}, u32[]{:S(2)}) collective-permute-start(bf16[640,1024]{1,0:T(8,128)(2,1)} %collective-permute-done.4), channel_id=1, source_target_pairs={{0,4},{4,8},{8,12},{12,0},{1,5},{5,9},{9,13},{13,1},{2,6},{6,10},{... | collective-permute-start | bytes 3932168 | tf_op jit(solution)/shard_map/ppermute | solution.py:105
  372.6 57.6 %collective-permute-start.17 = (bf16[640,1024]{1,0:T(8,128)(2,1)S(1)}, bf16[640,1024]{1,0:T(8,128)(2,1)}, u32[]{:S(2)}, u32[]{:S(2)}) collective-permute-start(bf16[640,1024]{1,0:T(8,128)(2,1)S(1)} %copy-done.51), channel_id=1, source_target_pairs={{0,4},{4,8},{8,12},{12,0},{1,5},{5,9},{9,13},{13,1},{2,6},{6,10},{... | collective-permute-start | bytes 3932168 | tf_op jit(solution)/shard_map/ppermute | solution.py:105
  396.2 38.9 %copy-start.21 = (bf16[1,2,192,2560]{3,2,1,0:T(8,128)(2,1)S(1)}, bf16[1,2,192,2560]{3,2,1,0:T(8,128)(2,1)}, u32[]{:S(2)}) copy-start(bf16[1,2,192,2560]{3,2,1,0:T(8,128)(2,1)} %copy-done.20) | copy-start | bytes 5898244
  439.1 13.3 %slice-start.3 = ((s8[5242880]{0:T(1024)(128)(4,1)}), s8[1048576]{0:T(1024)(128)(4,1)S(1)}, s32[]{:S(2)}) async-start(s8[5242880]{0:T(1024)(128)(4,1)} %bitcast.246), calls=%async_computation.23 | async-start | bytes 2097152
  503.8 310.8 %reduce-scatter.11.cloned.1.call-start = ((), (), s32[]{:S(2)}) async-start(), calls=%async_computation.19 | async-start | bytes 6553600 | tf_op jit(solution)/shard_map/reduce_scatter | solution.py:526
  503.9 12.2 %slice-start = ((s8[10485760]{0:T(1024)(128)(4,1)}), s8[4194304]{0:T(1024)(128)(4,1)S(1)}, s32[]{:S(2)}) async-start(s8[10485760]{0:T(1024)(128)(4,1)} %bitcast.235), calls=%async_computation.20 | async-start | bytes 8388608
  503.9 12.2 %slice-start.1 = ((s8[10485760]{0:T(1024)(128)(4,1)}), s8[4194304]{0:T(1024)(128)(4,1)S(1)}, s32[]{:S(2)}) async-start(s8[10485760]{0:T(1024)(128)(4,1)} %bitcast.235), calls=%async_computation.21 | async-start | bytes 8388608
  526.2 7.6 collective-permute-start.18
  549.9 24.2 %collective-permute-start.20 = (bf16[192,2560]{1,0:T(8,128)(2,1)}, bf16[192,2560]{1,0:T(8,128)(2,1)}, u32[]{:S(2)}, u32[]{:S(2)}) collective-permute-start(bf16[192,2560]{1,0:T(8,128)(2,1)} %get-tuple-element.161), channel_id=1, source_target_pairs={{0,16},{2,18},{16,0},{18,2},{1,17},{3,19},{17,1},{19,3},{4,20},{6,... | collective-permute-start | bytes 2949128 | tf_op jit(solution)/shard_map/ppermute | solution.py:557
  552.0 22.9 %collective-permute-start.19 = (bf16[192,2560]{1,0:T(8,128)(2,1)}, bf16[192,2560]{1,0:T(8,128)(2,1)}, u32[]{:S(2)}, u32[]{:S(2)}) collective-permute-start(bf16[192,2560]{1,0:T(8,128)(2,1)} %get-tuple-element.163), channel_id=1, source_target_pairs={{0,2},{2,0},{16,18},{18,16},{1,3},{3,1},{17,19},{19,17},{4,6},{6,4... | collective-permute-start | bytes 2949128 | tf_op jit(solution)/shard_map/ppermute | solution.py:557
  552.7 22.2 %copy-start.31 = (bf16[1536,2048]{1,0:T(8,128)(2,1)}, bf16[1536,2048]{1,0:T(8,128)(2,1)S(1)}, u32[]{:S(2)}) copy-start(bf16[1536,2048]{1,0:T(8,128)(2,1)S(1)} %pad_maximum_fusion.1) | copy-start | bytes 18874372
  587.3 237.7 %all-gather.14.cloned.1.call-start = ((), (), s32[]{:S(2)}) async-start(), calls=%async_computation.17 | async-start | bytes 8847360 | tf_op jit(solution)/shard_map/all_gather | solution.py:530
  588.1 285.3 %reduce-scatter.9.cloned.1.call-start = ((), (), s32[]{:S(2)}) async-start(), calls=%async_computation.18 | async-start | bytes 6553600 | tf_op jit(solution)/shard_map/reduce_scatter | solution.py:526
  590.4 22.6 %collective-permute-start.21 = (bf16[192,2560]{1,0:T(8,128)(2,1)S(1)}, bf16[192,2560]{1,0:T(8,128)(2,1)S(1)}, u32[]{:S(2)}, u32[]{:S(2)}) collective-permute-start(bf16[192,2560]{1,0:T(8,128)(2,1)S(1)} %copy-done.57), channel_id=1, source_target_pairs={{0,18},{2,16},{16,2},{18,0},{1,19},{3,17},{17,3},{19,1},{4,22},{6,... | collective-permute-start | bytes 2949128 | tf_op jit(solution)/shard_map/ppermute | solution.py:557
  604.4 10.9 copy-start.9
  616.5 20.9 %collective-permute-start.22 = (bf16[192,2560]{1,0:T(8,128)(2,1)S(1)}, bf16[192,2560]{1,0:T(8,128)(2,1)}, u32[]{:S(2)}, u32[]{:S(2)}) collective-permute-start(bf16[192,2560]{1,0:T(8,128)(2,1)S(1)} %copy-done.24), channel_id=1, source_target_pairs={{0,2},{2,0},{1,3},{3,1},{4,6},{6,4},{5,7},{7,5},{8,10},{10,8},{9,1... | collective-permute-start | bytes 2949128 | tf_op jit(solution)/shard_map/ppermute | solution.py:98
  640.7 43.0 %collective-permute-start.23 = (bf16[2,192,2560]{2,1,0:T(8,128)(2,1)}, bf16[2,192,2560]{2,1,0:T(8,128)(2,1)}, u32[]{:S(2)}, u32[]{:S(2)}) collective-permute-start(bf16[2,192,2560]{2,1,0:T(8,128)(2,1)} %pad_maximum_fusion.9), channel_id=1, source_target_pairs={{0,16},{16,0},{1,17},{17,1},{2,18},{18,2},{3,19},{19,3},{4,20},{20... | collective-permute-start | bytes 5898248 | tf_op jit(solution)/shard_map/ppermute | solution.py:98
  689.2 6.8 collective-permute-start.24
  692.6 81.3 %collective-permute-start.29 = (bf16[2,2,192,2560]{3,2,1,0:T(8,128)(2,1)}, bf16[2,2,192,2560]{3,2,1,0:T(8,128)(2,1)}, u32[]{:S(2)}, u32[]{:S(2)}) collective-permute-start(bf16[2,2,192,2560]{3,2,1,0:T(8,128)(2,1)} %pad_maximum_fusion.4), channel_id=1, source_target_pairs={{0,1},{1,0},{2,3},{3,2},{4,5},{5,4},{6,7},{7,6},{8,9},{9,8},{10,11... | collective-permute-start | bytes 11796488 | tf_op jit(solution)/shard_map/ppermute | solution.py:90
  699.0 25.2 %collective-permute-start.25 = (bf16[2,192,512]{2,1,0:T(8,128)(2,1)}, bf16[2,192,512]{2,1,0:T(8,128)(2,1)}, u32[]{:S(2)}, u32[]{:S(2)}) collective-permute-start(bf16[2,192,512]{2,1,0:T(8,128)(2,1)} %get-tuple-element.184), channel_id=1, source_target_pairs={{0,2},{2,0},{16,18},{18,16},{1,3},{3,1},{17,19},{19,17},{4,6},{6,4... | collective-permute-start | bytes 1179656 | tf_op jit(solution)/shard_map/ppermute | solution.py:137
  699.0 25.2 %collective-permute-start.27 = (bf16[2,192,512]{2,1,0:T(8,128)(2,1)}, bf16[2,192,512]{2,1,0:T(8,128)(2,1)}, u32[]{:S(2)}, u32[]{:S(2)}) collective-permute-start(bf16[2,192,512]{2,1,0:T(8,128)(2,1)} %get-tuple-element.185), channel_id=1, source_target_pairs={{0,18},{2,16},{16,2},{18,0},{1,19},{3,17},{17,3},{19,1},{4,22},{6,... | collective-permute-start | bytes 1179656 | tf_op jit(solution)/shard_map/ppermute | solution.py:137
  700.9 25.2 %collective-permute-start.26 = (bf16[2,192,512]{2,1,0:T(8,128)(2,1)S(1)}, bf16[2,192,512]{2,1,0:T(8,128)(2,1)}, u32[]{:S(2)}, u32[]{:S(2)}) collective-permute-start(bf16[2,192,512]{2,1,0:T(8,128)(2,1)S(1)} %get-tuple-element.186), channel_id=1, source_target_pairs={{0,16},{2,18},{16,0},{18,2},{1,17},{3,19},{17,1},{19,3},{4,20},{6,... | collective-permute-start | bytes 1179656 | tf_op jit(solution)/shard_map/ppermute | solution.py:137
  705.1 29.9 %copy-start.56 = (f32[192,128]{0,1:T(8,128)S(1)}, f32[192,128]{0,1:T(8,128)}, u32[]{:S(2)}) copy-start(f32[192,128]{0,1:T(8,128)} %copy-done.55) | copy-start | bytes 294916
  728.5 18.1 %collective-permute-start.28 = (bf16[192,512]{1,0:T(8,128)(2,1)}, bf16[192,512]{1,0:T(8,128)(2,1)}, u32[]{:S(2)}, u32[]{:S(2)}) collective-permute-start(bf16[192,512]{1,0:T(8,128)(2,1)} %dynamic-slice_bitcast_fusion.7), channel_id=1, source_target_pairs={{0,4},{4,0},{1,5},{5,1},{2,6},{6,2},{3,7},{7,3},{8,12},{12,8},{9,1... | collective-permute-start | bytes 589832 | tf_op jit(solution)/shard_map/ppermute | solution.py:90
  739.3 34.6 %all-to-all-start.2 = ((bf16[4,160,1024]{2,1,0:T(8,128)(2,1)}), bf16[4,160,1024]{2,1,0:T(8,128)(2,1)S(1)}, u32[]{:S(2)}, u32[]{:S(2)}) async-start(bf16[4,160,1024]{2,1,0:T(8,128)(2,1)} %bitcast.261), calls=%async_computation.3 | async-start | bytes 2621440 | tf_op jit(solution)/shard_map/all_to_all | solution.py:143
  749.9 28.9 %copy-start.34 = (bf16[192,3072]{0,1:T(8,128)(2,1)}, bf16[192,3072]{0,1:T(8,128)(2,1)S(1)}, u32[]{:S(2)}) copy-start(bf16[192,3072]{0,1:T(8,128)(2,1)S(1)} %pad_maximum_fusion.11) | copy-start | bytes 3538948
  778.8 33.4 %all-to-all-start.3 = ((bf16[8,192,704]{2,1,0:T(8,128)(2,1)}), bf16[8,192,704]{2,1,0:T(8,128)(2,1)}, u32[]{:S(2)}, u32[]{:S(2)}) async-start(bf16[8,192,704]{2,1,0:T(8,128)(2,1)} %maximum_bitcast_fusion), calls=%async_computation.4 | async-start | bytes 4718592 | tf_op jit(solution)/shard_map/all_to_all | solution.py:143
  784.6 307.7 %reduce-scatter.7.cloned.1.call-start = ((), (), s32[]{:S(2)}) async-start(), calls=%async_computation.16 | async-start | bytes 8847360 | tf_op jit(solution)/shard_map/reduce_scatter | solution.py:643
  814.6 58.8 %all-to-all-start.4 = ((bf16[4,160,1024]{2,1,0:T(8,128)(2,1)}), bf16[4,160,1024]{2,1,0:T(8,128)(2,1)S(1)}, u32[]{:S(2)}, u32[]{:S(2)}) async-start(bf16[4,160,1024]{2,1,0:T(8,128)(2,1)} %bitcast.262), calls=%async_computation.8 | async-start | bytes 2621440 | tf_op jit(solution)/shard_map/all_to_all | solution.py:143
  873.3 20.6 %all-to-all-start.5 = ((bf16[4,160,1024]{2,1,0:T(8,128)(2,1)}), bf16[4,160,1024]{2,1,0:T(8,128)(2,1)}, u32[]{:S(2)}, u32[]{:S(2)}) async-start(bf16[4,160,1024]{2,1,0:T(8,128)(2,1)} %bitcast.263), calls=%async_computation.9 | async-start | bytes 2621440 | tf_op jit(solution)/shard_map/all_to_all | solution.py:143
  900.1 93.6 %all-to-all-start.6 = ((bf16[16,160,704]{2,1,0:T(8,128)(2,1)}), bf16[16,160,704]{2,1,0:T(8,128)(2,1)}, u32[]{:S(2)}, u32[]{:S(2)}) async-start(bf16[16,160,704]{2,1,0:T(8,128)(2,1)} %bitcast.224), calls=%async_computation.10 | async-start | bytes 7864320 | tf_op jit(solution)/shard_map/all_to_all | solution.py:143
  909.3 110.1 %collective-permute-start.33 = (bf16[4,160,1024]{2,1,0:T(8,128)(2,1)S(1)}, bf16[4,160,1024]{2,1,0:T(8,128)(2,1)}, u32[]{:S(2)}, u32[]{:S(2)}) collective-permute-start(bf16[4,160,1024]{2,1,0:T(8,128)(2,1)S(1)} %all-to-all-done.2.refs_1_), channel_id=1, source_target_pairs={{0,16},{16,0},{1,17},{17,1},{2,18},{18,2},{3,19},{19,3},{4,20},{20... | collective-permute-start | bytes 3932168 | tf_op jit(solution)/shard_map/ppermute | solution.py:90
  910.5 126.5 %collective-permute-start.32 = (bf16[4,160,1024]{2,1,0:T(8,128)(2,1)S(1)}, bf16[4,160,1024]{2,1,0:T(8,128)(2,1)}, u32[]{:S(2)}, u32[]{:S(2)}) collective-permute-start(bf16[4,160,1024]{2,1,0:T(8,128)(2,1)S(1)} %all-to-all-done.4.refs_1_), channel_id=1, source_target_pairs={{0,16},{16,0},{1,17},{17,1},{2,18},{18,2},{3,19},{19,3},{4,20},{20... | collective-permute-start | bytes 3932168 | tf_op jit(solution)/shard_map/ppermute | solution.py:90
  910.8 144.7 %collective-permute-start.31 = (bf16[4,160,1024]{2,1,0:T(8,128)(2,1)}, bf16[4,160,1024]{2,1,0:T(8,128)(2,1)}, u32[]{:S(2)}, u32[]{:S(2)}) collective-permute-start(bf16[4,160,1024]{2,1,0:T(8,128)(2,1)} %all-to-all-done.5.refs_1_), channel_id=1, source_target_pairs={{0,16},{16,0},{1,17},{17,1},{2,18},{18,2},{3,19},{19,3},{4,20},{20... | collective-permute-start | bytes 3932168 | tf_op jit(solution)/shard_map/ppermute | solution.py:90
  997.6 77.4 %collective-permute-start.30 = (bf16[4,160,704]{2,1,0:T(8,128)(2,1)}, bf16[4,160,704]{2,1,0:T(8,128)(2,1)}, u32[]{:S(2)}, u32[]{:S(2)}) collective-permute-start(bf16[4,160,704]{2,1,0:T(8,128)(2,1)} %reduce_sum.111), channel_id=1, source_target_pairs={{0,16},{16,0},{1,17},{17,1},{2,18},{18,2},{3,19},{19,3},{4,20},{20... | collective-permute-start | bytes 2703368 | tf_op jit(solution)/shard_map/ppermute | solution.py:98
  1055.6 19.4 %copy-start.39 = (bf16[4,160,704]{2,1,0:T(8,128)(2,1)S(1)}, bf16[4,160,704]{2,1,0:T(8,128)(2,1)}, u32[]{:S(2)}) copy-start(bf16[4,160,704]{2,1,0:T(8,128)(2,1)} %reduce_sum.111) | copy-start | bytes 2703364
  (68 other events, 311.7 us)
Sparse Core Ops, SparseCore 0:
  12.4 69.7 all-gather.5
  85.2 107.3 all-gather.7
  195.1 116.6 all-gather.9
  370.2 56.3 all-gather.11
  503.9 97.5 reduce-scatter.4
  604.3 94.2 reduce-scatter.10
  700.5 74.9 all-gather.13
  778.3 94.9 reduce-scatter.8
  876.8 112.0 reduce-scatter.6

commit v9 on v8

--- a/solution.py
+++ b/solution.py
@@ -221,9 +221,9 @@
     second_out[0], weight_out[0] = adam_step(weight, first_ref[0], second_ref[0], grad, rate)
 
 
-def mlp_adam(part, side, pieces, states, gain, rate, outs):
+def mlp_adam(part, side, pieces, column, piece, states, gain, rate, outs):
     _, rows, ff_width = states[0].shape
-    members, _, piece = pieces[0].shape
+    members = pieces[0].shape[0]
     per_piece = piece // LANES
     per_side = members * per_piece
 
@@ -231,7 +231,7 @@
         def place(b, side_ref):
             used = (b // per_side == side_ref[0]) == own
             inner = jnp.where(used, b % per_side, 0)
-            return (inner // per_piece, 0, inner % per_piece)
+            return (inner // per_piece, 0, column // LANES + inner % per_piece)
 
         return pl.BlockSpec((1, rows, LANES), place)
 
@@ -589,7 +589,6 @@
         dot(grad_branch_low[:, index * half : (index + 1) * half], out_halves[index], (1, 1))
         for index in range(sides)
     )
-    down_pieces = in_plane(down_rows)
     grad_mixed_low = regrouped(low(grad_mixed), members, planes)
     delta = (wide(grad_mixed_low) * wide(attn_low)).reshape(tok_rows, head_count, HEAD_DIM)
     delta = jnp.sum(delta, axis=-1).T.reshape(log_total.shape)
@@ -609,12 +608,12 @@
     mlp_states = (mlp_planes, first_mlp.transpose(1, 0, 2), second_mlp.transpose(1, 0, 2))
     rate_main = 2.0 * D ** (-0.5)
 
-    def mlp_updated(part, pieces, outs):
-        *outs, gain_dot = mlp_adam(part, side, pieces, mlp_states, gain_two, rate_main, outs)
+    def mlp_updated(part, pieces, column, outs):
+        *outs, gain_dot = mlp_adam(
+            part, side, pieces, column, piece, mlp_states, gain_two, rate_main, outs
+        )
         return outs, gain_dot
 
-    mlp_outs, down_dot = mlp_updated(2, down_pieces, ())
-    grad_local = after(grad_local, down_dot)
     grad_query = grad_query.reshape(tok_rows, head_count, HEAD_DIM)
     grad_query_pre = rotate(
         grad_query * query_scale, cosine[:, None, :], -sine[:, None, :]
@@ -624,7 +623,7 @@
         jnp.concatenate([grad_query_pre, grad_key_pre, grad_local[:, HEAD_DIM:]], axis=1)
     )
 
-    all_columns = by_column(after(grad_proj, normed_one_others, down_pieces[0]), grad_branch_low)
+    all_columns = by_column(after(grad_proj, normed_one_others), grad_branch_low)
     qkv_share = grad_proj.shape[1] // shares
     by_core = all_columns.reshape(sides * columns, 2, tok_rows, -1)[:, :, :, :qkv_share]
 
@@ -636,15 +635,16 @@
     qkv_total = low(qkv_total + one_core_total(normed_one_others, 1 - core))
     out_columns = all_columns.reshape(shares * tok_rows, -1)[:, qkv_share:]
     out_total = low(dot(attn_all, out_columns, (0, 0)))
-    gate_pieces = in_plane(gate_rows, all_columns)
+    first_pieces = in_plane(jnp.concatenate([down_rows, gate_rows], axis=1), all_columns)
     total = jnp.concatenate([qkv_total, out_total], axis=1)
-    up_pieces = in_plane(up_rows, gate_pieces[0])
-    total = to_rows(after(total, up_pieces[0]))
+    total = to_rows(after(total, first_pieces[0]))
+    up_pieces = in_plane(up_rows, total)
     branch = lax.psum_scatter(
         after(branch, all_columns), GROUP, scatter_dimension=0, tiled=True
     )
-    mlp_outs, gate_dot = mlp_updated(0, gate_pieces, mlp_outs)
-    (grad_mlp, second_new_mlp, new_mlp), up_dot = mlp_updated(1, up_pieces, mlp_outs)
+    mlp_outs, _ = mlp_updated(2, first_pieces, 0, ())
+    mlp_outs, gate_dot = mlp_updated(0, first_pieces, piece, mlp_outs)
+    (grad_mlp, second_new_mlp, new_mlp), up_dot = mlp_updated(1, up_pieces, 0, mlp_outs)
     grad_gain_two = gate_dot + up_dot
     total = doubled(total, "seq", 1, 0).reshape(shares, own_rows, -1)
     grad_qkv = joined(total[:, :, :qkv_share])

time: 1110 us -> 1110 us (level)
    reduce_scatter x3, waiting for transfers between devices: 40.8 us -> 0.06 us  [to_owners(): return lax.psum_scatter(term, PLANES, scatter_dimension=0, tiled=True)]
    all_to_all x6 -> x5, waiting for transfers between devices: 166 us -> 192 us  [exchanged(): return lax.all_to_all(value, axes, split_axis=0, concat_axis=0, tiled=True)]
    all_to_all x6 -> x5, starting transfers between devices: 33.7 us -> 26.8 us  [exchanged(): return lax.all_to_all(value, axes, split_axis=0, concat_axis=0, tiled=True)]
  transfers between devices with their start and end apart: 49 -> 47, of which waited for: 22 -> 21; matrix products, arithmetic and copies ran while one was open for 32% -> 32% of each run, Pallas kernels for 10% -> 10%
where the time goes in v9:
time: 1110 us; the launch traced here: 1100 us
  waiting for transfers between devices  452 us (41%)
  matrix products  171 us (15%)
  local copies, waits for them, and re-layouts  127 us (11%)
  other arithmetic  120 us (11%)
  Pallas kernels  109 us (10%)
  starting transfers between devices  70.4 us (6%)
  blocking collectives  33.5 us (3%)
  between operations  15.5 us (1%)
    all_to_all x5, waiting for transfers between devices, exchanged(): return lax.all_to_all(value, axes, split_axis=0, concat_axis=0, tiled=True)  192 us
    dot_general x19, matrix products, dot(): lax.dot_general(left, right, ((contract[:1], contract[1:]), ((), ())), pr...  171 us
    ppermute x7, waiting for transfers between devices, next_plane(): lax.ppermute(block, PLANES, [(one, (one + 1) % count) for one in range(co...  130 us
    pallas_call x3, Pallas kernels, mlp_adam(): pl.pallas_call(lambda *refs: mlp_adam_kernel(rate, per_side, part < 2, *r...  55.3 us
    all_to_all x1, blocking collectives, exchanged(): return lax.all_to_all(value, axes, split_axis=0, concat_axis=0, tiled=True)  33.5 us
    ppermute x3, waiting for transfers between devices, on_device(): arrived.append(lax.ppermute(term, CHIPS, traded(CHIPS, step)))  30.9 us
    pallas_call x1, Pallas kernels, attend_back(): pl.pallas_call(attend_back_kernel, grid=(pairs,), in_specs=[pair, pair, w...  30.3 us
    all_gather x1, waiting for transfers between devices, on_device(): plane_rows = lax.all_gather(plane_rows, PLANES, axis=0, tiled=True)  29.1 us
  transfers between devices with their start and end apart: 47, of which 21 were waited for; matrix products, arithmetic and copies ran while one was open for 32% of the time, Pallas kernels for 10%

profile of v9, /device:TPU:13, one launch (start us, length us, event | category | flops | bytes accessed | tf_op | source)
XLA Modules:
  0.0 1097.9 jit_solution(15568614701855900086)
XLA Ops:
  12.4 7.2 mlp_chunks.1
  19.5 33.5 %all_to_all.30 = bf16[4,160,2048]{2,1,0:T(8,128)(2,1)} all-to-all(bf16[4,160,2048]{2,1,0:T(8,128)(2,1)S(1)} %get-tuple-element.54), channel_id=1, replica_groups=mesh['seq'=2,'g'=2,'h'=2,'k'=2,'c'=2] {'k','c'}, dimensions={0} | all-to-all | bytes 5242880 | tf_op jit(solution)/shard_map/all_to_all | solution.py:143
  53.0 29.1 %all-gather.6.cloned.1.call-done = bf16[640,2816]{1,0:T(8,128)(2,1)} async-done(((bf16[160,2816]{1,0:T(8,128)(2,1)}), bf16[640,2816]{1,0:T(8,128)(2,1)}) %all-gather.6.cloned.1.call-update) | async-done | bytes 3604496 | tf_op jit(solution)/shard_map/all_gather | solution.py:457
  88.1 5.7 all-to-all-start.1
  98.8 47.2 %all-to-all-done.1 = bf16[4,160,1024]{2,1,0:T(8,128)(2,1)S(1)} async-done(((bf16[4,160,1024]{2,1,0:T(8,128)(2,1)}), bf16[4,160,1024]{2,1,0:T(8,128)(2,1)S(1)}, u32[]{:S(2)}, u32[]{:S(2)}) %all-to-all-start.1) | async-done | bytes 1310752 | tf_op jit(solution)/shard_map/all_to_all | solution.py:143
  152.6 30.3 %collective-permute-done.2 = bf16[640,1024]{1,0:T(8,128)(2,1)} collective-permute-done((bf16[640,1024]{1,0:T(8,128)(2,1)S(1)}, bf16[640,1024]{1,0:T(8,128)(2,1)}, u32[]{:S(2)}, u32[]{:S(2)}) %collective-permute-start.2) | collective-permute-done | bytes 1310752 | tf_op jit(solution)/shard_map/ppermute | solution.py:105
  183.6 9.0 all-gather.8.cloned.1.call-done
  192.6 5.0 fusion.2
  211.0 6.6 collective-permute-done.6
  219.9 9.8 collective-permute-done.8
  232.8 6.0 fusion.6
  260.9 65.5 %collective-permute-done.4 = bf16[640,1024]{1,0:T(8,128)(2,1)} collective-permute-done((bf16[640,1024]{1,0:T(8,128)(2,1)}, bf16[640,1024]{1,0:T(8,128)(2,1)}, u32[]{:S(2)}, u32[]{:S(2)}) %collective-permute-start.4) | collective-permute-done | bytes 1310752 | tf_op jit(solution)/shard_map/ppermute | solution.py:105
  328.7 3.5 fusion.95
  333.6 16.5 %attend.1 = (bf16[192,2560]{1,0:T(8,128)(2,1)}, f32[5,1,384]{2,1,0:T(1,128)S(1)}) custom-call(bf16[192,2560]{1,0:T(8,128)(2,1)S(1)} %copy-done.5, bf16[3072,256]{1,0:T(8,128)(2,1)S(1)} %get-tuple-element.171.key_ref, bf16[256,3072]{1,0:T(8,128)(2,1)S(1)} %copy.196.value_t_ref, f32[3072,384]{1,0:T(8,128)} %pad_maximum_fusion.2.bias_ref), custom_call_target="tpu_custom_call" | custom-call | flops 6039797760 | bytes 18087936 | tf_op jit(solution)/shard_map/attend/pallas_call | solution.py:308
  357.8 4.8 fusion.18
  362.6 4.7 fusion.22
  376.3 5.4 broadcast_in_dim.87
  385.1 3.6 constant_dynamic-update-slice_fusion.2
  390.1 3.6 constant_dynamic-update-slice_fusion.1
  396.2 5.8 collective-permute-done.15
  401.9 28.2 %collective-permute-done.17 = bf16[640,1024]{1,0:T(8,128)(2,1)} collective-permute-done((bf16[640,1024]{1,0:T(8,128)(2,1)S(1)}, bf16[640,1024]{1,0:T(8,128)(2,1)}, u32[]{:S(2)}, u32[]{:S(2)}) %collective-permute-start.17) | collective-permute-done | bytes 1310752 | tf_op jit(solution)/shard_map/ppermute | solution.py:105
  435.1 4.1 select_bitcast_fusion.1
  439.2 6.1 pad_maximum_fusion
  445.4 7.1 copy.199
  452.5 11.9 %convolution_convert_fusion.6 = bf16[1536,1024]{1,0:T(8,128)(2,1)} fusion(bf16[1536,2560]{1,0:T(8,128)(2,1)} %bitcast.238, bf16[2560,1024]{1,0:T(8,128)(2,1)S(1)} %bitcast.250), kind=kOutput, calls=%fused_computation.54 | convolution fusion | flops 8054636544 | bytes 16252928 | tf_op jit(solution)/shard_map/dot_general | solution.py:79
  464.4 20.6 %fusion.96 = f32[1536,2048]{1,0:T(8,128)S(1)} fusion(bf16[1536,2560]{1,0:T(8,128)(2,1)} %all-gather.12.cloned.1.call-done, bf16[2560,2048]{1,0:T(8,128)(2,1)} %get-tuple-element.209), kind=kOutput, calls=%fused_computation.223 | convolution fusion | flops 16106127360 | bytes 30932992 | tf_op jit(solution)/shard_map/dot_general | solution.py:79
  485.0 4.8 copy-done.11
  493.7 10.3 convolution_convert_fusion.3
  504.0 8.8 fusion.8
  516.2 9.8 convolution_convert_fusion.4
  526.9 6.8 collective-permute-done.18
  533.6 12.8 %add_convert_fusion = bf16[768,2560]{1,0:T(8,128)(2,1)S(1)} fusion(bf16[768,2560]{1,0:T(8,128)(2,1)} %collective-permute-done.18, bf16[768,2048]{1,0:T(8,128)(2,1)} %bitcast.262, bf16[2560,2048]{1,0:T(8,128)(2,1)} %get-tuple-element.209), kind=kOutput, calls=%fused_computation.4 | convolution fusion | flops 8058961920 | bytes 21495808 | tf_op jit(solution)/shard_map/dot_general | solution.py:79
  552.7 21.4 %collective-permute-done.20 = bf16[192,2560]{1,0:T(8,128)(2,1)} collective-permute-done((bf16[192,2560]{1,0:T(8,128)(2,1)}, bf16[192,2560]{1,0:T(8,128)(2,1)}, u32[]{:S(2)}, u32[]{:S(2)}) %collective-permute-start.20) | collective-permute-done | bytes 983072 | tf_op jit(solution)/shard_map/ppermute | solution.py:557
  574.9 12.4 %convolution_convert_fusion.2 = bf16[2560,1024]{1,0:T(8,128)(2,1)} fusion(bf16[1536,2560]{1,0:T(8,128)(2,1)} %all-gather.12.cloned.1.call-done, bf16[1536,2048]{1,0:T(8,128)(2,1)S(1)} %pad_maximum_fusion.1), kind=kOutput, calls=%fused_computation.39 | convolution fusion | flops 8055685120 | bytes 16252928 | tf_op jit(solution)/shard_map/dot_general | solution.py:79
  590.6 13.8 %convolution_convert_fusion.1 = bf16[2560,1024]{1,0:T(8,128)(2,1)} fusion(bf16[1536,2560]{1,0:T(8,128)(2,1)} %all-gather.12.cloned.1.call-done, bf16[1536,2048]{1,0:T(8,128)(2,1)} %copy-done.30), kind=kOutput, calls=%fused_computation.38 | convolution fusion | flops 8055685120 | bytes 16252928 | tf_op jit(solution)/shard_map/dot_general | solution.py:79
  604.5 8.6 collective-permute-done.21
  620.2 5.6 fusion.16
  625.7 6.1 fusion.31
  650.8 30.3 %attend_back.1 = (f32[192,2560]{1,0:T(8,128)}, f32[3072,512]{1,0:T(8,128)}) custom-call(bf16[192,2560]{1,0:T(8,128)(2,1)S(1)} %copy-done.6, bf16[192,2560]{1,0:T(8,128)(2,1)S(1)} %copy.205.grad_ref, bf16[3072,256]{1,0:T(8,128)(2,1)S(1)} %copy-done.3, bf16[256,3072]{1,0:T(8,128)(2,1)S(1)} %copy-done.4, bf16[3072,256]{1,0:T(8,128)(2,1)} %get-tuple-element.168.value_ref, ...), custom_call_target="tpu_custom_call" | custom-call | flops 15099494400 | bytes 22806528 | tf_op jit(solution)/shard_map/attend_back/pallas_call | solution.py:367
  705.8 19.3 %collective-permute-done.25 = bf16[2,192,512]{2,1,0:T(8,128)(2,1)} collective-permute-done((bf16[2,192,512]{2,1,0:T(8,128)(2,1)}, bf16[2,192,512]{2,1,0:T(8,128)(2,1)}, u32[]{:S(2)}, u32[]{:S(2)}) %collective-permute-start.25) | collective-permute-done | bytes 393248 | tf_op jit(solution)/shard_map/ppermute | solution.py:137
  729.5 6.1 collective-permute-start.28
  746.7 5.2 all-to-all-start.2
  751.9 13.7 %convolution_convert_fusion = bf16[1536,2560]{1,0:T(8,128)(2,1)} fusion(bf16[1536,1024]{1,0:T(8,128)(2,1)} %copy-done.42, bf16[2560,1024]{1,0:T(8,128)(2,1)} %copy-done.35), kind=kOutput, calls=%fused_computation | convolution fusion | flops 8056995840 | bytes 16252928 | tf_op jit(solution)/shard_map/dot_general | solution.py:79
  765.6 20.8 %all-to-all-done.2 = bf16[8,192,704]{2,1,0:T(8,128)(2,1)S(1)} async-done(((bf16[8,192,704]{2,1,0:T(8,128)(2,1)}), bf16[8,192,704]{2,1,0:T(8,128)(2,1)S(1)}, u32[]{:S(2)}, u32[]{:S(2)}) %all-to-all-start.2) | async-done | bytes 2162720 | tf_op jit(solution)/shard_map/all_to_all | solution.py:143
  791.6 4.5 all-to-all-start.3
  796.1 5.9 fusion.97
  802.0 6.5 convolution_convert_fusion.5
  808.5 3.9 fusion.24
  814.5 11.1 %all-to-all-done.3.refs_1_ = bf16[4,160,2048]{2,1,0:T(8,128)(2,1)S(1)} async-done(((bf16[4,160,2048]{2,1,0:T(8,128)(2,1)}), bf16[4,160,2048]{2,1,0:T(8,128)(2,1)S(1)}, u32[]{:S(2)}, u32[]{:S(2)}) %all-to-all-start.3) | async-done | bytes 2621472 | tf_op jit(solution)/shard_map/all_to_all | solution.py:143
  825.6 6.1 copy.220
  831.7 6.9 all-to-all-start.4
  842.4 7.5 fusion
  850.0 113.3 %all-to-all-done.4 = bf16[16,160,704]{2,1,0:T(8,128)(2,1)} async-done(((bf16[16,160,704]{2,1,0:T(8,128)(2,1)}), bf16[16,160,704]{2,1,0:T(8,128)(2,1)}, u32[]{:S(2)}, u32[]{:S(2)}) %all-to-all-start.4) | async-done | bytes 3604512 | tf_op jit(solution)/shard_map/all_to_all | solution.py:143
  963.3 4.0 reduce_sum.111
  968.5 9.3 fusion.25
  980.8 3.5 copy.216
  990.3 4.5 all-to-all-start.5
  994.9 17.7 %mlp_adam.3 = (f32[3,160,7680]{2,1,0:T(8,128)}, f32[3,160,7680]{2,1,0:T(8,128)}, f32[3,160,7680]{2,1,0:T(8,128)}, f32[160,1]{1,0:T(8,128)}) custom-call(s32[1]{0:T(128)} %bitcast.4.refs_0_, bf16[4,160,2048]{2,1,0:T(8,128)(2,1)S(1)} %all-to-all-done.3.refs_1_, bf16[4,160,2048]{2,1,0:T(8,128)(2,1)} %collective-permute-done.32.refs_2_, ...), custom_call_target="tpu_custom_call" | custom-call | flops 24576000 | bytes 31948800 | tf_op jit(solution)/shard_map/mlp_adam/pallas_call | solution.py:241
  1012.7 18.8 %mlp_adam.4 = (f32[3,160,7680]{2,1,0:T(8,128)}, f32[3,160,7680]{2,1,0:T(8,128)}, f32[3,160,7680]{2,1,0:T(8,128)}, f32[160,1]{1,0:T(8,128)S(1)}) custom-call(s32[1]{0:T(128)} %bitcast.4.refs_0_, bf16[4,160,2048]{2,1,0:T(8,128)(2,1)S(1)} %all-to-all-done.3.refs_1_, ...), custom_call_target="tpu_custom_call", output_to_operand_aliasing={{0}: (7, {}), {1}: (8, {}), {2}: (9, {})} | custom-call | flops 24576000 | bytes 31948800 | tf_op jit(solution)/shard_map/mlp_adam/pallas_call | solution.py:241
  1035.9 7.5 multiply_subtract_fusion
  1048.7 5.8 multiply_subtract_fusion.2
  1054.5 11.6 %collective-permute-done.31.refs_2_ = bf16[4,160,1024]{2,1,0:T(8,128)(2,1)S(1)} collective-permute-done((bf16[4,160,1024]{2,1,0:T(8,128)(2,1)}, bf16[4,160,1024]{2,1,0:T(8,128)(2,1)S(1)}, u32[]{:S(2)}, u32[]{:S(2)}) %collective-permute-start.31) | collective-permute-done | bytes 1310752 | tf_op jit(solution)/shard_map/ppermute | solution.py:90
  1066.1 18.8 %mlp_adam.5 = (f32[3,160,7680]{2,1,0:T(8,128)}, f32[3,160,7680]{2,1,0:T(8,128)}, f32[3,160,7680]{2,1,0:T(8,128)}, f32[160,1]{1,0:T(8,128)S(1)}) custom-call(s32[1]{0:T(128)} %bitcast.4.refs_0_, bf16[4,160,1024]{2,1,0:T(8,128)(2,1)} %all-to-all-done.5.refs_1_, ...), custom_call_target="tpu_custom_call", output_to_operand_aliasing={{0}: (7, {}), {1}: (8, {}), {2}: (9, {})} | custom-call | flops 24576000 | bytes 31948800 | tf_op jit(solution)/shard_map/mlp_adam/pallas_call | solution.py:241
  1085.6 5.3 fusion.50
  (376 shorter events, 212.6 us)
Async XLA Ops:
  7.2 75.0 %all-gather.6.cloned.1.call-start = ((), (), s32[]{:S(2)}) async-start(), calls=%async_computation.10 | async-start | bytes 4505600 | tf_op jit(solution)/shard_map/all_gather | solution.py:457
  12.2 180.4 %all-gather.8.cloned.1.call-start = ((), (), s32[]{:S(2)}) async-start(), calls=%async_computation.11 | async-start | bytes 17694720 | tf_op jit(solution)/shard_map/all_gather | solution.py:450
  85.1 272.7 %all-gather.10.cloned.1.call-start = ((), (), s32[]{:S(2)}) async-start(), calls=%async_computation.12 | async-start | bytes 14745600 | tf_op jit(solution)/shard_map/all_gather | solution.py:450
  87.9 61.6 %collective-permute-start = (bf16[192,2560]{1,0:T(8,128)(2,1)}, bf16[192,2560]{1,0:T(8,128)(2,1)}, u32[]{:S(2)}, u32[]{:S(2)}) collective-permute-start(bf16[192,2560]{1,0:T(8,128)(2,1)} %bitcast.1), channel_id=1, source_target_pairs={{0,2},{2,0},{1,3},{3,1},{4,6},{6,4},{5,7},{7,5},{8,10},{10,8},{9,1... | collective-permute-start | bytes 2949128 | tf_op jit(solution)/shard_map/ppermute | solution.py:98
  88.1 57.8 %all-to-all-start.1 = ((bf16[4,160,1024]{2,1,0:T(8,128)(2,1)}), bf16[4,160,1024]{2,1,0:T(8,128)(2,1)S(1)}, u32[]{:S(2)}, u32[]{:S(2)}) async-start(bf16[4,160,1024]{2,1,0:T(8,128)(2,1)} %get-tuple-element.57), calls=%async_computation.1 | async-start | bytes 2621440 | tf_op jit(solution)/shard_map/all_to_all | solution.py:143
  93.8 370.5 %all-gather.12.cloned.1.call-start = ((), (), s32[]{:S(2)}) async-start(), calls=%async_computation.13 | async-start | bytes 8847360 | tf_op jit(solution)/shard_map/all_gather | solution.py:520
  94.7 51.2 %copy-start.58 = (f32[192]{0:T(256)}, f32[192]{0:T(256)S(1)}, u32[]{:S(2)}) copy-start(f32[192]{0:T(256)S(1)} %get-tuple-element.203) | copy-start | bytes 2308
  94.8 88.1 %collective-permute-start.1 = (bf16[640,2048]{1,0:T(8,128)(2,1)}, bf16[640,2048]{1,0:T(8,128)(2,1)}, u32[]{:S(2)}, u32[]{:S(2)}) collective-permute-start(bf16[640,2048]{1,0:T(8,128)(2,1)} %bitcast.228), channel_id=1, source_target_pairs={{0,4},{4,8},{8,12},{12,0},{1,5},{5,9},{9,13},{13,1},{2,6},{6,10},{... | collective-permute-start | bytes 7864328 | tf_op jit(solution)/shard_map/ppermute | solution.py:105
  98.5 99.2 %copy-start.60 = (f32[192]{0:T(256)}, f32[192]{0:T(256)S(1)}, u32[]{:S(2)}) copy-start(f32[192]{0:T(256)S(1)} %get-tuple-element.152) | copy-start | bytes 2308
  98.8 84.1 %copy-start.21 = (bf16[192,2560]{1,0:T(8,128)(2,1)}, bf16[192,2560]{1,0:T(8,128)(2,1)S(1)}, u32[]{:S(2)}) copy-start(bf16[192,2560]{1,0:T(8,128)(2,1)S(1)} %fusion.47) | copy-start | bytes 2949124
  146.0 36.9 %collective-permute-start.2 = (bf16[640,1024]{1,0:T(8,128)(2,1)S(1)}, bf16[640,1024]{1,0:T(8,128)(2,1)}, u32[]{:S(2)}, u32[]{:S(2)}) collective-permute-start(bf16[640,1024]{1,0:T(8,128)(2,1)S(1)} %bitcast.251), channel_id=1, source_target_pairs={{0,4},{4,8},{8,12},{12,0},{1,5},{5,9},{9,13},{13,1},{2,6},{6,10},{... | collective-permute-start | bytes 3932168 | tf_op jit(solution)/shard_map/ppermute | solution.py:105
  183.6 14.1 %copy-start.49 = (bf16[192,4,4,160]{0,3,2,1:T(8,128)(2,1)}, bf16[192,4,4,160]{0,3,2,1:T(8,128)(2,1)S(1)}, u32[]{:S(2)}) copy-start(bf16[192,4,4,160]{0,3,2,1:T(8,128)(2,1)S(1)} %copy.190) | copy-start | bytes 2949124
  199.5 8.7 collective-permute-start.5
  201.4 31.4 %copy-start.50 = (bf16[192,4,4,160]{0,3,2,1:T(8,128)(2,1)S(1)}, bf16[192,4,4,160]{0,3,2,1:T(8,128)(2,1)}, u32[]{:S(2)}) copy-start(bf16[192,4,4,160]{0,3,2,1:T(8,128)(2,1)} %copy-done.49) | copy-start | bytes 2949124
  201.4 29.6 %collective-permute-start.10 = (bf16[192,512]{1,0:T(8,128)(2,1)}, bf16[192,512]{1,0:T(8,128)(2,1)S(1)}, u32[]{:S(2)}, u32[]{:S(2)}) collective-permute-start(bf16[192,512]{1,0:T(8,128)(2,1)} %pad_maximum_fusion.15), channel_id=1, source_target_pairs={{0,20},{2,22},{4,16},{6,18},{16,4},{18,6},{20,0},{22,2},{1,21},{3,... | collective-permute-start | bytes 589832 | tf_op jit(solution)/shard_map/ppermute | solution.py:125
  203.6 26.8 %collective-permute-start.9 = (bf16[192,512]{1,0:T(8,128)(2,1)}, bf16[192,512]{1,0:T(8,128)(2,1)S(1)}, u32[]{:S(2)}, u32[]{:S(2)}) collective-permute-start(bf16[192,512]{1,0:T(8,128)(2,1)} %pad_maximum_fusion.15), channel_id=1, source_target_pairs={{0,18},{2,16},{4,22},{6,20},{16,2},{18,0},{20,6},{22,4},{1,19},{3,... | collective-permute-start | bytes 589832 | tf_op jit(solution)/shard_map/ppermute | solution.py:125
  204.7 24.9 %collective-permute-start.8 = (bf16[192,512]{1,0:T(8,128)(2,1)}, bf16[192,512]{1,0:T(8,128)(2,1)S(1)}, u32[]{:S(2)}, u32[]{:S(2)}) collective-permute-start(bf16[192,512]{1,0:T(8,128)(2,1)} %pad_maximum_fusion.15), channel_id=1, source_target_pairs={{0,16},{2,18},{4,20},{6,22},{16,0},{18,2},{20,4},{22,6},{1,17},{3,... | collective-permute-start | bytes 589832 | tf_op jit(solution)/shard_map/ppermute | solution.py:125
  205.9 13.2 %collective-permute-start.7 = (bf16[192,512]{1,0:T(8,128)(2,1)}, bf16[192,512]{1,0:T(8,128)(2,1)S(1)}, u32[]{:S(2)}, u32[]{:S(2)}) collective-permute-start(bf16[192,512]{1,0:T(8,128)(2,1)} %pad_maximum_fusion.15), channel_id=1, source_target_pairs={{0,6},{2,4},{4,2},{6,0},{16,22},{18,20},{20,18},{22,16},{1,7},{3,5... | collective-permute-start | bytes 589832 | tf_op jit(solution)/shard_map/ppermute | solution.py:125
  208.2 9.5 collective-permute-start.6
  217.6 14.1 %collective-permute-start.11 = (bf16[192,512]{1,0:T(8,128)(2,1)}, bf16[192,512]{1,0:T(8,128)(2,1)S(1)}, u32[]{:S(2)}, u32[]{:S(2)}) collective-permute-start(bf16[192,512]{1,0:T(8,128)(2,1)} %pad_maximum_fusion.15), channel_id=1, source_target_pairs={{0,22},{2,20},{4,18},{6,16},{16,6},{18,4},{20,2},{22,0},{1,23},{3,... | collective-permute-start | bytes 589832 | tf_op jit(solution)/shard_map/ppermute | solution.py:125
  232.4 18.6 %collective-permute-start.12 = (bf16[8,192,512]{2,1,0:T(8,128)(2,1)}, bf16[8,192,512]{2,1,0:T(8,128)(2,1)}, u32[]{:S(2)}, u32[]{:S(2)}) collective-permute-start(bf16[8,192,512]{2,1,0:T(8,128)(2,1)} %bitcast_dynamic-update-slice_fusion), channel_id=1, source_target_pairs={{0,1},{1,0},{2,3},{3,2},{4,5},{5,4},{6,7},{7,6},{8,9},{9,8},{10,11... | collective-permute-start | bytes 4718600 | tf_op jit(solution)/shard_map/ppermute | solution.py:98
  238.8 87.6 %collective-permute-start.3 = (bf16[640,2048]{1,0:T(8,128)(2,1)}, bf16[640,2048]{1,0:T(8,128)(2,1)}, u32[]{:S(2)}, u32[]{:S(2)}) collective-permute-start(bf16[640,2048]{1,0:T(8,128)(2,1)} %collective-permute-done.1), channel_id=1, source_target_pairs={{0,4},{4,8},{8,12},{12,0},{1,5},{5,9},{9,13},{13,1},{2,6},{6,10},{... | collective-permute-start | bytes 7864328 | tf_op jit(solution)/shard_map/ppermute | solution.py:105
  249.6 76.8 %collective-permute-start.4 = (bf16[640,1024]{1,0:T(8,128)(2,1)}, bf16[640,1024]{1,0:T(8,128)(2,1)}, u32[]{:S(2)}, u32[]{:S(2)}) collective-permute-start(bf16[640,1024]{1,0:T(8,128)(2,1)} %collective-permute-done.2), channel_id=1, source_target_pairs={{0,4},{4,8},{8,12},{12,0},{1,5},{5,9},{9,13},{13,1},{2,6},{6,10},{... | collective-permute-start | bytes 3932168 | tf_op jit(solution)/shard_map/ppermute | solution.py:105
  253.5 96.6 %collective-permute-start.13 = (bf16[2,192,2560]{2,1,0:T(8,128)(2,1)}, bf16[2,192,2560]{2,1,0:T(8,128)(2,1)}, u32[]{:S(2)}, u32[]{:S(2)}) collective-permute-start(bf16[2,192,2560]{2,1,0:T(8,128)(2,1)} %pad_maximum_fusion.9), channel_id=1, source_target_pairs={{0,16},{16,0},{1,17},{17,1},{2,18},{18,2},{3,19},{19,3},{4,20},{20... | collective-permute-start | bytes 5898248 | tf_op jit(solution)/shard_map/ppermute | solution.py:98
  258.6 75.0 %copy-start.2 = (bf16[3072,256]{1,0:T(8,128)(2,1)}, bf16[3072,256]{1,0:T(8,128)(2,1)S(1)}, u32[]{:S(2)}) copy-start(bf16[3072,256]{1,0:T(8,128)(2,1)S(1)} %get-tuple-element.171.key_ref) | copy-start | bytes 4718596
  332.3 37.8 %collective-permute-start.14 = (bf16[640,1024]{1,0:T(8,128)(2,1)}, bf16[640,1024]{1,0:T(8,128)(2,1)}, u32[]{:S(2)}, u32[]{:S(2)}) collective-permute-start(bf16[640,1024]{1,0:T(8,128)(2,1)} %get-tuple-element.179), channel_id=1, source_target_pairs={{0,4},{4,8},{8,12},{12,0},{1,5},{5,9},{9,13},{13,1},{2,6},{6,10},{... | collective-permute-start | bytes 3932168 | tf_op jit(solution)/shard_map/ppermute | solution.py:105
  370.1 418.0 %reduce-scatter.7.cloned.1.call-start = ((), (), s32[]{:S(2)}) async-start(), calls=%async_computation.16 | async-start | bytes 6553600 | tf_op jit(solution)/shard_map/reduce_scatter | solution.py:526
  370.1 64.9 %collective-permute-start.16 = (bf16[2,2,192,2560]{3,2,1,0:T(8,128)(2,1)}, bf16[2,2,192,2560]{3,2,1,0:T(8,128)(2,1)}, u32[]{:S(2)}, u32[]{:S(2)}) collective-permute-start(bf16[2,2,192,2560]{3,2,1,0:T(8,128)(2,1)} %pad_maximum_fusion.3), channel_id=1, source_target_pairs={{0,1},{1,0},{2,3},{3,2},{4,5},{5,4},{6,7},{7,6},{8,9},{9,8},{10,11... | collective-permute-start | bytes 11796488 | tf_op jit(solution)/shard_map/ppermute | solution.py:98
  371.4 30.6 %collective-permute-start.15 = (bf16[640,1024]{1,0:T(8,128)(2,1)}, bf16[640,1024]{1,0:T(8,128)(2,1)S(1)}, u32[]{:S(2)}, u32[]{:S(2)}) collective-permute-start(bf16[640,1024]{1,0:T(8,128)(2,1)} %collective-permute-done.4), channel_id=1, source_target_pairs={{0,4},{4,8},{8,12},{12,0},{1,5},{5,9},{9,13},{13,1},{2,6},{6,10},{... | collective-permute-start | bytes 3932168 | tf_op jit(solution)/shard_map/ppermute | solution.py:105
  372.6 57.5 %collective-permute-start.17 = (bf16[640,1024]{1,0:T(8,128)(2,1)S(1)}, bf16[640,1024]{1,0:T(8,128)(2,1)}, u32[]{:S(2)}, u32[]{:S(2)}) collective-permute-start(bf16[640,1024]{1,0:T(8,128)(2,1)S(1)} %copy-done.48), channel_id=1, source_target_pairs={{0,4},{4,8},{8,12},{12,0},{1,5},{5,9},{9,13},{13,1},{2,6},{6,10},{... | collective-permute-start | bytes 3932168 | tf_op jit(solution)/shard_map/ppermute | solution.py:105
  396.2 38.9 %copy-start.19 = (bf16[1,2,192,2560]{3,2,1,0:T(8,128)(2,1)S(1)}, bf16[1,2,192,2560]{3,2,1,0:T(8,128)(2,1)}, u32[]{:S(2)}) copy-start(bf16[1,2,192,2560]{3,2,1,0:T(8,128)(2,1)} %copy-done.18) | copy-start | bytes 5898244
  504.0 284.2 %reduce-scatter.9.cloned.1.call-start = ((), (), s32[]{:S(2)}) async-start(), calls=%async_computation.17 | async-start | bytes 6553600 | tf_op jit(solution)/shard_map/reduce_scatter | solution.py:526
  526.0 7.7 collective-permute-start.18
  549.9 24.2 %collective-permute-start.20 = (bf16[192,2560]{1,0:T(8,128)(2,1)}, bf16[192,2560]{1,0:T(8,128)(2,1)}, u32[]{:S(2)}, u32[]{:S(2)}) collective-permute-start(bf16[192,2560]{1,0:T(8,128)(2,1)} %get-tuple-element.163), channel_id=1, source_target_pairs={{0,16},{2,18},{16,0},{18,2},{1,17},{3,19},{17,1},{19,3},{4,20},{6,... | collective-permute-start | bytes 2949128 | tf_op jit(solution)/shard_map/ppermute | solution.py:557
  551.9 23.0 %collective-permute-start.19 = (bf16[192,2560]{1,0:T(8,128)(2,1)}, bf16[192,2560]{1,0:T(8,128)(2,1)}, u32[]{:S(2)}, u32[]{:S(2)}) collective-permute-start(bf16[192,2560]{1,0:T(8,128)(2,1)} %get-tuple-element.165), channel_id=1, source_target_pairs={{0,2},{2,0},{16,18},{18,16},{1,3},{3,1},{17,19},{19,17},{4,6},{6,4... | collective-permute-start | bytes 2949128 | tf_op jit(solution)/shard_map/ppermute | solution.py:557
  552.7 22.2 %copy-start.30 = (bf16[1536,2048]{1,0:T(8,128)(2,1)}, bf16[1536,2048]{1,0:T(8,128)(2,1)S(1)}, u32[]{:S(2)}) copy-start(bf16[1536,2048]{1,0:T(8,128)(2,1)S(1)} %pad_maximum_fusion.1) | copy-start | bytes 18874372
  587.3 214.7 %all-gather.14.cloned.1.call-start = ((), (), s32[]{:S(2)}) async-start(), calls=%async_computation.15 | async-start | bytes 8847360 | tf_op jit(solution)/shard_map/all_gather | solution.py:530
  588.1 402.3 %reduce-scatter.11.cloned.1.call-start = ((), (), s32[]{:S(2)}) async-start(), calls=%async_computation.18 | async-start | bytes 6553600 | tf_op jit(solution)/shard_map/reduce_scatter | solution.py:526
  590.4 22.6 %collective-permute-start.21 = (bf16[192,2560]{1,0:T(8,128)(2,1)S(1)}, bf16[192,2560]{1,0:T(8,128)(2,1)S(1)}, u32[]{:S(2)}, u32[]{:S(2)}) collective-permute-start(bf16[192,2560]{1,0:T(8,128)(2,1)S(1)} %copy-done.54), channel_id=1, source_target_pairs={{0,18},{2,16},{16,2},{18,0},{1,19},{3,17},{17,3},{19,1},{4,22},{6,... | collective-permute-start | bytes 2949128 | tf_op jit(solution)/shard_map/ppermute | solution.py:557
  616.6 20.9 %collective-permute-start.22 = (bf16[192,2560]{1,0:T(8,128)(2,1)S(1)}, bf16[192,2560]{1,0:T(8,128)(2,1)}, u32[]{:S(2)}, u32[]{:S(2)}) collective-permute-start(bf16[192,2560]{1,0:T(8,128)(2,1)S(1)} %copy-done.22), channel_id=1, source_target_pairs={{0,2},{2,0},{1,3},{3,1},{4,6},{6,4},{5,7},{7,5},{8,10},{10,8},{9,1... | collective-permute-start | bytes 2949128 | tf_op jit(solution)/shard_map/ppermute | solution.py:98
  641.3 43.2 %collective-permute-start.23 = (bf16[2,192,2560]{2,1,0:T(8,128)(2,1)}, bf16[2,192,2560]{2,1,0:T(8,128)(2,1)}, u32[]{:S(2)}, u32[]{:S(2)}) collective-permute-start(bf16[2,192,2560]{2,1,0:T(8,128)(2,1)} %pad_maximum_fusion.10), channel_id=1, source_target_pairs={{0,16},{16,0},{1,17},{17,1},{2,18},{18,2},{3,19},{19,3},{4,20},{20... | collective-permute-start | bytes 5898248 | tf_op jit(solution)/shard_map/ppermute | solution.py:98
  689.9 6.8 collective-permute-start.24
  693.3 49.6 %collective-permute-start.29 = (bf16[2,2,192,2560]{3,2,1,0:T(8,128)(2,1)}, bf16[2,2,192,2560]{3,2,1,0:T(8,128)(2,1)}, u32[]{:S(2)}, u32[]{:S(2)}) collective-permute-start(bf16[2,2,192,2560]{3,2,1,0:T(8,128)(2,1)} %pad_maximum_fusion.4), channel_id=1, source_target_pairs={{0,1},{1,0},{2,3},{3,2},{4,5},{5,4},{6,7},{7,6},{8,9},{9,8},{10,11... | collective-permute-start | bytes 11796488 | tf_op jit(solution)/shard_map/ppermute | solution.py:90
  699.6 25.4 %collective-permute-start.25 = (bf16[2,192,512]{2,1,0:T(8,128)(2,1)}, bf16[2,192,512]{2,1,0:T(8,128)(2,1)}, u32[]{:S(2)}, u32[]{:S(2)}) collective-permute-start(bf16[2,192,512]{2,1,0:T(8,128)(2,1)} %get-tuple-element.186), channel_id=1, source_target_pairs={{0,2},{2,0},{16,18},{18,16},{1,3},{3,1},{17,19},{19,17},{4,6},{6,4... | collective-permute-start | bytes 1179656 | tf_op jit(solution)/shard_map/ppermute | solution.py:137
  699.6 25.4 %collective-permute-start.27 = (bf16[2,192,512]{2,1,0:T(8,128)(2,1)}, bf16[2,192,512]{2,1,0:T(8,128)(2,1)}, u32[]{:S(2)}, u32[]{:S(2)}) collective-permute-start(bf16[2,192,512]{2,1,0:T(8,128)(2,1)} %get-tuple-element.187), channel_id=1, source_target_pairs={{0,18},{2,16},{16,2},{18,0},{1,19},{3,17},{17,3},{19,1},{4,22},{6,... | collective-permute-start | bytes 1179656 | tf_op jit(solution)/shard_map/ppermute | solution.py:137
  701.6 25.6 %collective-permute-start.26 = (bf16[2,192,512]{2,1,0:T(8,128)(2,1)S(1)}, bf16[2,192,512]{2,1,0:T(8,128)(2,1)}, u32[]{:S(2)}, u32[]{:S(2)}) collective-permute-start(bf16[2,192,512]{2,1,0:T(8,128)(2,1)S(1)} %get-tuple-element.188), channel_id=1, source_target_pairs={{0,16},{2,18},{16,0},{18,2},{1,17},{3,19},{17,1},{19,3},{4,20},{6,... | collective-permute-start | bytes 1179656 | tf_op jit(solution)/shard_map/ppermute | solution.py:137
  703.7 32.0 %copy-start.53 = (f32[192,128]{0,1:T(8,128)S(1)}, f32[192,128]{0,1:T(8,128)}, u32[]{:S(2)}) copy-start(f32[192,128]{0,1:T(8,128)} %copy-done.52) | copy-start | bytes 294916
  703.7 32.0 %copy-start.55 = (f32[192,128]{0,1:T(8,128)S(1)}, f32[192,128]{0,1:T(8,128)}, u32[]{:S(2)}) copy-start(f32[192,128]{0,1:T(8,128)} %copy.208) | copy-start | bytes 294916
  729.5 11.0 %collective-permute-start.28 = (bf16[192,512]{1,0:T(8,128)(2,1)}, bf16[192,512]{1,0:T(8,128)(2,1)}, u32[]{:S(2)}, u32[]{:S(2)}) collective-permute-start(bf16[192,512]{1,0:T(8,128)(2,1)} %dynamic-slice_bitcast_fusion.7), channel_id=1, source_target_pairs={{0,4},{4,0},{1,5},{5,1},{2,6},{6,2},{3,7},{7,3},{8,12},{12,8},{9,1... | collective-permute-start | bytes 589832 | tf_op jit(solution)/shard_map/ppermute | solution.py:90
  746.7 39.7 %all-to-all-start.2 = ((bf16[8,192,704]{2,1,0:T(8,128)(2,1)}), bf16[8,192,704]{2,1,0:T(8,128)(2,1)S(1)}, u32[]{:S(2)}, u32[]{:S(2)}) async-start(bf16[8,192,704]{2,1,0:T(8,128)(2,1)} %maximum_bitcast_fusion), calls=%async_computation.2 | async-start | bytes 4718592 | tf_op jit(solution)/shard_map/all_to_all | solution.py:143
  751.9 333.8 %reduce-scatter.5.cloned.1.call-start = ((), (), s32[]{:S(2)}) async-start(), calls=%async_computation.14 | async-start | bytes 8847360 | tf_op jit(solution)/shard_map/reduce_scatter | solution.py:642
  791.6 34.0 %all-to-all-start.3 = ((bf16[4,160,2048]{2,1,0:T(8,128)(2,1)}), bf16[4,160,2048]{2,1,0:T(8,128)(2,1)S(1)}, u32[]{:S(2)}, u32[]{:S(2)}) async-start(bf16[4,160,2048]{2,1,0:T(8,128)(2,1)} %bitcast.232), calls=%async_computation.6 | async-start | bytes 5242880 | tf_op jit(solution)/shard_map/all_to_all | solution.py:143
  831.7 131.7 %all-to-all-start.4 = ((bf16[16,160,704]{2,1,0:T(8,128)(2,1)}), bf16[16,160,704]{2,1,0:T(8,128)(2,1)}, u32[]{:S(2)}, u32[]{:S(2)}) async-start(bf16[16,160,704]{2,1,0:T(8,128)(2,1)} %bitcast.224), calls=%async_computation.7 | async-start | bytes 7864320 | tf_op jit(solution)/shard_map/all_to_all | solution.py:143
  838.5 156.4 %collective-permute-start.32 = (bf16[4,160,2048]{2,1,0:T(8,128)(2,1)S(1)}, bf16[4,160,2048]{2,1,0:T(8,128)(2,1)}, u32[]{:S(2)}, u32[]{:S(2)}) collective-permute-start(bf16[4,160,2048]{2,1,0:T(8,128)(2,1)S(1)} %all-to-all-done.3.refs_1_), channel_id=1, source_target_pairs={{0,16},{16,0},{1,17},{17,1},{2,18},{18,2},{3,19},{19,3},{4,20},{20... | collective-permute-start | bytes 7864328 | tf_op jit(solution)/shard_map/ppermute | solution.py:90
  967.3 64.2 %collective-permute-start.30 = (bf16[4,160,704]{2,1,0:T(8,128)(2,1)}, bf16[4,160,704]{2,1,0:T(8,128)(2,1)}, u32[]{:S(2)}, u32[]{:S(2)}) collective-permute-start(bf16[4,160,704]{2,1,0:T(8,128)(2,1)} %reduce_sum.111), channel_id=1, source_target_pairs={{0,16},{16,0},{1,17},{17,1},{2,18},{18,2},{3,19},{19,3},{4,20},{20... | collective-permute-start | bytes 2703368 | tf_op jit(solution)/shard_map/ppermute | solution.py:98
  990.3 45.5 %all-to-all-start.5 = ((bf16[4,160,1024]{2,1,0:T(8,128)(2,1)}), bf16[4,160,1024]{2,1,0:T(8,128)(2,1)}, u32[]{:S(2)}, u32[]{:S(2)}) async-start(bf16[4,160,1024]{2,1,0:T(8,128)(2,1)} %bitcast.264), calls=%async_computation.9 | async-start | bytes 2621440 | tf_op jit(solution)/shard_map/all_to_all | solution.py:143
  1012.7 18.8 %copy-start.40 = (bf16[4,160,704]{2,1,0:T(8,128)(2,1)S(1)}, bf16[4,160,704]{2,1,0:T(8,128)(2,1)}, u32[]{:S(2)}) copy-start(bf16[4,160,704]{2,1,0:T(8,128)(2,1)} %reduce_sum.111) | copy-start | bytes 2703364
  1035.9 30.2 %collective-permute-start.31 = (bf16[4,160,1024]{2,1,0:T(8,128)(2,1)}, bf16[4,160,1024]{2,1,0:T(8,128)(2,1)S(1)}, u32[]{:S(2)}, u32[]{:S(2)}) collective-permute-start(bf16[4,160,1024]{2,1,0:T(8,128)(2,1)} %all-to-all-done.5.refs_1_), channel_id=1, source_target_pairs={{0,16},{16,0},{1,17},{17,1},{2,18},{18,2},{3,19},{19,3},{4,20},{20... | collective-permute-start | bytes 3932168 | tf_op jit(solution)/shard_map/ppermute | solution.py:90
  1066.1 18.9 %copy-start.66 = (f32[160,2]{0,1:T(2,128)S(1)}, f32[160,2]{0,1:T(2,128)}, u32[]{:S(2)}) copy-start(f32[160,2]{0,1:T(2,128)} %param.27) | copy-start | bytes 3844
  1066.1 18.9 %copy-start.71 = (f32[160,2]{0,1:T(2,128)S(1)}, f32[160,2]{0,1:T(2,128)}, u32[]{:S(2)}) copy-start(f32[160,2]{0,1:T(2,128)} %param.28) | copy-start | bytes 3844
  1066.1 18.9 %copy-start.72 = (f32[160,2]{0,1:T(2,128)S(1)}, f32[160,2]{0,1:T(2,128)}, u32[]{:S(2)}) copy-start(f32[160,2]{0,1:T(2,128)} %param.29) | copy-start | bytes 3844
  1066.1 19.5 %copy-start.10 = (bf16[1,1,192,2560]{3,2,1,0:T(8,128)(2,1)S(1)}, bf16[1,1,192,2560]{3,2,1,0:T(8,128)(2,1)}, u32[]{:S(2)}) copy-start(bf16[1,1,192,2560]{3,2,1,0:T(8,128)(2,1)} %param.15) | copy-start | bytes 2949124
  1066.1 19.5 %copy-start.59 = (f32[192]{0:T(256)S(1)}, f32[192]{0:T(256)}, u32[]{:S(2)}) copy-start(f32[192]{0:T(256)} %copy-done.58) | copy-start | bytes 2308
  1066.1 19.5 %copy-start.67 = (f32[192]{0:T(256)S(1)}, f32[192]{0:T(256)}, u32[]{:S(2)}) copy-start(f32[192]{0:T(256)} %get-tuple-element.202) | copy-start | bytes 2308
  (65 other events, 303.6 us)
Sparse Core Ops, SparseCore 0:
  12.4 69.7 all-gather.5
  85.2 107.3 all-gather.7
  195.1 116.5 all-gather.9
  370.2 56.2 all-gather.11
  504.1 97.5 reduce-scatter.6
  604.4 94.2 reduce-scatter.8
  700.6 81.4 all-gather.13
  785.0 151.4 reduce-scatter.10
  939.9 93.2 reduce-scatter.4

commit v10 on v9

--- a/solution.py
+++ b/solution.py
@@ -527,7 +527,6 @@
 
     down_term = low(dot(incoming_all, activated_low, (0, 0)))
     down_rows = to_owners(down_term)
-    attn_all = lax.all_gather(after(attn_low, down_term), GROUP, axis=0, tiled=True)
     grad_gate, grad_up = glu_back(wide(after(grad_act, down_term)))
     grad_gate_up = low(jnp.concatenate([grad_gate, grad_up], axis=1))
 
@@ -563,6 +562,7 @@
 
     gate_rows = to_owners(gate_term)
     up_rows = to_owners(up_term)
+    attn_all = lax.all_gather(after(attn_low, up_term), GROUP, axis=0, tiled=True)
     grad_middle = (
         wide(incoming)
         + factor_two * grad_normed_two
@@ -637,8 +637,8 @@
     out_total = low(dot(attn_all, out_columns, (0, 0)))
     first_pieces = in_plane(jnp.concatenate([down_rows, gate_rows], axis=1), all_columns)
     total = jnp.concatenate([qkv_total, out_total], axis=1)
-    total = to_rows(after(total, first_pieces[0]))
-    up_pieces = in_plane(up_rows, total)
+    up_pieces = in_plane(up_rows, first_pieces[0])
+    total = to_rows(after(total, up_pieces[0]))
     branch = lax.psum_scatter(
         after(branch, all_columns), GROUP, scatter_dimension=0, tiled=True
     )
@@ -646,7 +646,7 @@
     mlp_outs, gate_dot = mlp_updated(0, first_pieces, piece, mlp_outs)
     (grad_mlp, second_new_mlp, new_mlp), up_dot = mlp_updated(1, up_pieces, 0, mlp_outs)
     grad_gain_two = gate_dot + up_dot
-    total = doubled(total, "seq", 1, 0).reshape(shares, own_rows, -1)
+    total = doubled(after(total, gate_dot), "seq", 1, 0).reshape(shares, own_rows, -1)
     grad_qkv = joined(total[:, :, :qkv_share])
     grad_out = joined(total[:, :, qkv_share:])
     hidden_out = low(middle + wide(branch)).reshape(1, 1, tok_rows, width)

time: 1110 us -> 1110 us (level)
    all_to_all x5, waiting for transfers between devices: 192 us -> 84.8 us  [exchanged(): return lax.all_to_all(value, axes, split_axis=0, concat_axis=0, tiled=True)]
    ppermute x6, waiting for transfers between devices: 21 us -> 93.8 us  [swapped(): return lax.ppermute(value, axis, [(0, 1), (1, 0)])]
    all_gather x1, waiting for transfers between devices: 0.01 us -> 34.9 us  [on_device(): lax.all_gather(after(attn_low, up_term), GROUP, axis=0, tiled=True)]
    ppermute x3, waiting for transfers between devices: 30.9 us -> 42.2 us  [on_device(): arrived.append(lax.ppermute(term, CHIPS, traded(CHIPS, step)))]
  transfers between devices with their start and end apart: 47 -> 47, of which waited for: 21 -> 22; matrix products, arithmetic and copies ran while one was open for 32% -> 31% of each run, Pallas kernels for 10% -> 10%
where the time goes in v10:
time: 1110 us; the launch traced here: 1100 us
  waiting for transfers between devices  455 us (41%)
  matrix products  168 us (15%)
  local copies, waits for them, and re-layouts  126 us (11%)
  other arithmetic  116 us (10%)
  Pallas kernels  109 us (10%)
  starting transfers between devices  73.8 us (7%)
  blocking collectives  33.5 us (3%)
  between operations  15.5 us (1%)
    dot_general x19, matrix products, dot(): lax.dot_general(left, right, ((contract[:1], contract[1:]), ((), ())), pr...  168 us
    ppermute x7, waiting for transfers between devices, next_plane(): lax.ppermute(block, PLANES, [(one, (one + 1) % count) for one in range(co...  130 us
    ppermute x6, waiting for transfers between devices, swapped(): return lax.ppermute(value, axis, [(0, 1), (1, 0)])  93.8 us
    all_to_all x5, waiting for transfers between devices, exchanged(): return lax.all_to_all(value, axes, split_axis=0, concat_axis=0, tiled=True)  84.8 us
    pallas_call x3, Pallas kernels, mlp_adam(): pl.pallas_call(lambda *refs: mlp_adam_kernel(rate, per_side, part < 2, *r...  55.3 us
    ppermute x3, waiting for transfers between devices, on_device(): arrived.append(lax.ppermute(term, CHIPS, traded(CHIPS, step)))  42.2 us
    all_gather x1, waiting for transfers between devices, on_device(): lax.all_gather(after(attn_low, up_term), GROUP, axis=0, tiled=True)  34.9 us
    all_to_all x1, blocking collectives, exchanged(): return lax.all_to_all(value, axes, split_axis=0, concat_axis=0, tiled=True)  33.5 us
  transfers between devices with their start and end apart: 47, of which 22 were waited for; matrix products, arithmetic and copies ran while one was open for 31% of the time, Pallas kernels for 10%

profile of v10, /device:TPU:13, one launch (start us, length us, event | category | flops | bytes accessed | tf_op | source)
XLA Modules:
  0.0 1096.3 jit_solution(7423997192152148202)
XLA Ops:
  12.4 7.2 mlp_chunks.1
  19.5 33.5 %all_to_all.30 = bf16[4,160,2048]{2,1,0:T(8,128)(2,1)} all-to-all(bf16[4,160,2048]{2,1,0:T(8,128)(2,1)S(1)} %get-tuple-element.55), channel_id=1, replica_groups=mesh['seq'=2,'g'=2,'h'=2,'k'=2,'c'=2] {'k','c'}, dimensions={0} | all-to-all | bytes 5242880 | tf_op jit(solution)/shard_map/all_to_all | solution.py:143
  53.0 29.1 %all-gather.6.cloned.1.call-done = bf16[640,2816]{1,0:T(8,128)(2,1)} async-done(((bf16[160,2816]{1,0:T(8,128)(2,1)}), bf16[640,2816]{1,0:T(8,128)(2,1)}) %all-gather.6.cloned.1.call-update) | async-done | bytes 3604496 | tf_op jit(solution)/shard_map/all_gather | solution.py:457
  88.1 5.7 all-to-all-start.1
  98.7 47.2 %all-to-all-done.1 = bf16[4,160,1024]{2,1,0:T(8,128)(2,1)S(1)} async-done(((bf16[4,160,1024]{2,1,0:T(8,128)(2,1)}), bf16[4,160,1024]{2,1,0:T(8,128)(2,1)S(1)}, u32[]{:S(2)}, u32[]{:S(2)}) %all-to-all-start.1) | async-done | bytes 1310752 | tf_op jit(solution)/shard_map/all_to_all | solution.py:143
  152.7 30.2 %collective-permute-done.2 = bf16[640,1024]{1,0:T(8,128)(2,1)} collective-permute-done((bf16[640,1024]{1,0:T(8,128)(2,1)S(1)}, bf16[640,1024]{1,0:T(8,128)(2,1)}, u32[]{:S(2)}, u32[]{:S(2)}) %collective-permute-start.2) | collective-permute-done | bytes 1310752 | tf_op jit(solution)/shard_map/ppermute | solution.py:105
  183.5 9.1 all-gather.8.cloned.1.call-done
  192.6 5.0 fusion.2
  211.0 6.6 collective-permute-done.6
  219.9 9.8 collective-permute-done.8
  232.8 6.0 fusion.6
  261.0 65.4 %collective-permute-done.4 = bf16[640,1024]{1,0:T(8,128)(2,1)} collective-permute-done((bf16[640,1024]{1,0:T(8,128)(2,1)}, bf16[640,1024]{1,0:T(8,128)(2,1)}, u32[]{:S(2)}, u32[]{:S(2)}) %collective-permute-start.4) | collective-permute-done | bytes 1310752 | tf_op jit(solution)/shard_map/ppermute | solution.py:105
  328.8 3.5 fusion.95
  333.5 16.5 %attend.1 = (bf16[192,2560]{1,0:T(8,128)(2,1)}, f32[5,1,384]{2,1,0:T(1,128)S(1)}) custom-call(bf16[192,2560]{1,0:T(8,128)(2,1)S(1)} %copy-done.5, bf16[3072,256]{1,0:T(8,128)(2,1)S(1)} %get-tuple-element.173.key_ref, bf16[256,3072]{1,0:T(8,128)(2,1)S(1)} %copy.196.value_t_ref, f32[3072,384]{1,0:T(8,128)} %pad_maximum_fusion.2.bias_ref), custom_call_target="tpu_custom_call" | custom-call | flops 6039797760 | bytes 18087936 | tf_op jit(solution)/shard_map/attend/pallas_call | solution.py:308
  357.7 4.8 fusion.18
  362.5 4.7 fusion.22
  376.4 5.4 broadcast_in_dim.87
  385.2 3.6 constant_dynamic-update-slice_fusion.2
  390.2 3.6 constant_dynamic-update-slice_fusion.1
  396.2 5.8 collective-permute-done.15
  402.0 28.2 %collective-permute-done.17 = bf16[640,1024]{1,0:T(8,128)(2,1)} collective-permute-done((bf16[640,1024]{1,0:T(8,128)(2,1)S(1)}, bf16[640,1024]{1,0:T(8,128)(2,1)}, u32[]{:S(2)}, u32[]{:S(2)}) %collective-permute-start.17) | collective-permute-done | bytes 1310752 | tf_op jit(solution)/shard_map/ppermute | solution.py:105
  435.2 4.1 select_bitcast_fusion.1
  439.4 6.1 pad_maximum_fusion
  445.5 7.1 copy.199
  452.6 11.8 %convolution_convert_fusion.6 = bf16[1536,1024]{1,0:T(8,128)(2,1)} fusion(bf16[1536,2560]{1,0:T(8,128)(2,1)} %bitcast.238, bf16[2560,1024]{1,0:T(8,128)(2,1)S(1)} %bitcast.250), kind=kOutput, calls=%fused_computation.54 | convolution fusion | flops 8054636544 | bytes 16252928 | tf_op jit(solution)/shard_map/dot_general | solution.py:79
  464.5 20.6 %fusion.96 = f32[1536,2048]{1,0:T(8,128)S(1)} fusion(bf16[1536,2560]{1,0:T(8,128)(2,1)} %all-gather.12.cloned.1.call-done, bf16[2560,2048]{1,0:T(8,128)(2,1)} %get-tuple-element.211), kind=kOutput, calls=%fused_computation.223 | convolution fusion | flops 16106127360 | bytes 30932992 | tf_op jit(solution)/shard_map/dot_general | solution.py:79
  485.1 4.8 copy-done.11
  493.8 10.3 convolution_convert_fusion.3
  504.2 8.8 fusion.8
  516.3 9.8 convolution_convert_fusion.4
  527.0 6.8 collective-permute-done.18
  533.7 12.6 %add_convert_fusion = bf16[768,2560]{1,0:T(8,128)(2,1)S(1)} fusion(bf16[768,2560]{1,0:T(8,128)(2,1)} %collective-permute-done.18, bf16[768,2048]{1,0:T(8,128)(2,1)} %bitcast.262, bf16[2560,2048]{1,0:T(8,128)(2,1)} %get-tuple-element.211), kind=kOutput, calls=%fused_computation.4 | convolution fusion | flops 8058961920 | bytes 21495808 | tf_op jit(solution)/shard_map/dot_general | solution.py:79
  552.5 21.4 %collective-permute-done.20 = bf16[192,2560]{1,0:T(8,128)(2,1)} collective-permute-done((bf16[192,2560]{1,0:T(8,128)(2,1)}, bf16[192,2560]{1,0:T(8,128)(2,1)}, u32[]{:S(2)}, u32[]{:S(2)}) %collective-permute-start.20) | collective-permute-done | bytes 983072 | tf_op jit(solution)/shard_map/ppermute | solution.py:556
  574.7 12.4 %convolution_convert_fusion.2 = bf16[2560,1024]{1,0:T(8,128)(2,1)} fusion(bf16[1536,2560]{1,0:T(8,128)(2,1)} %all-gather.12.cloned.1.call-done, bf16[1536,2048]{1,0:T(8,128)(2,1)S(1)} %pad_maximum_fusion.1), kind=kOutput, calls=%fused_computation.39 | convolution fusion | flops 8055685120 | bytes 16252928 | tf_op jit(solution)/shard_map/dot_general | solution.py:79
  587.2 13.9 %convolution_convert_fusion.1 = bf16[2560,1024]{1,0:T(8,128)(2,1)} fusion(bf16[1536,2560]{1,0:T(8,128)(2,1)} %all-gather.12.cloned.1.call-done, bf16[1536,2048]{1,0:T(8,128)(2,1)} %copy-done.31), kind=kOutput, calls=%fused_computation.38 | convolution fusion | flops 8055685120 | bytes 16252928 | tf_op jit(solution)/shard_map/dot_general | solution.py:79
  605.0 20.0 %collective-permute-done.21 = bf16[192,2560]{1,0:T(8,128)(2,1)S(1)} collective-permute-done((bf16[192,2560]{1,0:T(8,128)(2,1)S(1)}, bf16[192,2560]{1,0:T(8,128)(2,1)S(1)}, u32[]{:S(2)}, u32[]{:S(2)}) %collective-permute-start.21) | collective-permute-done | bytes 983072 | tf_op jit(solution)/shard_map/ppermute | solution.py:556
  632.1 5.5 fusion.16
  637.6 6.1 fusion.31
  662.5 29.9 %attend_back.1 = (f32[192,2560]{1,0:T(8,128)}, f32[3072,512]{1,0:T(8,128)}) custom-call(bf16[192,2560]{1,0:T(8,128)(2,1)S(1)} %copy-done.6, bf16[192,2560]{1,0:T(8,128)(2,1)S(1)} %copy.205.grad_ref, bf16[3072,256]{1,0:T(8,128)(2,1)S(1)} %copy-done.3, bf16[256,3072]{1,0:T(8,128)(2,1)S(1)} %copy-done.4, bf16[3072,256]{1,0:T(8,128)(2,1)} %get-tuple-element.170.value_ref, ...), custom_call_target="tpu_custom_call" | custom-call | flops 15099494400 | bytes 22806528 | tf_op jit(solution)/shard_map/attend_back/pallas_call | solution.py:367
  701.1 3.4 collective-permute-start.24
  717.7 12.7 %collective-permute-done.25 = bf16[2,192,512]{2,1,0:T(8,128)(2,1)} collective-permute-done((bf16[2,192,512]{2,1,0:T(8,128)(2,1)}, bf16[2,192,512]{2,1,0:T(8,128)(2,1)}, u32[]{:S(2)}, u32[]{:S(2)}) %collective-permute-start.25) | collective-permute-done | bytes 393248 | tf_op jit(solution)/shard_map/ppermute | solution.py:137
  741.2 7.7 collective-permute-done.28
  754.8 9.1 all-to-all-start.2
  763.9 3.5 pad_maximum_fusion.8
  767.4 24.0 %all-to-all-done.2 = bf16[8,192,704]{2,1,0:T(8,128)(2,1)S(1)} async-done(((bf16[8,192,704]{2,1,0:T(8,128)(2,1)}), bf16[8,192,704]{2,1,0:T(8,128)(2,1)S(1)}, u32[]{:S(2)}, u32[]{:S(2)}) %all-to-all-start.2) | async-done | bytes 2162720 | tf_op jit(solution)/shard_map/all_to_all | solution.py:143
  792.8 4.7 all-to-all-start.3
  797.5 13.5 %convolution_convert_fusion = bf16[1536,2560]{1,0:T(8,128)(2,1)} fusion(bf16[1536,1024]{1,0:T(8,128)(2,1)} %copy-done.43, bf16[2560,1024]{1,0:T(8,128)(2,1)} %copy-done.36), kind=kOutput, calls=%fused_computation | convolution fusion | flops 8056995840 | bytes 16252928 | tf_op jit(solution)/shard_map/dot_general | solution.py:79
  814.9 3.9 fusion.97
  818.7 5.1 fusion.24
  823.9 13.6 %all-to-all-done.3.refs_1_ = bf16[4,160,2048]{2,1,0:T(8,128)(2,1)S(1)} async-done(((bf16[4,160,2048]{2,1,0:T(8,128)(2,1)}), bf16[4,160,2048]{2,1,0:T(8,128)(2,1)S(1)}, u32[]{:S(2)}, u32[]{:S(2)}) %all-to-all-start.3) | async-done | bytes 2621472 | tf_op jit(solution)/shard_map/all_to_all | solution.py:143
  837.4 6.5 all-to-all-start.4
  843.9 34.9 %all-gather.14.cloned.1.call-done = bf16[1536,2560]{1,0:T(8,128)(2,1)} async-done(((bf16[192,2560]{1,0:T(8,128)(2,1)}), bf16[1536,2560]{1,0:T(8,128)(2,1)}) %all-gather.14.cloned.1.call-update) | async-done | bytes 7864336 | tf_op jit(solution)/shard_map/all_gather | solution.py:565
  878.9 6.4 convolution_convert_fusion.5
  887.3 6.4 copy.220
  893.7 6.0 all-to-all-start.5
  904.0 7.5 fusion
  911.5 76.7 %collective-permute-done.30.refs_2_ = bf16[4,160,2048]{2,1,0:T(8,128)(2,1)} collective-permute-done((bf16[4,160,2048]{2,1,0:T(8,128)(2,1)S(1)}, bf16[4,160,2048]{2,1,0:T(8,128)(2,1)}, u32[]{:S(2)}, u32[]{:S(2)}) %collective-permute-start.30) | collective-permute-done | bytes 2621472 | tf_op jit(solution)/shard_map/ppermute | solution.py:90
  988.2 17.6 %mlp_adam.3 = (f32[3,160,7680]{2,1,0:T(8,128)}, f32[3,160,7680]{2,1,0:T(8,128)}, f32[3,160,7680]{2,1,0:T(8,128)}, f32[160,1]{1,0:T(8,128)}) custom-call(s32[1]{0:T(128)} %bitcast.4.refs_0_, bf16[4,160,2048]{2,1,0:T(8,128)(2,1)S(1)} %all-to-all-done.3.refs_1_, bf16[4,160,2048]{2,1,0:T(8,128)(2,1)} %collective-permute-done.30.refs_2_, ...), custom_call_target="tpu_custom_call" | custom-call | flops 24576000 | bytes 31948800 | tf_op jit(solution)/shard_map/mlp_adam/pallas_call | solution.py:241
  1005.8 18.5 %mlp_adam.4 = (f32[3,160,7680]{2,1,0:T(8,128)}, f32[3,160,7680]{2,1,0:T(8,128)}, f32[3,160,7680]{2,1,0:T(8,128)}, f32[160,1]{1,0:T(8,128)S(1)}) custom-call(s32[1]{0:T(128)} %bitcast.4.refs_0_, bf16[4,160,2048]{2,1,0:T(8,128)(2,1)S(1)} %all-to-all-done.3.refs_1_, ...), custom_call_target="tpu_custom_call", output_to_operand_aliasing={{0}: (7, {}), {1}: (8, {}), {2}: (9, {})} | custom-call | flops 24576000 | bytes 31948800 | tf_op jit(solution)/shard_map/mlp_adam/pallas_call | solution.py:241
  1024.2 4.0 reduce_sum.111
  1030.6 7.8 fusion.25
  1047.5 19.3 %mlp_adam.5 = (f32[3,160,7680]{2,1,0:T(8,128)}, f32[3,160,7680]{2,1,0:T(8,128)}, f32[3,160,7680]{2,1,0:T(8,128)}, f32[160,1]{1,0:T(8,128)S(1)}) custom-call(s32[1]{0:T(128)} %bitcast.4.refs_0_, bf16[4,160,1024]{2,1,0:T(8,128)(2,1)} %all-to-all-done.4.refs_1_, ...), custom_call_target="tpu_custom_call", output_to_operand_aliasing={{0}: (7, {}), {1}: (8, {}), {2}: (9, {})} | custom-call | flops 24576000 | bytes 31948800 | tf_op jit(solution)/shard_map/mlp_adam/pallas_call | solution.py:241
  1073.3 7.5 multiply_subtract_fusion
  1084.5 4.8 fusion.50
  (384 shorter events, 212.7 us)
Async XLA Ops:
  7.2 75.0 %all-gather.6.cloned.1.call-start = ((), (), s32[]{:S(2)}) async-start(), calls=%async_computation.10 | async-start | bytes 4505600 | tf_op jit(solution)/shard_map/all_gather | solution.py:457
  12.2 180.4 %all-gather.8.cloned.1.call-start = ((), (), s32[]{:S(2)}) async-start(), calls=%async_computation.11 | async-start | bytes 17694720 | tf_op jit(solution)/shard_map/all_gather | solution.py:450
  85.1 272.6 %all-gather.10.cloned.1.call-start = ((), (), s32[]{:S(2)}) async-start(), calls=%async_computation.12 | async-start | bytes 14745600 | tf_op jit(solution)/shard_map/all_gather | solution.py:450
  87.9 61.7 %collective-permute-start = (bf16[192,2560]{1,0:T(8,128)(2,1)}, bf16[192,2560]{1,0:T(8,128)(2,1)}, u32[]{:S(2)}, u32[]{:S(2)}) collective-permute-start(bf16[192,2560]{1,0:T(8,128)(2,1)} %bitcast.1), channel_id=1, source_target_pairs={{0,2},{2,0},{1,3},{3,1},{4,6},{6,4},{5,7},{7,5},{8,10},{10,8},{9,1... | collective-permute-start | bytes 2949128 | tf_op jit(solution)/shard_map/ppermute | solution.py:98
  88.1 57.8 %all-to-all-start.1 = ((bf16[4,160,1024]{2,1,0:T(8,128)(2,1)}), bf16[4,160,1024]{2,1,0:T(8,128)(2,1)S(1)}, u32[]{:S(2)}, u32[]{:S(2)}) async-start(bf16[4,160,1024]{2,1,0:T(8,128)(2,1)} %get-tuple-element.58), calls=%async_computation.1 | async-start | bytes 2621440 | tf_op jit(solution)/shard_map/all_to_all | solution.py:143
  93.8 370.6 %all-gather.12.cloned.1.call-start = ((), (), s32[]{:S(2)}) async-start(), calls=%async_computation.13 | async-start | bytes 8847360 | tf_op jit(solution)/shard_map/all_gather | solution.py:520
  94.7 51.3 %copy-start.63 = (f32[192]{0:T(256)}, f32[192]{0:T(256)S(1)}, u32[]{:S(2)}) copy-start(f32[192]{0:T(256)S(1)} %get-tuple-element.205) | copy-start | bytes 2308
  94.8 88.1 %collective-permute-start.1 = (bf16[640,2048]{1,0:T(8,128)(2,1)}, bf16[640,2048]{1,0:T(8,128)(2,1)}, u32[]{:S(2)}, u32[]{:S(2)}) collective-permute-start(bf16[640,2048]{1,0:T(8,128)(2,1)} %bitcast.228), channel_id=1, source_target_pairs={{0,4},{4,8},{8,12},{12,0},{1,5},{5,9},{9,13},{13,1},{2,6},{6,10},{... | collective-permute-start | bytes 7864328 | tf_op jit(solution)/shard_map/ppermute | solution.py:105
  98.4 99.3 %copy-start.65 = (f32[192]{0:T(256)}, f32[192]{0:T(256)S(1)}, u32[]{:S(2)}) copy-start(f32[192]{0:T(256)S(1)} %get-tuple-element.154) | copy-start | bytes 2308
  98.7 84.1 %copy-start.23 = (bf16[192,2560]{1,0:T(8,128)(2,1)}, bf16[192,2560]{1,0:T(8,128)(2,1)S(1)}, u32[]{:S(2)}) copy-start(bf16[192,2560]{1,0:T(8,128)(2,1)S(1)} %fusion.47) | copy-start | bytes 2949124
  146.0 36.9 %collective-permute-start.2 = (bf16[640,1024]{1,0:T(8,128)(2,1)S(1)}, bf16[640,1024]{1,0:T(8,128)(2,1)}, u32[]{:S(2)}, u32[]{:S(2)}) collective-permute-start(bf16[640,1024]{1,0:T(8,128)(2,1)S(1)} %bitcast.251), channel_id=1, source_target_pairs={{0,4},{4,8},{8,12},{12,0},{1,5},{5,9},{9,13},{13,1},{2,6},{6,10},{... | collective-permute-start | bytes 3932168 | tf_op jit(solution)/shard_map/ppermute | solution.py:105
  183.5 14.1 %copy-start.54 = (bf16[192,4,4,160]{0,3,2,1:T(8,128)(2,1)}, bf16[192,4,4,160]{0,3,2,1:T(8,128)(2,1)S(1)}, u32[]{:S(2)}) copy-start(bf16[192,4,4,160]{0,3,2,1:T(8,128)(2,1)S(1)} %copy.190) | copy-start | bytes 2949124
  199.5 8.7 collective-permute-start.5
  201.4 31.4 %copy-start.55 = (bf16[192,4,4,160]{0,3,2,1:T(8,128)(2,1)S(1)}, bf16[192,4,4,160]{0,3,2,1:T(8,128)(2,1)}, u32[]{:S(2)}) copy-start(bf16[192,4,4,160]{0,3,2,1:T(8,128)(2,1)} %copy-done.54) | copy-start | bytes 2949124
  201.4 29.6 %collective-permute-start.10 = (bf16[192,512]{1,0:T(8,128)(2,1)}, bf16[192,512]{1,0:T(8,128)(2,1)S(1)}, u32[]{:S(2)}, u32[]{:S(2)}) collective-permute-start(bf16[192,512]{1,0:T(8,128)(2,1)} %pad_maximum_fusion.15), channel_id=1, source_target_pairs={{0,20},{2,22},{4,16},{6,18},{16,4},{18,6},{20,0},{22,2},{1,21},{3,... | collective-permute-start | bytes 589832 | tf_op jit(solution)/shard_map/ppermute | solution.py:125
  203.6 26.8 %collective-permute-start.9 = (bf16[192,512]{1,0:T(8,128)(2,1)}, bf16[192,512]{1,0:T(8,128)(2,1)S(1)}, u32[]{:S(2)}, u32[]{:S(2)}) collective-permute-start(bf16[192,512]{1,0:T(8,128)(2,1)} %pad_maximum_fusion.15), channel_id=1, source_target_pairs={{0,18},{2,16},{4,22},{6,20},{16,2},{18,0},{20,6},{22,4},{1,19},{3,... | collective-permute-start | bytes 589832 | tf_op jit(solution)/shard_map/ppermute | solution.py:125
  204.8 24.9 %collective-permute-start.8 = (bf16[192,512]{1,0:T(8,128)(2,1)}, bf16[192,512]{1,0:T(8,128)(2,1)S(1)}, u32[]{:S(2)}, u32[]{:S(2)}) collective-permute-start(bf16[192,512]{1,0:T(8,128)(2,1)} %pad_maximum_fusion.15), channel_id=1, source_target_pairs={{0,16},{2,18},{4,20},{6,22},{16,0},{18,2},{20,4},{22,6},{1,17},{3,... | collective-permute-start | bytes 589832 | tf_op jit(solution)/shard_map/ppermute | solution.py:125
  205.9 13.2 %collective-permute-start.7 = (bf16[192,512]{1,0:T(8,128)(2,1)}, bf16[192,512]{1,0:T(8,128)(2,1)S(1)}, u32[]{:S(2)}, u32[]{:S(2)}) collective-permute-start(bf16[192,512]{1,0:T(8,128)(2,1)} %pad_maximum_fusion.15), channel_id=1, source_target_pairs={{0,6},{2,4},{4,2},{6,0},{16,22},{18,20},{20,18},{22,16},{1,7},{3,5... | collective-permute-start | bytes 589832 | tf_op jit(solution)/shard_map/ppermute | solution.py:125
  208.2 9.5 collective-permute-start.6
  217.6 14.1 %collective-permute-start.11 = (bf16[192,512]{1,0:T(8,128)(2,1)}, bf16[192,512]{1,0:T(8,128)(2,1)S(1)}, u32[]{:S(2)}, u32[]{:S(2)}) collective-permute-start(bf16[192,512]{1,0:T(8,128)(2,1)} %pad_maximum_fusion.15), channel_id=1, source_target_pairs={{0,22},{2,20},{4,18},{6,16},{16,6},{18,4},{20,2},{22,0},{1,23},{3,... | collective-permute-start | bytes 589832 | tf_op jit(solution)/shard_map/ppermute | solution.py:125
  232.4 18.7 %collective-permute-start.12 = (bf16[8,192,512]{2,1,0:T(8,128)(2,1)}, bf16[8,192,512]{2,1,0:T(8,128)(2,1)}, u32[]{:S(2)}, u32[]{:S(2)}) collective-permute-start(bf16[8,192,512]{2,1,0:T(8,128)(2,1)} %bitcast_dynamic-update-slice_fusion), channel_id=1, source_target_pairs={{0,1},{1,0},{2,3},{3,2},{4,5},{5,4},{6,7},{7,6},{8,9},{9,8},{10,11... | collective-permute-start | bytes 4718600 | tf_op jit(solution)/shard_map/ppermute | solution.py:98
  238.8 87.6 %collective-permute-start.3 = (bf16[640,2048]{1,0:T(8,128)(2,1)}, bf16[640,2048]{1,0:T(8,128)(2,1)}, u32[]{:S(2)}, u32[]{:S(2)}) collective-permute-start(bf16[640,2048]{1,0:T(8,128)(2,1)} %collective-permute-done.1), channel_id=1, source_target_pairs={{0,4},{4,8},{8,12},{12,0},{1,5},{5,9},{9,13},{13,1},{2,6},{6,10},{... | collective-permute-start | bytes 7864328 | tf_op jit(solution)/shard_map/ppermute | solution.py:105
  249.7 76.8 %collective-permute-start.4 = (bf16[640,1024]{1,0:T(8,128)(2,1)}, bf16[640,1024]{1,0:T(8,128)(2,1)}, u32[]{:S(2)}, u32[]{:S(2)}) collective-permute-start(bf16[640,1024]{1,0:T(8,128)(2,1)} %collective-permute-done.2), channel_id=1, source_target_pairs={{0,4},{4,8},{8,12},{12,0},{1,5},{5,9},{9,13},{13,1},{2,6},{6,10},{... | collective-permute-start | bytes 3932168 | tf_op jit(solution)/shard_map/ppermute | solution.py:105
  253.6 96.4 %collective-permute-start.13 = (bf16[2,192,2560]{2,1,0:T(8,128)(2,1)}, bf16[2,192,2560]{2,1,0:T(8,128)(2,1)}, u32[]{:S(2)}, u32[]{:S(2)}) collective-permute-start(bf16[2,192,2560]{2,1,0:T(8,128)(2,1)} %pad_maximum_fusion.9), channel_id=1, source_target_pairs={{0,16},{16,0},{1,17},{17,1},{2,18},{18,2},{3,19},{19,3},{4,20},{20... | collective-permute-start | bytes 5898248 | tf_op jit(solution)/shard_map/ppermute | solution.py:98
  258.8 74.8 %copy-start.2 = (bf16[3072,256]{1,0:T(8,128)(2,1)}, bf16[3072,256]{1,0:T(8,128)(2,1)S(1)}, u32[]{:S(2)}) copy-start(bf16[3072,256]{1,0:T(8,128)(2,1)S(1)} %get-tuple-element.173.key_ref) | copy-start | bytes 4718596
  332.3 37.7 %collective-permute-start.14 = (bf16[640,1024]{1,0:T(8,128)(2,1)}, bf16[640,1024]{1,0:T(8,128)(2,1)}, u32[]{:S(2)}, u32[]{:S(2)}) collective-permute-start(bf16[640,1024]{1,0:T(8,128)(2,1)} %get-tuple-element.181), channel_id=1, source_target_pairs={{0,4},{4,8},{8,12},{12,0},{1,5},{5,9},{9,13},{13,1},{2,6},{6,10},{... | collective-permute-start | bytes 3932168 | tf_op jit(solution)/shard_map/ppermute | solution.py:105
  370.0 393.9 %reduce-scatter.9.cloned.1.call-start = ((), (), s32[]{:S(2)}) async-start(), calls=%async_computation.17 | async-start | bytes 6553600 | tf_op jit(solution)/shard_map/reduce_scatter | solution.py:526
  370.0 65.2 %collective-permute-start.16 = (bf16[2,2,192,2560]{3,2,1,0:T(8,128)(2,1)}, bf16[2,2,192,2560]{3,2,1,0:T(8,128)(2,1)}, u32[]{:S(2)}, u32[]{:S(2)}) collective-permute-start(bf16[2,2,192,2560]{3,2,1,0:T(8,128)(2,1)} %pad_maximum_fusion.3), channel_id=1, source_target_pairs={{0,1},{1,0},{2,3},{3,2},{4,5},{5,4},{6,7},{7,6},{8,9},{9,8},{10,11... | collective-permute-start | bytes 11796488 | tf_op jit(solution)/shard_map/ppermute | solution.py:98
  371.3 30.7 %collective-permute-start.15 = (bf16[640,1024]{1,0:T(8,128)(2,1)}, bf16[640,1024]{1,0:T(8,128)(2,1)S(1)}, u32[]{:S(2)}, u32[]{:S(2)}) collective-permute-start(bf16[640,1024]{1,0:T(8,128)(2,1)} %collective-permute-done.4), channel_id=1, source_target_pairs={{0,4},{4,8},{8,12},{12,0},{1,5},{5,9},{9,13},{13,1},{2,6},{6,10},{... | collective-permute-start | bytes 3932168 | tf_op jit(solution)/shard_map/ppermute | solution.py:105
  372.6 57.6 %collective-permute-start.17 = (bf16[640,1024]{1,0:T(8,128)(2,1)S(1)}, bf16[640,1024]{1,0:T(8,128)(2,1)}, u32[]{:S(2)}, u32[]{:S(2)}) collective-permute-start(bf16[640,1024]{1,0:T(8,128)(2,1)S(1)} %copy-done.53), channel_id=1, source_target_pairs={{0,4},{4,8},{8,12},{12,0},{1,5},{5,9},{9,13},{13,1},{2,6},{6,10},{... | collective-permute-start | bytes 3932168 | tf_op jit(solution)/shard_map/ppermute | solution.py:105
  396.2 39.0 %copy-start.21 = (bf16[1,2,192,2560]{3,2,1,0:T(8,128)(2,1)S(1)}, bf16[1,2,192,2560]{3,2,1,0:T(8,128)(2,1)}, u32[]{:S(2)}) copy-start(bf16[1,2,192,2560]{3,2,1,0:T(8,128)(2,1)} %copy-done.20) | copy-start | bytes 5898244
  439.4 13.3 %slice-start.3 = ((s8[5242880]{0:T(1024)(128)(4,1)}), s8[1048576]{0:T(1024)(128)(4,1)S(1)}, s32[]{:S(2)}) async-start(s8[5242880]{0:T(1024)(128)(4,1)} %bitcast.249), calls=%async_computation.22 | async-start | bytes 2097152
  504.1 259.8 %reduce-scatter.11.cloned.1.call-start = ((), (), s32[]{:S(2)}) async-start(), calls=%async_computation.18 | async-start | bytes 6553600 | tf_op jit(solution)/shard_map/reduce_scatter | solution.py:526
  504.2 11.9 %slice-start = ((s8[10485760]{0:T(1024)(128)(4,1)}), s8[4194304]{0:T(1024)(128)(4,1)S(1)}, s32[]{:S(2)}) async-start(s8[10485760]{0:T(1024)(128)(4,1)} %bitcast.236), calls=%async_computation.19 | async-start | bytes 8388608
  504.2 11.9 %slice-start.1 = ((s8[10485760]{0:T(1024)(128)(4,1)}), s8[4194304]{0:T(1024)(128)(4,1)S(1)}, s32[]{:S(2)}) async-start(s8[10485760]{0:T(1024)(128)(4,1)} %bitcast.236), calls=%async_computation.20 | async-start | bytes 8388608
  526.1 7.6 collective-permute-start.18
  549.7 24.2 %collective-permute-start.20 = (bf16[192,2560]{1,0:T(8,128)(2,1)}, bf16[192,2560]{1,0:T(8,128)(2,1)}, u32[]{:S(2)}, u32[]{:S(2)}) collective-permute-start(bf16[192,2560]{1,0:T(8,128)(2,1)} %get-tuple-element.165), channel_id=1, source_target_pairs={{0,16},{2,18},{16,0},{18,2},{1,17},{3,19},{17,1},{19,3},{4,20},{6,... | collective-permute-start | bytes 2949128 | tf_op jit(solution)/shard_map/ppermute | solution.py:556
  551.8 22.9 %collective-permute-start.19 = (bf16[192,2560]{1,0:T(8,128)(2,1)}, bf16[192,2560]{1,0:T(8,128)(2,1)}, u32[]{:S(2)}, u32[]{:S(2)}) collective-permute-start(bf16[192,2560]{1,0:T(8,128)(2,1)} %get-tuple-element.167), channel_id=1, source_target_pairs={{0,2},{2,0},{16,18},{18,16},{1,3},{3,1},{17,19},{19,17},{4,6},{6,4... | collective-permute-start | bytes 2949128 | tf_op jit(solution)/shard_map/ppermute | solution.py:556
  552.5 22.2 %copy-start.31 = (bf16[1536,2048]{1,0:T(8,128)(2,1)}, bf16[1536,2048]{1,0:T(8,128)(2,1)S(1)}, u32[]{:S(2)}) copy-start(bf16[1536,2048]{1,0:T(8,128)(2,1)S(1)} %pad_maximum_fusion.1) | copy-start | bytes 18874372
  587.1 236.7 %reduce-scatter.7.cloned.1.call-start = ((), (), s32[]{:S(2)}) async-start(), calls=%async_computation.16 | async-start | bytes 6553600 | tf_op jit(solution)/shard_map/reduce_scatter | solution.py:526
  601.1 277.8 %all-gather.14.cloned.1.call-start = ((), (), s32[]{:S(2)}) async-start(), calls=%async_computation.15 | async-start | bytes 8847360 | tf_op jit(solution)/shard_map/all_gather | solution.py:565
  602.3 22.7 %collective-permute-start.21 = (bf16[192,2560]{1,0:T(8,128)(2,1)S(1)}, bf16[192,2560]{1,0:T(8,128)(2,1)S(1)}, u32[]{:S(2)}, u32[]{:S(2)}) collective-permute-start(bf16[192,2560]{1,0:T(8,128)(2,1)S(1)} %copy-done.59), channel_id=1, source_target_pairs={{0,18},{2,16},{16,2},{18,0},{1,19},{3,17},{17,3},{19,1},{4,22},{6,... | collective-permute-start | bytes 2949128 | tf_op jit(solution)/shard_map/ppermute | solution.py:556
  605.0 22.3 %copy-start.9 = (bf16[1,1,192,2560]{3,2,1,0:T(8,128)(2,1)S(1)}, bf16[1,1,192,2560]{3,2,1,0:T(8,128)(2,1)}, u32[]{:S(2)}) copy-start(bf16[1,1,192,2560]{3,2,1,0:T(8,128)(2,1)} %param.15) | copy-start | bytes 2949124
  605.0 22.3 %copy-start.15 = (f32[192,1280]{1,0:T(8,128)S(1)}, f32[192,1280]{1,0:T(8,128)}, u32[]{:S(2)}) copy-start(f32[192,1280]{1,0:T(8,128)} %copy-done.14) | copy-start | bytes 2949124
  605.0 22.3 %copy-start.18 = (f32[192,1280]{1,0:T(8,128)S(1)}, f32[192,1280]{1,0:T(8,128)}, u32[]{:S(2)}) copy-start(f32[192,1280]{1,0:T(8,128)} %copy-done.17) | copy-start | bytes 2949124
  628.5 21.0 %collective-permute-start.22 = (bf16[192,2560]{1,0:T(8,128)(2,1)S(1)}, bf16[192,2560]{1,0:T(8,128)(2,1)}, u32[]{:S(2)}, u32[]{:S(2)}) collective-permute-start(bf16[192,2560]{1,0:T(8,128)(2,1)S(1)} %copy-done.24), channel_id=1, source_target_pairs={{0,2},{2,0},{1,3},{3,1},{4,6},{6,4},{5,7},{7,5},{8,10},{10,8},{9,1... | collective-permute-start | bytes 2949128 | tf_op jit(solution)/shard_map/ppermute | solution.py:98
  653.2 42.6 %collective-permute-start.23 = (bf16[2,192,2560]{2,1,0:T(8,128)(2,1)}, bf16[2,192,2560]{2,1,0:T(8,128)(2,1)}, u32[]{:S(2)}, u32[]{:S(2)}) collective-permute-start(bf16[2,192,2560]{2,1,0:T(8,128)(2,1)} %pad_maximum_fusion.10), channel_id=1, source_target_pairs={{0,16},{16,0},{1,17},{17,1},{2,18},{18,2},{3,19},{19,3},{4,20},{20... | collective-permute-start | bytes 5898248 | tf_op jit(solution)/shard_map/ppermute | solution.py:98
  701.1 6.8 collective-permute-start.24
  704.6 46.5 %collective-permute-start.29 = (bf16[2,2,192,2560]{3,2,1,0:T(8,128)(2,1)}, bf16[2,2,192,2560]{3,2,1,0:T(8,128)(2,1)}, u32[]{:S(2)}, u32[]{:S(2)}) collective-permute-start(bf16[2,2,192,2560]{3,2,1,0:T(8,128)(2,1)} %pad_maximum_fusion.4), channel_id=1, source_target_pairs={{0,1},{1,0},{2,3},{3,2},{4,5},{5,4},{6,7},{7,6},{8,9},{9,8},{10,11... | collective-permute-start | bytes 11796488 | tf_op jit(solution)/shard_map/ppermute | solution.py:90
  711.4 19.1 %collective-permute-start.25 = (bf16[2,192,512]{2,1,0:T(8,128)(2,1)}, bf16[2,192,512]{2,1,0:T(8,128)(2,1)}, u32[]{:S(2)}, u32[]{:S(2)}) collective-permute-start(bf16[2,192,512]{2,1,0:T(8,128)(2,1)} %get-tuple-element.188), channel_id=1, source_target_pairs={{0,2},{2,0},{16,18},{18,16},{1,3},{3,1},{17,19},{19,17},{4,6},{6,4... | collective-permute-start | bytes 1179656 | tf_op jit(solution)/shard_map/ppermute | solution.py:137
  711.7 18.7 %collective-permute-start.27 = (bf16[2,192,512]{2,1,0:T(8,128)(2,1)}, bf16[2,192,512]{2,1,0:T(8,128)(2,1)}, u32[]{:S(2)}, u32[]{:S(2)}) collective-permute-start(bf16[2,192,512]{2,1,0:T(8,128)(2,1)} %get-tuple-element.189), channel_id=1, source_target_pairs={{0,18},{2,16},{16,2},{18,0},{1,19},{3,17},{17,3},{19,1},{4,22},{6,... | collective-permute-start | bytes 1179656 | tf_op jit(solution)/shard_map/ppermute | solution.py:137
  713.3 18.1 %collective-permute-start.26 = (bf16[2,192,512]{2,1,0:T(8,128)(2,1)S(1)}, bf16[2,192,512]{2,1,0:T(8,128)(2,1)}, u32[]{:S(2)}, u32[]{:S(2)}) collective-permute-start(bf16[2,192,512]{2,1,0:T(8,128)(2,1)S(1)} %get-tuple-element.190), channel_id=1, source_target_pairs={{0,16},{2,18},{16,0},{18,2},{1,17},{3,19},{17,1},{19,3},{4,20},{6,... | collective-permute-start | bytes 1179656 | tf_op jit(solution)/shard_map/ppermute | solution.py:137
  715.4 21.2 %copy-start.58 = (f32[192,128]{0,1:T(8,128)S(1)}, f32[192,128]{0,1:T(8,128)}, u32[]{:S(2)}) copy-start(f32[192,128]{0,1:T(8,128)} %copy-done.57) | copy-start | bytes 294916
  715.4 21.2 %copy-start.60 = (f32[192,128]{0,1:T(8,128)S(1)}, f32[192,128]{0,1:T(8,128)}, u32[]{:S(2)}) copy-start(f32[192,128]{0,1:T(8,128)} %copy.208) | copy-start | bytes 294916
  733.7 15.2 %collective-permute-start.28 = (bf16[192,512]{1,0:T(8,128)(2,1)}, bf16[192,512]{1,0:T(8,128)(2,1)}, u32[]{:S(2)}, u32[]{:S(2)}) collective-permute-start(bf16[192,512]{1,0:T(8,128)(2,1)} %dynamic-slice_bitcast_fusion.7), channel_id=1, source_target_pairs={{0,4},{4,0},{1,5},{5,1},{2,6},{6,2},{3,7},{7,3},{8,12},{12,8},{9,1... | collective-permute-start | bytes 589832 | tf_op jit(solution)/shard_map/ppermute | solution.py:90
  754.8 36.6 %all-to-all-start.2 = ((bf16[8,192,704]{2,1,0:T(8,128)(2,1)}), bf16[8,192,704]{2,1,0:T(8,128)(2,1)S(1)}, u32[]{:S(2)}, u32[]{:S(2)}) async-start(bf16[8,192,704]{2,1,0:T(8,128)(2,1)} %maximum_bitcast_fusion), calls=%async_computation.2 | async-start | bytes 4718592 | tf_op jit(solution)/shard_map/all_to_all | solution.py:143
  792.8 44.6 %all-to-all-start.3 = ((bf16[4,160,2048]{2,1,0:T(8,128)(2,1)}), bf16[4,160,2048]{2,1,0:T(8,128)(2,1)S(1)}, u32[]{:S(2)}, u32[]{:S(2)}) async-start(bf16[4,160,2048]{2,1,0:T(8,128)(2,1)} %bitcast.231), calls=%async_computation.7 | async-start | bytes 5242880 | tf_op jit(solution)/shard_map/all_to_all | solution.py:143
  797.5 287.0 %reduce-scatter.5.cloned.1.call-start = ((), (), s32[]{:S(2)}) async-start(), calls=%async_computation.14 | async-start | bytes 8847360 | tf_op jit(solution)/shard_map/reduce_scatter | solution.py:642
  837.4 49.9 %all-to-all-start.4 = ((bf16[4,160,1024]{2,1,0:T(8,128)(2,1)}), bf16[4,160,1024]{2,1,0:T(8,128)(2,1)}, u32[]{:S(2)}, u32[]{:S(2)}) async-start(bf16[4,160,1024]{2,1,0:T(8,128)(2,1)} %bitcast.264), calls=%async_computation.8 | async-start | bytes 2621440 | tf_op jit(solution)/shard_map/all_to_all | solution.py:143
  893.7 130.5 %all-to-all-start.5 = ((bf16[16,160,704]{2,1,0:T(8,128)(2,1)}), bf16[16,160,704]{2,1,0:T(8,128)(2,1)}, u32[]{:S(2)}, u32[]{:S(2)}) async-start(bf16[16,160,704]{2,1,0:T(8,128)(2,1)} %bitcast.224), calls=%async_computation.9 | async-start | bytes 7864320 | tf_op jit(solution)/shard_map/all_to_all | solution.py:143
  899.7 88.5 %collective-permute-start.30 = (bf16[4,160,2048]{2,1,0:T(8,128)(2,1)S(1)}, bf16[4,160,2048]{2,1,0:T(8,128)(2,1)}, u32[]{:S(2)}, u32[]{:S(2)}) collective-permute-start(bf16[4,160,2048]{2,1,0:T(8,128)(2,1)S(1)} %all-to-all-done.3.refs_1_), channel_id=1, source_target_pairs={{0,16},{16,0},{1,17},{17,1},{2,18},{18,2},{3,19},{19,3},{4,20},{20... | collective-permute-start | bytes 7864328 | tf_op jit(solution)/shard_map/ppermute | solution.py:90
  903.7 84.5 %copy-start.1 = (f32[160,1]{1,0:T(8,128)S(1)}, f32[160,1]{1,0:T(8,128)}, u32[]{:S(2)}) copy-start(f32[160,1]{1,0:T(8,128)} %copy-done) | copy-start | bytes 1924
  903.7 143.8 %collective-permute-start.32 = (bf16[4,160,1024]{2,1,0:T(8,128)(2,1)}, bf16[4,160,1024]{2,1,0:T(8,128)(2,1)}, u32[]{:S(2)}, u32[]{:S(2)}) collective-permute-start(bf16[4,160,1024]{2,1,0:T(8,128)(2,1)} %all-to-all-done.4.refs_1_), channel_id=1, source_target_pairs={{0,16},{16,0},{1,17},{17,1},{2,18},{18,2},{3,19},{19,3},{4,20},{20... | collective-permute-start | bytes 3932168 | tf_op jit(solution)/shard_map/ppermute | solution.py:90
  1028.3 38.6 %collective-permute-start.31 = (bf16[4,160,704]{2,1,0:T(8,128)(2,1)}, bf16[4,160,704]{2,1,0:T(8,128)(2,1)}, u32[]{:S(2)}, u32[]{:S(2)}) collective-permute-start(bf16[4,160,704]{2,1,0:T(8,128)(2,1)} %reduce_sum.111), channel_id=1, source_target_pairs={{0,16},{16,0},{1,17},{17,1},{2,18},{18,2},{3,19},{19,3},{4,20},{20... | collective-permute-start | bytes 2703368 | tf_op jit(solution)/shard_map/ppermute | solution.py:98
  (69 other events, 321.2 us)
Sparse Core Ops, SparseCore 0:
  12.4 69.7 all-gather.5
  85.2 107.3 all-gather.7
  195.1 116.5 all-gather.9
  370.1 56.4 all-gather.11
  504.2 97.4 reduce-scatter.8
  604.5 94.2 reduce-scatter.10
  701.7 96.4 reduce-scatter.6
  800.1 78.7 all-gather.13
  882.3 109.7 reduce-scatter.4
